TPU v7x, 32 devices: a whole 2x2x4 slice. The times are simulated.
32 devices in a mesh: loop: 2 (over x), row: 4 (over y, core), col: 4 (over z).
Axes of the slice: x: 2, y: 2, z: 4, core: 2. Of those that a mesh axis runs over, the one named last changes fastest.
Arguments:
- interval_blocks: bfloat16 [2, 4, 2048, 2048], P('loop', None, 'row', 'col'), may hold values from -0.15625 to 0.15625
- interval_pivots: int32 [2, 3, 2048], P('loop'), may hold values from 0 to 2047, each once within a row
- boundary_pivots: int32 [2, 2048], replicated, may hold values from 0 to 2047, each once within a row
- interval_residuals: bfloat16 [2, 4, 2048], P('loop', None, ('row', 'col')), may hold values from -0.23925781 to 0.23925781
Outputs:
- reduced_block: bfloat16 [2, 2048, 2048], P('loop', 'row', 'col')
- reduced_rhs: float32 [2, 2048], P('loop', ('row', 'col'))
Inputs may be any that keep to these rules, and one draw needn't show every extreme that they name: Each row of interval_pivots is a permutation of 0 to 2047. Each row of boundary_pivots is a permutation of 0 to 2047.
All inputs are finite; a program needn't handle non-finite values.
Results may differ from a plain program's by a relative error of at most 0.018.
Values may be sent and summed in bfloat16 or wider, within the bound.
No kernel may reach another device: no remote copies, remote signals or barrier semaphores. Data moves between devices by JAX's collectives and lax.ppermute only.
A program may use at most 64 MiB of HBM per device.

v0:
```python
import jax
import jax.numpy as jnp
from jax import lax
from jax.sharding import PartitionSpec as P


def from_behind(value, axis, by):
    devices = lax.axis_size(axis)
    return lax.ppermute(value, axis, [(i, (i + by) % devices) for i in range(devices)])


def compose(left_block, right_block, right_vector, pivots, added):
    column_panel = lax.all_gather(right_block, "row", axis=0, tiled=True)
    full_vector = lax.all_gather(right_vector, ("row", "col"), axis=0, tiled=True)
    permuted = jnp.take(column_panel, pivots, axis=0)
    moved = jnp.take(full_vector, pivots, axis=0)
    segment = lax.all_gather(left_block, "col", axis=1, tiled=True)
    product = jnp.dot(segment, permuted, preferred_element_type=jnp.float32)
    applied = jnp.dot(segment, moved, preferred_element_type=jnp.float32)
    share_size = added.shape[0]
    own_part = lax.dynamic_slice_in_dim(applied, lax.axis_index("col") * share_size, share_size, 0)
    return (product, own_part + added.astype(jnp.float32))


def shards(interval_blocks, interval_pivots, boundary_pivots, interval_residuals):
    blocks = interval_blocks[0]
    pivot_rows = interval_pivots[0]
    residuals = interval_residuals[0]
    matrix = blocks[0]
    vector = residuals[0]
    for interval in range(1, blocks.shape[0]):
        product, applied = compose(
            blocks[interval], matrix, vector, pivot_rows[interval - 1], residuals[interval]
        )
        matrix = product.astype(jnp.bfloat16)
        vector = applied.astype(jnp.bfloat16)
    position = lax.axis_index("loop")
    count_loop = lax.axis_size("loop")
    own_pivots = lax.dynamic_index_in_dim(boundary_pivots, position, 0, keepdims=False)
    back_pivots = lax.dynamic_index_in_dim(
        boundary_pivots, (position + count_loop - 1) % count_loop, 0, keepdims=False
    )
    earlier, earlier_vector = from_behind((matrix, vector), "loop", 1)
    product, applied = compose(matrix, earlier, earlier_vector, own_pivots, vector)
    halved = product.astype(jnp.bfloat16)
    halved_vector = applied.astype(jnp.bfloat16)
    distant, distant_vector = from_behind((halved, halved_vector), "loop", 2)
    reduced, reduced_vector = compose(halved, distant, distant_vector, back_pivots, halved_vector)
    return (reduced.astype(jnp.bfloat16)[None], reduced_vector[None])


def solution(mesh):
    placed = (
        P("loop", None, "row", "col"),
        P("loop", None, None),
        P(),
        P("loop", None, ("row", "col")),
    )
    return jax.shard_map(
        shards,
        mesh=mesh,
        in_specs=placed,
        out_specs=(P("loop", "row", "col"), P("loop", ("row", "col"))),
        check_vma=False,
    )
```

profile of v0, /device:TPU:0, one launch (start us, length us, event | category | flops | bytes accessed | tf_op | source)
XLA Modules:
  0.0 410.5 jit_solution(16464463368672821712)
XLA Ops:
  7.2 2.8 fusion.83
  10.9 33.7 %all-gather.4 = bf16[1,1,2048]{2,1,0:T(2,128)(2,1)S(1)} all-gather(bf16[1,1,128]{2,1,0:T(2,128)(2,1)S(1)} %slice.51), channel_id=6, replica_groups=mesh['loop'=2,'row'=4,'col'=4] {'row','col'}, dimensions={2}, use_global_device_ids=true | all-gather | bytes 4352 | tf_op jit(solution)/shard_map/all_gather | solution.py:14
  44.6 13.1 %gather_fusion.5 = bf16[2048]{0:T(1024)(128)(2,1)S(1)} fusion(bf16[2048]{0:T(1024)(128)(2,1)S(1)} %reduce, s32[2048]{0:T(1024)S(1)} %fusion.68), kind=kCustom, calls=%fused_computation.1.clone | custom fusion | bytes 16384 | tf_op jit(solution)/shard_map/jit(_take)/gather | solution.py:16
  57.8 9.5 %gather_fusion = bf16[2048,512]{1,0:T(8,128)(2,1)S(1)} fusion(bf16[2048,512]{1,0:T(8,128)(2,1)} %bitcast.80, s32[2048]{0:T(1024)S(1)} %fusion.68), kind=kCustom, calls=%fused_computation.clone | custom fusion | bytes 4202496 | tf_op jit(solution)/shard_map/jit(_take)/gather | solution.py:15
  67.2 15.8 %all-gather.34.cloned.1.call-done = bf16[1,1,512,2048]{3,2,1,0:T(8,128)(2,1)} async-done(((bf16[1,1,512,512]{3,2,1,0:T(8,128)(2,1)}), bf16[1,1,512,2048]{3,2,1,0:T(8,128)(2,1)}) %all-gather.34.cloned.1.call-update) | async-done | bytes 2097168 | tf_op jit(solution)/shard_map/all_gather | solution.py:17
  83.1 4.1 fusion.55
  87.8 2.2 fusion.8
  90.2 29.9 %all-gather.5 = bf16[16,1,128]{2,1,0:T(2,128)(2,1)S(1)} all-gather(bf16[1,1,128]{2,1,0:T(2,128)(2,1)S(1)} %fusion.77), channel_id=1, replica_groups=mesh['loop'=2,'row'=4,'col'=4] {'row','col'}, dimensions={0}, use_global_device_ids=true | all-gather | bytes 4352 | tf_op jit(solution)/shard_map/all_gather | solution.py:14
  120.1 13.1 %gather_fusion.6 = bf16[2048]{0:T(1024)(128)(2,1)S(1)} fusion(bf16[2048]{0:T(1024)(128)(2,1)S(1)} %bitcast.77, s32[2048]{0:T(1024)S(1)} %fusion.69), kind=kCustom, calls=%fused_computation.6.clone | custom fusion | bytes 16384 | tf_op jit(solution)/shard_map/jit(_take)/gather | solution.py:16
  133.2 2.9 copy.8
  136.1 9.2 %gather_fusion.1 = bf16[2048,512]{1,0:T(8,128)(2,1)} fusion(bf16[2048,512]{1,0:T(8,128)(2,1)S(1)} %copy.8, s32[2048]{0:T(1024)S(1)} %fusion.69), kind=kCustom, calls=%fused_computation.2.clone | custom fusion | bytes 4202496 | tf_op jit(solution)/shard_map/jit(_take)/gather | solution.py:15
  145.3 10.8 %all-gather.36.cloned.1.call-done = bf16[1,1,512,2048]{3,2,1,0:T(8,128)(2,1)} async-done(((bf16[1,1,512,512]{3,2,1,0:T(8,128)(2,1)}), bf16[1,1,512,2048]{3,2,1,0:T(8,128)(2,1)}) %all-gather.36.cloned.1.call-update) | async-done | bytes 2097168 | tf_op jit(solution)/shard_map/all_gather | solution.py:17
  156.1 4.8 %fusion.50 = bf16[512,512]{0,1:T(8,128)(2,1)} fusion(bf16[1,1,512,2048]{3,2,1,0:T(8,128)(2,1)} %all-gather.36.cloned.1.call-done, bf16[2048,512]{1,0:T(8,128)(2,1)} %gather_fusion.1, pred[2048]{0:T(1024)(128)(4,1)S(1)} %get-tuple-element.11), kind=kOutput, calls=%fused_computation.40 | convolution fusion | flops 1075052544 | bytes 4720640 | tf_op jit(solution)/shard_map/dot_general | solution.py:18
  162.3 29.9 %all-gather.6 = bf16[16,1,128]{2,1,0:T(2,128)(2,1)S(1)} all-gather(bf16[1,1,128]{2,1,0:T(2,128)(2,1)S(1)} %fusion.75), channel_id=1, replica_groups=mesh['loop'=2,'row'=4,'col'=4] {'row','col'}, dimensions={0}, use_global_device_ids=true | all-gather | bytes 4352 | tf_op jit(solution)/shard_map/all_gather | solution.py:14
  192.3 13.1 %gather_fusion.7 = bf16[2048]{0:T(1024)(128)(2,1)S(1)} fusion(bf16[2048]{0:T(1024)(128)(2,1)S(1)} %bitcast.78, s32[2048]{0:T(1024)S(1)} %fusion.70), kind=kCustom, calls=%fused_computation.7.clone | custom fusion | bytes 16384 | tf_op jit(solution)/shard_map/jit(_take)/gather | solution.py:16
  205.4 2.9 copy.9
  208.3 9.2 %gather_fusion.2 = bf16[2048,512]{1,0:T(8,128)(2,1)} fusion(bf16[2048,512]{1,0:T(8,128)(2,1)S(1)} %copy.9, s32[2048]{0:T(1024)S(1)} %fusion.70), kind=kCustom, calls=%fused_computation.3.clone | custom fusion | bytes 4202496 | tf_op jit(solution)/shard_map/jit(_take)/gather | solution.py:15
  217.5 12.4 %all-gather.38.cloned.1.call-done = bf16[1,1,512,2048]{3,2,1,0:T(8,128)(2,1)} async-done(((bf16[1,1,512,512]{3,2,1,0:T(8,128)(2,1)}), bf16[1,1,512,2048]{3,2,1,0:T(8,128)(2,1)}) %all-gather.38.cloned.1.call-update) | async-done | bytes 2097168 | tf_op jit(solution)/shard_map/all_gather | solution.py:17
  229.8 4.0 fusion.45
  235.4 12.2 %collective-permute-done = bf16[512,512]{0,1:T(8,128)(2,1)S(1)} collective-permute-done((bf16[512,512]{0,1:T(8,128)(2,1)S(1)}, bf16[512,512]{0,1:T(8,128)(2,1)S(1)}, u32[]{:S(2)}, u32[]{:S(2)}) %collective-permute-start) | collective-permute-done | bytes 524320 | tf_op jit(solution)/shard_map/ppermute | solution.py:9
  253.5 28.4 %all-gather.7 = bf16[16,1,128]{2,1,0:T(2,128)(2,1)S(1)} all-gather(bf16[1,1,128]{2,1,0:T(2,128)(2,1)S(1)} %bitcast.97), channel_id=1, replica_groups=mesh['loop'=2,'row'=4,'col'=4] {'row','col'}, dimensions={0}, use_global_device_ids=true | all-gather | bytes 4352 | tf_op jit(solution)/shard_map/all_gather | solution.py:14
  282.0 13.1 %gather_fusion.8 = bf16[2048]{0:T(1024)(128)(2,1)S(1)} fusion(bf16[2048]{0:T(1024)(128)(2,1)S(1)} %bitcast.79, s32[2048]{0:T(1024)S(1)} %fusion.71), kind=kCustom, calls=%fused_computation.8.clone | custom fusion | bytes 16384 | tf_op jit(solution)/shard_map/jit(_take)/gather | solution.py:16
  295.2 2.9 copy.10
  298.0 9.2 %gather_fusion.3 = bf16[2048,512]{1,0:T(8,128)(2,1)} fusion(bf16[2048,512]{1,0:T(8,128)(2,1)S(1)} %copy.10, s32[2048]{0:T(1024)S(1)} %fusion.71), kind=kCustom, calls=%fused_computation.4.clone | custom fusion | bytes 4202496 | tf_op jit(solution)/shard_map/jit(_take)/gather | solution.py:15
  307.2 11.0 %all-gather.24.cloned.1.call-done = bf16[512,2048]{0,1:T(8,128)(2,1)} async-done(((bf16[512,512]{0,1:T(8,128)(2,1)}), bf16[512,2048]{0,1:T(8,128)(2,1)}) %all-gather.24.cloned.1.call-update) | async-done | bytes 2097168 | tf_op jit(solution)/shard_map/all_gather | solution.py:17
  318.2 4.5 %fusion.24 = bf16[512,512]{1,0:T(8,128)(2,1)} fusion(bf16[512,2048]{0,1:T(8,128)(2,1)} %all-gather.24.cloned.1.call-done, bf16[2048,512]{1,0:T(8,128)(2,1)} %gather_fusion.3, pred[2048]{0:T(1024)(128)(4,1)S(1)} %get-tuple-element.7), kind=kOutput, calls=%fused_computation.34 | convolution fusion | flops 1075052544 | bytes 4720640 | tf_op jit(solution)/shard_map/dot_general | solution.py:18
  325.2 30.5 %all-gather.8 = bf16[16,1,128]{2,1,0:T(2,128)(2,1)S(1)} all-gather(bf16[1,1,128]{2,1,0:T(2,128)(2,1)S(1)} %bitcast.96), channel_id=1, replica_groups=mesh['loop'=2,'row'=4,'col'=4] {'row','col'}, dimensions={0}, use_global_device_ids=true | all-gather | bytes 4352 | tf_op jit(solution)/shard_map/all_gather | solution.py:14
  355.7 13.1 %gather_fusion.9 = bf16[2048]{0:T(1024)(128)(2,1)S(1)} fusion(bf16[2048]{0:T(1024)(128)(2,1)S(1)} %bitcast.76, s32[2048]{0:T(1024)S(1)} %fusion.72), kind=kCustom, calls=%fused_computation.9.clone | custom fusion | bytes 16384 | tf_op jit(solution)/shard_map/jit(_take)/gather | solution.py:16
  368.9 2.2 fusion.86
  371.7 18.8 %all-gather.30.cloned.1.call-done = bf16[2048,512]{1,0:T(8,128)(2,1)} async-done(((bf16[512,512]{1,0:T(8,128)(2,1)}), bf16[2048,512]{1,0:T(8,128)(2,1)}) %all-gather.30.cloned.1.call-update) | async-done | bytes 2097168 | tf_op jit(solution)/shard_map/all_gather | solution.py:13
  390.5 9.4 %gather_fusion.4 = bf16[2048,512]{1,0:T(8,128)(2,1)S(1)} fusion(bf16[2048,512]{1,0:T(8,128)(2,1)} %all-gather.30.cloned.1.call-done, s32[2048]{0:T(1024)S(1)} %fusion.72), kind=kCustom, calls=%fused_computation.5.clone | custom fusion | bytes 4202496 | tf_op jit(solution)/shard_map/jit(_take)/gather | solution.py:15
  400.0 3.7 fusion.60
  (81 shorter events, 13.7 us)
Async XLA Ops:
  7.2 3.7 copy-start.8
  7.2 37.4 %copy-start.6 = (s32[1,3,2048]{2,0,1:T(1,128)S(1)}, s32[1,3,2048]{2,0,1:T(1,128)}, u32[]{:S(2)}) copy-start(s32[1,3,2048]{2,0,1:T(1,128)} %param.9) | copy-start | bytes 73732
  7.2 50.6 %all-gather.32.cloned.1.call-start = ((), (), s32[]{:S(2)}) async-start(), calls=%async_computation.6 | async-start | bytes 2621440 | tf_op jit(solution)/shard_map/all_gather | solution.py:13
  10.1 73.0 %all-gather.34.cloned.1.call-start = ((), (), s32[]{:S(2)}) async-start(), calls=%async_computation.7 | async-start | bytes 2621440 | tf_op jit(solution)/shard_map/all_gather | solution.py:17
  10.9 122.4 %all-gather.20.cloned.1.call-start = ((), (), s32[]{:S(2)}) async-start(), calls=%async_computation | async-start | bytes 2621440 | tf_op jit(solution)/shard_map/all_gather | solution.py:13
  87.2 68.9 %all-gather.36.cloned.1.call-start = ((), (), s32[]{:S(2)}) async-start(), calls=%async_computation.8 | async-start | bytes 2621440 | tf_op jit(solution)/shard_map/all_gather | solution.py:17
  87.7 117.6 %all-gather.22.cloned.1.call-start = ((), (), s32[]{:S(2)}) async-start(), calls=%async_computation.1 | async-start | bytes 2621440 | tf_op jit(solution)/shard_map/all_gather | solution.py:13
  156.1 5.5 %copy-start.2 = (bf16[1,1,512,2048]{3,2,1,0:T(8,128)(2,1)S(1)}, bf16[1,1,512,2048]{3,2,1,0:T(8,128)(2,1)}, u32[]{:S(2)}) copy-start(bf16[1,1,512,2048]{3,2,1,0:T(8,128)(2,1)} %all-gather.36.cloned.1.call-done) | copy-start | bytes 6291460
  160.9 68.9 %all-gather.38.cloned.1.call-start = ((), (), s32[]{:S(2)}) async-start(), calls=%async_computation.9 | async-start | bytes 2621440 | tf_op jit(solution)/shard_map/all_gather | solution.py:17
  161.5 133.7 %all-gather.26.cloned.1.call-start = ((), (), s32[]{:S(2)}) async-start(), calls=%async_computation.3 | async-start | bytes 2621440 | tf_op jit(solution)/shard_map/all_gather | solution.py:13
  229.8 19.4 %copy-start.7 = (s32[2,2048]{1,0:T(2,128)S(1)}, s32[2,2048]{1,0:T(2,128)}, u32[]{:S(2)}) copy-start(s32[2,2048]{1,0:T(2,128)} %param.10) | copy-start | bytes 49156
  229.8 19.4 %copy-start.1 = (bf16[1,1,512,2048]{3,2,1,0:T(8,128)(2,1)S(1)}, bf16[1,1,512,2048]{3,2,1,0:T(8,128)(2,1)}, u32[]{:S(2)}) copy-start(bf16[1,1,512,2048]{3,2,1,0:T(8,128)(2,1)} %all-gather.38.cloned.1.call-done) | copy-start | bytes 6291460
  233.9 14.6 %copy-start.3 = (bf16[512,512]{0,1:T(8,128)(2,1)}, bf16[512,512]{0,1:T(8,128)(2,1)S(1)}, u32[]{:S(2)}) copy-start(bf16[512,512]{0,1:T(8,128)(2,1)S(1)} %fusion.45) | copy-start | bytes 1572868
  233.9 13.7 %collective-permute-start = (bf16[512,512]{0,1:T(8,128)(2,1)S(1)}, bf16[512,512]{0,1:T(8,128)(2,1)S(1)}, u32[]{:S(2)}, u32[]{:S(2)}) collective-permute-start(bf16[512,512]{0,1:T(8,128)(2,1)S(1)} %fusion.45), channel_id=1, source_target_pairs={{0,16},{16,0},{1,17},{17,1},{2,18},{18,2},{3,19},{19,3},{4,20},{20... | collective-permute-start | bytes 1572872 | tf_op jit(solution)/shard_map/ppermute | solution.py:9
  247.6 0.8 copy-start.4
  248.4 69.9 %all-gather.24.cloned.1.call-start = ((), (), s32[]{:S(2)}) async-start(), calls=%async_computation.2 | async-start | bytes 2621440 | tf_op jit(solution)/shard_map/all_gather | solution.py:17
  249.1 119.7 %all-gather.28.cloned.1.call-start = ((), (), s32[]{:S(2)}) async-start(), calls=%async_computation.4 | async-start | bytes 2621440 | tf_op jit(solution)/shard_map/all_gather | solution.py:17
  250.0 3.5 collective-permute-start.2
  318.2 6.5 %copy-start = (bf16[512,2048]{0,1:T(8,128)(2,1)S(1)}, bf16[512,2048]{0,1:T(8,128)(2,1)}, u32[]{:S(2)}) copy-start(bf16[512,2048]{0,1:T(8,128)(2,1)} %all-gather.24.cloned.1.call-done) | copy-start | bytes 6291460
  322.8 67.8 %all-gather.30.cloned.1.call-start = ((), (), s32[]{:S(2)}) async-start(), calls=%async_computation.5 | async-start | bytes 2621440 | tf_op jit(solution)/shard_map/all_gather | solution.py:13
  322.8 1.0 collective-permute-start.1
  323.9 0.8 copy-start.5
  (1 other events, 0.0 us)
Sparse Core Ops, SparseCore 0:
  10.2 25.2 all-gather.31
  37.1 45.9 all-gather.33
  87.3 21.3 all-gather.19
  110.1 45.9 all-gather.35
  161.0 21.3 all-gather.21
  183.8 45.9 all-gather.37
  248.5 21.5 all-gather.25
  272.3 45.9 all-gather.23
  322.9 44.7 all-gather.27
  369.1 21.3 all-gather.29
where the time goes:
time: 411 us
  blocking collectives  152 us (37%)
  local copies, waits for them, and re-layouts  125 us (30%)
  waiting for transfers between devices  85.6 us (21%)
  matrix products  27.3 us (7%)
  between operations  14.5 us (4%)
  starting transfers between devices  4.45 us (1%)
    all_gather x5, blocking collectives, compose(): lax.all_gather(right_vector, ('row', 'col'), axis=0, tiled=True)  152 us
    gather x5, local copies, waits for them, and re-layouts, compose(): moved = jnp.take(full_vector, pivots, axis=0)  65.4 us
    all_gather x5, waiting for transfers between devices, compose(): segment = lax.all_gather(left_block, 'col', axis=1, tiled=True)  50 us
    gather x5, local copies, waits for them, and re-layouts, compose(): permuted = jnp.take(column_panel, pivots, axis=0)  46.5 us
    dot_general x5, matrix products, compose(): product = jnp.dot(segment, permuted, preferred_element_type=jnp.float32)  21.1 us
    all_gather x5, waiting for transfers between devices, compose(): column_panel = lax.all_gather(right_block, 'row', axis=0, tiled=True)  18.9 us
    ppermute x4, waiting for transfers between devices, from_behind(): lax.ppermute(value, axis, [(i, (i + by) % devices) for i in range(devices)])  14.2 us
    all_gather x3, local copies, waits for them, and re-layouts, compose(): column_panel = lax.all_gather(right_block, 'row', axis=0, tiled=True)  8.62 us
  transfers between devices with their start and end apart: 14, of which 7 were waited for; matrix products, arithmetic and copies ran while one was open for 29% of the time, Pallas kernels for 0%

commit v1 on v0

v1 whole, which is shorter than its diff:
```python
import jax
import jax.numpy as jnp
from jax import lax
from jax.experimental import pallas as pl
from jax.experimental.pallas import tpu as pltpu
from jax.sharding import PartitionSpec as P

EXTRA = 16
VMEM = 48 * 1024 * 1024
NT = (((1,), (1,)), ((), ()))


def from_behind(value, axis, by):
    devices = lax.axis_size(axis)
    if by % devices == 0:
        return value
    return lax.ppermute(value, axis, [(i, (i + by) % devices) for i in range(devices)])


def swap_rows(value, flip):
    rows, cols = lax.axis_size("row"), lax.axis_size("col")
    pairs = [(r * cols + c, (r ^ flip) * cols + c) for r in range(rows) for c in (1, 2)]
    return lax.ppermute(value, ("row", "col"), pairs)


def swap_middle(value):
    return lax.ppermute(value, "col", [(1, 2), (2, 1)])


def inward(value):
    return lax.ppermute(value, "col", [(0, 1), (3, 2)])


def outward(value):
    return lax.ppermute(value, "col", [(1, 0), (2, 3)])


def row_tiles(tile):
    across = swap_rows(tile, 2)
    return [tile, swap_rows(tile, 1), across, swap_rows(across, 1)]


def spread(tiles, q_ref, first, size, count):
    def block(n):
        total = None
        for b, tile in enumerate(tiles):
            at = lax.broadcasted_iota(jnp.int32, (size, size), 0) + n * size
            hot = jnp.where(at == q_ref[first + b : first + b + 1, :], 1.0, 0.0).astype(jnp.bfloat16)
            part = lax.dot_general(tile[0:size, :], hot, NT, preferred_element_type=jnp.float32)
            total = part if total is None else total + part
        return total

    return block


def spread_kernel(q_ref, own_o, own_e, out):
    size = out.shape[0]
    count = out.shape[1] // size
    block = spread((own_o, own_e), q_ref, 0, size, count)

    @pl.loop(0, count)
    def _(n):
        out[:, pl.ds(pl.multiple_of(n * size, size), size)] = block(n).astype(out.dtype)


def compose_kernel(riding, q_ref, partial, other_o, other_e, added, *rest):
    if riding:
        vector = None
    else:
        vector, rest = rest[0], rest[1:]
    right_o, right_e = rest[0:4], rest[4:8]
    out_o, out_e, out_v, left = rest[8:]
    size = partial.shape[0]
    count = partial.shape[1] // size
    block = spread((other_o, other_e), q_ref, 2, size, count)

    @pl.loop(0, count)
    def _(n):
        here = pl.ds(pl.multiple_of(n * size, size), size)
        left[:, here] = partial[:, here] + block(n).astype(left.dtype)

    applied = added[...]
    for right, out in ((right_o, out_o), (right_e, out_e)):
        total = None
        for b in range(count):
            part = jnp.dot(
                left[:, b * size : (b + 1) * size],
                right[b][0:size, :],
                preferred_element_type=jnp.float32,
            )
            total = part if total is None else total + part
        out[0:size, :] = total.astype(out.dtype)
    for b in range(count):
        if riding:
            rows = right_o[b][size : size + EXTRA, :]
        else:
            rows = vector[:, b * size : (b + 1) * size]
        applied = applied + lax.dot_general(
            rows, left[:, b * size : (b + 1) * size], NT, preferred_element_type=jnp.float32
        )
    out_v[...] = applied
    out_o[size : size + EXTRA, :] = applied.astype(out_o.dtype)


def spread_own(pivots, own_o, own_e, size, count):
    return pl.pallas_call(
        spread_kernel,
        out_shape=jax.ShapeDtypeStruct((size, size * count), jnp.bfloat16),
        compiler_params=pltpu.CompilerParams(vmem_limit_bytes=VMEM),
        cost_estimate=pl.CostEstimate(
            flops=4 * size * size * size * count, bytes_accessed=8 * size * size, transcendentals=0
        ),
    )(pivots, own_o, own_e)


def compose(pivots, partial, other, added, right_o, right_e, vector=None):
    size = partial.shape[0]
    count = partial.shape[1] // size
    riding = vector is None

    def body(*refs):
        compose_kernel(riding, *refs)

    extra = () if riding else (vector,)
    return pl.pallas_call(
        body,
        out_shape=(
            jax.ShapeDtypeStruct((size + EXTRA, size), jnp.bfloat16),
            jax.ShapeDtypeStruct((size, size), jnp.bfloat16),
            jax.ShapeDtypeStruct((EXTRA, size), jnp.float32),
        ),
        scratch_shapes=[pltpu.VMEM((size, size * count), jnp.bfloat16)],
        compiler_params=pltpu.CompilerParams(vmem_limit_bytes=VMEM),
        cost_estimate=pl.CostEstimate(
            flops=8 * size * size * size * count, bytes_accessed=24 * size * size, transcendentals=0
        ),
    )(pivots, partial, *other, added, *extra, *right_o, *right_e)


def shards(interval_blocks, interval_pivots, boundary_pivots, interval_residuals):
    blocks = interval_blocks[0]
    size = blocks.shape[1]
    row, col = lax.axis_index("row"), lax.axis_index("col")
    count = lax.axis_size("row")
    position = lax.axis_index("loop")
    positions = lax.axis_size("loop")

    own = lax.dynamic_index_in_dim(boundary_pivots, position, 0, keepdims=True)
    back = lax.dynamic_index_in_dim(
        boundary_pivots, (position + positions - 1) % positions, 0, keepdims=True
    )
    pivots = jnp.concatenate([interval_pivots[0], own, back], axis=0)
    pivots = (((pivots // size) ^ row) * size + pivots % size).reshape(pivots.shape[0], count, size)
    order = [
        lax.dynamic_index_in_dim(pivots, col ^ flip, 1, keepdims=True) for flip in (0, 1, 3, 2)
    ]
    pivots = jnp.concatenate(order, axis=1)

    residuals = lax.all_gather(interval_residuals[0], ("row", "col"), axis=0)
    residuals = residuals.reshape(count, -1, *interval_residuals.shape[1:])
    residuals = jnp.moveaxis(residuals, 2, 0).reshape(blocks.shape[0], count, size)
    tiles = [
        lax.dynamic_index_in_dim(residuals, row ^ flip, 1, keepdims=False) for flip in range(count)
    ]
    full = jnp.concatenate(tiles, axis=1)
    vectors = [jnp.broadcast_to(full[k][None], (EXTRA, full.shape[1])) for k in (0, 2)]
    adds = [
        jnp.broadcast_to(tiles[0][k][None], (EXTRA, size)).astype(jnp.float32) for k in (1, 3)
    ]

    ends = {k: inward(blocks[k]) for k in (3, 2, 1, 0)}

    def first(left, right, turn, vector, added):
        other = [swap_middle(blocks[left]), swap_middle(ends[left])]
        partial = spread_own(pivots[turn], blocks[left], ends[left], size, count)
        right_o, right_e = row_tiles(blocks[right]), row_tiles(ends[right])
        return compose(pivots[turn], partial, other, added, right_o, right_e, vector)

    def later(left, right, turn):
        left_o, left_e, added = left
        right_o, right_e = right
        other = [swap_middle(left_o), swap_middle(left_e)]
        partial = spread_own(pivots[turn], left_o, left_e, size, count)
        return compose(
            pivots[turn], partial, other, added, row_tiles(right_o), row_tiles(right_e)
        )

    upper = first(3, 2, 2, vectors[1], adds[1])
    lower = first(1, 0, 0, vectors[0], adds[0])
    whole = later(upper, lower[:2], 1)
    earlier = [from_behind(tile, "loop", 1) for tile in whole[:2]]
    halved = later(whole, earlier, 3)
    distant = [from_behind(tile, "loop", 2) for tile in halved[:2]]
    reduced_o, reduced_e, applied = later(halved, distant, 4)

    middle = (col == 1) | (col == 2)
    block = jnp.where(middle, reduced_o[:size], outward(reduced_e))
    vector = applied[:1]
    vector = jnp.where(middle, vector, outward(vector))
    share = interval_residuals.shape[2]
    return (block[None], lax.dynamic_slice_in_dim(vector, col * share, share, 1))


def solution(mesh):
    placed = (
        P("loop", None, "row", "col"),
        P("loop", None, None),
        P(),
        P("loop", None, ("row", "col")),
    )
    return jax.shard_map(
        shards,
        mesh=mesh,
        in_specs=placed,
        out_specs=(P("loop", "row", "col"), P("loop", ("row", "col"))),
        check_vma=False,
    )
```

time: 411 us -> 297 us (0.72)
  local copies, waits for them, and re-layouts: 125 us -> 12.2 us
  blocking collectives: 152 us -> 48.9 us
  Pallas kernels: 0 us -> 55 us
  starting transfers between devices: 4.45 us -> 49.6 us
  waiting for transfers between devices: 85.6 us -> 126 us
  matrix products: 27.3 us -> 0 us
  between operations: 14.5 us -> 1.61 us
    gather x10 -> x0, local copies, waits for them, and re-layouts: 112 us -> none  [the longest x5 65.4 us: compose(): moved = jnp.take(full_vector, pivots, axis=0)]
    ppermute x0 -> x46, waiting for transfers between devices: none -> 109 us  [the longest x2 104 us: outward(): return lax.ppermute(value, 'col', [(1, 0), (2, 3)])]
    all_gather x5 -> x1, blocking collectives: 152 us -> 48.9 us  [shards(): residuals = lax.all_gather(interval_residuals[0], ('row', 'col'), axis=0)]
    all_gather x10 -> x0, waiting for transfers between devices: 68.9 us -> none  [the longest x5 50 us: compose(): segment = lax.all_gather(left_block, 'col', axis=1, tiled=True)]
    pallas_call x0 -> x10, Pallas kernels: none -> 55 us  [the longest x5 39 us: compose(): pl.pallas_call(body, out_shape=(jax.ShapeDtypeStruct((size + EXTRA, size)...]
    ppermute x0 -> x46, starting transfers between devices: none -> 47.5 us  [the longest x30 21 us: swap_rows(): return lax.ppermute(value, ('row', 'col'), pairs)]
    dot_general x10 -> x0, matrix products: 27.3 us -> none  [the longest x5 21.1 us: compose(): product = jnp.dot(segment, permuted, preferred_element_type=jnp.float32)]
    all_gather x3 -> x0, local copies, waits for them, and re-layouts: 8.62 us -> none  [compose(): column_panel = lax.all_gather(right_block, 'row', axis=0, tiled=True)]
  transfers between devices with their start and end apart: 14 -> 48, of which waited for: 7 -> 4; matrix products, arithmetic and copies ran while one was open for 29% -> 0% of each run, Pallas kernels for 0% -> 11%
where the time goes in v1:
time: 297 us; the launch traced here: 295 us
  waiting for transfers between devices  126 us (42%)
  Pallas kernels  55 us (19%)
  starting transfers between devices  49.6 us (17%)
  blocking collectives  48.9 us (16%)
  local copies, waits for them, and re-layouts  12.2 us (4%)
    ppermute x2, waiting for transfers between devices, outward(): return lax.ppermute(value, 'col', [(1, 0), (2, 3)])  104 us
    all_gather x1, blocking collectives, shards(): residuals = lax.all_gather(interval_residuals[0], ('row', 'col'), axis=0)  48.9 us
    pallas_call x5, Pallas kernels, compose(): pl.pallas_call(body, out_shape=(jax.ShapeDtypeStruct((size + EXTRA, size)...  39 us
    ppermute x30, starting transfers between devices, swap_rows(): return lax.ppermute(value, ('row', 'col'), pairs)  21 us
    ppermute x2, waiting for transfers between devices, from_behind(): lax.ppermute(value, axis, [(i, (i + by) % devices) for i in range(devices)])  17.6 us
    ppermute x4, starting transfers between devices, inward(): return lax.ppermute(value, 'col', [(0, 1), (3, 2)])  17 us
    pallas_call x5, Pallas kernels, spread_own(): pl.pallas_call(spread_kernel, out_shape=jax.ShapeDtypeStruct((size, size...  16 us
    unnamed x30, local copies, waits for them, and re-layouts  10.2 us
  transfers between devices with their start and end apart: 48, of which 4 were waited for; matrix products, arithmetic and copies ran while one was open for 0% of the time, Pallas kernels for 11%

profile of v1, /device:TPU:0, one launch (start us, length us, event | category | flops | bytes accessed | tf_op | source)
XLA Modules:
  0.0 295.0 jit_solution(14742058384661595256)
XLA Ops:
  0.7 1.7 slice_bitcast_fusion
  2.3 5.7 %collective-permute-start = (bf16[512,512]{1,0:T(8,128)(2,1)S(1)}, bf16[512,512]{1,0:T(8,128)(2,1)}, u32[]{:S(2)}, u32[]{:S(2)}) collective-permute-start(bf16[512,512]{1,0:T(8,128)(2,1)S(1)} %get-tuple-element.36.own_o), channel_id=1, source_target_pairs={{0,1},{3,2},{4,5},{7,6},{8,9},{11,10},{12,13},{15,14},{16,17},{19,... | collective-permute-start | bytes 1572872 | tf_op jit(solution)/shard_map/ppermute | solution.py:31
  9.5 6.8 %collective-permute-start.6 = (bf16[512,512]{1,0:T(8,128)(2,1)S(1)}, bf16[512,512]{1,0:T(8,128)(2,1)}, u32[]{:S(2)}, u32[]{:S(2)}) collective-permute-start(bf16[512,512]{1,0:T(8,128)(2,1)S(1)} %get-tuple-element.35.refs_6_), channel_id=1, source_target_pairs={{0,1},{3,2},{4,5},{7,6},{8,9},{11,10},{12,13},{15,14},{16,17},{19,... | collective-permute-start | bytes 1572872 | tf_op jit(solution)/shard_map/ppermute | solution.py:31
  16.3 2.1 collective-permute-start.18
  18.7 48.9 %all_gather.3 = bf16[16,4,128]{2,1,0:T(4,128)(2,1)S(1)} all-gather(bf16[1,4,128]{2,1,0:T(4,128)(2,1)S(1)} %copy-done.9), channel_id=1, replica_groups=mesh['loop'=2,'row'=4,'col'=4] {'row','col'}, dimensions={0}, use_global_device_ids=true | all-gather | bytes 17408 | tf_op jit(solution)/shard_map/all_gather | solution.py:159
  67.9 2.4 collective-permute-start.12
  73.2 4.9 %collective-permute-done.12.own_e = bf16[512,512]{1,0:T(8,128)(2,1)S(1)} collective-permute-done((bf16[512,512]{1,0:T(8,128)(2,1)S(1)}, bf16[512,512]{1,0:T(8,128)(2,1)S(1)}, u32[]{:S(2)}, u32[]{:S(2)}) %collective-permute-start.12) | collective-permute-done | bytes 524320 | tf_op jit(solution)/shard_map/ppermute | solution.py:31
  81.7 4.0 %shard_map.59.refs_1_ = bf16[512,2048]{1,0:T(8,128)(2,1)S(1)} custom-call(s32[4,512]{1,0:T(4,128)S(1)} %get-tuple-element.39.q_ref.refs_0_, bf16[512,512]{1,0:T(8,128)(2,1)S(1)} %get-tuple-element.36.own_o, bf16[512,512]{1,0:T(8,128)(2,1)} %collective-permute-done.own_e), custom_call_target="tpu_custom_call" | custom-call | flops 2147483648 | bytes 2097152 | tf_op jit(solution)/shard_map/pallas_call | solution.py:106
  85.7 1.3 copy-done.5
  90.6 3.0 %shard_map.62.refs_1_ = bf16[512,2048]{1,0:T(8,128)(2,1)S(1)} custom-call(s32[4,512]{1,0:T(4,128)S(1)} %get-tuple-element.38.q_ref.refs_0_, bf16[512,512]{1,0:T(8,128)(2,1)S(1)} %get-tuple-element.37.own_o, bf16[512,512]{1,0:T(8,128)(2,1)S(1)} %collective-permute-done.12.own_e), custom_call_target="tpu_custom_call" | custom-call | flops 2147483648 | bytes 2097152 | tf_op jit(solution)/shard_map/pallas_call | solution.py:106
  93.6 1.4 copy-done.6
  95.0 8.3 %shard_map.63 = (bf16[528,512]{1,0:T(8,128)(2,1)}, bf16[512,512]{1,0:T(8,128)(2,1)S(1)}, f32[16,512]{1,0:T(8,128)}) custom-call(s32[4,512]{1,0:T(4,128)S(1)} %get-tuple-element.38.q_ref.refs_0_, bf16[512,2048]{1,0:T(8,128)(2,1)} %copy-done.6, bf16[512,512]{1,0:T(8,128)(2,1)S(1)} %collective-permute-done.13.refs_2_, ...), custom_call_target="tpu_custom_call" | custom-call | flops 4294967296 | bytes 6291456 | tf_op jit(solution)/shard_map/pallas_call | solution.py:125
  104.1 8.3 %shard_map.60 = (bf16[528,512]{1,0:T(8,128)(2,1)}, bf16[512,512]{1,0:T(8,128)(2,1)S(1)}, f32[16,512]{1,0:T(8,128)S(1)}) custom-call(s32[4,512]{1,0:T(4,128)S(1)} %get-tuple-element.39.q_ref.refs_0_, bf16[512,2048]{1,0:T(8,128)(2,1)} %copy-done.5, bf16[512,512]{1,0:T(8,128)(2,1)S(1)} %collective-permute-done.1.refs_2_, ...), custom_call_target="tpu_custom_call" | custom-call | flops 4294967296 | bytes 6291456 | tf_op jit(solution)/shard_map/pallas_call | solution.py:125
  116.7 0.9 collective-permute-start.27
  117.5 1.0 copy-done.1
  118.6 3.0 %shard_map.61.refs_1_ = bf16[512,2048]{1,0:T(8,128)(2,1)S(1)} custom-call(s32[4,512]{1,0:T(4,128)S(1)} %get-tuple-element.40.q_ref.refs_0_, bf16[528,512]{1,0:T(8,128)(2,1)S(1)} %copy-done.1, bf16[512,512]{1,0:T(8,128)(2,1)S(1)} %get-tuple-element.17.own_e), custom_call_target="tpu_custom_call" | custom-call | flops 2147483648 | bytes 2097152 | tf_op jit(solution)/shard_map/pallas_call | solution.py:106
  121.6 1.3 copy-done.2
  123.0 0.8 copy-done.10
  123.8 7.4 %shard_map.64 = (bf16[528,512]{1,0:T(8,128)(2,1)S(1)}, bf16[512,512]{1,0:T(8,128)(2,1)S(1)}, f32[16,512]{1,0:T(8,128)S(1)}) custom-call(s32[4,512]{1,0:T(4,128)S(1)} %get-tuple-element.40.q_ref.refs_0_, bf16[512,2048]{1,0:T(8,128)(2,1)} %copy-done.2, bf16[528,512]{1,0:T(8,128)(2,1)S(1)} %collective-permute-done.10.refs_2_, ...), custom_call_target="tpu_custom_call" | custom-call | flops 4294967296 | bytes 6291456 | tf_op jit(solution)/shard_map/pallas_call | solution.py:125
  131.2 1.5 collective-permute-start.30
  133.3 13.2 %collective-permute-done.30.refs_5_ = bf16[528,512]{1,0:T(8,128)(2,1)S(1)} collective-permute-done((bf16[528,512]{1,0:T(8,128)(2,1)S(1)}, bf16[528,512]{1,0:T(8,128)(2,1)S(1)}, u32[]{:S(2)}, u32[]{:S(2)}) %collective-permute-start.30) | collective-permute-done | bytes 540704 | tf_op jit(solution)/shard_map/ppermute | solution.py:17
  147.9 4.4 %collective-permute-done.34.refs_9_ = bf16[512,512]{1,0:T(8,128)(2,1)S(1)} collective-permute-done((bf16[512,512]{1,0:T(8,128)(2,1)S(1)}, bf16[512,512]{1,0:T(8,128)(2,1)S(1)}, u32[]{:S(2)}, u32[]{:S(2)}) %collective-permute-start.34) | collective-permute-done | bytes 524320 | tf_op jit(solution)/shard_map/ppermute | solution.py:17
  156.5 3.0 %shard_map.65.refs_1_ = bf16[512,2048]{1,0:T(8,128)(2,1)S(1)} custom-call(s32[4,512]{1,0:T(4,128)S(1)} %get-tuple-element.41.q_ref.refs_0_, bf16[528,512]{1,0:T(8,128)(2,1)S(1)} %get-tuple-element.21.own_o, bf16[512,512]{1,0:T(8,128)(2,1)S(1)} %get-tuple-element.22.own_e), custom_call_target="tpu_custom_call" | custom-call | flops 2147483648 | bytes 2097152 | tf_op jit(solution)/shard_map/pallas_call | solution.py:106
  159.5 1.3 copy-done.3
  161.7 7.4 %shard_map.66 = (bf16[528,512]{1,0:T(8,128)(2,1)S(1)}, bf16[512,512]{1,0:T(8,128)(2,1)S(1)}, f32[16,512]{1,0:T(8,128)S(1)}) custom-call(s32[4,512]{1,0:T(4,128)S(1)} %get-tuple-element.41.q_ref.refs_0_, bf16[512,2048]{1,0:T(8,128)(2,1)} %copy-done.3, bf16[528,512]{1,0:T(8,128)(2,1)S(1)} %collective-permute-done.28.refs_2_, ...), custom_call_target="tpu_custom_call" | custom-call | flops 4294967296 | bytes 6291456 | tf_op jit(solution)/shard_map/pallas_call | solution.py:125
  174.8 3.0 %shard_map.67.refs_1_ = bf16[512,2048]{1,0:T(8,128)(2,1)S(1)} custom-call(s32[4,512]{1,0:T(4,128)S(1)} %get-tuple-element.42.q_ref.refs_0_, bf16[528,512]{1,0:T(8,128)(2,1)S(1)} %get-tuple-element.24.own_o.refs_5_, bf16[512,512]{1,0:T(8,128)(2,1)S(1)} %get-tuple-element.25.own_e.refs_9_), custom_call_target="tpu_custom_call" | custom-call | flops 2147483648 | bytes 2097152 | tf_op jit(solution)/shard_map/pallas_call | solution.py:106
  177.8 1.3 copy-done.4
  180.0 7.5 %shard_map.68 = (bf16[528,512]{1,0:T(8,128)(2,1)S(1)}, bf16[512,512]{1,0:T(8,128)(2,1)S(1)}, f32[16,512]{1,0:T(8,128)S(1)}) custom-call(s32[4,512]{1,0:T(4,128)S(1)} %get-tuple-element.42.q_ref.refs_0_, bf16[512,2048]{1,0:T(8,128)(2,1)} %copy-done.4, bf16[528,512]{1,0:T(8,128)(2,1)S(1)} %collective-permute-done.38.refs_2_, ...), custom_call_target="tpu_custom_call" | custom-call | flops 4294967296 | bytes 6291456 | tf_op jit(solution)/shard_map/pallas_call | solution.py:125
  187.5 1.3 collective-permute-start.46
  188.8 1.3 collective-permute-start.47
  190.1 103.6 %collective-permute-done.47 = f32[1,512]{1,0:T(1,128)S(1)} collective-permute-done((f32[1,512]{1,0:T(1,128)S(1)}, f32[1,512]{1,0:T(1,128)S(1)}, u32[]{:S(2)}, u32[]{:S(2)}) %collective-permute-start.47) | collective-permute-done | bytes 2080 | tf_op jit(solution)/shard_map/ppermute | solution.py:35
  294.2 0.8 select_bitcast_fusion
  (129 shorter events, 30.4 us)
Async XLA Ops:
  2.3 65.5 %collective-permute-start = (bf16[512,512]{1,0:T(8,128)(2,1)S(1)}, bf16[512,512]{1,0:T(8,128)(2,1)}, u32[]{:S(2)}, u32[]{:S(2)}) collective-permute-start(bf16[512,512]{1,0:T(8,128)(2,1)S(1)} %get-tuple-element.36.own_o), channel_id=1, source_target_pairs={{0,1},{3,2},{4,5},{7,6},{8,9},{11,10},{12,13},{15,14},{16,17},{19,... | collective-permute-start | bytes 1572872 | tf_op jit(solution)/shard_map/ppermute | solution.py:31
  8.1 62.2 %collective-permute-start.1 = (bf16[512,512]{1,0:T(8,128)(2,1)S(1)}, bf16[512,512]{1,0:T(8,128)(2,1)S(1)}, u32[]{:S(2)}, u32[]{:S(2)}) collective-permute-start(bf16[512,512]{1,0:T(8,128)(2,1)S(1)} %get-tuple-element.36.own_o), channel_id=1, source_target_pairs={{1,2},{2,1},{5,6},{6,5},{9,10},{10,9},{13,14},{14,13},{17,18},{18,... | collective-permute-start | bytes 1572872 | tf_op jit(solution)/shard_map/ppermute | solution.py:27
  8.8 62.2 %collective-permute-start.4 = (bf16[512,512]{1,0:T(8,128)(2,1)S(1)}, bf16[512,512]{1,0:T(8,128)(2,1)S(1)}, u32[]{:S(2)}, u32[]{:S(2)}) collective-permute-start(bf16[512,512]{1,0:T(8,128)(2,1)S(1)} %get-tuple-element.35.refs_6_), channel_id=1, source_target_pairs={{1,9},{2,10},{5,13},{6,14},{9,1},{10,2},{13,5},{14,6},{17,25},{18,... | collective-permute-start | bytes 1572872 | tf_op jit(solution)/shard_map/ppermute | solution.py:23
  9.5 62.2 %collective-permute-start.6 = (bf16[512,512]{1,0:T(8,128)(2,1)S(1)}, bf16[512,512]{1,0:T(8,128)(2,1)}, u32[]{:S(2)}, u32[]{:S(2)}) collective-permute-start(bf16[512,512]{1,0:T(8,128)(2,1)S(1)} %get-tuple-element.35.refs_6_), channel_id=1, source_target_pairs={{0,1},{3,2},{4,5},{7,6},{8,9},{11,10},{12,13},{15,14},{16,17},{19,... | collective-permute-start | bytes 1572872 | tf_op jit(solution)/shard_map/ppermute | solution.py:31
  16.3 56.1 %collective-permute-start.18 = (bf16[512,512]{1,0:T(8,128)(2,1)S(1)}, bf16[512,512]{1,0:T(8,128)(2,1)}, u32[]{:S(2)}, u32[]{:S(2)}) collective-permute-start(bf16[512,512]{1,0:T(8,128)(2,1)S(1)} %get-tuple-element.34.refs_6_), channel_id=1, source_target_pairs={{0,1},{3,2},{4,5},{7,6},{8,9},{11,10},{12,13},{15,14},{16,17},{19,... | collective-permute-start | bytes 1572872 | tf_op jit(solution)/shard_map/ppermute | solution.py:31
  67.9 10.2 %collective-permute-start.12 = (bf16[512,512]{1,0:T(8,128)(2,1)S(1)}, bf16[512,512]{1,0:T(8,128)(2,1)S(1)}, u32[]{:S(2)}, u32[]{:S(2)}) collective-permute-start(bf16[512,512]{1,0:T(8,128)(2,1)S(1)} %get-tuple-element.37.own_o), channel_id=1, source_target_pairs={{0,1},{3,2},{4,5},{7,6},{8,9},{11,10},{12,13},{15,14},{16,17},{19,... | collective-permute-start | bytes 1572872 | tf_op jit(solution)/shard_map/ppermute | solution.py:31
  70.3 8.5 %collective-permute-start.13 = (bf16[512,512]{1,0:T(8,128)(2,1)S(1)}, bf16[512,512]{1,0:T(8,128)(2,1)S(1)}, u32[]{:S(2)}, u32[]{:S(2)}) collective-permute-start(bf16[512,512]{1,0:T(8,128)(2,1)S(1)} %get-tuple-element.37.own_o), channel_id=1, source_target_pairs={{1,2},{2,1},{5,6},{6,5},{9,10},{10,9},{13,14},{14,13},{17,18},{18,... | collective-permute-start | bytes 1572872 | tf_op jit(solution)/shard_map/ppermute | solution.py:27
  71.0 8.5 %collective-permute-start.15 = (bf16[512,512]{1,0:T(8,128)(2,1)S(1)}, bf16[512,512]{1,0:T(8,128)(2,1)S(1)}, u32[]{:S(2)}, u32[]{:S(2)}) collective-permute-start(bf16[512,512]{1,0:T(8,128)(2,1)S(1)} %get-tuple-element.34.refs_6_), channel_id=1, source_target_pairs={{1,5},{2,6},{5,1},{6,2},{9,13},{10,14},{13,9},{14,10},{17,21},{18,... | collective-permute-start | bytes 1572872 | tf_op jit(solution)/shard_map/ppermute | solution.py:23
  71.7 8.5 %collective-permute-start.16 = (bf16[512,512]{1,0:T(8,128)(2,1)S(1)}, bf16[512,512]{1,0:T(8,128)(2,1)S(1)}, u32[]{:S(2)}, u32[]{:S(2)}) collective-permute-start(bf16[512,512]{1,0:T(8,128)(2,1)S(1)} %get-tuple-element.34.refs_6_), channel_id=1, source_target_pairs={{1,9},{2,10},{5,13},{6,14},{9,1},{10,2},{13,5},{14,6},{17,25},{18,... | collective-permute-start | bytes 1572872 | tf_op jit(solution)/shard_map/ppermute | solution.py:23
  72.4 8.5 %collective-permute-start.20 = (bf16[512,512]{1,0:T(8,128)(2,1)}, bf16[512,512]{1,0:T(8,128)(2,1)S(1)}, u32[]{:S(2)}, u32[]{:S(2)}) collective-permute-start(bf16[512,512]{1,0:T(8,128)(2,1)} %collective-permute-done.18.refs_10_), channel_id=1, source_target_pairs={{1,9},{2,10},{5,13},{6,14},{9,1},{10,2},{13,5},{14,6},{17,25},{18,... | collective-permute-start | bytes 1572872 | tf_op jit(solution)/shard_map/ppermute | solution.py:23
  78.1 11.1 %collective-permute-start.19 = (bf16[512,512]{1,0:T(8,128)(2,1)}, bf16[512,512]{1,0:T(8,128)(2,1)S(1)}, u32[]{:S(2)}, u32[]{:S(2)}) collective-permute-start(bf16[512,512]{1,0:T(8,128)(2,1)} %collective-permute-done.18.refs_10_), channel_id=1, source_target_pairs={{1,5},{2,6},{5,1},{6,2},{9,13},{10,14},{13,9},{14,10},{17,21},{18,... | collective-permute-start | bytes 1572872 | tf_op jit(solution)/shard_map/ppermute | solution.py:23
  78.8 8.3 %collective-permute-start.8 = (bf16[512,512]{1,0:T(8,128)(2,1)}, bf16[512,512]{1,0:T(8,128)(2,1)S(1)}, u32[]{:S(2)}, u32[]{:S(2)}) collective-permute-start(bf16[512,512]{1,0:T(8,128)(2,1)} %collective-permute-done.6.refs_10_), channel_id=1, source_target_pairs={{1,9},{2,10},{5,13},{6,14},{9,1},{10,2},{13,5},{14,6},{17,25},{18,... | collective-permute-start | bytes 1572872 | tf_op jit(solution)/shard_map/ppermute | solution.py:23
  79.5 8.3 %collective-permute-start.14 = (bf16[512,512]{1,0:T(8,128)(2,1)S(1)}, bf16[512,512]{1,0:T(8,128)(2,1)S(1)}, u32[]{:S(2)}, u32[]{:S(2)}) collective-permute-start(bf16[512,512]{1,0:T(8,128)(2,1)S(1)} %collective-permute-done.12.own_e), channel_id=1, source_target_pairs={{1,2},{2,1},{5,6},{6,5},{9,10},{10,9},{13,14},{14,13},{17,18},{18,... | collective-permute-start | bytes 1572872 | tf_op jit(solution)/shard_map/ppermute | solution.py:27
  80.2 8.3 %collective-permute-start.17 = (bf16[512,512]{1,0:T(8,128)(2,1)S(1)}, bf16[512,512]{1,0:T(8,128)(2,1)S(1)}, u32[]{:S(2)}, u32[]{:S(2)}) collective-permute-start(bf16[512,512]{1,0:T(8,128)(2,1)S(1)} %collective-permute-done.16.refs_8_), channel_id=1, source_target_pairs={{1,5},{2,6},{5,1},{6,2},{9,13},{10,14},{13,9},{14,10},{17,21},{18,... | collective-permute-start | bytes 1572872 | tf_op jit(solution)/shard_map/ppermute | solution.py:23
  80.9 9.0 %collective-permute-start.21 = (bf16[512,512]{1,0:T(8,128)(2,1)S(1)}, bf16[512,512]{1,0:T(8,128)(2,1)S(1)}, u32[]{:S(2)}, u32[]{:S(2)}) collective-permute-start(bf16[512,512]{1,0:T(8,128)(2,1)S(1)} %collective-permute-done.20.refs_12_), channel_id=1, source_target_pairs={{1,5},{2,6},{5,1},{6,2},{9,13},{10,14},{13,9},{14,10},{17,21},{18,... | collective-permute-start | bytes 1572872 | tf_op jit(solution)/shard_map/ppermute | solution.py:23
  87.1 16.2 %collective-permute-start.3 = (bf16[512,512]{1,0:T(8,128)(2,1)S(1)}, bf16[512,512]{1,0:T(8,128)(2,1)S(1)}, u32[]{:S(2)}, u32[]{:S(2)}) collective-permute-start(bf16[512,512]{1,0:T(8,128)(2,1)S(1)} %get-tuple-element.35.refs_6_), channel_id=1, source_target_pairs={{1,5},{2,6},{5,1},{6,2},{9,13},{10,14},{13,9},{14,10},{17,21},{18,... | collective-permute-start | bytes 1572872 | tf_op jit(solution)/shard_map/ppermute | solution.py:23
  87.8 16.2 %collective-permute-start.2 = (bf16[512,512]{1,0:T(8,128)(2,1)}, bf16[512,512]{1,0:T(8,128)(2,1)S(1)}, u32[]{:S(2)}, u32[]{:S(2)}) collective-permute-start(bf16[512,512]{1,0:T(8,128)(2,1)} %collective-permute-done.own_e), channel_id=1, source_target_pairs={{1,2},{2,1},{5,6},{6,5},{9,10},{10,9},{13,14},{14,13},{17,18},{18,... | collective-permute-start | bytes 1572872 | tf_op jit(solution)/shard_map/ppermute | solution.py:27
  88.5 15.5 %collective-permute-start.7 = (bf16[512,512]{1,0:T(8,128)(2,1)}, bf16[512,512]{1,0:T(8,128)(2,1)S(1)}, u32[]{:S(2)}, u32[]{:S(2)}) collective-permute-start(bf16[512,512]{1,0:T(8,128)(2,1)} %collective-permute-done.6.refs_10_), channel_id=1, source_target_pairs={{1,5},{2,6},{5,1},{6,2},{9,13},{10,14},{13,9},{14,10},{17,21},{18,... | collective-permute-start | bytes 1572872 | tf_op jit(solution)/shard_map/ppermute | solution.py:23
  89.2 14.8 %collective-permute-start.5 = (bf16[512,512]{1,0:T(8,128)(2,1)S(1)}, bf16[512,512]{1,0:T(8,128)(2,1)S(1)}, u32[]{:S(2)}, u32[]{:S(2)}) collective-permute-start(bf16[512,512]{1,0:T(8,128)(2,1)S(1)} %collective-permute-done.4.refs_8_), channel_id=1, source_target_pairs={{1,5},{2,6},{5,1},{6,2},{9,13},{10,14},{13,9},{14,10},{17,21},{18,... | collective-permute-start | bytes 1572872 | tf_op jit(solution)/shard_map/ppermute | solution.py:23
  89.9 14.1 %collective-permute-start.9 = (bf16[512,512]{1,0:T(8,128)(2,1)S(1)}, bf16[512,512]{1,0:T(8,128)(2,1)S(1)}, u32[]{:S(2)}, u32[]{:S(2)}) collective-permute-start(bf16[512,512]{1,0:T(8,128)(2,1)S(1)} %collective-permute-done.8.refs_12_), channel_id=1, source_target_pairs={{1,5},{2,6},{5,1},{6,2},{9,13},{10,14},{13,9},{14,10},{17,21},{18,... | collective-permute-start | bytes 1572872 | tf_op jit(solution)/shard_map/ppermute | solution.py:23
  103.3 11.9 %collective-permute-start.23 = (bf16[528,512]{1,0:T(8,128)(2,1)}, bf16[528,512]{1,0:T(8,128)(2,1)S(1)}, u32[]{:S(2)}, u32[]{:S(2)}) collective-permute-start(bf16[528,512]{1,0:T(8,128)(2,1)} %get-tuple-element.19.refs_5_), channel_id=1, source_target_pairs={{1,9},{2,10},{5,13},{6,14},{9,1},{10,2},{13,5},{14,6},{17,25},{18,... | collective-permute-start | bytes 1622024 | tf_op jit(solution)/shard_map/ppermute | solution.py:23
  113.8 9.1 %collective-permute-start.10 = (bf16[528,512]{1,0:T(8,128)(2,1)}, bf16[528,512]{1,0:T(8,128)(2,1)S(1)}, u32[]{:S(2)}, u32[]{:S(2)}) collective-permute-start(bf16[528,512]{1,0:T(8,128)(2,1)} %get-tuple-element.16.own_o), channel_id=1, source_target_pairs={{1,2},{2,1},{5,6},{6,5},{9,10},{10,9},{13,14},{14,13},{17,18},{18,... | collective-permute-start | bytes 1622024 | tf_op jit(solution)/shard_map/ppermute | solution.py:27
  114.5 8.4 %collective-permute-start.22 = (bf16[528,512]{1,0:T(8,128)(2,1)S(1)}, bf16[528,512]{1,0:T(8,128)(2,1)S(1)}, u32[]{:S(2)}, u32[]{:S(2)}) collective-permute-start(bf16[528,512]{1,0:T(8,128)(2,1)S(1)} %copy-done), channel_id=1, source_target_pairs={{1,5},{2,6},{5,1},{6,2},{9,13},{10,14},{13,9},{14,10},{17,21},{18,... | collective-permute-start | bytes 1622024 | tf_op jit(solution)/shard_map/ppermute | solution.py:23
  115.2 7.7 %collective-permute-start.24 = (bf16[528,512]{1,0:T(8,128)(2,1)S(1)}, bf16[528,512]{1,0:T(8,128)(2,1)S(1)}, u32[]{:S(2)}, u32[]{:S(2)}) collective-permute-start(bf16[528,512]{1,0:T(8,128)(2,1)S(1)} %collective-permute-done.23.refs_7_), channel_id=1, source_target_pairs={{1,5},{2,6},{5,1},{6,2},{9,13},{10,14},{13,9},{14,10},{17,21},{18,... | collective-permute-start | bytes 1622024 | tf_op jit(solution)/shard_map/ppermute | solution.py:23
  131.2 15.2 %collective-permute-start.30 = (bf16[528,512]{1,0:T(8,128)(2,1)S(1)}, bf16[528,512]{1,0:T(8,128)(2,1)S(1)}, u32[]{:S(2)}, u32[]{:S(2)}) collective-permute-start(bf16[528,512]{1,0:T(8,128)(2,1)S(1)} %get-tuple-element.21.own_o), channel_id=1, source_target_pairs={{0,16},{16,0},{1,17},{17,1},{2,18},{18,2},{3,19},{19,3},{4,20},{20... | collective-permute-start | bytes 1622024 | tf_op jit(solution)/shard_map/ppermute | solution.py:17
  132.7 19.6 %collective-permute-start.34 = (bf16[512,512]{1,0:T(8,128)(2,1)S(1)}, bf16[512,512]{1,0:T(8,128)(2,1)S(1)}, u32[]{:S(2)}, u32[]{:S(2)}) collective-permute-start(bf16[512,512]{1,0:T(8,128)(2,1)S(1)} %get-tuple-element.22.own_e), channel_id=1, source_target_pairs={{0,16},{16,0},{1,17},{17,1},{2,18},{18,2},{3,19},{19,3},{4,20},{20... | collective-permute-start | bytes 1572872 | tf_op jit(solution)/shard_map/ppermute | solution.py:17
  146.5 7.9 %collective-permute-start.32 = (bf16[528,512]{1,0:T(8,128)(2,1)S(1)}, bf16[528,512]{1,0:T(8,128)(2,1)S(1)}, u32[]{:S(2)}, u32[]{:S(2)}) collective-permute-start(bf16[528,512]{1,0:T(8,128)(2,1)S(1)} %collective-permute-done.30.refs_5_), channel_id=1, source_target_pairs={{1,9},{2,10},{5,13},{6,14},{9,1},{10,2},{13,5},{14,6},{17,25},{18,... | collective-permute-start | bytes 1622024 | tf_op jit(solution)/shard_map/ppermute | solution.py:23
  147.1 8.0 %collective-permute-start.29 = (bf16[512,512]{1,0:T(8,128)(2,1)S(1)}, bf16[512,512]{1,0:T(8,128)(2,1)S(1)}, u32[]{:S(2)}, u32[]{:S(2)}) collective-permute-start(bf16[512,512]{1,0:T(8,128)(2,1)S(1)} %get-tuple-element.22.own_e), channel_id=1, source_target_pairs={{1,2},{2,1},{5,6},{6,5},{9,10},{10,9},{13,14},{14,13},{17,18},{18,... | collective-permute-start | bytes 1572872 | tf_op jit(solution)/shard_map/ppermute | solution.py:27
  153.0 7.9 %collective-permute-start.28 = (bf16[528,512]{1,0:T(8,128)(2,1)S(1)}, bf16[528,512]{1,0:T(8,128)(2,1)S(1)}, u32[]{:S(2)}, u32[]{:S(2)}) collective-permute-start(bf16[528,512]{1,0:T(8,128)(2,1)S(1)} %get-tuple-element.21.own_o), channel_id=1, source_target_pairs={{1,2},{2,1},{5,6},{6,5},{9,10},{10,9},{13,14},{14,13},{17,18},{18,... | collective-permute-start | bytes 1622024 | tf_op jit(solution)/shard_map/ppermute | solution.py:27
  171.3 7.9 %collective-permute-start.38 = (bf16[528,512]{1,0:T(8,128)(2,1)S(1)}, bf16[528,512]{1,0:T(8,128)(2,1)S(1)}, u32[]{:S(2)}, u32[]{:S(2)}) collective-permute-start(bf16[528,512]{1,0:T(8,128)(2,1)S(1)} %get-tuple-element.24.own_o.refs_5_), channel_id=1, source_target_pairs={{1,2},{2,1},{5,6},{6,5},{9,10},{10,9},{13,14},{14,13},{17,18},{18,... | collective-permute-start | bytes 1622024 | tf_op jit(solution)/shard_map/ppermute | solution.py:27
  187.5 106.7 %collective-permute-start.46 = (bf16[512,512]{1,0:T(8,128)(2,1)S(1)}, bf16[512,512]{1,0:T(8,128)(2,1)S(1)}, u32[]{:S(2)}, u32[]{:S(2)}) collective-permute-start(bf16[512,512]{1,0:T(8,128)(2,1)S(1)} %get-tuple-element.28), channel_id=1, source_target_pairs={{1,0},{2,3},{5,4},{6,7},{9,8},{10,11},{13,12},{14,15},{17,16},{18,... | collective-permute-start | bytes 1572872 | tf_op jit(solution)/shard_map/ppermute | solution.py:35
  188.8 104.9 %collective-permute-start.47 = (f32[1,512]{1,0:T(1,128)S(1)}, f32[1,512]{1,0:T(1,128)S(1)}, u32[]{:S(2)}, u32[]{:S(2)}) collective-permute-start(f32[1,512]{1,0:T(1,128)S(1)} %slice.76), channel_id=1, source_target_pairs={{1,0},{2,3},{5,4},{6,7},{9,8},{10,11},{13,12},{14,15},{17,16},{18,... | collective-permute-start | bytes 6152 | tf_op jit(solution)/shard_map/ppermute | solution.py:35
  (29 other events, 158.0 us)

commit v2 on v0

v2 whole, which is shorter than its diff:
```python
import jax
import jax.numpy as jnp
from jax import lax
from jax.experimental import pallas as pl
from jax.experimental.pallas import tpu as pltpu
from jax.sharding import PartitionSpec as P

EXTRA = 16
VMEM = 24 * 1024 * 1024
NT = (((1,), (1,)), ((), ()))


def from_behind(value, axis, by):
    devices = lax.axis_size(axis)
    if by % devices == 0:
        return value
    return lax.ppermute(value, axis, [(i, (i + by) % devices) for i in range(devices)])


def swap_rows(value, flip):
    rows, cols = lax.axis_size("row"), lax.axis_size("col")
    pairs = [(r * cols + c, (r ^ flip) * cols + c) for r in range(rows) for c in (1, 2)]
    return lax.ppermute(value, ("row", "col"), pairs)


def swap_middle(value):
    return lax.ppermute(value, "col", [(1, 2), (2, 1)])


def inward(value):
    return lax.ppermute(value, "col", [(0, 1), (3, 2)])


def outward(value):
    return lax.ppermute(value, "col", [(1, 0), (2, 3)])


class Operands:
    def __init__(self):
        self.arrays = []

    def add(self, view):
        array, lead, column = view
        for i, known in enumerate(self.arrays):
            if known is array:
                return i, lead, column
        self.arrays.append(array)
        return len(self.arrays) - 1, lead, column


def read(refs, view, size, rows=None):
    which, lead, column = view
    ref = refs[which] if lead is None else refs[which].at[lead]
    return ref[rows or slice(0, size), column : column + size]


def spread(refs, views, q_ref, first, size, n):
    total = None
    for b, view in enumerate(views):
        at = lax.broadcasted_iota(jnp.int32, (size, size), 0) + n * size
        hot = jnp.where(at == q_ref[first + b : first + b + 1, :], 1.0, 0.0).astype(jnp.bfloat16)
        part = lax.dot_general(
            read(refs, view, size), hot, NT, preferred_element_type=jnp.float32
        )
        total = part if total is None else total + part
    return total


def spread_own(pivots, own, size, count):
    operands = Operands()
    views = [operands.add(view) for view in own]

    def kernel(q_ref, *refs):
        out = refs[-1]

        @pl.loop(0, count)
        def _(n):
            here = pl.ds(pl.multiple_of(n * size, size), size)
            out[:, here] = spread(refs, views, q_ref, 0, size, n).astype(out.dtype)

    return pl.pallas_call(
        kernel,
        out_shape=jax.ShapeDtypeStruct((size, size * count), jnp.bfloat16),
        compiler_params=pltpu.CompilerParams(vmem_limit_bytes=VMEM),
        cost_estimate=pl.CostEstimate(
            flops=4 * size * size * size * count, bytes_accessed=8 * size * size, transcendentals=0
        ),
    )(pivots, *operands.arrays)


def compose(pivots, partial, other, added, right, vector, form, size):
    count = partial.shape[1] // size
    operands = Operands()
    left_views = [operands.add(view) for view in other]
    right_views = [[operands.add(view) for view in half] for half in right]
    tall, wide = size + EXTRA, 2 * size
    shapes = {
        "joint": [(tall, wide)],
        "both": [(tall, wide), (tall, size), (size, size)],
        "split": [(size, size), (size, size)],
    }[form]
    outs = [jax.ShapeDtypeStruct(shape, jnp.bfloat16) for shape in shapes]
    outs.append(jax.ShapeDtypeStruct((EXTRA, size), jnp.float32))
    extra = [] if vector is None else [vector]

    def kernel(q_ref, partial_ref, added_ref, *rest):
        vector_ref = None if vector is None else rest[0]
        rest = rest[len(extra) :]
        refs = rest[: len(operands.arrays)]
        results = rest[len(refs) : -1]
        left = rest[-1]

        @pl.loop(0, count)
        def _(n):
            here = pl.ds(pl.multiple_of(n * size, size), size)
            moved = spread(refs, left_views, q_ref, 2, size, n)
            left[:, here] = partial_ref[:, here] + moved.astype(left.dtype)

        for half in range(2):
            total = None
            for b in range(count):
                part = jnp.dot(
                    left[:, b * size : (b + 1) * size],
                    read(refs, right_views[half][b], size),
                    preferred_element_type=jnp.float32,
                )
                total = part if total is None else total + part
            total = total.astype(jnp.bfloat16)
            if form != "split":
                results[0][0:size, half * size : (half + 1) * size] = total
            if form != "joint":
                results[half + len(results) - 3][0:size, :] = total

        applied = added_ref[...]
        for b in range(count):
            if vector is None:
                rows = read(refs, right_views[0][b], size, slice(size, tall))
            else:
                rows = vector_ref[:, b * size : (b + 1) * size]
            applied = applied + lax.dot_general(
                rows, left[:, b * size : (b + 1) * size], NT, preferred_element_type=jnp.float32
            )
        results[-1][...] = applied
        if form != "split":
            results[0][size:tall, 0:size] = applied.astype(jnp.bfloat16)
            results[0][size:tall, size:wide] = applied.astype(jnp.bfloat16)
        if form == "both":
            results[1][size:tall, :] = applied.astype(jnp.bfloat16)

    return pl.pallas_call(
        kernel,
        out_shape=tuple(outs),
        scratch_shapes=[pltpu.VMEM((size, size * count), jnp.bfloat16)],
        compiler_params=pltpu.CompilerParams(vmem_limit_bytes=VMEM),
        cost_estimate=pl.CostEstimate(
            flops=8 * size * size * size * count, bytes_accessed=24 * size * size, transcendentals=0
        ),
    )(pivots, partial, added, *extra, *operands.arrays)


def shards(interval_blocks, interval_pivots, boundary_pivots, interval_residuals):
    blocks = interval_blocks[0]
    size = blocks.shape[1]
    row, col = lax.axis_index("row"), lax.axis_index("col")
    count = lax.axis_size("row")
    position = lax.axis_index("loop")
    positions = lax.axis_size("loop")

    def halves(array):
        return [(array, None, 0), (array, None, size)]

    lefts, rights = blocks[1::2], blocks[0::2]
    ends_upper = inward(blocks[2:4])
    lefts_other = swap_middle(lefts)
    rights_across = swap_rows(rights, 2)
    residuals = interval_residuals[0]
    beside = lax.ppermute(residuals, "col", [(0, 1), (1, 0), (2, 3), (3, 2)])
    ends_lower_left = inward(blocks[1])
    ends_lower_right = inward(blocks[0])
    rights_beside = swap_rows(rights, 1)
    rights_last = swap_rows(rights_across, 1)

    beyond = swap_middle(jnp.stack([residuals, beside]))
    near = (residuals, beside, beyond[0], beyond[1])
    residuals = jnp.where(
        col == 1,
        jnp.concatenate([near[i] for i in (1, 0, 2, 3)], axis=1),
        jnp.concatenate([near[i] for i in (3, 2, 0, 1)], axis=1),
    )
    vectors = residuals[0::2]
    vectors = jnp.concatenate([vectors, swap_rows(vectors, 1)], axis=1)
    vectors = jnp.concatenate([vectors, swap_rows(vectors, 2)], axis=1)
    vectors = [jnp.broadcast_to(vectors[k][None], (EXTRA, vectors.shape[1])) for k in (0, 1)]
    adds = [
        jnp.broadcast_to(residuals[k][None], (EXTRA, size)).astype(jnp.float32) for k in (1, 3)
    ]

    own = lax.dynamic_index_in_dim(boundary_pivots, position, 0, keepdims=True)
    back = lax.dynamic_index_in_dim(
        boundary_pivots, (position + positions - 1) % positions, 0, keepdims=True
    )
    pivots = jnp.concatenate([interval_pivots[0], own, back], axis=0)
    pivots = (((pivots // size) ^ row) * size + pivots % size).reshape(pivots.shape[0], count, size)
    order = [
        lax.dynamic_index_in_dim(pivots, col ^ flip, 1, keepdims=True) for flip in (0, 1, 3, 2)
    ]
    pivots = jnp.concatenate(order, axis=1)

    def first(turn, k, end_left, end_right, vector, added, form):
        other = [(lefts_other, k, 0), (swap_middle(end_left), None, 0)]
        across = swap_rows(end_right, 2)
        ends = [end_right, swap_rows(end_right, 1), across, swap_rows(across, 1)]
        right = [
            [(tile, k, 0) for tile in (rights, rights_beside, rights_across, rights_last)],
            [(tile, None, 0) for tile in ends],
        ]
        partial = spread_own(pivots[turn], [(lefts, k, 0), (end_left, None, 0)], size, count)
        return compose(pivots[turn], partial, other, added, right, vector, form, size)

    upper, upper_vector = first(2, 1, ends_upper[1], ends_upper[0], vectors[1], adds[1], "joint")
    lower, _ = first(0, 0, ends_lower_left, ends_lower_right, vectors[0], adds[0], "joint")

    def later(turn, left, added, right, form):
        other = swap_middle(left)
        parts = []
        for tile in right:
            across = swap_rows(tile, 2)
            parts.append([tile, swap_rows(tile, 1), across, swap_rows(across, 1)])
        if len(parts) == 1:
            views = [[(tile, None, column) for tile in parts[0]] for column in (0, size)]
        else:
            views = [[(tile, None, 0) for tile in part] for part in parts]
        partial = spread_own(pivots[turn], halves(left), size, count)
        return compose(pivots[turn], partial, halves(other), added, views, None, form, size)

    whole, whole_o, whole_e, whole_vector = later(1, upper, upper_vector, [lower], "both")
    earlier = [from_behind(tile, "loop", 1) for tile in (whole_o, whole_e)]
    halved, halved_vector = later(3, whole, whole_vector, earlier, "joint")
    distant = from_behind(halved, "loop", 2)
    reduced_o, reduced_e, applied = later(4, halved, halved_vector, [distant], "split")

    middle = (col == 1) | (col == 2)
    block = jnp.where(middle, reduced_o, outward(reduced_e))
    vector = applied[:1]
    vector = jnp.where(middle, vector, outward(vector))
    share = interval_residuals.shape[2]
    return (block[None], lax.dynamic_slice_in_dim(vector, col * share, share, 1))


def solution(mesh):
    placed = (
        P("loop", None, "row", "col"),
        P("loop", None, None),
        P(),
        P("loop", None, ("row", "col")),
    )
    return jax.shard_map(
        shards,
        mesh=mesh,
        in_specs=placed,
        out_specs=(P("loop", "row", "col"), P("loop", ("row", "col"))),
        check_vma=False,
    )
```

time: 411 us -> 262 us (0.64)
  blocking collectives: 152 us -> 0 us
  local copies, waits for them, and re-layouts: 125 us -> 5.18 us
  waiting for transfers between devices: 85.6 us -> 164 us
  Pallas kernels: 0 us -> 46.7 us
  starting transfers between devices: 4.45 us -> 41.3 us
  matrix products: 27.3 us -> 0 us
  between operations: 14.5 us -> 1.43 us
    all_gather x5 -> x0, blocking collectives: 152 us -> none  [compose(): lax.all_gather(right_vector, ('row', 'col'), axis=0, tiled=True)]
    ppermute x0 -> x36, waiting for transfers between devices: none -> 143 us  [the longest x2 115 us: outward(): return lax.ppermute(value, 'col', [(1, 0), (2, 3)])]
    gather x10 -> x0, local copies, waits for them, and re-layouts: 112 us -> none  [the longest x5 65.4 us: compose(): moved = jnp.take(full_vector, pivots, axis=0)]
    all_gather x10 -> x0, waiting for transfers between devices: 68.9 us -> none  [the longest x5 50 us: compose(): segment = lax.all_gather(left_block, 'col', axis=1, tiled=True)]
    pallas_call x0 -> x10, Pallas kernels: none -> 46.7 us  [the longest x5 30.7 us: compose(): pl.pallas_call(kernel, out_shape=tuple(outs), scratch_shapes=[pltpu.VMEM(...]
    ppermute x0 -> x36, starting transfers between devices: none -> 39.3 us  [the longest x23 16.3 us: swap_rows(): return lax.ppermute(value, ('row', 'col'), pairs)]
    dot_general x10 -> x0, matrix products: 27.3 us -> none  [the longest x5 21.1 us: compose(): product = jnp.dot(segment, permuted, preferred_element_type=jnp.float32)]
    all_gather x3 -> x0, local copies, waits for them, and re-layouts: 8.62 us -> none  [compose(): column_panel = lax.all_gather(right_block, 'row', axis=0, tiled=True)]
  transfers between devices with their start and end apart: 14 -> 38, of which waited for: 7 -> 6; matrix products, arithmetic and copies ran while one was open for 29% -> 1% of each run, Pallas kernels for 0% -> 11%
where the time goes in v2:
time: 262 us; the launch traced here: 260 us
  waiting for transfers between devices  164 us (63%)
  Pallas kernels  46.7 us (18%)
  starting transfers between devices  41.3 us (16%)
  local copies, waits for them, and re-layouts  5.18 us (2%)
    ppermute x2, waiting for transfers between devices, outward(): return lax.ppermute(value, 'col', [(1, 0), (2, 3)])  115 us
    pallas_call x5, Pallas kernels, compose(): pl.pallas_call(kernel, out_shape=tuple(outs), scratch_shapes=[pltpu.VMEM(...  30.7 us
    ppermute x2, waiting for transfers between devices, from_behind(): lax.ppermute(value, axis, [(i, (i + by) % devices) for i in range(devices)])  20.9 us
    ppermute x3, waiting for transfers between devices, inward(): return lax.ppermute(value, 'col', [(0, 1), (3, 2)])  17.4 us
    ppermute x23, starting transfers between devices, swap_rows(): return lax.ppermute(value, ('row', 'col'), pairs)  16.3 us
    pallas_call x5, Pallas kernels, spread_own(): pl.pallas_call(kernel, out_shape=jax.ShapeDtypeStruct((size, size * count...  16 us
    ppermute x3, starting transfers between devices, inward(): return lax.ppermute(value, 'col', [(0, 1), (3, 2)])  15.4 us
    ppermute x1, waiting for transfers between devices, shards(): beside = lax.ppermute(residuals, 'col', [(0, 1), (1, 0), (2, 3), (3, 2)])  11.3 us
  transfers between devices with their start and end apart: 38, of which 6 were waited for; matrix products, arithmetic and copies ran while one was open for 1% of the time, Pallas kernels for 11%

profile of v2, /device:TPU:0, one launch (start us, length us, event | category | flops | bytes accessed | tf_op | source)
XLA Modules:
  0.0 260.5 jit_solution(3800362375914165537)
XLA Ops:
  0.6 2.4 slice_bitcast_fusion
  3.1 5.9 %collective-permute-start = (bf16[2,512,512]{2,1,0:T(8,128)(2,1)}, bf16[2,512,512]{2,1,0:T(8,128)(2,1)}, u32[]{:S(2)}, u32[]{:S(2)}) collective-permute-start(bf16[2,512,512]{2,1,0:T(8,128)(2,1)} %slice_bitcast_fusion), channel_id=1, source_target_pairs={{0,1},{3,2},{4,5},{7,6},{8,9},{11,10},{12,13},{15,14},{16,17},{19,... | collective-permute-start | bytes 3145736 | tf_op jit(solution)/shard_map/ppermute | solution.py:31
  9.9 1.0 slice_bitcast_fusion.3
  10.9 7.4 %collective-permute-start.14 = (bf16[512,512]{1,0:T(8,128)(2,1)}, bf16[512,512]{1,0:T(8,128)(2,1)}, u32[]{:S(2)}, u32[]{:S(2)}) collective-permute-start(bf16[512,512]{1,0:T(8,128)(2,1)} %get-tuple-element.31), channel_id=1, source_target_pairs={{0,1},{3,2},{4,5},{7,6},{8,9},{11,10},{12,13},{15,14},{16,17},{19,... | collective-permute-start | bytes 1572872 | tf_op jit(solution)/shard_map/ppermute | solution.py:31
  18.3 2.1 collective-permute-start.16
  20.6 11.3 %collective-permute-done.1 = bf16[4,128]{1,0:T(4,128)(2,1)S(1)} collective-permute-done((bf16[4,128]{1,0:T(4,128)(2,1)S(1)}, bf16[4,128]{1,0:T(4,128)(2,1)S(1)}, u32[]{:S(2)}, u32[]{:S(2)}) %collective-permute-start.1) | collective-permute-done | bytes 1056 | tf_op jit(solution)/shard_map/ppermute | solution.py:177
  35.1 8.1 %collective-permute-done.14.refs_1_ = bf16[512,512]{1,0:T(8,128)(2,1)} collective-permute-done((bf16[512,512]{1,0:T(8,128)(2,1)}, bf16[512,512]{1,0:T(8,128)(2,1)}, u32[]{:S(2)}, u32[]{:S(2)}) %collective-permute-start.14) | collective-permute-done | bytes 524320 | tf_op jit(solution)/shard_map/ppermute | solution.py:31
  43.9 9.4 %collective-permute-done.16.rest_7_ = bf16[512,512]{1,0:T(8,128)(2,1)} collective-permute-done((bf16[512,512]{1,0:T(8,128)(2,1)}, bf16[512,512]{1,0:T(8,128)(2,1)}, u32[]{:S(2)}, u32[]{:S(2)}) %collective-permute-start.16) | collective-permute-done | bytes 524320 | tf_op jit(solution)/shard_map/ppermute | solution.py:31
  56.9 4.0 %shard_map.62.partial_ref = bf16[512,2048]{1,0:T(8,128)(2,1)S(1)} custom-call(s32[4,512]{1,0:T(4,128)S(1)} %get-tuple-element.36.q_ref, bf16[2,512,512]{2,1,0:T(8,128)(2,1)S(1)} %get-tuple-element.33.refs_0_, bf16[512,512]{1,0:T(8,128)(2,1)} %collective-permute-done.14.refs_1_), custom_call_target="tpu_custom_call" | custom-call | flops 2147483648 | bytes 2097152 | tf_op jit(solution)/shard_map/pallas_call | solution.py:81
  60.9 1.3 slice_bitcast_fusion.1
  63.0 7.4 %shard_map.63 = (bf16[528,1024]{1,0:T(8,128)(2,1)S(1)}, f32[16,512]{1,0:T(8,128)}) custom-call(s32[4,512]{1,0:T(4,128)S(1)} %get-tuple-element.36.q_ref, bf16[512,2048]{1,0:T(8,128)(2,1)S(1)} %shard_map.62.partial_ref, f32[16,512]{1,0:T(8,128)S(1)} %broadcast_in_dim.30.added_ref, bf16[16,2048]{1,0:T(8,128)(2,1)S(1)} %broadcast_in_dim.32.rest_0_, ...), custom_call_target="tpu_custom_call" | custom-call | flops 4294967296 | bytes 6291456 | tf_op jit(solution)/shard_map/pallas_call | solution.py:150
  73.3 3.0 %shard_map.59.partial_ref = bf16[512,2048]{1,0:T(8,128)(2,1)S(1)} custom-call(s32[4,512]{1,0:T(4,128)S(1)} %get-tuple-element.37.q_ref, bf16[2,512,512]{2,1,0:T(8,128)(2,1)S(1)} %get-tuple-element.33.refs_0_, bf16[512,512]{1,0:T(8,128)(2,1)S(1)} %get-tuple-element.35.refs_1_), custom_call_target="tpu_custom_call" | custom-call | flops 2147483648 | bytes 2097152 | tf_op jit(solution)/shard_map/pallas_call | solution.py:81
  76.3 0.7 collective-permute-start.20
  77.1 5.8 %shard_map.60 = (bf16[528,1024]{1,0:T(8,128)(2,1)S(1)}, f32[16,512]{1,0:T(8,128)S(1)}) custom-call(s32[4,512]{1,0:T(4,128)S(1)} %get-tuple-element.37.q_ref, bf16[512,2048]{1,0:T(8,128)(2,1)S(1)} %shard_map.59.partial_ref, f32[16,512]{1,0:T(8,128)S(1)} %broadcast_in_dim.27.added_ref, bf16[16,2048]{1,0:T(8,128)(2,1)S(1)} %broadcast_in_dim.29.rest_0_, ...), custom_call_target="tpu_custom_call" | custom-call | flops 4294967296 | bytes 6291456 | tf_op jit(solution)/shard_map/pallas_call | solution.py:150
  82.9 0.7 collective-permute-start.13
  83.6 0.9 collective-permute-start.22
  84.5 3.0 %shard_map.61.partial_ref = bf16[512,2048]{1,0:T(8,128)(2,1)S(1)} custom-call(s32[4,512]{1,0:T(4,128)S(1)} %get-tuple-element.38.q_ref, bf16[528,1024]{1,0:T(8,128)(2,1)S(1)} %get-tuple-element.14.refs_0_), custom_call_target="tpu_custom_call" | custom-call | flops 2147483648 | bytes 2097152 | tf_op jit(solution)/shard_map/pallas_call | solution.py:81
  87.6 5.8 %shard_map.64 = (bf16[528,1024]{1,0:T(8,128)(2,1)S(1)}, bf16[528,512]{1,0:T(8,128)(2,1)S(1)}, bf16[512,512]{1,0:T(8,128)(2,1)S(1)}, f32[16,512]{1,0:T(8,128)S(1)}) custom-call(s32[4,512]{1,0:T(4,128)S(1)} %get-tuple-element.38.q_ref, bf16[512,2048]{1,0:T(8,128)(2,1)S(1)} %shard_map.61.partial_ref, f32[16,512]{1,0:T(8,128)S(1)} %get-tuple-element.15.added_ref, ...), custom_call_target="tpu_custom_call" | custom-call | flops 4294967296 | bytes 6291456 | tf_op jit(solution)/shard_map/pallas_call | solution.py:150
  93.4 1.5 collective-permute-start.24
  96.2 12.5 %collective-permute-done.24.rest_1_ = bf16[528,512]{1,0:T(8,128)(2,1)S(1)} collective-permute-done((bf16[528,512]{1,0:T(8,128)(2,1)S(1)}, bf16[528,512]{1,0:T(8,128)(2,1)S(1)}, u32[]{:S(2)}, u32[]{:S(2)}) %collective-permute-start.24) | collective-permute-done | bytes 540704 | tf_op jit(solution)/shard_map/ppermute | solution.py:17
  109.3 8.5 %collective-permute-done.28.rest_5_ = bf16[512,512]{1,0:T(8,128)(2,1)S(1)} collective-permute-done((bf16[512,512]{1,0:T(8,128)(2,1)S(1)}, bf16[512,512]{1,0:T(8,128)(2,1)S(1)}, u32[]{:S(2)}, u32[]{:S(2)}) %collective-permute-start.28) | collective-permute-done | bytes 524320 | tf_op jit(solution)/shard_map/ppermute | solution.py:17
  121.3 3.0 %shard_map.65.partial_ref = bf16[512,2048]{1,0:T(8,128)(2,1)S(1)} custom-call(s32[4,512]{1,0:T(4,128)S(1)} %get-tuple-element.39.q_ref, bf16[528,1024]{1,0:T(8,128)(2,1)S(1)} %get-tuple-element.17.refs_0_), custom_call_target="tpu_custom_call" | custom-call | flops 2147483648 | bytes 2097152 | tf_op jit(solution)/shard_map/pallas_call | solution.py:81
  124.4 5.8 %shard_map.66 = (bf16[528,1024]{1,0:T(8,128)(2,1)S(1)}, f32[16,512]{1,0:T(8,128)S(1)}) custom-call(s32[4,512]{1,0:T(4,128)S(1)} %get-tuple-element.39.q_ref, bf16[512,2048]{1,0:T(8,128)(2,1)S(1)} %shard_map.65.partial_ref, f32[16,512]{1,0:T(8,128)S(1)} %get-tuple-element.18.added_ref, bf16[528,1024]{1,0:T(8,128)(2,1)S(1)} %collective-permute-done.23.rest_0_, ...), custom_call_target="tpu_custom_call" | custom-call | flops 4294967296 | bytes 6291456 | tf_op jit(solution)/shard_map/pallas_call | solution.py:150
  130.2 0.7 collective-permute-start.34
  130.9 0.7 collective-permute-start.32
  131.6 0.7 collective-permute-start.33
  133.1 3.0 %shard_map.67.partial_ref = bf16[512,2048]{1,0:T(8,128)(2,1)S(1)} custom-call(s32[4,512]{1,0:T(4,128)S(1)} %get-tuple-element.40.q_ref, bf16[528,1024]{1,0:T(8,128)(2,1)S(1)} %get-tuple-element.21.refs_0_.rest_1_), custom_call_target="tpu_custom_call" | custom-call | flops 2147483648 | bytes 2097152 | tf_op jit(solution)/shard_map/pallas_call | solution.py:81
  136.2 5.8 %shard_map.68 = (bf16[512,512]{1,0:T(8,128)(2,1)S(1)}, bf16[512,512]{1,0:T(8,128)(2,1)S(1)}, f32[16,512]{1,0:T(8,128)S(1)}) custom-call(s32[4,512]{1,0:T(4,128)S(1)} %get-tuple-element.40.q_ref, bf16[512,2048]{1,0:T(8,128)(2,1)S(1)} %shard_map.67.partial_ref, f32[16,512]{1,0:T(8,128)S(1)} %get-tuple-element.22.added_ref, ...), custom_call_target="tpu_custom_call" | custom-call | flops 4294967296 | bytes 6291456 | tf_op jit(solution)/shard_map/pallas_call | solution.py:150
  142.0 1.3 collective-permute-start.36
  143.3 1.3 collective-permute-start.37
  144.6 114.5 %collective-permute-done.37 = f32[1,512]{1,0:T(1,128)S(1)} collective-permute-done((f32[1,512]{1,0:T(1,128)S(1)}, f32[1,512]{1,0:T(1,128)S(1)}, u32[]{:S(2)}, u32[]{:S(2)}) %collective-permute-start.37) | collective-permute-done | bytes 2080 | tf_op jit(solution)/shard_map/ppermute | solution.py:35
  259.6 0.8 select_bitcast_fusion
  (93 shorter events, 18.6 us)
Async XLA Ops:
  3.1 51.6 %collective-permute-start = (bf16[2,512,512]{2,1,0:T(8,128)(2,1)}, bf16[2,512,512]{2,1,0:T(8,128)(2,1)}, u32[]{:S(2)}, u32[]{:S(2)}) collective-permute-start(bf16[2,512,512]{2,1,0:T(8,128)(2,1)} %slice_bitcast_fusion), channel_id=1, source_target_pairs={{0,1},{3,2},{4,5},{7,6},{8,9},{11,10},{12,13},{15,14},{16,17},{19,... | collective-permute-start | bytes 3145736 | tf_op jit(solution)/shard_map/ppermute | solution.py:31
  9.0 22.9 %collective-permute-start.1 = (bf16[4,128]{1,0:T(4,128)(2,1)S(1)}, bf16[4,128]{1,0:T(4,128)(2,1)S(1)}, u32[]{:S(2)}, u32[]{:S(2)}) collective-permute-start(bf16[4,128]{1,0:T(4,128)(2,1)S(1)} %bitcast.34), channel_id=1, source_target_pairs={{0,1},{1,0},{2,3},{3,2},{4,5},{5,4},{6,7},{7,6},{8,9},{9,8},{10,11... | collective-permute-start | bytes 3080 | tf_op jit(solution)/shard_map/ppermute | solution.py:177
  9.1 44.8 %collective-permute-start.8 = (bf16[2,512,512]{2,1,0:T(8,128)(2,1)S(1)}, bf16[2,512,512]{2,1,0:T(8,128)(2,1)S(1)}, u32[]{:S(2)}, u32[]{:S(2)}) collective-permute-start(bf16[2,512,512]{2,1,0:T(8,128)(2,1)S(1)} %get-tuple-element.32.rest_3_), channel_id=1, source_target_pairs={{1,9},{2,10},{5,13},{6,14},{9,1},{10,2},{13,5},{14,6},{17,25},{18,... | collective-permute-start | bytes 3145736 | tf_op jit(solution)/shard_map/ppermute | solution.py:23
  10.9 32.2 %collective-permute-start.14 = (bf16[512,512]{1,0:T(8,128)(2,1)}, bf16[512,512]{1,0:T(8,128)(2,1)}, u32[]{:S(2)}, u32[]{:S(2)}) collective-permute-start(bf16[512,512]{1,0:T(8,128)(2,1)} %get-tuple-element.31), channel_id=1, source_target_pairs={{0,1},{3,2},{4,5},{7,6},{8,9},{11,10},{12,13},{15,14},{16,17},{19,... | collective-permute-start | bytes 1572872 | tf_op jit(solution)/shard_map/ppermute | solution.py:31
  18.3 34.9 %collective-permute-start.16 = (bf16[512,512]{1,0:T(8,128)(2,1)}, bf16[512,512]{1,0:T(8,128)(2,1)}, u32[]{:S(2)}, u32[]{:S(2)}) collective-permute-start(bf16[512,512]{1,0:T(8,128)(2,1)} %get-tuple-element.30), channel_id=1, source_target_pairs={{0,1},{3,2},{4,5},{7,6},{8,9},{11,10},{12,13},{15,14},{16,17},{19,... | collective-permute-start | bytes 1572872 | tf_op jit(solution)/shard_map/ppermute | solution.py:31
  34.1 21.3 %collective-permute-start.5 = (bf16[2,512,512]{2,1,0:T(8,128)(2,1)S(1)}, bf16[2,512,512]{2,1,0:T(8,128)(2,1)S(1)}, u32[]{:S(2)}, u32[]{:S(2)}) collective-permute-start(bf16[2,512,512]{2,1,0:T(8,128)(2,1)S(1)} %get-tuple-element.33.refs_0_), channel_id=1, source_target_pairs={{1,2},{2,1},{5,6},{6,5},{9,10},{10,9},{13,14},{14,13},{17,18},{18,... | collective-permute-start | bytes 3145736 | tf_op jit(solution)/shard_map/ppermute | solution.py:27
  43.1 19.1 %collective-permute-start.7 = (bf16[2,512,512]{2,1,0:T(8,128)(2,1)S(1)}, bf16[2,512,512]{2,1,0:T(8,128)(2,1)S(1)}, u32[]{:S(2)}, u32[]{:S(2)}) collective-permute-start(bf16[2,512,512]{2,1,0:T(8,128)(2,1)S(1)} %get-tuple-element.32.rest_3_), channel_id=1, source_target_pairs={{1,5},{2,6},{5,1},{6,2},{9,13},{10,14},{13,9},{14,10},{17,21},{18,... | collective-permute-start | bytes 3145736 | tf_op jit(solution)/shard_map/ppermute | solution.py:23
  53.9 9.0 %collective-permute-start.9 = (bf16[2,512,512]{2,1,0:T(8,128)(2,1)S(1)}, bf16[2,512,512]{2,1,0:T(8,128)(2,1)S(1)}, u32[]{:S(2)}, u32[]{:S(2)}) collective-permute-start(bf16[2,512,512]{2,1,0:T(8,128)(2,1)S(1)} %collective-permute-done.8.rest_5_), channel_id=1, source_target_pairs={{1,5},{2,6},{5,1},{6,2},{9,13},{10,14},{13,9},{14,10},{17,21},{18,... | collective-permute-start | bytes 3145736 | tf_op jit(solution)/shard_map/ppermute | solution.py:23
  54.7 8.2 %collective-permute-start.17 = (bf16[512,512]{1,0:T(8,128)(2,1)}, bf16[512,512]{1,0:T(8,128)(2,1)S(1)}, u32[]{:S(2)}, u32[]{:S(2)}) collective-permute-start(bf16[512,512]{1,0:T(8,128)(2,1)} %collective-permute-done.16.rest_7_), channel_id=1, source_target_pairs={{1,5},{2,6},{5,1},{6,2},{9,13},{10,14},{13,9},{14,10},{17,21},{18,... | collective-permute-start | bytes 1572872 | tf_op jit(solution)/shard_map/ppermute | solution.py:23
  55.4 7.5 %collective-permute-start.15 = (bf16[512,512]{1,0:T(8,128)(2,1)}, bf16[512,512]{1,0:T(8,128)(2,1)S(1)}, u32[]{:S(2)}, u32[]{:S(2)}) collective-permute-start(bf16[512,512]{1,0:T(8,128)(2,1)} %collective-permute-done.14.refs_1_), channel_id=1, source_target_pairs={{1,2},{2,1},{5,6},{6,5},{9,10},{10,9},{13,14},{14,13},{17,18},{18,... | collective-permute-start | bytes 1572872 | tf_op jit(solution)/shard_map/ppermute | solution.py:27
  56.1 6.8 %collective-permute-start.19 = (bf16[512,512]{1,0:T(8,128)(2,1)S(1)}, bf16[512,512]{1,0:T(8,128)(2,1)S(1)}, u32[]{:S(2)}, u32[]{:S(2)}) collective-permute-start(bf16[512,512]{1,0:T(8,128)(2,1)S(1)} %collective-permute-done.18.rest_9_), channel_id=1, source_target_pairs={{1,5},{2,6},{5,1},{6,2},{9,13},{10,14},{13,9},{14,10},{17,21},{18,... | collective-permute-start | bytes 1572872 | tf_op jit(solution)/shard_map/ppermute | solution.py:23
  62.2 10.4 %collective-permute-start.11 = (bf16[512,512]{1,0:T(8,128)(2,1)S(1)}, bf16[512,512]{1,0:T(8,128)(2,1)S(1)}, u32[]{:S(2)}, u32[]{:S(2)}) collective-permute-start(bf16[512,512]{1,0:T(8,128)(2,1)S(1)} %get-tuple-element.34.rest_7_), channel_id=1, source_target_pairs={{1,9},{2,10},{5,13},{6,14},{9,1},{10,2},{13,5},{14,6},{17,25},{18,... | collective-permute-start | bytes 1572872 | tf_op jit(solution)/shard_map/ppermute | solution.py:23
  70.4 13.2 %collective-permute-start.21 = (bf16[528,1024]{1,0:T(8,128)(2,1)S(1)}, bf16[528,1024]{1,0:T(8,128)(2,1)S(1)}, u32[]{:S(2)}, u32[]{:S(2)}) collective-permute-start(bf16[528,1024]{1,0:T(8,128)(2,1)S(1)} %get-tuple-element.16.rest_1_), channel_id=1, source_target_pairs={{1,9},{2,10},{5,13},{6,14},{9,1},{10,2},{13,5},{14,6},{17,25},{18,... | collective-permute-start | bytes 3244040 | tf_op jit(solution)/shard_map/ppermute | solution.py:23
  71.2 5.9 %collective-permute-start.10 = (bf16[512,512]{1,0:T(8,128)(2,1)S(1)}, bf16[512,512]{1,0:T(8,128)(2,1)S(1)}, u32[]{:S(2)}, u32[]{:S(2)}) collective-permute-start(bf16[512,512]{1,0:T(8,128)(2,1)S(1)} %get-tuple-element.34.rest_7_), channel_id=1, source_target_pairs={{1,5},{2,6},{5,1},{6,2},{9,13},{10,14},{13,9},{14,10},{17,21},{18,... | collective-permute-start | bytes 1572872 | tf_op jit(solution)/shard_map/ppermute | solution.py:23
  71.9 5.2 %collective-permute-start.6 = (bf16[512,512]{1,0:T(8,128)(2,1)S(1)}, bf16[512,512]{1,0:T(8,128)(2,1)S(1)}, u32[]{:S(2)}, u32[]{:S(2)}) collective-permute-start(bf16[512,512]{1,0:T(8,128)(2,1)S(1)} %get-tuple-element.35.refs_1_), channel_id=1, source_target_pairs={{1,2},{2,1},{5,6},{6,5},{9,10},{10,9},{13,14},{14,13},{17,18},{18,... | collective-permute-start | bytes 1572872 | tf_op jit(solution)/shard_map/ppermute | solution.py:27
  72.6 4.5 %collective-permute-start.12 = (bf16[512,512]{1,0:T(8,128)(2,1)S(1)}, bf16[512,512]{1,0:T(8,128)(2,1)S(1)}, u32[]{:S(2)}, u32[]{:S(2)}) collective-permute-start(bf16[512,512]{1,0:T(8,128)(2,1)S(1)} %collective-permute-done.11.rest_9_), channel_id=1, source_target_pairs={{1,5},{2,6},{5,1},{6,2},{9,13},{10,14},{13,9},{14,10},{17,21},{18,... | collective-permute-start | bytes 1572872 | tf_op jit(solution)/shard_map/ppermute | solution.py:23
  76.3 11.3 %collective-permute-start.20 = (bf16[528,1024]{1,0:T(8,128)(2,1)S(1)}, bf16[528,1024]{1,0:T(8,128)(2,1)S(1)}, u32[]{:S(2)}, u32[]{:S(2)}) collective-permute-start(bf16[528,1024]{1,0:T(8,128)(2,1)S(1)} %get-tuple-element.16.rest_1_), channel_id=1, source_target_pairs={{1,5},{2,6},{5,1},{6,2},{9,13},{10,14},{13,9},{14,10},{17,21},{18,... | collective-permute-start | bytes 3244040 | tf_op jit(solution)/shard_map/ppermute | solution.py:23
  82.9 4.7 %collective-permute-start.13 = (bf16[528,1024]{1,0:T(8,128)(2,1)S(1)}, bf16[528,1024]{1,0:T(8,128)(2,1)S(1)}, u32[]{:S(2)}, u32[]{:S(2)}) collective-permute-start(bf16[528,1024]{1,0:T(8,128)(2,1)S(1)} %get-tuple-element.14.refs_0_), channel_id=1, source_target_pairs={{1,2},{2,1},{5,6},{6,5},{9,10},{10,9},{13,14},{14,13},{17,18},{18,... | collective-permute-start | bytes 3244040 | tf_op jit(solution)/shard_map/ppermute | solution.py:27
  83.6 3.9 %collective-permute-start.22 = (bf16[528,1024]{1,0:T(8,128)(2,1)S(1)}, bf16[528,1024]{1,0:T(8,128)(2,1)S(1)}, u32[]{:S(2)}, u32[]{:S(2)}) collective-permute-start(bf16[528,1024]{1,0:T(8,128)(2,1)S(1)} %collective-permute-done.21.rest_3_), channel_id=1, source_target_pairs={{1,5},{2,6},{5,1},{6,2},{9,13},{10,14},{13,9},{14,10},{17,21},{18,... | collective-permute-start | bytes 3244040 | tf_op jit(solution)/shard_map/ppermute | solution.py:23
  93.4 15.2 %collective-permute-start.24 = (bf16[528,512]{1,0:T(8,128)(2,1)S(1)}, bf16[528,512]{1,0:T(8,128)(2,1)S(1)}, u32[]{:S(2)}, u32[]{:S(2)}) collective-permute-start(bf16[528,512]{1,0:T(8,128)(2,1)S(1)} %get-tuple-element.19), channel_id=1, source_target_pairs={{0,16},{16,0},{1,17},{17,1},{2,18},{18,2},{3,19},{19,3},{4,20},{20... | collective-permute-start | bytes 1622024 | tf_op jit(solution)/shard_map/ppermute | solution.py:17
  94.9 22.9 %collective-permute-start.28 = (bf16[512,512]{1,0:T(8,128)(2,1)S(1)}, bf16[512,512]{1,0:T(8,128)(2,1)S(1)}, u32[]{:S(2)}, u32[]{:S(2)}) collective-permute-start(bf16[512,512]{1,0:T(8,128)(2,1)S(1)} %get-tuple-element.20), channel_id=1, source_target_pairs={{0,16},{16,0},{1,17},{17,1},{2,18},{18,2},{3,19},{19,3},{4,20},{20... | collective-permute-start | bytes 1572872 | tf_op jit(solution)/shard_map/ppermute | solution.py:17
  95.4 28.9 %collective-permute-start.23 = (bf16[528,1024]{1,0:T(8,128)(2,1)S(1)}, bf16[528,1024]{1,0:T(8,128)(2,1)S(1)}, u32[]{:S(2)}, u32[]{:S(2)}) collective-permute-start(bf16[528,1024]{1,0:T(8,128)(2,1)S(1)} %get-tuple-element.17.refs_0_), channel_id=1, source_target_pairs={{1,2},{2,1},{5,6},{6,5},{9,10},{10,9},{13,14},{14,13},{17,18},{18,... | collective-permute-start | bytes 3244040 | tf_op jit(solution)/shard_map/ppermute | solution.py:27
  108.6 10.6 %collective-permute-start.26 = (bf16[528,512]{1,0:T(8,128)(2,1)S(1)}, bf16[528,512]{1,0:T(8,128)(2,1)S(1)}, u32[]{:S(2)}, u32[]{:S(2)}) collective-permute-start(bf16[528,512]{1,0:T(8,128)(2,1)S(1)} %collective-permute-done.24.rest_1_), channel_id=1, source_target_pairs={{1,9},{2,10},{5,13},{6,14},{9,1},{10,2},{13,5},{14,6},{17,25},{18,... | collective-permute-start | bytes 1622024 | tf_op jit(solution)/shard_map/ppermute | solution.py:23
  118.5 5.9 %collective-permute-start.25 = (bf16[528,512]{1,0:T(8,128)(2,1)S(1)}, bf16[528,512]{1,0:T(8,128)(2,1)S(1)}, u32[]{:S(2)}, u32[]{:S(2)}) collective-permute-start(bf16[528,512]{1,0:T(8,128)(2,1)S(1)} %collective-permute-done.24.rest_1_), channel_id=1, source_target_pairs={{1,5},{2,6},{5,1},{6,2},{9,13},{10,14},{13,9},{14,10},{17,21},{18,... | collective-permute-start | bytes 1622024 | tf_op jit(solution)/shard_map/ppermute | solution.py:23
  119.2 5.2 %collective-permute-start.27 = (bf16[528,512]{1,0:T(8,128)(2,1)S(1)}, bf16[528,512]{1,0:T(8,128)(2,1)S(1)}, u32[]{:S(2)}, u32[]{:S(2)}) collective-permute-start(bf16[528,512]{1,0:T(8,128)(2,1)S(1)} %collective-permute-done.26.rest_3_), channel_id=1, source_target_pairs={{1,5},{2,6},{5,1},{6,2},{9,13},{10,14},{13,9},{14,10},{17,21},{18,... | collective-permute-start | bytes 1622024 | tf_op jit(solution)/shard_map/ppermute | solution.py:23
  119.9 4.4 %collective-permute-start.29 = (bf16[512,512]{1,0:T(8,128)(2,1)S(1)}, bf16[512,512]{1,0:T(8,128)(2,1)S(1)}, u32[]{:S(2)}, u32[]{:S(2)}) collective-permute-start(bf16[512,512]{1,0:T(8,128)(2,1)S(1)} %collective-permute-done.28.rest_5_), channel_id=1, source_target_pairs={{1,5},{2,6},{5,1},{6,2},{9,13},{10,14},{13,9},{14,10},{17,21},{18,... | collective-permute-start | bytes 1572872 | tf_op jit(solution)/shard_map/ppermute | solution.py:23
  120.6 3.7 %collective-permute-start.31 = (bf16[512,512]{1,0:T(8,128)(2,1)S(1)}, bf16[512,512]{1,0:T(8,128)(2,1)S(1)}, u32[]{:S(2)}, u32[]{:S(2)}) collective-permute-start(bf16[512,512]{1,0:T(8,128)(2,1)S(1)} %collective-permute-done.30.rest_7_), channel_id=1, source_target_pairs={{1,5},{2,6},{5,1},{6,2},{9,13},{10,14},{13,9},{14,10},{17,21},{18,... | collective-permute-start | bytes 1572872 | tf_op jit(solution)/shard_map/ppermute | solution.py:23
  130.9 5.2 %collective-permute-start.32 = (bf16[528,1024]{1,0:T(8,128)(2,1)S(1)}, bf16[528,1024]{1,0:T(8,128)(2,1)S(1)}, u32[]{:S(2)}, u32[]{:S(2)}) collective-permute-start(bf16[528,1024]{1,0:T(8,128)(2,1)S(1)} %get-tuple-element.21.refs_0_.rest_1_), channel_id=1, source_target_pairs={{1,2},{2,1},{5,6},{6,5},{9,10},{10,9},{13,14},{14,13},{17,18},{18,... | collective-permute-start | bytes 3244040 | tf_op jit(solution)/shard_map/ppermute | solution.py:27
  131.6 4.5 %collective-permute-start.33 = (bf16[528,1024]{1,0:T(8,128)(2,1)S(1)}, bf16[528,1024]{1,0:T(8,128)(2,1)S(1)}, u32[]{:S(2)}, u32[]{:S(2)}) collective-permute-start(bf16[528,1024]{1,0:T(8,128)(2,1)S(1)} %get-tuple-element.21.refs_0_.rest_1_), channel_id=1, source_target_pairs={{1,5},{2,6},{5,1},{6,2},{9,13},{10,14},{13,9},{14,10},{17,21},{18,... | collective-permute-start | bytes 3244040 | tf_op jit(solution)/shard_map/ppermute | solution.py:23
  132.4 3.8 %collective-permute-start.35 = (bf16[528,1024]{1,0:T(8,128)(2,1)S(1)}, bf16[528,1024]{1,0:T(8,128)(2,1)S(1)}, u32[]{:S(2)}, u32[]{:S(2)}) collective-permute-start(bf16[528,1024]{1,0:T(8,128)(2,1)S(1)} %collective-permute-done.34.rest_3_), channel_id=1, source_target_pairs={{1,5},{2,6},{5,1},{6,2},{9,13},{10,14},{13,9},{14,10},{17,21},{18,... | collective-permute-start | bytes 3244040 | tf_op jit(solution)/shard_map/ppermute | solution.py:23
  142.0 117.7 %collective-permute-start.36 = (bf16[512,512]{1,0:T(8,128)(2,1)S(1)}, bf16[512,512]{1,0:T(8,128)(2,1)S(1)}, u32[]{:S(2)}, u32[]{:S(2)}) collective-permute-start(bf16[512,512]{1,0:T(8,128)(2,1)S(1)} %get-tuple-element.24), channel_id=1, source_target_pairs={{1,0},{2,3},{5,4},{6,7},{9,8},{10,11},{13,12},{14,15},{17,16},{18,... | collective-permute-start | bytes 1572872 | tf_op jit(solution)/shard_map/ppermute | solution.py:35
  143.3 115.8 %collective-permute-start.37 = (f32[1,512]{1,0:T(1,128)S(1)}, f32[1,512]{1,0:T(1,128)S(1)}, u32[]{:S(2)}, u32[]{:S(2)}) collective-permute-start(f32[1,512]{1,0:T(1,128)S(1)} %slice.90), channel_id=1, source_target_pairs={{1,0},{2,3},{5,4},{6,7},{9,8},{10,11},{13,12},{14,15},{17,16},{18,... | collective-permute-start | bytes 6152 | tf_op jit(solution)/shard_map/ppermute | solution.py:35
  (10 other events, 61.5 us)

commit v3 on v2

v3 whole, which is shorter than its diff:
```python
import jax
import jax.numpy as jnp
from jax import lax
from jax.experimental import pallas as pl
from jax.experimental.pallas import tpu as pltpu
from jax.sharding import PartitionSpec as P

EXTRA = 16
VMEM = 24 * 1024 * 1024
NT = (((1,), (1,)), ((), ()))


def from_behind(value, axis, by):
    devices = lax.axis_size(axis)
    if by % devices == 0:
        return value
    return lax.ppermute(value, axis, [(i, (i + by) % devices) for i in range(devices)])


def swap_rows(value, flip):
    rows, cols = lax.axis_size("row"), lax.axis_size("col")
    pairs = [(r * cols + c, (r ^ flip) * cols + c) for r in range(rows) for c in (1, 2)]
    return lax.ppermute(value, ("row", "col"), pairs)


def swap_middle(value):
    return lax.ppermute(value, "col", [(1, 2), (2, 1)])


def inward(value):
    return lax.ppermute(value, "col", [(0, 1), (3, 2)])


def outward(value):
    return lax.ppermute(value, "col", [(1, 0), (2, 3)])


class Operands:
    def __init__(self):
        self.arrays = []

    def add(self, view):
        array, lead, column = view
        for i, known in enumerate(self.arrays):
            if known is array:
                return i, lead, column
        self.arrays.append(array)
        return len(self.arrays) - 1, lead, column


def read(refs, view, size, rows=None):
    which, lead, column = view
    ref = refs[which] if lead is None else refs[which].at[lead]
    return ref[rows or slice(0, size), column : column + size]


def spread(refs, views, q_ref, first, size, n):
    total = None
    for b, view in enumerate(views):
        at = lax.broadcasted_iota(jnp.int32, (size, size), 0) + n * size
        hot = jnp.where(at == q_ref[first + b : first + b + 1, :], 1.0, 0.0).astype(jnp.bfloat16)
        part = lax.dot_general(
            read(refs, view, size), hot, NT, preferred_element_type=jnp.float32
        )
        total = part if total is None else total + part
    return total


def spread_columns(pivots, first, tiles, size, count, onto=None):
    operands = Operands()
    views = [operands.add(view) for view in tiles]
    extra = [] if onto is None else [onto]

    def kernel(q_ref, *refs):
        out = refs[-1]

        @pl.loop(0, count)
        def _(n):
            here = pl.ds(pl.multiple_of(n * size, size), size)
            moved = spread(refs[len(extra) :], views, q_ref, first, size, n).astype(out.dtype)
            out[:, here] = moved if onto is None else moved + refs[0][:, here]

    return pl.pallas_call(
        kernel,
        out_shape=jax.ShapeDtypeStruct((size, size * count), jnp.bfloat16),
        compiler_params=pltpu.CompilerParams(vmem_limit_bytes=VMEM),
        cost_estimate=pl.CostEstimate(
            flops=4 * size * size * size * count, bytes_accessed=12 * size * size, transcendentals=0
        ),
    )(pivots, *extra, *operands.arrays)


def product(left, right, added, form, size, share=None, turn=0):
    count = left.shape[1] // size
    operands = Operands()
    views = [[operands.add(view) for view in half] for half in right]
    tall, wide = size + EXTRA, 2 * size
    shapes = {
        "joint": [(tall, wide)],
        "both": [(tall, wide), (tall, size), (size, size)],
        "split": [(size, size), (size, size)],
    }[form]
    outs = [jax.ShapeDtypeStruct(shape, jnp.bfloat16) for shape in shapes]
    outs.append(jax.ShapeDtypeStruct((EXTRA, size), jnp.float32))

    def kernel(left_ref, added_ref, *rest):
        refs = rest[: len(operands.arrays)]
        results = rest[len(refs) :]

        for half in range(2):
            total = None
            for b in range(count):
                part = jnp.dot(
                    left_ref[:, b * size : (b + 1) * size],
                    read(refs, views[half][b], size),
                    preferred_element_type=jnp.float32,
                )
                total = part if total is None else total + part
            total = total.astype(jnp.bfloat16)
            if form != "split":
                results[0][0:size, half * size : (half + 1) * size] = total
            if form != "joint":
                results[half + len(results) - 3][0:size, :] = total

        def pieces(b, k):
            here = slice(k * share, (k + 1) * share)
            own, end = (read(refs, views[half][b], size, slice(size, tall))[:, here] for half in (0, 1))
            return jnp.concatenate([end, own, own, end], axis=1) * added_ref[...]

        applied = added_ref[...] if share is None else pieces(0, turn + 1).astype(jnp.float32)
        for b in range(count):
            if share is None:
                rows = read(refs, views[0][b], size, slice(size, tall))
            else:
                rows = pieces(b, turn)
            applied = applied + lax.dot_general(
                rows, left_ref[:, b * size : (b + 1) * size], NT, preferred_element_type=jnp.float32
            )
        results[-1][...] = applied
        if form != "split":
            results[0][size:tall, 0:size] = applied.astype(jnp.bfloat16)
            results[0][size:tall, size:wide] = applied.astype(jnp.bfloat16)
        if form == "both":
            results[1][size:tall, :] = applied.astype(jnp.bfloat16)

    return pl.pallas_call(
        kernel,
        out_shape=tuple(outs),
        compiler_params=pltpu.CompilerParams(vmem_limit_bytes=VMEM),
        cost_estimate=pl.CostEstimate(
            flops=4 * size * size * size * count, bytes_accessed=24 * size * size, transcendentals=0
        ),
    )(left, added, *operands.arrays)


def after(value, *others):
    return lax.optimization_barrier((value, *others))[0]


def shards(interval_blocks, interval_pivots, boundary_pivots, interval_residuals):
    blocks = interval_blocks[0]
    size, share = blocks.shape[1], interval_residuals.shape[2]
    row, col = lax.axis_index("row"), lax.axis_index("col")
    count = lax.axis_size("row")
    position = lax.axis_index("loop")
    positions = lax.axis_size("loop")

    lefts = blocks[1::2]
    riding = jnp.broadcast_to(interval_residuals[0].reshape(1, -1), (EXTRA, size))
    tiles = [jnp.concatenate([blocks[k], riding], axis=0) for k in (0, 2)]
    rights = jnp.stack(tiles)
    ends_left = inward(lefts)
    lefts_other = swap_middle(lefts)
    rights_across = swap_rows(rights, 2)
    ends_right = {2: inward(tiles[1])}
    ends_right[0] = inward(tiles[0])
    rights_beside = swap_rows(rights, 1)

    own = lax.dynamic_index_in_dim(boundary_pivots, position, 0, keepdims=True)
    back = lax.dynamic_index_in_dim(
        boundary_pivots, (position + positions - 1) % positions, 0, keepdims=True
    )
    pivots = jnp.concatenate([interval_pivots[0], own, back], axis=0)
    pivots = (((pivots // size) ^ row) * size + pivots % size).reshape(pivots.shape[0], count, size)
    order = [
        lax.dynamic_index_in_dim(pivots, col ^ flip, 1, keepdims=True) for flip in (0, 1, 3, 2)
    ]
    pivots = jnp.concatenate(order, axis=1)
    places = lax.broadcasted_iota(jnp.int32, (EXTRA, size), 1)
    held = ((places < 2 * share) == (col == 1)).astype(jnp.bfloat16)

    ends_other = swap_middle(ends_left)
    rights_last = swap_rows(rights_across, 1)

    def panel(turn, k):
        own_tiles = [(lefts, k, 0), (ends_left, k, 0)]
        other_tiles = [(lefts_other, k, 0), (ends_other, k, 0)]
        partial = spread_columns(pivots[turn], 0, own_tiles, size, count)
        return spread_columns(pivots[turn], 2, other_tiles, size, count, partial)

    def first(turn, k, left):
        end = ends_right[turn]
        across = swap_rows(end, 2)
        ends = [end, swap_rows(end, 1), across, swap_rows(across, 1)]
        right = [
            [(tile, k, 0) for tile in (rights, rights_beside, rights_across, rights_last)],
            [(tile, None, 0) for tile in ends],
        ]
        return product(left, right, held, "joint", size, share, turn)

    upper, upper_vector = first(2, 1, panel(2, 1))
    lower, _ = first(0, 0, panel(0, 0))

    def later(turn, left, added, right, form):
        other = swap_middle(left)
        partial = spread_columns(pivots[turn], 0, [(left, None, 0), (left, None, size)], size, count)
        parts = []
        for tile in right:
            beside, across = swap_rows(tile, 1), swap_rows(tile, 2)
            parts.append([tile, beside, across, swap_rows(after(across, partial), 1)])
        if len(parts) == 1:
            views = [[(tile, None, column) for tile in parts[0]] for column in (0, size)]
        else:
            views = [[(tile, None, 0) for tile in part] for part in parts]
        other_tiles = [(other, None, 0), (other, None, size)]
        moved = spread_columns(pivots[turn], 2, other_tiles, size, count, partial)
        return product(moved, views, added, form, size)

    whole, whole_o, whole_e, whole_vector = later(1, upper, upper_vector, [lower], "both")
    earlier = [from_behind(tile, "loop", 1) for tile in (whole_o, whole_e)]
    halved, halved_vector = later(3, whole, whole_vector, earlier, "joint")
    distant = from_behind(halved, "loop", 2)
    reduced_o, reduced_e, applied = later(4, halved, halved_vector, [distant], "split")

    middle = (col == 1) | (col == 2)
    block = jnp.where(middle, reduced_o, outward(reduced_e))
    vector = applied[:1]
    vector = vector + swap_middle(vector)
    vector = jnp.where(middle, vector, outward(vector))
    return (block[None], lax.dynamic_slice_in_dim(vector, col * share, share, 1))


def solution(mesh):
    placed = (
        P("loop", None, "row", "col"),
        P("loop", None, None),
        P(),
        P("loop", None, ("row", "col")),
    )
    return jax.shard_map(
        shards,
        mesh=mesh,
        in_specs=placed,
        out_specs=(P("loop", "row", "col"), P("loop", ("row", "col"))),
        check_vma=False,
    )
```

time: 262 us -> 244 us (0.931)
  waiting for transfers between devices: 164 us -> 141 us
  Pallas kernels: 46.7 us -> 54 us
    ppermute x2, waiting for transfers between devices: 115 us -> 88 us  [outward(): return lax.ppermute(value, 'col', [(1, 0), (2, 3)])]
    ppermute x3, waiting for transfers between devices: 17.4 us -> 31.7 us  [inward(): return lax.ppermute(value, 'col', [(0, 1), (3, 2)])]
    ppermute x1 -> x0, waiting for transfers between devices: 11.3 us -> none  [shards(): beside = lax.ppermute(residuals, 'col', [(0, 1), (1, 0), (2, 3), (3, 2)])]
    pallas_call x10 -> x15, Pallas kernels: 46.7 us -> 54 us  [the longest x10 36.1 us: spread_columns(): pl.pallas_call(kernel, out_shape=jax.ShapeDtypeStruct((size, size * count...]
    ppermute x23 -> x21, starting transfers between devices: 16.3 us -> 18.3 us  [swap_rows(): return lax.ppermute(value, ('row', 'col'), pairs)]
    ppermute x7 -> x6, starting transfers between devices: 4.95 us -> 6.19 us  [swap_middle(): return lax.ppermute(value, 'col', [(1, 2), (2, 1)])]
  transfers between devices with their start and end apart: 38 -> 34, of which waited for: 6 -> 5; matrix products, arithmetic and copies ran while one was open for 1% -> 0% of each run, Pallas kernels for 11% -> 19%
where the time goes in v3:
time: 244 us; the launch traced here: 243 us
  waiting for transfers between devices  141 us (58%)
  Pallas kernels  54 us (22%)
  starting transfers between devices  42.2 us (17%)
  local copies, waits for them, and re-layouts  2.68 us (1%)
    ppermute x2, waiting for transfers between devices, outward(): return lax.ppermute(value, 'col', [(1, 0), (2, 3)])  88 us
    pallas_call x10, Pallas kernels, spread_columns(): pl.pallas_call(kernel, out_shape=jax.ShapeDtypeStruct((size, size * count...  36.1 us
    ppermute x3, waiting for transfers between devices, inward(): return lax.ppermute(value, 'col', [(0, 1), (3, 2)])  31.7 us
    ppermute x2, waiting for transfers between devices, from_behind(): lax.ppermute(value, axis, [(i, (i + by) % devices) for i in range(devices)])  20.9 us
    ppermute x21, starting transfers between devices, swap_rows(): return lax.ppermute(value, ('row', 'col'), pairs)  18.3 us
    pallas_call x5, Pallas kernels, product(): pl.pallas_call(kernel, out_shape=tuple(outs), compiler_params=pltpu.Compi...  17.8 us
    ppermute x3, starting transfers between devices, inward(): return lax.ppermute(value, 'col', [(0, 1), (3, 2)])  13 us
    ppermute x6, starting transfers between devices, swap_middle(): return lax.ppermute(value, 'col', [(1, 2), (2, 1)])  6.19 us
  transfers between devices with their start and end apart: 34, of which 5 were waited for; matrix products, arithmetic and copies ran while one was open for 0% of the time, Pallas kernels for 19%

profile of v3, /device:TPU:0, one launch (start us, length us, event | category | flops | bytes accessed | tf_op | source)
XLA Modules:
  0.0 242.6 jit_solution(9384896355362175556)
XLA Ops:
  0.6 2.4 slice.38.refs_0_
  3.1 6.0 %collective-permute-start = (bf16[2,512,512]{2,1,0:T(8,128)(2,1)}, bf16[2,512,512]{2,1,0:T(8,128)(2,1)}, u32[]{:S(2)}, u32[]{:S(2)}) collective-permute-start(bf16[2,512,512]{2,1,0:T(8,128)(2,1)} %slice.38.refs_0_), channel_id=1, source_target_pairs={{0,1},{3,2},{4,5},{7,6},{8,9},{11,10},{12,13},{15,14},{16,17},{19,... | collective-permute-start | bytes 3145736 | tf_op jit(solution)/shard_map/ppermute | solution.py:31
  10.2 3.8 %collective-permute-start.11 = (bf16[528,512]{1,0:T(8,128)(2,1)S(1)}, bf16[528,512]{1,0:T(8,128)(2,1)}, u32[]{:S(2)}, u32[]{:S(2)}) collective-permute-start(bf16[528,512]{1,0:T(8,128)(2,1)S(1)} %get-tuple-element.38), channel_id=1, source_target_pairs={{0,1},{3,2},{4,5},{7,6},{8,9},{11,10},{12,13},{15,14},{16,17},{19,... | collective-permute-start | bytes 1622024 | tf_op jit(solution)/shard_map/ppermute | solution.py:31
  14.1 1.7 collective-permute-start.1
  15.7 3.1 %collective-permute-start.6 = (bf16[528,512]{1,0:T(8,128)(2,1)S(1)}, bf16[528,512]{1,0:T(8,128)(2,1)}, u32[]{:S(2)}, u32[]{:S(2)}) collective-permute-start(bf16[528,512]{1,0:T(8,128)(2,1)S(1)} %get-tuple-element.52), channel_id=1, source_target_pairs={{0,1},{3,2},{4,5},{7,6},{8,9},{11,10},{12,13},{15,14},{16,17},{19,... | collective-permute-start | bytes 1622024 | tf_op jit(solution)/shard_map/ppermute | solution.py:31
  19.1 24.4 %collective-permute-done.11.rest_4_ = bf16[528,512]{1,0:T(8,128)(2,1)} collective-permute-done((bf16[528,512]{1,0:T(8,128)(2,1)S(1)}, bf16[528,512]{1,0:T(8,128)(2,1)}, u32[]{:S(2)}, u32[]{:S(2)}) %collective-permute-start.11) | collective-permute-done | bytes 540704 | tf_op jit(solution)/shard_map/ppermute | solution.py:31
  43.5 1.5 collective-permute-start.13
  44.9 1.7 collective-permute-start.2
  46.6 7.3 %collective-permute-done.6.rest_4_ = bf16[528,512]{1,0:T(8,128)(2,1)} collective-permute-done((bf16[528,512]{1,0:T(8,128)(2,1)S(1)}, bf16[528,512]{1,0:T(8,128)(2,1)}, u32[]{:S(2)}, u32[]{:S(2)}) %collective-permute-start.6) | collective-permute-done | bytes 540704 | tf_op jit(solution)/shard_map/ppermute | solution.py:31
  54.6 1.7 collective-permute-start.5
  56.5 1.5 collective-permute-start.12
  58.0 1.5 collective-permute-start.14
  59.5 4.5 %shard_map.64.refs_0_ = bf16[512,2048]{1,0:T(8,128)(2,1)S(1)} custom-call(s32[4,512]{1,0:T(4,128)S(1)} %get-tuple-element.42.q_ref, bf16[2,512,512]{2,1,0:T(8,128)(2,1)} %slice.38.refs_0_, bf16[2,512,512]{2,1,0:T(8,128)(2,1)} %collective-permute-done.refs_1_), custom_call_target="tpu_custom_call" | custom-call | flops 2147483648 | bytes 3145728 | tf_op jit(solution)/shard_map/pallas_call | solution.py:83
  64.7 4.5 %shard_map.65.left_ref = bf16[512,2048]{1,0:T(8,128)(2,1)S(1)} custom-call(s32[4,512]{1,0:T(4,128)S(1)} %get-tuple-element.42.q_ref, bf16[512,2048]{1,0:T(8,128)(2,1)S(1)} %shard_map.64.refs_0_, bf16[2,512,512]{2,1,0:T(8,128)(2,1)} %collective-permute-done.1.refs_1_, bf16[2,512,512]{2,1,0:T(8,128)(2,1)} %collective-permute-done.2.refs_2_), custom_call_target="tpu_custom_call" | custom-call | flops 2147483648 | bytes 3145728 | tf_op jit(solution)/shard_map/pallas_call | solution.py:83
  69.3 5.3 %shard_map.66 = (bf16[528,1024]{1,0:T(8,128)(2,1)S(1)}, f32[16,512]{1,0:T(8,128)}) custom-call(bf16[512,2048]{1,0:T(8,128)(2,1)S(1)} %shard_map.65.left_ref, bf16[16,512]{1,0:T(8,128)(2,1)S(1)} %iota.7.added_ref, bf16[2,528,512]{2,1,0:T(8,128)(2,1)S(1)} %pad_maximum_fusion.rest_0_, bf16[2,528,512]{2,1,0:T(8,128)(2,1)S(1)} %collective-permute-done.3.rest_1_, ...), custom_call_target="tpu_custom_call" | custom-call | flops 2147483648 | bytes 6291456 | tf_op jit(solution)/shard_map/pallas_call | solution.py:146
  76.7 4.5 %shard_map.59.refs_0_ = bf16[512,2048]{1,0:T(8,128)(2,1)S(1)} custom-call(s32[4,512]{1,0:T(4,128)S(1)} %get-tuple-element.43.q_ref, bf16[2,512,512]{2,1,0:T(8,128)(2,1)} %slice.38.refs_0_, bf16[2,512,512]{2,1,0:T(8,128)(2,1)} %collective-permute-done.refs_1_), custom_call_target="tpu_custom_call" | custom-call | flops 2147483648 | bytes 3145728 | tf_op jit(solution)/shard_map/pallas_call | solution.py:83
  81.3 4.6 %shard_map.60.left_ref = bf16[512,2048]{1,0:T(8,128)(2,1)S(1)} custom-call(s32[4,512]{1,0:T(4,128)S(1)} %get-tuple-element.43.q_ref, bf16[512,2048]{1,0:T(8,128)(2,1)S(1)} %shard_map.59.refs_0_, bf16[2,512,512]{2,1,0:T(8,128)(2,1)} %collective-permute-done.1.refs_1_, bf16[2,512,512]{2,1,0:T(8,128)(2,1)} %collective-permute-done.2.refs_2_), custom_call_target="tpu_custom_call" | custom-call | flops 2147483648 | bytes 3145728 | tf_op jit(solution)/shard_map/pallas_call | solution.py:83
  86.6 4.2 %shard_map.61 = (bf16[528,1024]{1,0:T(8,128)(2,1)S(1)}, f32[16,512]{1,0:T(8,128)S(1)}) custom-call(bf16[512,2048]{1,0:T(8,128)(2,1)S(1)} %shard_map.60.left_ref, bf16[16,512]{1,0:T(8,128)(2,1)S(1)} %iota.7.added_ref, bf16[2,528,512]{2,1,0:T(8,128)(2,1)S(1)} %pad_maximum_fusion.rest_0_, bf16[2,528,512]{2,1,0:T(8,128)(2,1)S(1)} %collective-permute-done.3.rest_1_, ...), custom_call_target="tpu_custom_call" | custom-call | flops 2147483648 | bytes 6291456 | tf_op jit(solution)/shard_map/pallas_call | solution.py:146
  91.5 3.0 %shard_map.62.refs_0_ = bf16[512,2048]{1,0:T(8,128)(2,1)S(1)} custom-call(s32[4,512]{1,0:T(4,128)S(1)} %get-tuple-element.44.q_ref, bf16[528,1024]{1,0:T(8,128)(2,1)S(1)} %get-tuple-element.18.refs_0_), custom_call_target="tpu_custom_call" | custom-call | flops 2147483648 | bytes 3145728 | tf_op jit(solution)/shard_map/pallas_call | solution.py:83
  95.3 3.0 %shard_map.63.left_ref = bf16[512,2048]{1,0:T(8,128)(2,1)S(1)} custom-call(s32[4,512]{1,0:T(4,128)S(1)} %get-tuple-element.44.q_ref, bf16[512,2048]{1,0:T(8,128)(2,1)S(1)} %shard_map.62.refs_0_, bf16[528,1024]{1,0:T(8,128)(2,1)S(1)} %collective-permute-done.10.refs_1_), custom_call_target="tpu_custom_call" | custom-call | flops 2147483648 | bytes 3145728 | tf_op jit(solution)/shard_map/pallas_call | solution.py:83
  98.3 2.8 %shard_map.67 = (bf16[528,1024]{1,0:T(8,128)(2,1)S(1)}, bf16[528,512]{1,0:T(8,128)(2,1)S(1)}, bf16[512,512]{1,0:T(8,128)(2,1)S(1)}, f32[16,512]{1,0:T(8,128)S(1)}) custom-call(bf16[512,2048]{1,0:T(8,128)(2,1)S(1)} %shard_map.63.left_ref, f32[16,512]{1,0:T(8,128)S(1)} %get-tuple-element.19.added_ref, bf16[528,1024]{1,0:T(8,128)(2,1)S(1)} %get-tuple-element.20.rest_0_, ...), custom_call_target="tpu_custom_call" | custom-call | flops 2147483648 | bytes 6291456 | tf_op jit(solution)/shard_map/pallas_call | solution.py:146
  101.1 1.5 collective-permute-start.19
  103.9 12.5 %collective-permute-done.19.rest_0_ = bf16[528,512]{1,0:T(8,128)(2,1)S(1)} collective-permute-done((bf16[528,512]{1,0:T(8,128)(2,1)S(1)}, bf16[528,512]{1,0:T(8,128)(2,1)S(1)}, u32[]{:S(2)}, u32[]{:S(2)}) %collective-permute-start.19) | collective-permute-done | bytes 540704 | tf_op jit(solution)/shard_map/ppermute | solution.py:17
  117.1 8.5 %collective-permute-done.23.rest_4_ = bf16[512,512]{1,0:T(8,128)(2,1)S(1)} collective-permute-done((bf16[512,512]{1,0:T(8,128)(2,1)S(1)}, bf16[512,512]{1,0:T(8,128)(2,1)S(1)}, u32[]{:S(2)}, u32[]{:S(2)}) %collective-permute-start.23) | collective-permute-done | bytes 524320 | tf_op jit(solution)/shard_map/ppermute | solution.py:17
  126.4 3.0 %shard_map.68.refs_0_ = bf16[512,2048]{1,0:T(8,128)(2,1)S(1)} custom-call(s32[4,512]{1,0:T(4,128)S(1)} %get-tuple-element.45.q_ref, bf16[528,1024]{1,0:T(8,128)(2,1)S(1)} %get-tuple-element.22.refs_0_), custom_call_target="tpu_custom_call" | custom-call | flops 2147483648 | bytes 3145728 | tf_op jit(solution)/shard_map/pallas_call | solution.py:83
  132.3 3.0 %shard_map.69.left_ref = bf16[512,2048]{1,0:T(8,128)(2,1)S(1)} custom-call(s32[4,512]{1,0:T(4,128)S(1)} %get-tuple-element.45.q_ref, bf16[512,2048]{1,0:T(8,128)(2,1)S(1)} %shard_map.68.refs_0_, bf16[528,1024]{1,0:T(8,128)(2,1)S(1)} %collective-permute-done.18.refs_1_), custom_call_target="tpu_custom_call" | custom-call | flops 2147483648 | bytes 3145728 | tf_op jit(solution)/shard_map/pallas_call | solution.py:83
  135.3 2.8 %shard_map.70 = (bf16[528,1024]{1,0:T(8,128)(2,1)S(1)}, f32[16,512]{1,0:T(8,128)S(1)}) custom-call(bf16[512,2048]{1,0:T(8,128)(2,1)S(1)} %shard_map.69.left_ref, f32[16,512]{1,0:T(8,128)S(1)} %get-tuple-element.23.added_ref, bf16[528,512]{1,0:T(8,128)(2,1)S(1)} %collective-permute-done.19.rest_0_, bf16[528,512]{1,0:T(8,128)(2,1)S(1)} %collective-permute-done.20.rest_1_, ...), custom_call_target="tpu_custom_call" | custom-call | flops 2147483648 | bytes 6291456 | tf_op jit(solution)/shard_map/pallas_call | solution.py:146
  140.3 3.0 %shard_map.71.refs_0_ = bf16[512,2048]{1,0:T(8,128)(2,1)S(1)} custom-call(s32[4,512]{1,0:T(4,128)S(1)} %get-tuple-element.46.q_ref, bf16[528,1024]{1,0:T(8,128)(2,1)S(1)} %get-tuple-element.28.refs_0_.rest_0_), custom_call_target="tpu_custom_call" | custom-call | flops 2147483648 | bytes 3145728 | tf_op jit(solution)/shard_map/pallas_call | solution.py:83
  144.1 3.0 %shard_map.72.left_ref = bf16[512,2048]{1,0:T(8,128)(2,1)S(1)} custom-call(s32[4,512]{1,0:T(4,128)S(1)} %get-tuple-element.46.q_ref, bf16[512,2048]{1,0:T(8,128)(2,1)S(1)} %shard_map.71.refs_0_, bf16[528,1024]{1,0:T(8,128)(2,1)S(1)} %collective-permute-done.27.refs_1_), custom_call_target="tpu_custom_call" | custom-call | flops 2147483648 | bytes 3145728 | tf_op jit(solution)/shard_map/pallas_call | solution.py:83
  147.1 2.8 %shard_map.73 = (bf16[512,512]{1,0:T(8,128)(2,1)S(1)}, bf16[512,512]{1,0:T(8,128)(2,1)S(1)}, f32[16,512]{1,0:T(8,128)S(1)}) custom-call(bf16[512,2048]{1,0:T(8,128)(2,1)S(1)} %shard_map.72.left_ref, f32[16,512]{1,0:T(8,128)S(1)} %get-tuple-element.29.added_ref, bf16[528,1024]{1,0:T(8,128)(2,1)S(1)} %get-tuple-element.28.refs_0_.rest_0_, ...), custom_call_target="tpu_custom_call" | custom-call | flops 2147483648 | bytes 6291456 | tf_op jit(solution)/shard_map/pallas_call | solution.py:146
  149.9 1.3 collective-permute-start.31
  153.3 88.0 %collective-permute-done.33 = f32[1,512]{1,0:T(1,128)S(1)} collective-permute-done((f32[1,512]{1,0:T(1,128)S(1)}, f32[1,512]{1,0:T(1,128)S(1)}, u32[]{:S(2)}, u32[]{:S(2)}) %collective-permute-start.33) | collective-permute-done | bytes 2080 | tf_op jit(solution)/shard_map/ppermute | solution.py:35
  (82 shorter events, 19.1 us)
Async XLA Ops:
  3.1 41.9 %collective-permute-start = (bf16[2,512,512]{2,1,0:T(8,128)(2,1)}, bf16[2,512,512]{2,1,0:T(8,128)(2,1)}, u32[]{:S(2)}, u32[]{:S(2)}) collective-permute-start(bf16[2,512,512]{2,1,0:T(8,128)(2,1)} %slice.38.refs_0_), channel_id=1, source_target_pairs={{0,1},{3,2},{4,5},{7,6},{8,9},{11,10},{12,13},{15,14},{16,17},{19,... | collective-permute-start | bytes 3145736 | tf_op jit(solution)/shard_map/ppermute | solution.py:31
  9.5 45.1 %collective-permute-start.4 = (bf16[2,528,512]{2,1,0:T(8,128)(2,1)S(1)}, bf16[2,528,512]{2,1,0:T(8,128)(2,1)S(1)}, u32[]{:S(2)}, u32[]{:S(2)}) collective-permute-start(bf16[2,528,512]{2,1,0:T(8,128)(2,1)S(1)} %pad_maximum_fusion.rest_0_), channel_id=1, source_target_pairs={{1,9},{2,10},{5,13},{6,14},{9,1},{10,2},{13,5},{14,6},{17,25},{18,... | collective-permute-start | bytes 3244040 | tf_op jit(solution)/shard_map/ppermute | solution.py:23
  10.2 33.2 %collective-permute-start.11 = (bf16[528,512]{1,0:T(8,128)(2,1)S(1)}, bf16[528,512]{1,0:T(8,128)(2,1)}, u32[]{:S(2)}, u32[]{:S(2)}) collective-permute-start(bf16[528,512]{1,0:T(8,128)(2,1)S(1)} %get-tuple-element.38), channel_id=1, source_target_pairs={{0,1},{3,2},{4,5},{7,6},{8,9},{11,10},{12,13},{15,14},{16,17},{19,... | collective-permute-start | bytes 1622024 | tf_op jit(solution)/shard_map/ppermute | solution.py:31
  14.1 42.4 %collective-permute-start.1 = (bf16[2,512,512]{2,1,0:T(8,128)(2,1)}, bf16[2,512,512]{2,1,0:T(8,128)(2,1)}, u32[]{:S(2)}, u32[]{:S(2)}) collective-permute-start(bf16[2,512,512]{2,1,0:T(8,128)(2,1)} %slice.38.refs_0_), channel_id=1, source_target_pairs={{1,2},{2,1},{5,6},{6,5},{9,10},{10,9},{13,14},{14,13},{17,18},{18,... | collective-permute-start | bytes 3145736 | tf_op jit(solution)/shard_map/ppermute | solution.py:27
  15.7 38.2 %collective-permute-start.6 = (bf16[528,512]{1,0:T(8,128)(2,1)S(1)}, bf16[528,512]{1,0:T(8,128)(2,1)}, u32[]{:S(2)}, u32[]{:S(2)}) collective-permute-start(bf16[528,512]{1,0:T(8,128)(2,1)S(1)} %get-tuple-element.52), channel_id=1, source_target_pairs={{0,1},{3,2},{4,5},{7,6},{8,9},{11,10},{12,13},{15,14},{16,17},{19,... | collective-permute-start | bytes 1622024 | tf_op jit(solution)/shard_map/ppermute | solution.py:31
  43.5 14.5 %collective-permute-start.13 = (bf16[528,512]{1,0:T(8,128)(2,1)}, bf16[528,512]{1,0:T(8,128)(2,1)}, u32[]{:S(2)}, u32[]{:S(2)}) collective-permute-start(bf16[528,512]{1,0:T(8,128)(2,1)} %collective-permute-done.11.rest_4_), channel_id=1, source_target_pairs={{1,9},{2,10},{5,13},{6,14},{9,1},{10,2},{13,5},{14,6},{17,25},{18,... | collective-permute-start | bytes 1622024 | tf_op jit(solution)/shard_map/ppermute | solution.py:23
  44.9 19.1 %collective-permute-start.2 = (bf16[2,512,512]{2,1,0:T(8,128)(2,1)}, bf16[2,512,512]{2,1,0:T(8,128)(2,1)}, u32[]{:S(2)}, u32[]{:S(2)}) collective-permute-start(bf16[2,512,512]{2,1,0:T(8,128)(2,1)} %collective-permute-done.refs_1_), channel_id=1, source_target_pairs={{1,2},{2,1},{5,6},{6,5},{9,10},{10,9},{13,14},{14,13},{17,18},{18,... | collective-permute-start | bytes 3145736 | tf_op jit(solution)/shard_map/ppermute | solution.py:27
  53.9 15.4 %collective-permute-start.3 = (bf16[2,528,512]{2,1,0:T(8,128)(2,1)S(1)}, bf16[2,528,512]{2,1,0:T(8,128)(2,1)S(1)}, u32[]{:S(2)}, u32[]{:S(2)}) collective-permute-start(bf16[2,528,512]{2,1,0:T(8,128)(2,1)S(1)} %pad_maximum_fusion.rest_0_), channel_id=1, source_target_pairs={{1,5},{2,6},{5,1},{6,2},{9,13},{10,14},{13,9},{14,10},{17,21},{18,... | collective-permute-start | bytes 3244040 | tf_op jit(solution)/shard_map/ppermute | solution.py:23
  54.6 14.7 %collective-permute-start.5 = (bf16[2,528,512]{2,1,0:T(8,128)(2,1)S(1)}, bf16[2,528,512]{2,1,0:T(8,128)(2,1)}, u32[]{:S(2)}, u32[]{:S(2)}) collective-permute-start(bf16[2,528,512]{2,1,0:T(8,128)(2,1)S(1)} %collective-permute-done.4.rest_2_), channel_id=1, source_target_pairs={{1,5},{2,6},{5,1},{6,2},{9,13},{10,14},{13,9},{14,10},{17,21},{18,... | collective-permute-start | bytes 3244040 | tf_op jit(solution)/shard_map/ppermute | solution.py:23
  56.5 12.8 %collective-permute-start.12 = (bf16[528,512]{1,0:T(8,128)(2,1)}, bf16[528,512]{1,0:T(8,128)(2,1)}, u32[]{:S(2)}, u32[]{:S(2)}) collective-permute-start(bf16[528,512]{1,0:T(8,128)(2,1)} %collective-permute-done.11.rest_4_), channel_id=1, source_target_pairs={{1,5},{2,6},{5,1},{6,2},{9,13},{10,14},{13,9},{14,10},{17,21},{18,... | collective-permute-start | bytes 1622024 | tf_op jit(solution)/shard_map/ppermute | solution.py:23
  58.0 11.3 %collective-permute-start.14 = (bf16[528,512]{1,0:T(8,128)(2,1)}, bf16[528,512]{1,0:T(8,128)(2,1)}, u32[]{:S(2)}, u32[]{:S(2)}) collective-permute-start(bf16[528,512]{1,0:T(8,128)(2,1)} %collective-permute-done.13.rest_6_), channel_id=1, source_target_pairs={{1,5},{2,6},{5,1},{6,2},{9,13},{10,14},{13,9},{14,10},{17,21},{18,... | collective-permute-start | bytes 1622024 | tf_op jit(solution)/shard_map/ppermute | solution.py:23
  64.0 12.0 %collective-permute-start.8 = (bf16[528,512]{1,0:T(8,128)(2,1)}, bf16[528,512]{1,0:T(8,128)(2,1)S(1)}, u32[]{:S(2)}, u32[]{:S(2)}) collective-permute-start(bf16[528,512]{1,0:T(8,128)(2,1)} %collective-permute-done.6.rest_4_), channel_id=1, source_target_pairs={{1,9},{2,10},{5,13},{6,14},{9,1},{10,2},{13,5},{14,6},{17,25},{18,... | collective-permute-start | bytes 1622024 | tf_op jit(solution)/shard_map/ppermute | solution.py:23
  74.6 19.9 %collective-permute-start.16 = (bf16[528,1024]{1,0:T(8,128)(2,1)S(1)}, bf16[528,1024]{1,0:T(8,128)(2,1)S(1)}, u32[]{:S(2)}, u32[]{:S(2)}) collective-permute-start(bf16[528,1024]{1,0:T(8,128)(2,1)S(1)} %get-tuple-element.20.rest_0_), channel_id=1, source_target_pairs={{1,9},{2,10},{5,13},{6,14},{9,1},{10,2},{13,5},{14,6},{17,25},{18,... | collective-permute-start | bytes 3244040 | tf_op jit(solution)/shard_map/ppermute | solution.py:23
  75.3 11.3 %collective-permute-start.7 = (bf16[528,512]{1,0:T(8,128)(2,1)}, bf16[528,512]{1,0:T(8,128)(2,1)S(1)}, u32[]{:S(2)}, u32[]{:S(2)}) collective-permute-start(bf16[528,512]{1,0:T(8,128)(2,1)} %collective-permute-done.6.rest_4_), channel_id=1, source_target_pairs={{1,5},{2,6},{5,1},{6,2},{9,13},{10,14},{13,9},{14,10},{17,21},{18,... | collective-permute-start | bytes 1622024 | tf_op jit(solution)/shard_map/ppermute | solution.py:23
  76.0 10.6 %collective-permute-start.9 = (bf16[528,512]{1,0:T(8,128)(2,1)S(1)}, bf16[528,512]{1,0:T(8,128)(2,1)S(1)}, u32[]{:S(2)}, u32[]{:S(2)}) collective-permute-start(bf16[528,512]{1,0:T(8,128)(2,1)S(1)} %collective-permute-done.8.rest_6_), channel_id=1, source_target_pairs={{1,5},{2,6},{5,1},{6,2},{9,13},{10,14},{13,9},{14,10},{17,21},{18,... | collective-permute-start | bytes 1622024 | tf_op jit(solution)/shard_map/ppermute | solution.py:23
  85.8 12.5 %collective-permute-start.15 = (bf16[528,1024]{1,0:T(8,128)(2,1)S(1)}, bf16[528,1024]{1,0:T(8,128)(2,1)S(1)}, u32[]{:S(2)}, u32[]{:S(2)}) collective-permute-start(bf16[528,1024]{1,0:T(8,128)(2,1)S(1)} %get-tuple-element.20.rest_0_), channel_id=1, source_target_pairs={{1,5},{2,6},{5,1},{6,2},{9,13},{10,14},{13,9},{14,10},{17,21},{18,... | collective-permute-start | bytes 3244040 | tf_op jit(solution)/shard_map/ppermute | solution.py:23
  90.8 4.5 %collective-permute-start.10 = (bf16[528,1024]{1,0:T(8,128)(2,1)S(1)}, bf16[528,1024]{1,0:T(8,128)(2,1)S(1)}, u32[]{:S(2)}, u32[]{:S(2)}) collective-permute-start(bf16[528,1024]{1,0:T(8,128)(2,1)S(1)} %get-tuple-element.18.refs_0_), channel_id=1, source_target_pairs={{1,2},{2,1},{5,6},{6,5},{9,10},{10,9},{13,14},{14,13},{17,18},{18,... | collective-permute-start | bytes 3244040 | tf_op jit(solution)/shard_map/ppermute | solution.py:27
  94.5 3.8 %collective-permute-start.17 = (bf16[528,1024]{1,0:T(8,128)(2,1)S(1)}, bf16[528,1024]{1,0:T(8,128)(2,1)S(1)}, u32[]{:S(2)}, u32[]{:S(2)}) collective-permute-start(bf16[528,1024]{1,0:T(8,128)(2,1)S(1)} %collective-permute-done.16.rest_2_), channel_id=1, source_target_pairs={{1,5},{2,6},{5,1},{6,2},{9,13},{10,14},{13,9},{14,10},{17,21},{18,... | collective-permute-start | bytes 3244040 | tf_op jit(solution)/shard_map/ppermute | solution.py:23
  101.1 15.2 %collective-permute-start.19 = (bf16[528,512]{1,0:T(8,128)(2,1)S(1)}, bf16[528,512]{1,0:T(8,128)(2,1)S(1)}, u32[]{:S(2)}, u32[]{:S(2)}) collective-permute-start(bf16[528,512]{1,0:T(8,128)(2,1)S(1)} %get-tuple-element.24), channel_id=1, source_target_pairs={{0,16},{16,0},{1,17},{17,1},{2,18},{18,2},{3,19},{19,3},{4,20},{20... | collective-permute-start | bytes 1622024 | tf_op jit(solution)/shard_map/ppermute | solution.py:17
  102.7 22.9 %collective-permute-start.23 = (bf16[512,512]{1,0:T(8,128)(2,1)S(1)}, bf16[512,512]{1,0:T(8,128)(2,1)S(1)}, u32[]{:S(2)}, u32[]{:S(2)}) collective-permute-start(bf16[512,512]{1,0:T(8,128)(2,1)S(1)} %get-tuple-element.26), channel_id=1, source_target_pairs={{0,16},{16,0},{1,17},{17,1},{2,18},{18,2},{3,19},{19,3},{4,20},{20... | collective-permute-start | bytes 1572872 | tf_op jit(solution)/shard_map/ppermute | solution.py:17
  103.2 29.1 %collective-permute-start.18 = (bf16[528,1024]{1,0:T(8,128)(2,1)S(1)}, bf16[528,1024]{1,0:T(8,128)(2,1)S(1)}, u32[]{:S(2)}, u32[]{:S(2)}) collective-permute-start(bf16[528,1024]{1,0:T(8,128)(2,1)S(1)} %get-tuple-element.22.refs_0_), channel_id=1, source_target_pairs={{1,2},{2,1},{5,6},{6,5},{9,10},{10,9},{13,14},{14,13},{17,18},{18,... | collective-permute-start | bytes 3244040 | tf_op jit(solution)/shard_map/ppermute | solution.py:27
  116.4 13.8 %collective-permute-start.21 = (bf16[528,512]{1,0:T(8,128)(2,1)S(1)}, bf16[528,512]{1,0:T(8,128)(2,1)S(1)}, u32[]{:S(2)}, u32[]{:S(2)}) collective-permute-start(bf16[528,512]{1,0:T(8,128)(2,1)S(1)} %collective-permute-done.19.rest_0_), channel_id=1, source_target_pairs={{1,9},{2,10},{5,13},{6,14},{9,1},{10,2},{13,5},{14,6},{17,25},{18,... | collective-permute-start | bytes 1622024 | tf_op jit(solution)/shard_map/ppermute | solution.py:23
  125.6 6.0 %collective-permute-start.25 = (bf16[512,512]{1,0:T(8,128)(2,1)S(1)}, bf16[512,512]{1,0:T(8,128)(2,1)S(1)}, u32[]{:S(2)}, u32[]{:S(2)}) collective-permute-start(bf16[512,512]{1,0:T(8,128)(2,1)S(1)} %collective-permute-done.23.rest_4_), channel_id=1, source_target_pairs={{1,9},{2,10},{5,13},{6,14},{9,1},{10,2},{13,5},{14,6},{17,25},{18,... | collective-permute-start | bytes 1572872 | tf_op jit(solution)/shard_map/ppermute | solution.py:23
  129.4 5.9 %collective-permute-start.20 = (bf16[528,512]{1,0:T(8,128)(2,1)S(1)}, bf16[528,512]{1,0:T(8,128)(2,1)S(1)}, u32[]{:S(2)}, u32[]{:S(2)}) collective-permute-start(bf16[528,512]{1,0:T(8,128)(2,1)S(1)} %collective-permute-done.19.rest_0_), channel_id=1, source_target_pairs={{1,5},{2,6},{5,1},{6,2},{9,13},{10,14},{13,9},{14,10},{17,21},{18,... | collective-permute-start | bytes 1622024 | tf_op jit(solution)/shard_map/ppermute | solution.py:23
  130.2 5.2 %collective-permute-start.22 = (bf16[528,512]{1,0:T(8,128)(2,1)S(1)}, bf16[528,512]{1,0:T(8,128)(2,1)S(1)}, u32[]{:S(2)}, u32[]{:S(2)}) collective-permute-start(bf16[528,512]{1,0:T(8,128)(2,1)S(1)} %collective-permute-done.21.rest_2_), channel_id=1, source_target_pairs={{1,5},{2,6},{5,1},{6,2},{9,13},{10,14},{13,9},{14,10},{17,21},{18,... | collective-permute-start | bytes 1622024 | tf_op jit(solution)/shard_map/ppermute | solution.py:23
  130.9 4.4 %collective-permute-start.24 = (bf16[512,512]{1,0:T(8,128)(2,1)S(1)}, bf16[512,512]{1,0:T(8,128)(2,1)S(1)}, u32[]{:S(2)}, u32[]{:S(2)}) collective-permute-start(bf16[512,512]{1,0:T(8,128)(2,1)S(1)} %collective-permute-done.23.rest_4_), channel_id=1, source_target_pairs={{1,5},{2,6},{5,1},{6,2},{9,13},{10,14},{13,9},{14,10},{17,21},{18,... | collective-permute-start | bytes 1572872 | tf_op jit(solution)/shard_map/ppermute | solution.py:23
  138.1 5.2 %collective-permute-start.29 = (bf16[528,1024]{1,0:T(8,128)(2,1)S(1)}, bf16[528,1024]{1,0:T(8,128)(2,1)S(1)}, u32[]{:S(2)}, u32[]{:S(2)}) collective-permute-start(bf16[528,1024]{1,0:T(8,128)(2,1)S(1)} %get-tuple-element.28.refs_0_.rest_0_), channel_id=1, source_target_pairs={{1,9},{2,10},{5,13},{6,14},{9,1},{10,2},{13,5},{14,6},{17,25},{18,... | collective-permute-start | bytes 3244040 | tf_op jit(solution)/shard_map/ppermute | solution.py:23
  138.9 5.2 %collective-permute-start.27 = (bf16[528,1024]{1,0:T(8,128)(2,1)S(1)}, bf16[528,1024]{1,0:T(8,128)(2,1)S(1)}, u32[]{:S(2)}, u32[]{:S(2)}) collective-permute-start(bf16[528,1024]{1,0:T(8,128)(2,1)S(1)} %get-tuple-element.28.refs_0_.rest_0_), channel_id=1, source_target_pairs={{1,2},{2,1},{5,6},{6,5},{9,10},{10,9},{13,14},{14,13},{17,18},{18,... | collective-permute-start | bytes 3244040 | tf_op jit(solution)/shard_map/ppermute | solution.py:27
  139.6 7.5 %collective-permute-start.28 = (bf16[528,1024]{1,0:T(8,128)(2,1)S(1)}, bf16[528,1024]{1,0:T(8,128)(2,1)S(1)}, u32[]{:S(2)}, u32[]{:S(2)}) collective-permute-start(bf16[528,1024]{1,0:T(8,128)(2,1)S(1)} %get-tuple-element.28.refs_0_.rest_0_), channel_id=1, source_target_pairs={{1,5},{2,6},{5,1},{6,2},{9,13},{10,14},{13,9},{14,10},{17,21},{18,... | collective-permute-start | bytes 3244040 | tf_op jit(solution)/shard_map/ppermute | solution.py:23
  143.3 3.8 %collective-permute-start.30 = (bf16[528,1024]{1,0:T(8,128)(2,1)S(1)}, bf16[528,1024]{1,0:T(8,128)(2,1)S(1)}, u32[]{:S(2)}, u32[]{:S(2)}) collective-permute-start(bf16[528,1024]{1,0:T(8,128)(2,1)S(1)} %collective-permute-done.29.rest_2_), channel_id=1, source_target_pairs={{1,5},{2,6},{5,1},{6,2},{9,13},{10,14},{13,9},{14,10},{17,21},{18,... | collective-permute-start | bytes 3244040 | tf_op jit(solution)/shard_map/ppermute | solution.py:23
  149.9 91.9 %collective-permute-start.31 = (bf16[512,512]{1,0:T(8,128)(2,1)S(1)}, bf16[512,512]{1,0:T(8,128)(2,1)S(1)}, u32[]{:S(2)}, u32[]{:S(2)}) collective-permute-start(bf16[512,512]{1,0:T(8,128)(2,1)S(1)} %get-tuple-element.32), channel_id=1, source_target_pairs={{1,0},{2,3},{5,4},{6,7},{9,8},{10,11},{13,12},{14,15},{17,16},{18,... | collective-permute-start | bytes 1572872 | tf_op jit(solution)/shard_map/ppermute | solution.py:35
  152.0 89.3 %collective-permute-start.33 = (f32[1,512]{1,0:T(1,128)S(1)}, f32[1,512]{1,0:T(1,128)S(1)}, u32[]{:S(2)}, u32[]{:S(2)}) collective-permute-start(f32[1,512]{1,0:T(1,128)S(1)} %slice_add_fusion), channel_id=1, source_target_pairs={{1,0},{2,3},{5,4},{6,7},{9,8},{10,11},{13,12},{14,15},{17,16},{18,... | collective-permute-start | bytes 6152 | tf_op jit(solution)/shard_map/ppermute | solution.py:35
  (6 other events, 38.0 us)

commit v4 on v3

v4 whole, which is shorter than its diff:
```python
import jax
import jax.numpy as jnp
from jax import lax
from jax.experimental import pallas as pl
from jax.experimental.pallas import tpu as pltpu
from jax.sharding import PartitionSpec as P

EXTRA = 16
VMEM = 24 * 1024 * 1024
LIGHT = pl.CostEstimate(flops=1, bytes_accessed=1, transcendentals=0)
NT = (((1,), (1,)), ((), ()))


def from_behind(value, axis, by):
    devices = lax.axis_size(axis)
    if by % devices == 0:
        return value
    return lax.ppermute(value, axis, [(i, (i + by) % devices) for i in range(devices)])


def swap_rows(value, flip):
    rows, cols = lax.axis_size("row"), lax.axis_size("col")
    pairs = [(r * cols + c, (r ^ flip) * cols + c) for r in range(rows) for c in (1, 2)]
    return lax.ppermute(value, ("row", "col"), pairs)


def swap_middle(value):
    return lax.ppermute(value, "col", [(1, 2), (2, 1)])


def inward(value):
    return lax.ppermute(value, "col", [(0, 1), (3, 2)])


def outward(value):
    return lax.ppermute(value, "col", [(1, 0), (2, 3)])


class Operands:
    def __init__(self):
        self.arrays = []

    def add(self, view):
        array, lead, column = view
        for i, known in enumerate(self.arrays):
            if known is array:
                return i, lead, column
        self.arrays.append(array)
        return len(self.arrays) - 1, lead, column


def read(refs, view, size, rows=None):
    which, lead, column = view
    ref = refs[which] if lead is None else refs[which].at[lead]
    return ref[rows or slice(0, size), column : column + size]


def spread(refs, views, q_ref, size, n):
    total = None
    for (block, _), view in views:
        at = lax.broadcasted_iota(jnp.int32, (size, size), 0) + n * size
        hot = jnp.where(at == q_ref[block : block + 1, :], 1.0, 0.0).astype(jnp.bfloat16)
        part = lax.dot_general(
            read(refs, view, size), hot, NT, preferred_element_type=jnp.float32
        )
        total = part if total is None else total + part
    return total


def spread_columns(pivots, tiles, size, count, onto=None):
    operands = Operands()
    views = [((block, None), operands.add(view)) for block, view in tiles]
    extra = [] if onto is None else [onto]

    def kernel(q_ref, *refs):
        out = refs[-1]

        @pl.loop(0, count)
        def _(n):
            here = pl.ds(pl.multiple_of(n * size, size), size)
            moved = spread(refs[len(extra) :], views, q_ref, size, n).astype(out.dtype)
            out[:, here] = moved if onto is None else moved + refs[0][:, here]

    return pl.pallas_call(
        kernel,
        out_shape=jax.ShapeDtypeStruct((size, size * count), jnp.bfloat16),
        compiler_params=pltpu.CompilerParams(vmem_limit_bytes=VMEM),
        cost_estimate=pl.CostEstimate(
            flops=2 * len(tiles) * size * size * size * count,
            bytes_accessed=8 * size * size,
            transcendentals=0,
        ),
    )(pivots, *extra, *operands.arrays)


def product(left, right, size, vector=None, held=None, turn=0):
    count = left.shape[1] // size
    operands = Operands()
    views = [operands.add(view) for view in right]
    tall = size if vector is None else size + EXTRA
    outs = [jax.ShapeDtypeStruct((tall, size), jnp.bfloat16)]
    extra = []
    if held is not None:
        own_views = [operands.add(view) for view in vector]
        share = size // 4
        extra = [held]
    elif vector is not None:
        extra = [vector]
    if vector is not None:
        outs.append(jax.ShapeDtypeStruct((EXTRA, size), jnp.float32))

    def kernel(left_ref, *rest):
        extra_refs = rest[: len(extra)]
        refs = rest[len(extra) : len(extra) + len(operands.arrays)]
        results = rest[len(extra) + len(refs) :]

        total = None
        for b in range(count):
            part = jnp.dot(
                left_ref[:, b * size : (b + 1) * size],
                read(refs, views[b], size),
                preferred_element_type=jnp.float32,
            )
            total = part if total is None else total + part
        results[0][0:size, :] = total.astype(jnp.bfloat16)
        if vector is None:
            return

        def pieces(b, k):
            here = slice(k * share, (k + 1) * share)
            own, end = (
                read(refs, kind[b], size, slice(size, tall))[:, here] for kind in (own_views, views)
            )
            return jnp.concatenate([end, own, own, end], axis=1) * extra_refs[0][...]

        applied = extra_refs[0][...] if held is None else pieces(0, turn + 1).astype(jnp.float32)
        for b in range(count):
            if held is None:
                rows = read(refs, views[b], size, slice(size, tall))
            else:
                rows = pieces(b, turn)
            applied = applied + lax.dot_general(
                rows, left_ref[:, b * size : (b + 1) * size], NT, preferred_element_type=jnp.float32
            )
        results[1][...] = applied
        results[0][size:tall, :] = applied.astype(jnp.bfloat16)

    found = pl.pallas_call(
        kernel,
        out_shape=tuple(outs),
        compiler_params=pltpu.CompilerParams(vmem_limit_bytes=VMEM),
        cost_estimate=LIGHT,
    )(left, *extra, *operands.arrays)
    return found[0] if vector is None else found


def after(value, *others):
    return lax.optimization_barrier((value, *others))[0]


def plain(*tiles):
    return [(tile, None, 0) for tile in tiles]


def shards(interval_blocks, interval_pivots, boundary_pivots, interval_residuals):
    blocks = interval_blocks[0]
    size, share = blocks.shape[1], interval_residuals.shape[2]
    row, col = lax.axis_index("row"), lax.axis_index("col")
    count = lax.axis_size("row")
    position = lax.axis_index("loop")
    positions = lax.axis_size("loop")

    lefts = blocks[1::2]
    riding = jnp.broadcast_to(interval_residuals[0].reshape(1, -1), (EXTRA, size))
    tiles = [jnp.concatenate([blocks[k], riding], axis=0) for k in (0, 2)]
    rights = jnp.stack(tiles)
    ends_left = inward(lefts)
    lefts_other = swap_middle(lefts)
    rights_across = swap_rows(rights, 2)
    end_upper = inward(tiles[1])
    rights_beside = swap_rows(rights, 1)

    own = lax.dynamic_index_in_dim(boundary_pivots, position, 0, keepdims=True)
    back = lax.dynamic_index_in_dim(
        boundary_pivots, (position + positions - 1) % positions, 0, keepdims=True
    )
    pivots = jnp.concatenate([interval_pivots[0], own, back], axis=0)
    pivots = (((pivots // size) ^ row) * size + pivots % size).reshape(pivots.shape[0], count, size)
    order = [
        lax.dynamic_index_in_dim(pivots, col ^ flip, 1, keepdims=True) for flip in (0, 1, 3, 2)
    ]
    pivots = jnp.concatenate(order, axis=1)
    places = lax.broadcasted_iota(jnp.int32, (EXTRA, size), 1)
    held = ((places < 2 * share) == (col == 1)).astype(jnp.bfloat16)

    def tile_row(tile, across):
        return [tile, swap_rows(tile, 1), across, swap_rows(across, 1)]

    own_panels = [spread_columns(pivots[t], [(0, (lefts, k, 0))], size, count) for t, k in ((0, 0), (2, 1))]
    end_lower = inward(after(tiles[0], own_panels[1]))
    ends_far = [swap_middle(ends_left[k]) for k in (1, 0)][::-1]
    rights_last = swap_rows(rights_across, 1)
    panels = [
        spread_columns(
            pivots[t], [(1, (ends_left, k, 0)), (2, (lefts_other, k, 0))], size, count, own_panels[k]
        )
        for t, k in ((0, 0), (2, 1))
    ]
    end_upper = after(end_upper, *panels)
    upper_across = swap_rows(end_upper, 2)

    def own_tiles(k):
        return [(tile, k, 0) for tile in (rights, rights_beside, rights_across, rights_last)]

    panel = spread_columns(pivots[2], [(3, (ends_far[1], None, 0))], size, count, panels[1])
    upper_o = product(panel, own_tiles(1), size)
    lower_panel = after(panels[0], upper_o)
    lower_panel = spread_columns(pivots[0], [(3, (ends_far[0], None, 0))], size, count, lower_panel)
    lower_o = product(lower_panel, own_tiles(0), size)
    end_lower = after(end_lower, lower_panel)
    lower_across = swap_rows(end_lower, 2)
    upper_ends = plain(*tile_row(end_upper, upper_across))
    upper_e, vector = product(after(panel, lower_o), upper_ends, size, own_tiles(1), held, 2)
    lower_ends = plain(*tile_row(end_lower, lower_across))
    lower_e, _ = product(after(lower_panel, upper_e), lower_ends, size, own_tiles(0), held, 0)

    def stage(turn, left_o, left_e, added, right_o, right_e):
        other_o = swap_middle(left_o)
        across_o = swap_rows(right_o, 2)
        other_e = swap_middle(left_e)
        across_e = swap_rows(right_e, 2)
        panel = spread_columns(pivots[turn], [(0, (left_o, None, 0))], size, count)
        panel = spread_columns(
            pivots[turn], [(1, (left_e, None, 0)), (2, (other_o, None, 0))], size, count, panel
        )
        panel = spread_columns(pivots[turn], [(3, (other_e, None, 0))], size, count, panel)
        product_o = product(panel, plain(*tile_row(right_o, across_o)), size)
        panel = after(panel, product_o)
        product_e, vector = product(panel, plain(*tile_row(right_e, across_e)), size, added)
        return product_o, product_e, vector

    whole_o, whole_e, vector = stage(1, upper_o, upper_e, vector, lower_o, lower_e)
    earlier_o, earlier_e = from_behind(whole_o, "loop", 1), from_behind(whole_e, "loop", 1)
    halved_o, halved_e, vector = stage(3, whole_o, whole_e, vector, earlier_o, earlier_e)
    distant_o, distant_e = from_behind(halved_o, "loop", 2), from_behind(halved_e, "loop", 2)
    reduced_o, reduced_e, vector = stage(4, halved_o, halved_e, vector, distant_o, distant_e)

    middle = (col == 1) | (col == 2)
    block = jnp.where(middle, reduced_o, outward(reduced_e)[:size])
    vector = vector[:1]
    vector = vector + swap_middle(vector)
    vector = jnp.where(middle, vector, outward(vector))
    return (block[None], lax.dynamic_slice_in_dim(vector, col * share, share, 1))


def solution(mesh):
    placed = (
        P("loop", None, "row", "col"),
        P("loop", None, None),
        P(),
        P("loop", None, ("row", "col")),
    )
    return jax.shard_map(
        shards,
        mesh=mesh,
        in_specs=placed,
        out_specs=(P("loop", "row", "col"), P("loop", ("row", "col"))),
        check_vma=False,
    )
```

time: 244 us -> 261 us (1.070)
  starting transfers between devices: 42.2 us -> 57.1 us
  waiting for transfers between devices: 141 us -> 131 us
  local copies, waits for them, and re-layouts: 2.68 us -> 8.76 us
  Pallas kernels: 54 us -> 58 us
    ppermute x3, waiting for transfers between devices: 31.7 us -> 20.2 us  [inward(): return lax.ppermute(value, 'col', [(0, 1), (3, 2)])]
    ppermute x3, starting transfers between devices: 13 us -> 20.8 us  [inward(): return lax.ppermute(value, 'col', [(0, 1), (3, 2)])]
    ppermute x21 -> x27, starting transfers between devices: 18.3 us -> 23.8 us  [swap_rows(): return lax.ppermute(value, ('row', 'col'), pairs)]
    unnamed x10 -> x34, local copies, waits for them, and re-layouts: 0.03 us -> 5.02 us
    pallas_call x10 -> x15, Pallas kernels: 36.1 us -> 39.6 us  [spread_columns(): pl.pallas_call(kernel, out_shape=jax.ShapeDtypeStruct((size, size * count...]
    ppermute x6 -> x10, starting transfers between devices: 6.19 us -> 7.85 us  [swap_middle(): return lax.ppermute(value, 'col', [(1, 2), (2, 1)])]
    pallas_call x5 -> x10, Pallas kernels: 17.8 us -> 18.4 us  [product(): pl.pallas_call(kernel, out_shape=tuple(outs), compiler_params=pltpu.Compi...]
  transfers between devices with their start and end apart: 34 -> 44, of which waited for: 5 -> 5; matrix products, arithmetic and copies ran while one was open for 0% -> 1% of each run, Pallas kernels for 19% -> 19%
where the time goes in v4:
time: 261 us; the launch traced here: 259 us
  waiting for transfers between devices  131 us (50%)
  Pallas kernels  58 us (22%)
  starting transfers between devices  57.1 us (22%)
  local copies, waits for them, and re-layouts  8.76 us (3%)
  other arithmetic  2.83 us (1%)
    ppermute x2, waiting for transfers between devices, outward(): return lax.ppermute(value, 'col', [(1, 0), (2, 3)])  90.4 us
    pallas_call x15, Pallas kernels, spread_columns(): pl.pallas_call(kernel, out_shape=jax.ShapeDtypeStruct((size, size * count...  39.6 us
    ppermute x27, starting transfers between devices, swap_rows(): return lax.ppermute(value, ('row', 'col'), pairs)  23.8 us
    ppermute x3, starting transfers between devices, inward(): return lax.ppermute(value, 'col', [(0, 1), (3, 2)])  20.8 us
    ppermute x3, waiting for transfers between devices, inward(): return lax.ppermute(value, 'col', [(0, 1), (3, 2)])  20.2 us
    ppermute x2, waiting for transfers between devices, from_behind(): lax.ppermute(value, axis, [(i, (i + by) % devices) for i in range(devices)])  20 us
    pallas_call x10, Pallas kernels, product(): pl.pallas_call(kernel, out_shape=tuple(outs), compiler_params=pltpu.Compi...  18.4 us
    ppermute x10, starting transfers between devices, swap_middle(): return lax.ppermute(value, 'col', [(1, 2), (2, 1)])  7.85 us
  transfers between devices with their start and end apart: 44, of which 5 were waited for; matrix products, arithmetic and copies ran while one was open for 1% of the time, Pallas kernels for 19%

profile of v4, /device:TPU:0, one launch (start us, length us, event | category | flops | bytes accessed | tf_op | source)
XLA Modules:
  0.0 259.0 jit_solution(7412383123726702752)
XLA Ops:
  5.0 8.7 %collective-permute-start = (bf16[2,512,512]{2,1,0:T(8,128)(2,1)}, bf16[2,512,512]{2,1,0:T(8,128)(2,1)}, u32[]{:S(2)}, u32[]{:S(2)}) collective-permute-start(bf16[2,512,512]{2,1,0:T(8,128)(2,1)} %slice.52.refs_0_), channel_id=1, source_target_pairs={{0,1},{3,2},{4,5},{7,6},{8,9},{11,10},{12,13},{15,14},{16,17},{19,... | collective-permute-start | bytes 3145736 | tf_op jit(solution)/shard_map/ppermute | solution.py:32
  13.7 1.6 collective-permute-start.1
  16.0 4.1 %collective-permute-start.7 = (bf16[528,512]{1,0:T(8,128)(2,1)}, bf16[528,512]{1,0:T(8,128)(2,1)}, u32[]{:S(2)}, u32[]{:S(2)}) collective-permute-start(bf16[528,512]{1,0:T(8,128)(2,1)} %get-tuple-element.58), channel_id=1, source_target_pairs={{0,1},{3,2},{4,5},{7,6},{8,9},{11,10},{12,13},{15,14},{16,17},{19,... | collective-permute-start | bytes 1622024 | tf_op jit(solution)/shard_map/ppermute | solution.py:32
  21.4 15.1 %collective-permute-done.refs_1_ = bf16[2,512,512]{2,1,0:T(8,128)(2,1)} collective-permute-done((bf16[2,512,512]{2,1,0:T(8,128)(2,1)}, bf16[2,512,512]{2,1,0:T(8,128)(2,1)}, u32[]{:S(2)}, u32[]{:S(2)}) %collective-permute-start) | collective-permute-done | bytes 1048608 | tf_op jit(solution)/shard_map/ppermute | solution.py:32
  38.5 3.1 %shard_map.59.refs_0_ = bf16[512,2048]{1,0:T(8,128)(2,1)S(1)} custom-call(s32[4,512]{1,0:T(4,128)S(1)} %get-tuple-element.49.q_ref, bf16[2,512,512]{2,1,0:T(8,128)(2,1)} %slice.52.refs_0_), custom_call_target="tpu_custom_call" | custom-call | flops 1073741824 | bytes 2097152 | tf_op jit(solution)/shard_map/pallas_call | solution.py:84
  41.6 5.0 %collective-permute-done.7.rest_1_ = bf16[528,512]{1,0:T(8,128)(2,1)} collective-permute-done((bf16[528,512]{1,0:T(8,128)(2,1)}, bf16[528,512]{1,0:T(8,128)(2,1)}, u32[]{:S(2)}, u32[]{:S(2)}) %collective-permute-start.7) | collective-permute-done | bytes 540704 | tf_op jit(solution)/shard_map/ppermute | solution.py:32
  47.3 3.1 %shard_map.64.refs_0_ = bf16[512,2048]{1,0:T(8,128)(2,1)S(1)} custom-call(s32[4,512]{1,0:T(4,128)S(1)} %get-tuple-element.48.q_ref, bf16[2,512,512]{2,1,0:T(8,128)(2,1)} %slice.52.refs_0_), custom_call_target="tpu_custom_call" | custom-call | flops 1073741824 | bytes 2097152 | tf_op jit(solution)/shard_map/pallas_call | solution.py:84
  50.5 8.0 %collective-permute-start.16 = (bf16[528,512]{1,0:T(8,128)(2,1)S(1)}, bf16[528,512]{1,0:T(8,128)(2,1)}, u32[]{:S(2)}, u32[]{:S(2)}) collective-permute-start(bf16[528,512]{1,0:T(8,128)(2,1)S(1)} %copy-done.12), channel_id=1, source_target_pairs={{0,1},{3,2},{4,5},{7,6},{8,9},{11,10},{12,13},{15,14},{16,17},{19,... | collective-permute-start | bytes 1622024 | tf_op jit(solution)/shard_map/ppermute | solution.py:32
  58.5 4.5 %shard_map.60.refs_0_ = bf16[512,2048]{1,0:T(8,128)(2,1)S(1)} custom-call(s32[4,512]{1,0:T(4,128)S(1)} %get-tuple-element.49.q_ref, bf16[512,2048]{1,0:T(8,128)(2,1)S(1)} %shard_map.59.refs_0_, bf16[2,512,512]{2,1,0:T(8,128)(2,1)} %collective-permute-done.refs_1_, bf16[2,512,512]{2,1,0:T(8,128)(2,1)} %collective-permute-done.1.refs_2_), custom_call_target="tpu_custom_call" | custom-call | flops 2147483648 | bytes 2097152 | tf_op jit(solution)/shard_map/pallas_call | solution.py:84
  63.0 4.5 %shard_map.65.refs_0_ = bf16[512,2048]{1,0:T(8,128)(2,1)S(1)} custom-call(s32[4,512]{1,0:T(4,128)S(1)} %get-tuple-element.48.q_ref, bf16[512,2048]{1,0:T(8,128)(2,1)S(1)} %shard_map.64.refs_0_, bf16[2,512,512]{2,1,0:T(8,128)(2,1)} %collective-permute-done.refs_1_, bf16[2,512,512]{2,1,0:T(8,128)(2,1)} %collective-permute-done.1.refs_2_), custom_call_target="tpu_custom_call" | custom-call | flops 2147483648 | bytes 2097152 | tf_op jit(solution)/shard_map/pallas_call | solution.py:84
  67.6 1.5 collective-permute-start.9
  69.1 1.9 shard_map.61.left_ref
  73.0 1.9 shard_map.66.left_ref
  79.4 1.5 collective-permute-start.17
  80.9 1.5 collective-permute-start.19
  88.0 3.2 %shard_map.68 = (bf16[528,512]{1,0:T(8,128)(2,1)S(1)}, f32[16,512]{1,0:T(8,128)S(1)}) custom-call(bf16[512,2048]{1,0:T(8,128)(2,1)S(1)} %copy-done.1, bf16[16,512]{1,0:T(8,128)(2,1)S(1)} %iota.7.rest_0_, bf16[528,512]{1,0:T(8,128)(2,1)} %collective-permute-done.7.rest_1_, bf16[528,512]{1,0:T(8,128)(2,1)} %collective-permute-done.8.rest_2_, ...), custom_call_target="tpu_custom_call" | custom-call | flops 1 | bytes 1 | tf_op jit(solution)/shard_map/pallas_call | solution.py:148
  91.3 3.9 %shard_map.73 = (bf16[528,512]{1,0:T(8,128)(2,1)S(1)}, f32[16,512]{1,0:T(8,128)}) custom-call(bf16[512,2048]{1,0:T(8,128)(2,1)S(1)} %shard_map.66.left_ref, bf16[16,512]{1,0:T(8,128)(2,1)S(1)} %iota.7.rest_0_, bf16[528,512]{1,0:T(8,128)(2,1)} %collective-permute-done.16.rest_1_, bf16[528,512]{1,0:T(8,128)(2,1)} %collective-permute-done.17.rest_2_, ...), custom_call_target="tpu_custom_call" | custom-call | flops 1 | bytes 1 | tf_op jit(solution)/shard_map/pallas_call | solution.py:148
  101.0 1.9 shard_map.63.refs_0_
  102.9 3.0 %shard_map.69.refs_0_ = bf16[512,2048]{1,0:T(8,128)(2,1)S(1)} custom-call(s32[4,512]{1,0:T(4,128)S(1)} %get-tuple-element.50.q_ref, bf16[512,2048]{1,0:T(8,128)(2,1)S(1)} %shard_map.63.refs_0_, bf16[528,512]{1,0:T(8,128)(2,1)S(1)} %get-tuple-element.23.refs_1_, bf16[512,512]{1,0:T(8,128)(2,1)S(1)} %collective-permute-done.11.refs_2_), custom_call_target="tpu_custom_call" | custom-call | flops 2147483648 | bytes 2097152 | tf_op jit(solution)/shard_map/pallas_call | solution.py:84
  105.9 1.9 shard_map.70.left_ref
  109.1 1.7 shard_map.74
  112.9 13.2 %collective-permute-done.29.rest_1_ = bf16[528,512]{1,0:T(8,128)(2,1)S(1)} collective-permute-done((bf16[528,512]{1,0:T(8,128)(2,1)S(1)}, bf16[528,512]{1,0:T(8,128)(2,1)S(1)}, u32[]{:S(2)}, u32[]{:S(2)}) %collective-permute-start.29) | collective-permute-done | bytes 540704 | tf_op jit(solution)/shard_map/ppermute | solution.py:18
  127.5 6.9 %collective-permute-done.25.rest_0_ = bf16[512,512]{1,0:T(8,128)(2,1)S(1)} collective-permute-done((bf16[512,512]{1,0:T(8,128)(2,1)S(1)}, bf16[512,512]{1,0:T(8,128)(2,1)S(1)}, u32[]{:S(2)}, u32[]{:S(2)}) %collective-permute-start.25) | collective-permute-done | bytes 524320 | tf_op jit(solution)/shard_map/ppermute | solution.py:18
  138.6 1.9 shard_map.72.refs_0_
  140.5 3.0 %shard_map.75.refs_0_ = bf16[512,2048]{1,0:T(8,128)(2,1)S(1)} custom-call(s32[4,512]{1,0:T(4,128)S(1)} %get-tuple-element.51.q_ref, bf16[512,2048]{1,0:T(8,128)(2,1)S(1)} %shard_map.72.refs_0_, bf16[528,512]{1,0:T(8,128)(2,1)S(1)} %get-tuple-element.30.refs_1_, bf16[512,512]{1,0:T(8,128)(2,1)S(1)} %collective-permute-done.23.refs_2_), custom_call_target="tpu_custom_call" | custom-call | flops 2147483648 | bytes 2097152 | tf_op jit(solution)/shard_map/pallas_call | solution.py:84
  143.5 1.9 shard_map.76.left_ref
  146.7 1.7 shard_map.79
  154.1 1.9 shard_map.78.refs_0_
  156.0 3.0 %shard_map.80.refs_0_ = bf16[512,2048]{1,0:T(8,128)(2,1)S(1)} custom-call(s32[4,512]{1,0:T(4,128)S(1)} %get-tuple-element.52.q_ref, bf16[512,2048]{1,0:T(8,128)(2,1)S(1)} %shard_map.78.refs_0_, bf16[528,512]{1,0:T(8,128)(2,1)S(1)} %get-tuple-element.33.refs_1_.rest_1_, bf16[512,512]{1,0:T(8,128)(2,1)S(1)} %collective-permute-done.33.refs_2_), custom_call_target="tpu_custom_call" | custom-call | flops 2147483648 | bytes 2097152 | tf_op jit(solution)/shard_map/pallas_call | solution.py:84
  159.0 1.9 shard_map.81.left_ref
  162.2 1.7 shard_map.83
  167.2 90.4 %collective-permute-done.43 = f32[1,512]{1,0:T(1,128)S(1)} collective-permute-done((f32[1,512]{1,0:T(1,128)S(1)}, f32[1,512]{1,0:T(1,128)S(1)}, u32[]{:S(2)}, u32[]{:S(2)}) %collective-permute-start.43) | collective-permute-done | bytes 2080 | tf_op jit(solution)/shard_map/ppermute | solution.py:36
  (137 shorter events, 48.1 us)
Async XLA Ops:
  3.2 17.4 %collective-permute-start.4 = (bf16[2,528,512]{2,1,0:T(8,128)(2,1)S(1)}, bf16[2,528,512]{2,1,0:T(8,128)(2,1)S(1)}, u32[]{:S(2)}, u32[]{:S(2)}) collective-permute-start(bf16[2,528,512]{2,1,0:T(8,128)(2,1)S(1)} %pad_maximum_fusion.rest_0_.rest_5_), channel_id=1, source_target_pairs={{1,9},{2,10},{5,13},{6,14},{9,1},{10,2},{13,5},{14,6},{17,25},{18,... | collective-permute-start | bytes 3244040 | tf_op jit(solution)/shard_map/ppermute | solution.py:24
  5.0 31.5 %collective-permute-start = (bf16[2,512,512]{2,1,0:T(8,128)(2,1)}, bf16[2,512,512]{2,1,0:T(8,128)(2,1)}, u32[]{:S(2)}, u32[]{:S(2)}) collective-permute-start(bf16[2,512,512]{2,1,0:T(8,128)(2,1)} %slice.52.refs_0_), channel_id=1, source_target_pairs={{0,1},{3,2},{4,5},{7,6},{8,9},{11,10},{12,13},{15,14},{16,17},{19,... | collective-permute-start | bytes 3145736 | tf_op jit(solution)/shard_map/ppermute | solution.py:32
  13.7 36.8 %collective-permute-start.1 = (bf16[2,512,512]{2,1,0:T(8,128)(2,1)}, bf16[2,512,512]{2,1,0:T(8,128)(2,1)}, u32[]{:S(2)}, u32[]{:S(2)}) collective-permute-start(bf16[2,512,512]{2,1,0:T(8,128)(2,1)} %slice.52.refs_0_), channel_id=1, source_target_pairs={{1,2},{2,1},{5,6},{6,5},{9,10},{10,9},{13,14},{14,13},{17,18},{18,... | collective-permute-start | bytes 3145736 | tf_op jit(solution)/shard_map/ppermute | solution.py:28
  15.3 55.7 %collective-permute-start.3 = (bf16[2,528,512]{2,1,0:T(8,128)(2,1)S(1)}, bf16[2,528,512]{2,1,0:T(8,128)(2,1)S(1)}, u32[]{:S(2)}, u32[]{:S(2)}) collective-permute-start(bf16[2,528,512]{2,1,0:T(8,128)(2,1)S(1)} %pad_maximum_fusion.rest_0_.rest_5_), channel_id=1, source_target_pairs={{1,5},{2,6},{5,1},{6,2},{9,13},{10,14},{13,9},{14,10},{17,21},{18,... | collective-permute-start | bytes 3244040 | tf_op jit(solution)/shard_map/ppermute | solution.py:24
  16.0 30.6 %collective-permute-start.7 = (bf16[528,512]{1,0:T(8,128)(2,1)}, bf16[528,512]{1,0:T(8,128)(2,1)}, u32[]{:S(2)}, u32[]{:S(2)}) collective-permute-start(bf16[528,512]{1,0:T(8,128)(2,1)} %get-tuple-element.58), channel_id=1, source_target_pairs={{0,1},{3,2},{4,5},{7,6},{8,9},{11,10},{12,13},{15,14},{16,17},{19,... | collective-permute-start | bytes 1622024 | tf_op jit(solution)/shard_map/ppermute | solution.py:32
  20.6 50.4 %collective-permute-start.5 = (bf16[2,528,512]{2,1,0:T(8,128)(2,1)S(1)}, bf16[2,528,512]{2,1,0:T(8,128)(2,1)S(1)}, u32[]{:S(2)}, u32[]{:S(2)}) collective-permute-start(bf16[2,528,512]{2,1,0:T(8,128)(2,1)S(1)} %collective-permute-done.4.rest_2_.rest_7_), channel_id=1, source_target_pairs={{1,5},{2,6},{5,1},{6,2},{9,13},{10,14},{13,9},{14,10},{17,21},{18,... | collective-permute-start | bytes 3244040 | tf_op jit(solution)/shard_map/ppermute | solution.py:24
  37.8 29.8 %collective-permute-start.2 = (bf16[512,512]{1,0:T(8,128)(2,1)S(1)}, bf16[512,512]{1,0:T(8,128)(2,1)S(1)}, u32[]{:S(2)}, u32[]{:S(2)}) collective-permute-start(bf16[512,512]{1,0:T(8,128)(2,1)S(1)} %get-tuple-element.43), channel_id=1, source_target_pairs={{1,2},{2,1},{5,6},{6,5},{9,10},{10,9},{13,14},{14,13},{17,18},{18,... | collective-permute-start | bytes 1572872 | tf_op jit(solution)/shard_map/ppermute | solution.py:28
  46.6 26.4 %collective-permute-start.6 = (bf16[512,512]{1,0:T(8,128)(2,1)S(1)}, bf16[512,512]{1,0:T(8,128)(2,1)S(1)}, u32[]{:S(2)}, u32[]{:S(2)}) collective-permute-start(bf16[512,512]{1,0:T(8,128)(2,1)S(1)} %get-tuple-element.42), channel_id=1, source_target_pairs={{1,2},{2,1},{5,6},{6,5},{9,10},{10,9},{13,14},{14,13},{17,18},{18,... | collective-permute-start | bytes 1572872 | tf_op jit(solution)/shard_map/ppermute | solution.py:28
  50.5 24.5 %collective-permute-start.16 = (bf16[528,512]{1,0:T(8,128)(2,1)S(1)}, bf16[528,512]{1,0:T(8,128)(2,1)}, u32[]{:S(2)}, u32[]{:S(2)}) collective-permute-start(bf16[528,512]{1,0:T(8,128)(2,1)S(1)} %copy-done.12), channel_id=1, source_target_pairs={{0,1},{3,2},{4,5},{7,6},{8,9},{11,10},{12,13},{15,14},{16,17},{19,... | collective-permute-start | bytes 1622024 | tf_op jit(solution)/shard_map/ppermute | solution.py:32
  67.6 10.3 %collective-permute-start.9 = (bf16[528,512]{1,0:T(8,128)(2,1)}, bf16[528,512]{1,0:T(8,128)(2,1)}, u32[]{:S(2)}, u32[]{:S(2)}) collective-permute-start(bf16[528,512]{1,0:T(8,128)(2,1)} %collective-permute-done.7.rest_1_), channel_id=1, source_target_pairs={{1,9},{2,10},{5,13},{6,14},{9,1},{10,2},{13,5},{14,6},{17,25},{18,... | collective-permute-start | bytes 1622024 | tf_op jit(solution)/shard_map/ppermute | solution.py:24
  76.4 10.9 %collective-permute-start.8 = (bf16[528,512]{1,0:T(8,128)(2,1)}, bf16[528,512]{1,0:T(8,128)(2,1)}, u32[]{:S(2)}, u32[]{:S(2)}) collective-permute-start(bf16[528,512]{1,0:T(8,128)(2,1)} %collective-permute-done.7.rest_1_), channel_id=1, source_target_pairs={{1,5},{2,6},{5,1},{6,2},{9,13},{10,14},{13,9},{14,10},{17,21},{18,... | collective-permute-start | bytes 1622024 | tf_op jit(solution)/shard_map/ppermute | solution.py:24
  77.9 9.5 %collective-permute-start.10 = (bf16[528,512]{1,0:T(8,128)(2,1)}, bf16[528,512]{1,0:T(8,128)(2,1)}, u32[]{:S(2)}, u32[]{:S(2)}) collective-permute-start(bf16[528,512]{1,0:T(8,128)(2,1)} %collective-permute-done.9.rest_3_), channel_id=1, source_target_pairs={{1,5},{2,6},{5,1},{6,2},{9,13},{10,14},{13,9},{14,10},{17,21},{18,... | collective-permute-start | bytes 1622024 | tf_op jit(solution)/shard_map/ppermute | solution.py:24
  79.4 11.9 %collective-permute-start.17 = (bf16[528,512]{1,0:T(8,128)(2,1)}, bf16[528,512]{1,0:T(8,128)(2,1)}, u32[]{:S(2)}, u32[]{:S(2)}) collective-permute-start(bf16[528,512]{1,0:T(8,128)(2,1)} %collective-permute-done.16.rest_1_), channel_id=1, source_target_pairs={{1,5},{2,6},{5,1},{6,2},{9,13},{10,14},{13,9},{14,10},{17,21},{18,... | collective-permute-start | bytes 1622024 | tf_op jit(solution)/shard_map/ppermute | solution.py:24
  80.9 10.4 %collective-permute-start.19 = (bf16[528,512]{1,0:T(8,128)(2,1)}, bf16[528,512]{1,0:T(8,128)(2,1)}, u32[]{:S(2)}, u32[]{:S(2)}) collective-permute-start(bf16[528,512]{1,0:T(8,128)(2,1)} %collective-permute-done.18.rest_3_), channel_id=1, source_target_pairs={{1,5},{2,6},{5,1},{6,2},{9,13},{10,14},{13,9},{14,10},{17,21},{18,... | collective-permute-start | bytes 1622024 | tf_op jit(solution)/shard_map/ppermute | solution.py:24
  97.3 8.6 %collective-permute-start.12 = (bf16[528,512]{1,0:T(8,128)(2,1)S(1)}, bf16[528,512]{1,0:T(8,128)(2,1)S(1)}, u32[]{:S(2)}, u32[]{:S(2)}) collective-permute-start(bf16[528,512]{1,0:T(8,128)(2,1)S(1)} %get-tuple-element.23.refs_1_), channel_id=1, source_target_pairs={{1,2},{2,1},{5,6},{6,5},{9,10},{10,9},{13,14},{14,13},{17,18},{18,... | collective-permute-start | bytes 1622024 | tf_op jit(solution)/shard_map/ppermute | solution.py:28
  98.0 11.1 %collective-permute-start.20 = (bf16[528,512]{1,0:T(8,128)(2,1)S(1)}, bf16[528,512]{1,0:T(8,128)(2,1)S(1)}, u32[]{:S(2)}, u32[]{:S(2)}) collective-permute-start(bf16[528,512]{1,0:T(8,128)(2,1)S(1)} %get-tuple-element.29.rest_1_), channel_id=1, source_target_pairs={{1,5},{2,6},{5,1},{6,2},{9,13},{10,14},{13,9},{14,10},{17,21},{18,... | collective-permute-start | bytes 1622024 | tf_op jit(solution)/shard_map/ppermute | solution.py:24
  98.7 10.4 %collective-permute-start.22 = (bf16[528,512]{1,0:T(8,128)(2,1)S(1)}, bf16[528,512]{1,0:T(8,128)(2,1)S(1)}, u32[]{:S(2)}, u32[]{:S(2)}) collective-permute-start(bf16[528,512]{1,0:T(8,128)(2,1)S(1)} %collective-permute-done.21.rest_3_), channel_id=1, source_target_pairs={{1,5},{2,6},{5,1},{6,2},{9,13},{10,14},{13,9},{14,10},{17,21},{18,... | collective-permute-start | bytes 1622024 | tf_op jit(solution)/shard_map/ppermute | solution.py:24
  99.4 8.4 %collective-permute-start.13 = (bf16[512,512]{1,0:T(8,128)(2,1)S(1)}, bf16[512,512]{1,0:T(8,128)(2,1)S(1)}, u32[]{:S(2)}, u32[]{:S(2)}) collective-permute-start(bf16[512,512]{1,0:T(8,128)(2,1)S(1)} %shard_map.67.rest_0_), channel_id=1, source_target_pairs={{1,5},{2,6},{5,1},{6,2},{9,13},{10,14},{13,9},{14,10},{17,21},{18,... | collective-permute-start | bytes 1572872 | tf_op jit(solution)/shard_map/ppermute | solution.py:24
  110.8 15.3 %collective-permute-start.29 = (bf16[528,512]{1,0:T(8,128)(2,1)S(1)}, bf16[528,512]{1,0:T(8,128)(2,1)S(1)}, u32[]{:S(2)}, u32[]{:S(2)}) collective-permute-start(bf16[528,512]{1,0:T(8,128)(2,1)S(1)} %get-tuple-element.30.refs_1_), channel_id=1, source_target_pairs={{0,16},{16,0},{1,17},{17,1},{2,18},{18,2},{3,19},{19,3},{4,20},{20... | collective-permute-start | bytes 1622024 | tf_op jit(solution)/shard_map/ppermute | solution.py:18
  112.3 22.0 %collective-permute-start.25 = (bf16[512,512]{1,0:T(8,128)(2,1)S(1)}, bf16[512,512]{1,0:T(8,128)(2,1)S(1)}, u32[]{:S(2)}, u32[]{:S(2)}) collective-permute-start(bf16[512,512]{1,0:T(8,128)(2,1)S(1)} %shard_map.71.refs_0_), channel_id=1, source_target_pairs={{0,16},{16,0},{1,17},{17,1},{2,18},{18,2},{3,19},{19,3},{4,20},{20... | collective-permute-start | bytes 1572872 | tf_op jit(solution)/shard_map/ppermute | solution.py:18
  126.1 10.4 %collective-permute-start.31 = (bf16[528,512]{1,0:T(8,128)(2,1)S(1)}, bf16[528,512]{1,0:T(8,128)(2,1)S(1)}, u32[]{:S(2)}, u32[]{:S(2)}) collective-permute-start(bf16[528,512]{1,0:T(8,128)(2,1)S(1)} %collective-permute-done.29.rest_1_), channel_id=1, source_target_pairs={{1,9},{2,10},{5,13},{6,14},{9,1},{10,2},{13,5},{14,6},{17,25},{18,... | collective-permute-start | bytes 1622024 | tf_op jit(solution)/shard_map/ppermute | solution.py:24
  126.8 10.4 %collective-permute-start.23 = (bf16[512,512]{1,0:T(8,128)(2,1)S(1)}, bf16[512,512]{1,0:T(8,128)(2,1)S(1)}, u32[]{:S(2)}, u32[]{:S(2)}) collective-permute-start(bf16[512,512]{1,0:T(8,128)(2,1)S(1)} %shard_map.71.refs_0_), channel_id=1, source_target_pairs={{1,2},{2,1},{5,6},{6,5},{9,10},{10,9},{13,14},{14,13},{17,18},{18,... | collective-permute-start | bytes 1572872 | tf_op jit(solution)/shard_map/ppermute | solution.py:28
  135.0 8.5 %collective-permute-start.24 = (bf16[528,512]{1,0:T(8,128)(2,1)S(1)}, bf16[528,512]{1,0:T(8,128)(2,1)S(1)}, u32[]{:S(2)}, u32[]{:S(2)}) collective-permute-start(bf16[528,512]{1,0:T(8,128)(2,1)S(1)} %get-tuple-element.30.refs_1_), channel_id=1, source_target_pairs={{1,2},{2,1},{5,6},{6,5},{9,10},{10,9},{13,14},{14,13},{17,18},{18,... | collective-permute-start | bytes 1622024 | tf_op jit(solution)/shard_map/ppermute | solution.py:28
  135.7 11.0 %collective-permute-start.30 = (bf16[528,512]{1,0:T(8,128)(2,1)S(1)}, bf16[528,512]{1,0:T(8,128)(2,1)S(1)}, u32[]{:S(2)}, u32[]{:S(2)}) collective-permute-start(bf16[528,512]{1,0:T(8,128)(2,1)S(1)} %collective-permute-done.29.rest_1_), channel_id=1, source_target_pairs={{1,5},{2,6},{5,1},{6,2},{9,13},{10,14},{13,9},{14,10},{17,21},{18,... | collective-permute-start | bytes 1622024 | tf_op jit(solution)/shard_map/ppermute | solution.py:24
  136.4 10.3 %collective-permute-start.32 = (bf16[528,512]{1,0:T(8,128)(2,1)S(1)}, bf16[528,512]{1,0:T(8,128)(2,1)S(1)}, u32[]{:S(2)}, u32[]{:S(2)}) collective-permute-start(bf16[528,512]{1,0:T(8,128)(2,1)S(1)} %collective-permute-done.31.rest_3_), channel_id=1, source_target_pairs={{1,5},{2,6},{5,1},{6,2},{9,13},{10,14},{13,9},{14,10},{17,21},{18,... | collective-permute-start | bytes 1622024 | tf_op jit(solution)/shard_map/ppermute | solution.py:24
  137.2 8.3 %collective-permute-start.26 = (bf16[512,512]{1,0:T(8,128)(2,1)S(1)}, bf16[512,512]{1,0:T(8,128)(2,1)S(1)}, u32[]{:S(2)}, u32[]{:S(2)}) collective-permute-start(bf16[512,512]{1,0:T(8,128)(2,1)S(1)} %collective-permute-done.25.rest_0_), channel_id=1, source_target_pairs={{1,5},{2,6},{5,1},{6,2},{9,13},{10,14},{13,9},{14,10},{17,21},{18,... | collective-permute-start | bytes 1572872 | tf_op jit(solution)/shard_map/ppermute | solution.py:24
  150.5 8.5 %collective-permute-start.34 = (bf16[528,512]{1,0:T(8,128)(2,1)S(1)}, bf16[528,512]{1,0:T(8,128)(2,1)S(1)}, u32[]{:S(2)}, u32[]{:S(2)}) collective-permute-start(bf16[528,512]{1,0:T(8,128)(2,1)S(1)} %get-tuple-element.33.refs_1_.rest_1_), channel_id=1, source_target_pairs={{1,2},{2,1},{5,6},{6,5},{9,10},{10,9},{13,14},{14,13},{17,18},{18,... | collective-permute-start | bytes 1622024 | tf_op jit(solution)/shard_map/ppermute | solution.py:28
  151.2 11.0 %collective-permute-start.38 = (bf16[528,512]{1,0:T(8,128)(2,1)S(1)}, bf16[528,512]{1,0:T(8,128)(2,1)S(1)}, u32[]{:S(2)}, u32[]{:S(2)}) collective-permute-start(bf16[528,512]{1,0:T(8,128)(2,1)S(1)} %get-tuple-element.33.refs_1_.rest_1_), channel_id=1, source_target_pairs={{1,5},{2,6},{5,1},{6,2},{9,13},{10,14},{13,9},{14,10},{17,21},{18,... | collective-permute-start | bytes 1622024 | tf_op jit(solution)/shard_map/ppermute | solution.py:24
  151.9 10.3 %collective-permute-start.40 = (bf16[528,512]{1,0:T(8,128)(2,1)S(1)}, bf16[528,512]{1,0:T(8,128)(2,1)S(1)}, u32[]{:S(2)}, u32[]{:S(2)}) collective-permute-start(bf16[528,512]{1,0:T(8,128)(2,1)S(1)} %collective-permute-done.39.rest_3_), channel_id=1, source_target_pairs={{1,5},{2,6},{5,1},{6,2},{9,13},{10,14},{13,9},{14,10},{17,21},{18,... | collective-permute-start | bytes 1622024 | tf_op jit(solution)/shard_map/ppermute | solution.py:24
  152.7 8.3 %collective-permute-start.35 = (bf16[512,512]{1,0:T(8,128)(2,1)S(1)}, bf16[512,512]{1,0:T(8,128)(2,1)S(1)}, u32[]{:S(2)}, u32[]{:S(2)}) collective-permute-start(bf16[512,512]{1,0:T(8,128)(2,1)S(1)} %shard_map.77.refs_0_.rest_0_), channel_id=1, source_target_pairs={{1,5},{2,6},{5,1},{6,2},{9,13},{10,14},{13,9},{14,10},{17,21},{18,... | collective-permute-start | bytes 1572872 | tf_op jit(solution)/shard_map/ppermute | solution.py:24
  163.9 94.2 %collective-permute-start.41 = (bf16[528,512]{1,0:T(8,128)(2,1)S(1)}, bf16[528,512]{1,0:T(8,128)(2,1)S(1)}, u32[]{:S(2)}, u32[]{:S(2)}) collective-permute-start(bf16[528,512]{1,0:T(8,128)(2,1)S(1)} %get-tuple-element.36), channel_id=1, source_target_pairs={{1,0},{2,3},{5,4},{6,7},{9,8},{10,11},{13,12},{14,15},{17,16},{18,... | collective-permute-start | bytes 1622024 | tf_op jit(solution)/shard_map/ppermute | solution.py:36
  165.9 91.7 %collective-permute-start.43 = (f32[1,512]{1,0:T(1,128)S(1)}, f32[1,512]{1,0:T(1,128)S(1)}, u32[]{:S(2)}, u32[]{:S(2)}) collective-permute-start(f32[1,512]{1,0:T(1,128)S(1)} %slice_add_fusion), channel_id=1, source_target_pairs={{1,0},{2,3},{5,4},{6,7},{9,8},{10,11},{13,12},{14,15},{17,16},{18,... | collective-permute-start | bytes 6152 | tf_op jit(solution)/shard_map/ppermute | solution.py:36
  (28 other events, 170.4 us)

commit v5 on v3

--- a/solution.py
+++ b/solution.py
@@ -54,11 +54,11 @@
     return ref[rows or slice(0, size), column : column + size]
 
 
-def spread(refs, views, q_ref, first, size, n):
+def spread(refs, views, q_ref, size, n):
     total = None
-    for b, view in enumerate(views):
+    for block, view in views:
         at = lax.broadcasted_iota(jnp.int32, (size, size), 0) + n * size
-        hot = jnp.where(at == q_ref[first + b : first + b + 1, :], 1.0, 0.0).astype(jnp.bfloat16)
+        hot = jnp.where(at == q_ref[block : block + 1, :], 1.0, 0.0).astype(jnp.bfloat16)
         part = lax.dot_general(
             read(refs, view, size), hot, NT, preferred_element_type=jnp.float32
         )
@@ -66,9 +66,9 @@
     return total
 
 
-def spread_columns(pivots, first, tiles, size, count, onto=None):
+def spread_columns(pivots, tiles, size, count, onto=None):
     operands = Operands()
-    views = [operands.add(view) for view in tiles]
+    views = [(block, operands.add(view)) for block, view in tiles]
     extra = [] if onto is None else [onto]
 
     def kernel(q_ref, *refs):
@@ -77,7 +77,7 @@
         @pl.loop(0, count)
         def _(n):
             here = pl.ds(pl.multiple_of(n * size, size), size)
-            moved = spread(refs[len(extra) :], views, q_ref, first, size, n).astype(out.dtype)
+            moved = spread(refs[len(extra) :], views, q_ref, size, n).astype(out.dtype)
             out[:, here] = moved if onto is None else moved + refs[0][:, here]
 
     return pl.pallas_call(
@@ -85,7 +85,9 @@
         out_shape=jax.ShapeDtypeStruct((size, size * count), jnp.bfloat16),
         compiler_params=pltpu.CompilerParams(vmem_limit_bytes=VMEM),
         cost_estimate=pl.CostEstimate(
-            flops=4 * size * size * size * count, bytes_accessed=12 * size * size, transcendentals=0
+            flops=2 * len(tiles) * size * size * size * count,
+            bytes_accessed=8 * size * size,
+            transcendentals=0,
         ),
     )(pivots, *extra, *operands.arrays)
 
@@ -172,8 +174,7 @@
     ends_left = inward(lefts)
     lefts_other = swap_middle(lefts)
     rights_across = swap_rows(rights, 2)
-    ends_right = {2: inward(tiles[1])}
-    ends_right[0] = inward(tiles[0])
+    end_upper, end_lower = inward(tiles[1]), inward(tiles[0])
     rights_beside = swap_rows(rights, 1)
 
     own = lax.dynamic_index_in_dim(boundary_pivots, position, 0, keepdims=True)
@@ -189,18 +190,22 @@
     places = lax.broadcasted_iota(jnp.int32, (EXTRA, size), 1)
     held = ((places < 2 * share) == (col == 1)).astype(jnp.bfloat16)
 
+    def panel(turn, tiles, onto=None):
+        return spread_columns(pivots[turn], tiles, size, count, onto)
+
     ends_other = swap_middle(ends_left)
     rights_last = swap_rows(rights_across, 1)
-
-    def panel(turn, k):
-        own_tiles = [(lefts, k, 0), (ends_left, k, 0)]
-        other_tiles = [(lefts_other, k, 0), (ends_other, k, 0)]
-        partial = spread_columns(pivots[turn], 0, own_tiles, size, count)
-        return spread_columns(pivots[turn], 2, other_tiles, size, count, partial)
-
-    def first(turn, k, left):
-        end = ends_right[turn]
-        across = swap_rows(end, 2)
+    upper_panel, lower_panel = panel(2, [(0, (lefts, 1, 0))]), panel(0, [(0, (lefts, 0, 0))])
+    upper_panel = panel(2, [(1, (ends_left, 1, 0)), (2, (lefts_other, 1, 0))], upper_panel)
+    end_upper = after(end_upper, upper_panel)
+    upper_across = swap_rows(end_upper, 2)
+    lower_panel = panel(0, [(1, (ends_left, 0, 0)), (2, (lefts_other, 0, 0))], lower_panel)
+    end_lower = after(end_lower, lower_panel)
+    lower_across = swap_rows(end_lower, 2)
+    upper_panel = panel(2, [(3, (ends_other, 1, 0))], upper_panel)
+    lower_panel = panel(0, [(3, (ends_other, 0, 0))], lower_panel)
+
+    def first(turn, k, left, end, across):
         ends = [end, swap_rows(end, 1), across, swap_rows(across, 1)]
         right = [
             [(tile, k, 0) for tile in (rights, rights_beside, rights_across, rights_last)],
@@ -208,12 +213,12 @@
         ]
         return product(left, right, held, "joint", size, share, turn)
 
-    upper, upper_vector = first(2, 1, panel(2, 1))
-    lower, _ = first(0, 0, panel(0, 0))
+    upper, upper_vector = first(2, 1, upper_panel, end_upper, upper_across)
+    lower, _ = first(0, 0, lower_panel, end_lower, after(lower_across, upper))
 
     def later(turn, left, added, right, form):
         other = swap_middle(left)
-        partial = spread_columns(pivots[turn], 0, [(left, None, 0), (left, None, size)], size, count)
+        partial = panel(turn, [(0, (left, None, 0)), (1, (left, None, size))])
         parts = []
         for tile in right:
             beside, across = swap_rows(tile, 1), swap_rows(tile, 2)
@@ -222,8 +227,7 @@
             views = [[(tile, None, column) for tile in parts[0]] for column in (0, size)]
         else:
             views = [[(tile, None, 0) for tile in part] for part in parts]
-        other_tiles = [(other, None, 0), (other, None, size)]
-        moved = spread_columns(pivots[turn], 2, other_tiles, size, count, partial)
+        moved = panel(turn, [(2, (other, None, 0)), (3, (other, None, size))], partial)
         return product(moved, views, added, form, size)
 
     whole, whole_o, whole_e, whole_vector = later(1, upper, upper_vector, [lower], "both")

time: 244 us -> 233 us (0.955)
  waiting for transfers between devices: 141 us -> 115 us
  starting transfers between devices: 42.2 us -> 49.9 us
  local copies, waits for them, and re-layouts: 2.68 us -> 7.84 us
    ppermute x3, waiting for transfers between devices: 31.7 us -> 11 us  [inward(): return lax.ppermute(value, 'col', [(0, 1), (3, 2)])]
    ppermute x3, starting transfers between devices: 13 us -> 20.9 us  [inward(): return lax.ppermute(value, 'col', [(0, 1), (3, 2)])]
    unnamed x10 -> x26, local copies, waits for them, and re-layouts: 0.03 us -> 5.17 us
    ppermute x2, waiting for transfers between devices: 88 us -> 84.2 us  [outward(): return lax.ppermute(value, 'col', [(1, 0), (2, 3)])]
    pallas_call x10 -> x12, Pallas kernels: 36.1 us -> 37.2 us  [spread_columns(): pl.pallas_call(kernel, out_shape=jax.ShapeDtypeStruct((size, size * count...]
  transfers between devices with their start and end apart: 34 -> 34, of which waited for: 5 -> 4; matrix products, arithmetic and copies ran while one was open for 0% -> 1% of each run, Pallas kernels for 19% -> 18%
where the time goes in v5:
time: 233 us; the launch traced here: 232 us
  waiting for transfers between devices  115 us (49%)
  Pallas kernels  55.3 us (24%)
  starting transfers between devices  49.9 us (21%)
  local copies, waits for them, and re-layouts  7.84 us (3%)
  other arithmetic  2.83 us (1%)
    ppermute x2, waiting for transfers between devices, outward(): return lax.ppermute(value, 'col', [(1, 0), (2, 3)])  84.2 us
    pallas_call x12, Pallas kernels, spread_columns(): pl.pallas_call(kernel, out_shape=jax.ShapeDtypeStruct((size, size * count...  37.2 us
    ppermute x3, starting transfers between devices, inward(): return lax.ppermute(value, 'col', [(0, 1), (3, 2)])  20.9 us
    ppermute x2, waiting for transfers between devices, from_behind(): lax.ppermute(value, axis, [(i, (i + by) % devices) for i in range(devices)])  19.3 us
    ppermute x21, starting transfers between devices, swap_rows(): return lax.ppermute(value, ('row', 'col'), pairs)  19.2 us
    pallas_call x5, Pallas kernels, product(): pl.pallas_call(kernel, out_shape=tuple(outs), compiler_params=pltpu.Compi...  18.1 us
    ppermute x3, waiting for transfers between devices, inward(): return lax.ppermute(value, 'col', [(0, 1), (3, 2)])  11 us
    ppermute x6, starting transfers between devices, swap_middle(): return lax.ppermute(value, 'col', [(1, 2), (2, 1)])  5.18 us
  transfers between devices with their start and end apart: 34, of which 4 were waited for; matrix products, arithmetic and copies ran while one was open for 1% of the time, Pallas kernels for 18%

profile of v5, /device:TPU:0, one launch (start us, length us, event | category | flops | bytes accessed | tf_op | source)
XLA Modules:
  0.0 232.0 jit_solution(12877099003070894262)
XLA Ops:
  0.6 2.4 %slice.40.refs_0_ = bf16[2,512,512]{2,1,0:T(8,128)(2,1)} slice(bf16[4,512,512]{2,1,0:T(8,128)(2,1)} %bitcast.22), slice={[1:4:2], [0:512:1], [0:512:1]} | slice | bytes 2097152 | tf_op jit(solution)/shard_map/slice | solution.py:170
  3.1 6.0 %collective-permute-start = (bf16[2,512,512]{2,1,0:T(8,128)(2,1)}, bf16[2,512,512]{2,1,0:T(8,128)(2,1)}, u32[]{:S(2)}, u32[]{:S(2)}) collective-permute-start(bf16[2,512,512]{2,1,0:T(8,128)(2,1)} %slice.40.refs_0_), channel_id=1, source_target_pairs={{0,1},{3,2},{4,5},{7,6},{8,9},{11,10},{12,13},{15,14},{16,17},{19,... | collective-permute-start | bytes 3145736 | tf_op jit(solution)/shard_map/ppermute | solution.py:31
  9.1 1.6 collective-permute-start.1
  13.6 6.9 %collective-permute-start.6 = (bf16[528,512]{1,0:T(8,128)(2,1)}, bf16[528,512]{1,0:T(8,128)(2,1)}, u32[]{:S(2)}, u32[]{:S(2)}) collective-permute-start(bf16[528,512]{1,0:T(8,128)(2,1)} %get-tuple-element.58), channel_id=1, source_target_pairs={{0,1},{3,2},{4,5},{7,6},{8,9},{11,10},{12,13},{15,14},{16,17},{19,... | collective-permute-start | bytes 1622024 | tf_op jit(solution)/shard_map/ppermute | solution.py:31
  20.9 11.0 %collective-permute-done.refs_1_ = bf16[2,512,512]{2,1,0:T(8,128)(2,1)} collective-permute-done((bf16[2,512,512]{2,1,0:T(8,128)(2,1)}, bf16[2,512,512]{2,1,0:T(8,128)(2,1)}, u32[]{:S(2)}, u32[]{:S(2)}) %collective-permute-start) | collective-permute-done | bytes 1048608 | tf_op jit(solution)/shard_map/ppermute | solution.py:31
  32.7 3.2 %shard_map.59.refs_0_ = bf16[512,2048]{1,0:T(8,128)(2,1)S(1)} custom-call(s32[4,512]{1,0:T(4,128)S(1)} %get-tuple-element.49.q_ref, bf16[2,512,512]{2,1,0:T(8,128)(2,1)} %slice.40.refs_0_), custom_call_target="tpu_custom_call" | custom-call | flops 1073741824 | bytes 2097152 | tf_op jit(solution)/shard_map/pallas_call | solution.py:83
  35.9 7.9 %collective-permute-start.11 = (bf16[528,512]{1,0:T(8,128)(2,1)S(1)}, bf16[528,512]{1,0:T(8,128)(2,1)}, u32[]{:S(2)}, u32[]{:S(2)}) collective-permute-start(bf16[528,512]{1,0:T(8,128)(2,1)S(1)} %copy-done.8), channel_id=1, source_target_pairs={{0,1},{3,2},{4,5},{7,6},{8,9},{11,10},{12,13},{15,14},{16,17},{19,... | collective-permute-start | bytes 1622024 | tf_op jit(solution)/shard_map/ppermute | solution.py:31
  43.9 4.5 %shard_map.60.refs_0_ = bf16[512,2048]{1,0:T(8,128)(2,1)S(1)} custom-call(s32[4,512]{1,0:T(4,128)S(1)} %get-tuple-element.49.q_ref, bf16[512,2048]{1,0:T(8,128)(2,1)S(1)} %shard_map.59.refs_0_, bf16[2,512,512]{2,1,0:T(8,128)(2,1)} %collective-permute-done.refs_1_, bf16[2,512,512]{2,1,0:T(8,128)(2,1)} %collective-permute-done.1.refs_2_), custom_call_target="tpu_custom_call" | custom-call | flops 2147483648 | bytes 2097152 | tf_op jit(solution)/shard_map/pallas_call | solution.py:83
  48.4 1.5 collective-permute-start.8
  50.0 1.7 collective-permute-start.5
  51.6 3.1 %shard_map.65.refs_0_ = bf16[512,2048]{1,0:T(8,128)(2,1)S(1)} custom-call(s32[4,512]{1,0:T(4,128)S(1)} %get-tuple-element.48.q_ref, bf16[2,512,512]{2,1,0:T(8,128)(2,1)} %slice.40.refs_0_), custom_call_target="tpu_custom_call" | custom-call | flops 1073741824 | bytes 2097152 | tf_op jit(solution)/shard_map/pallas_call | solution.py:83
  54.8 1.5 collective-permute-start.7
  56.3 1.5 collective-permute-start.9
  57.8 4.5 %shard_map.66.refs_0_ = bf16[512,2048]{1,0:T(8,128)(2,1)S(1)} custom-call(s32[4,512]{1,0:T(4,128)S(1)} %get-tuple-element.48.q_ref, bf16[512,2048]{1,0:T(8,128)(2,1)S(1)} %shard_map.65.refs_0_, bf16[2,512,512]{2,1,0:T(8,128)(2,1)} %collective-permute-done.refs_1_, bf16[2,512,512]{2,1,0:T(8,128)(2,1)} %collective-permute-done.1.refs_2_), custom_call_target="tpu_custom_call" | custom-call | flops 2147483648 | bytes 2097152 | tf_op jit(solution)/shard_map/pallas_call | solution.py:83
  67.4 1.6 copy-done.6
  69.0 1.9 shard_map.61.left_ref
  71.7 4.8 %shard_map.62 = (bf16[528,1024]{1,0:T(8,128)(2,1)S(1)}, f32[16,512]{1,0:T(8,128)S(1)}) custom-call(bf16[512,2048]{1,0:T(8,128)(2,1)S(1)} %shard_map.61.left_ref, bf16[16,512]{1,0:T(8,128)(2,1)S(1)} %iota.7.added_ref, bf16[2,528,512]{2,1,0:T(8,128)(2,1)S(1)} %pad_maximum_fusion.rest_0_, bf16[2,528,512]{2,1,0:T(8,128)(2,1)S(1)} %collective-permute-done.3.rest_1_, ...), custom_call_target="tpu_custom_call" | custom-call | flops 2147483648 | bytes 6291456 | tf_op jit(solution)/shard_map/pallas_call | solution.py:148
  77.2 1.9 shard_map.67.left_ref
  79.1 5.0 %shard_map.68 = (bf16[528,1024]{1,0:T(8,128)(2,1)S(1)}, f32[16,512]{1,0:T(8,128)}) custom-call(bf16[512,2048]{1,0:T(8,128)(2,1)S(1)} %shard_map.67.left_ref, bf16[16,512]{1,0:T(8,128)(2,1)S(1)} %iota.7.added_ref, bf16[2,528,512]{2,1,0:T(8,128)(2,1)S(1)} %pad_maximum_fusion.rest_0_, bf16[2,528,512]{2,1,0:T(8,128)(2,1)S(1)} %collective-permute-done.3.rest_1_, ...), custom_call_target="tpu_custom_call" | custom-call | flops 2147483648 | bytes 6291456 | tf_op jit(solution)/shard_map/pallas_call | solution.py:148
  85.6 3.0 %shard_map.63.refs_0_ = bf16[512,2048]{1,0:T(8,128)(2,1)S(1)} custom-call(s32[4,512]{1,0:T(4,128)S(1)} %get-tuple-element.50.q_ref, bf16[528,1024]{1,0:T(8,128)(2,1)S(1)} %get-tuple-element.22.refs_0_), custom_call_target="tpu_custom_call" | custom-call | flops 2147483648 | bytes 2097152 | tf_op jit(solution)/shard_map/pallas_call | solution.py:83
  90.1 3.0 %shard_map.64.left_ref = bf16[512,2048]{1,0:T(8,128)(2,1)S(1)} custom-call(s32[4,512]{1,0:T(4,128)S(1)} %get-tuple-element.50.q_ref, bf16[512,2048]{1,0:T(8,128)(2,1)S(1)} %shard_map.63.refs_0_, bf16[528,1024]{1,0:T(8,128)(2,1)S(1)} %collective-permute-done.10.refs_1_), custom_call_target="tpu_custom_call" | custom-call | flops 2147483648 | bytes 2097152 | tf_op jit(solution)/shard_map/pallas_call | solution.py:83
  93.1 2.8 %shard_map.69 = (bf16[528,1024]{1,0:T(8,128)(2,1)S(1)}, bf16[528,512]{1,0:T(8,128)(2,1)S(1)}, bf16[512,512]{1,0:T(8,128)(2,1)S(1)}, f32[16,512]{1,0:T(8,128)S(1)}) custom-call(bf16[512,2048]{1,0:T(8,128)(2,1)S(1)} %shard_map.64.left_ref, f32[16,512]{1,0:T(8,128)S(1)} %get-tuple-element.23.added_ref, bf16[528,1024]{1,0:T(8,128)(2,1)S(1)} %get-tuple-element.26.rest_0_, ...), custom_call_target="tpu_custom_call" | custom-call | flops 2147483648 | bytes 6291456 | tf_op jit(solution)/shard_map/pallas_call | solution.py:148
  95.9 1.5 collective-permute-start.19
  98.7 12.5 %collective-permute-done.19.rest_0_ = bf16[528,512]{1,0:T(8,128)(2,1)S(1)} collective-permute-done((bf16[528,512]{1,0:T(8,128)(2,1)S(1)}, bf16[528,512]{1,0:T(8,128)(2,1)S(1)}, u32[]{:S(2)}, u32[]{:S(2)}) %collective-permute-start.19) | collective-permute-done | bytes 540704 | tf_op jit(solution)/shard_map/ppermute | solution.py:17
  111.8 6.8 %collective-permute-done.23.rest_4_ = bf16[512,512]{1,0:T(8,128)(2,1)S(1)} collective-permute-done((bf16[512,512]{1,0:T(8,128)(2,1)S(1)}, bf16[512,512]{1,0:T(8,128)(2,1)S(1)}, u32[]{:S(2)}, u32[]{:S(2)}) %collective-permute-start.23) | collective-permute-done | bytes 524320 | tf_op jit(solution)/shard_map/ppermute | solution.py:17
  119.5 3.0 %shard_map.70.refs_0_ = bf16[512,2048]{1,0:T(8,128)(2,1)S(1)} custom-call(s32[4,512]{1,0:T(4,128)S(1)} %get-tuple-element.51.q_ref, bf16[528,1024]{1,0:T(8,128)(2,1)S(1)} %get-tuple-element.28.refs_0_), custom_call_target="tpu_custom_call" | custom-call | flops 2147483648 | bytes 2097152 | tf_op jit(solution)/shard_map/pallas_call | solution.py:83
  125.4 3.0 %shard_map.71.left_ref = bf16[512,2048]{1,0:T(8,128)(2,1)S(1)} custom-call(s32[4,512]{1,0:T(4,128)S(1)} %get-tuple-element.51.q_ref, bf16[512,2048]{1,0:T(8,128)(2,1)S(1)} %shard_map.70.refs_0_, bf16[528,1024]{1,0:T(8,128)(2,1)S(1)} %collective-permute-done.18.refs_1_), custom_call_target="tpu_custom_call" | custom-call | flops 2147483648 | bytes 2097152 | tf_op jit(solution)/shard_map/pallas_call | solution.py:83
  128.4 2.8 %shard_map.72 = (bf16[528,1024]{1,0:T(8,128)(2,1)S(1)}, f32[16,512]{1,0:T(8,128)S(1)}) custom-call(bf16[512,2048]{1,0:T(8,128)(2,1)S(1)} %shard_map.71.left_ref, f32[16,512]{1,0:T(8,128)S(1)} %get-tuple-element.29.added_ref, bf16[528,512]{1,0:T(8,128)(2,1)S(1)} %collective-permute-done.19.rest_0_, bf16[528,512]{1,0:T(8,128)(2,1)S(1)} %collective-permute-done.20.rest_1_, ...), custom_call_target="tpu_custom_call" | custom-call | flops 2147483648 | bytes 6291456 | tf_op jit(solution)/shard_map/pallas_call | solution.py:148
  133.4 3.0 %shard_map.73.refs_0_ = bf16[512,2048]{1,0:T(8,128)(2,1)S(1)} custom-call(s32[4,512]{1,0:T(4,128)S(1)} %get-tuple-element.52.q_ref, bf16[528,1024]{1,0:T(8,128)(2,1)S(1)} %get-tuple-element.34.refs_0_.rest_0_), custom_call_target="tpu_custom_call" | custom-call | flops 2147483648 | bytes 2097152 | tf_op jit(solution)/shard_map/pallas_call | solution.py:83
  137.2 3.0 %shard_map.74.left_ref = bf16[512,2048]{1,0:T(8,128)(2,1)S(1)} custom-call(s32[4,512]{1,0:T(4,128)S(1)} %get-tuple-element.52.q_ref, bf16[512,2048]{1,0:T(8,128)(2,1)S(1)} %shard_map.73.refs_0_, bf16[528,1024]{1,0:T(8,128)(2,1)S(1)} %collective-permute-done.27.refs_1_), custom_call_target="tpu_custom_call" | custom-call | flops 2147483648 | bytes 2097152 | tf_op jit(solution)/shard_map/pallas_call | solution.py:83
  140.2 2.8 %shard_map.75 = (bf16[512,512]{1,0:T(8,128)(2,1)S(1)}, bf16[512,512]{1,0:T(8,128)(2,1)S(1)}, f32[16,512]{1,0:T(8,128)S(1)}) custom-call(bf16[512,2048]{1,0:T(8,128)(2,1)S(1)} %shard_map.74.left_ref, f32[16,512]{1,0:T(8,128)S(1)} %get-tuple-element.35.added_ref, bf16[528,1024]{1,0:T(8,128)(2,1)S(1)} %get-tuple-element.34.refs_0_.rest_0_, ...), custom_call_target="tpu_custom_call" | custom-call | flops 2147483648 | bytes 6291456 | tf_op jit(solution)/shard_map/pallas_call | solution.py:148
  146.4 84.2 %collective-permute-done.33 = f32[1,512]{1,0:T(1,128)S(1)} collective-permute-done((f32[1,512]{1,0:T(1,128)S(1)}, f32[1,512]{1,0:T(1,128)S(1)}, u32[]{:S(2)}, u32[]{:S(2)}) %collective-permute-start.33) | collective-permute-done | bytes 2080 | tf_op jit(solution)/shard_map/ppermute | solution.py:35
  (100 shorter events, 26.5 us)
Async XLA Ops:
  3.1 28.9 %collective-permute-start = (bf16[2,512,512]{2,1,0:T(8,128)(2,1)}, bf16[2,512,512]{2,1,0:T(8,128)(2,1)}, u32[]{:S(2)}, u32[]{:S(2)}) collective-permute-start(bf16[2,512,512]{2,1,0:T(8,128)(2,1)} %slice.40.refs_0_), channel_id=1, source_target_pairs={{0,1},{3,2},{4,5},{7,6},{8,9},{11,10},{12,13},{15,14},{16,17},{19,... | collective-permute-start | bytes 3145736 | tf_op jit(solution)/shard_map/ppermute | solution.py:31
  9.1 26.8 %collective-permute-start.1 = (bf16[2,512,512]{2,1,0:T(8,128)(2,1)}, bf16[2,512,512]{2,1,0:T(8,128)(2,1)}, u32[]{:S(2)}, u32[]{:S(2)}) collective-permute-start(bf16[2,512,512]{2,1,0:T(8,128)(2,1)} %slice.40.refs_0_), channel_id=1, source_target_pairs={{1,2},{2,1},{5,6},{6,5},{9,10},{10,9},{13,14},{14,13},{17,18},{18,... | collective-permute-start | bytes 3145736 | tf_op jit(solution)/shard_map/ppermute | solution.py:27
  12.1 37.9 %collective-permute-start.4 = (bf16[2,528,512]{2,1,0:T(8,128)(2,1)S(1)}, bf16[2,528,512]{2,1,0:T(8,128)(2,1)S(1)}, u32[]{:S(2)}, u32[]{:S(2)}) collective-permute-start(bf16[2,528,512]{2,1,0:T(8,128)(2,1)S(1)} %pad_maximum_fusion.rest_0_), channel_id=1, source_target_pairs={{1,9},{2,10},{5,13},{6,14},{9,1},{10,2},{13,5},{14,6},{17,25},{18,... | collective-permute-start | bytes 3244040 | tf_op jit(solution)/shard_map/ppermute | solution.py:23
  12.8 58.0 %collective-permute-start.3 = (bf16[2,528,512]{2,1,0:T(8,128)(2,1)S(1)}, bf16[2,528,512]{2,1,0:T(8,128)(2,1)S(1)}, u32[]{:S(2)}, u32[]{:S(2)}) collective-permute-start(bf16[2,528,512]{2,1,0:T(8,128)(2,1)S(1)} %pad_maximum_fusion.rest_0_), channel_id=1, source_target_pairs={{1,5},{2,6},{5,1},{6,2},{9,13},{10,14},{13,9},{14,10},{17,21},{18,... | collective-permute-start | bytes 3244040 | tf_op jit(solution)/shard_map/ppermute | solution.py:23
  13.6 34.9 %collective-permute-start.6 = (bf16[528,512]{1,0:T(8,128)(2,1)}, bf16[528,512]{1,0:T(8,128)(2,1)}, u32[]{:S(2)}, u32[]{:S(2)}) collective-permute-start(bf16[528,512]{1,0:T(8,128)(2,1)} %get-tuple-element.58), channel_id=1, source_target_pairs={{0,1},{3,2},{4,5},{7,6},{8,9},{11,10},{12,13},{15,14},{16,17},{19,... | collective-permute-start | bytes 1622024 | tf_op jit(solution)/shard_map/ppermute | solution.py:31
  32.0 31.7 %collective-permute-start.2 = (bf16[2,512,512]{2,1,0:T(8,128)(2,1)}, bf16[2,512,512]{2,1,0:T(8,128)(2,1)S(1)}, u32[]{:S(2)}, u32[]{:S(2)}) collective-permute-start(bf16[2,512,512]{2,1,0:T(8,128)(2,1)} %collective-permute-done.refs_1_), channel_id=1, source_target_pairs={{1,2},{2,1},{5,6},{6,5},{9,10},{10,9},{13,14},{14,13},{17,18},{18,... | collective-permute-start | bytes 3145736 | tf_op jit(solution)/shard_map/ppermute | solution.py:27
  35.9 18.8 %collective-permute-start.11 = (bf16[528,512]{1,0:T(8,128)(2,1)S(1)}, bf16[528,512]{1,0:T(8,128)(2,1)}, u32[]{:S(2)}, u32[]{:S(2)}) collective-permute-start(bf16[528,512]{1,0:T(8,128)(2,1)S(1)} %copy-done.8), channel_id=1, source_target_pairs={{0,1},{3,2},{4,5},{7,6},{8,9},{11,10},{12,13},{15,14},{16,17},{19,... | collective-permute-start | bytes 1622024 | tf_op jit(solution)/shard_map/ppermute | solution.py:31
  48.4 7.9 %collective-permute-start.8 = (bf16[528,512]{1,0:T(8,128)(2,1)}, bf16[528,512]{1,0:T(8,128)(2,1)}, u32[]{:S(2)}, u32[]{:S(2)}) collective-permute-start(bf16[528,512]{1,0:T(8,128)(2,1)} %collective-permute-done.6.rest_4_), channel_id=1, source_target_pairs={{1,9},{2,10},{5,13},{6,14},{9,1},{10,2},{13,5},{14,6},{17,25},{18,... | collective-permute-start | bytes 1622024 | tf_op jit(solution)/shard_map/ppermute | solution.py:23
  50.0 21.7 %collective-permute-start.5 = (bf16[2,528,512]{2,1,0:T(8,128)(2,1)S(1)}, bf16[2,528,512]{2,1,0:T(8,128)(2,1)}, u32[]{:S(2)}, u32[]{:S(2)}) collective-permute-start(bf16[2,528,512]{2,1,0:T(8,128)(2,1)S(1)} %collective-permute-done.4.rest_2_), channel_id=1, source_target_pairs={{1,5},{2,6},{5,1},{6,2},{9,13},{10,14},{13,9},{14,10},{17,21},{18,... | collective-permute-start | bytes 3244040 | tf_op jit(solution)/shard_map/ppermute | solution.py:23
  54.8 16.8 %collective-permute-start.7 = (bf16[528,512]{1,0:T(8,128)(2,1)}, bf16[528,512]{1,0:T(8,128)(2,1)}, u32[]{:S(2)}, u32[]{:S(2)}) collective-permute-start(bf16[528,512]{1,0:T(8,128)(2,1)} %collective-permute-done.6.rest_4_), channel_id=1, source_target_pairs={{1,5},{2,6},{5,1},{6,2},{9,13},{10,14},{13,9},{14,10},{17,21},{18,... | collective-permute-start | bytes 1622024 | tf_op jit(solution)/shard_map/ppermute | solution.py:23
  56.3 15.3 %collective-permute-start.9 = (bf16[528,512]{1,0:T(8,128)(2,1)}, bf16[528,512]{1,0:T(8,128)(2,1)}, u32[]{:S(2)}, u32[]{:S(2)}) collective-permute-start(bf16[528,512]{1,0:T(8,128)(2,1)} %collective-permute-done.8.rest_6_), channel_id=1, source_target_pairs={{1,5},{2,6},{5,1},{6,2},{9,13},{10,14},{13,9},{14,10},{17,21},{18,... | collective-permute-start | bytes 1622024 | tf_op jit(solution)/shard_map/ppermute | solution.py:23
  64.7 11.8 %collective-permute-start.13 = (bf16[528,512]{1,0:T(8,128)(2,1)}, bf16[528,512]{1,0:T(8,128)(2,1)}, u32[]{:S(2)}, u32[]{:S(2)}) collective-permute-start(bf16[528,512]{1,0:T(8,128)(2,1)} %collective-permute-done.11.rest_4_), channel_id=1, source_target_pairs={{1,9},{2,10},{5,13},{6,14},{9,1},{10,2},{13,5},{14,6},{17,25},{18,... | collective-permute-start | bytes 1622024 | tf_op jit(solution)/shard_map/ppermute | solution.py:23
  70.9 8.2 %collective-permute-start.12 = (bf16[528,512]{1,0:T(8,128)(2,1)}, bf16[528,512]{1,0:T(8,128)(2,1)S(1)}, u32[]{:S(2)}, u32[]{:S(2)}) collective-permute-start(bf16[528,512]{1,0:T(8,128)(2,1)} %collective-permute-done.11.rest_4_), channel_id=1, source_target_pairs={{1,5},{2,6},{5,1},{6,2},{9,13},{10,14},{13,9},{14,10},{17,21},{18,... | collective-permute-start | bytes 1622024 | tf_op jit(solution)/shard_map/ppermute | solution.py:23
  84.1 5.2 %collective-permute-start.16 = (bf16[528,1024]{1,0:T(8,128)(2,1)S(1)}, bf16[528,1024]{1,0:T(8,128)(2,1)S(1)}, u32[]{:S(2)}, u32[]{:S(2)}) collective-permute-start(bf16[528,1024]{1,0:T(8,128)(2,1)S(1)} %get-tuple-element.26.rest_0_), channel_id=1, source_target_pairs={{1,9},{2,10},{5,13},{6,14},{9,1},{10,2},{13,5},{14,6},{17,25},{18,... | collective-permute-start | bytes 3244040 | tf_op jit(solution)/shard_map/ppermute | solution.py:23
  84.8 5.2 %collective-permute-start.10 = (bf16[528,1024]{1,0:T(8,128)(2,1)S(1)}, bf16[528,1024]{1,0:T(8,128)(2,1)S(1)}, u32[]{:S(2)}, u32[]{:S(2)}) collective-permute-start(bf16[528,1024]{1,0:T(8,128)(2,1)S(1)} %get-tuple-element.22.refs_0_), channel_id=1, source_target_pairs={{1,2},{2,1},{5,6},{6,5},{9,10},{10,9},{13,14},{14,13},{17,18},{18,... | collective-permute-start | bytes 3244040 | tf_op jit(solution)/shard_map/ppermute | solution.py:27
  88.6 4.5 %collective-permute-start.15 = (bf16[528,1024]{1,0:T(8,128)(2,1)S(1)}, bf16[528,1024]{1,0:T(8,128)(2,1)S(1)}, u32[]{:S(2)}, u32[]{:S(2)}) collective-permute-start(bf16[528,1024]{1,0:T(8,128)(2,1)S(1)} %get-tuple-element.26.rest_0_), channel_id=1, source_target_pairs={{1,5},{2,6},{5,1},{6,2},{9,13},{10,14},{13,9},{14,10},{17,21},{18,... | collective-permute-start | bytes 3244040 | tf_op jit(solution)/shard_map/ppermute | solution.py:23
  89.3 3.8 %collective-permute-start.17 = (bf16[528,1024]{1,0:T(8,128)(2,1)S(1)}, bf16[528,1024]{1,0:T(8,128)(2,1)S(1)}, u32[]{:S(2)}, u32[]{:S(2)}) collective-permute-start(bf16[528,1024]{1,0:T(8,128)(2,1)S(1)} %collective-permute-done.16.rest_2_), channel_id=1, source_target_pairs={{1,5},{2,6},{5,1},{6,2},{9,13},{10,14},{13,9},{14,10},{17,21},{18,... | collective-permute-start | bytes 3244040 | tf_op jit(solution)/shard_map/ppermute | solution.py:23
  95.9 15.2 %collective-permute-start.19 = (bf16[528,512]{1,0:T(8,128)(2,1)S(1)}, bf16[528,512]{1,0:T(8,128)(2,1)S(1)}, u32[]{:S(2)}, u32[]{:S(2)}) collective-permute-start(bf16[528,512]{1,0:T(8,128)(2,1)S(1)} %get-tuple-element.30), channel_id=1, source_target_pairs={{0,16},{16,0},{1,17},{17,1},{2,18},{18,2},{3,19},{19,3},{4,20},{20... | collective-permute-start | bytes 1622024 | tf_op jit(solution)/shard_map/ppermute | solution.py:17
  97.4 21.3 %collective-permute-start.23 = (bf16[512,512]{1,0:T(8,128)(2,1)S(1)}, bf16[512,512]{1,0:T(8,128)(2,1)S(1)}, u32[]{:S(2)}, u32[]{:S(2)}) collective-permute-start(bf16[512,512]{1,0:T(8,128)(2,1)S(1)} %get-tuple-element.32), channel_id=1, source_target_pairs={{0,16},{16,0},{1,17},{17,1},{2,18},{18,2},{3,19},{19,3},{4,20},{20... | collective-permute-start | bytes 1572872 | tf_op jit(solution)/shard_map/ppermute | solution.py:17
  97.9 27.4 %collective-permute-start.18 = (bf16[528,1024]{1,0:T(8,128)(2,1)S(1)}, bf16[528,1024]{1,0:T(8,128)(2,1)S(1)}, u32[]{:S(2)}, u32[]{:S(2)}) collective-permute-start(bf16[528,1024]{1,0:T(8,128)(2,1)S(1)} %get-tuple-element.28.refs_0_), channel_id=1, source_target_pairs={{1,2},{2,1},{5,6},{6,5},{9,10},{10,9},{13,14},{14,13},{17,18},{18,... | collective-permute-start | bytes 3244040 | tf_op jit(solution)/shard_map/ppermute | solution.py:27
  111.1 12.1 %collective-permute-start.21 = (bf16[528,512]{1,0:T(8,128)(2,1)S(1)}, bf16[528,512]{1,0:T(8,128)(2,1)S(1)}, u32[]{:S(2)}, u32[]{:S(2)}) collective-permute-start(bf16[528,512]{1,0:T(8,128)(2,1)S(1)} %collective-permute-done.19.rest_0_), channel_id=1, source_target_pairs={{1,9},{2,10},{5,13},{6,14},{9,1},{10,2},{13,5},{14,6},{17,25},{18,... | collective-permute-start | bytes 1622024 | tf_op jit(solution)/shard_map/ppermute | solution.py:23
  118.6 6.0 %collective-permute-start.25 = (bf16[512,512]{1,0:T(8,128)(2,1)S(1)}, bf16[512,512]{1,0:T(8,128)(2,1)S(1)}, u32[]{:S(2)}, u32[]{:S(2)}) collective-permute-start(bf16[512,512]{1,0:T(8,128)(2,1)S(1)} %collective-permute-done.23.rest_4_), channel_id=1, source_target_pairs={{1,9},{2,10},{5,13},{6,14},{9,1},{10,2},{13,5},{14,6},{17,25},{18,... | collective-permute-start | bytes 1572872 | tf_op jit(solution)/shard_map/ppermute | solution.py:23
  122.5 5.9 %collective-permute-start.20 = (bf16[528,512]{1,0:T(8,128)(2,1)S(1)}, bf16[528,512]{1,0:T(8,128)(2,1)S(1)}, u32[]{:S(2)}, u32[]{:S(2)}) collective-permute-start(bf16[528,512]{1,0:T(8,128)(2,1)S(1)} %collective-permute-done.19.rest_0_), channel_id=1, source_target_pairs={{1,5},{2,6},{5,1},{6,2},{9,13},{10,14},{13,9},{14,10},{17,21},{18,... | collective-permute-start | bytes 1622024 | tf_op jit(solution)/shard_map/ppermute | solution.py:23
  123.2 5.2 %collective-permute-start.22 = (bf16[528,512]{1,0:T(8,128)(2,1)S(1)}, bf16[528,512]{1,0:T(8,128)(2,1)S(1)}, u32[]{:S(2)}, u32[]{:S(2)}) collective-permute-start(bf16[528,512]{1,0:T(8,128)(2,1)S(1)} %collective-permute-done.21.rest_2_), channel_id=1, source_target_pairs={{1,5},{2,6},{5,1},{6,2},{9,13},{10,14},{13,9},{14,10},{17,21},{18,... | collective-permute-start | bytes 1622024 | tf_op jit(solution)/shard_map/ppermute | solution.py:23
  123.9 4.4 %collective-permute-start.24 = (bf16[512,512]{1,0:T(8,128)(2,1)S(1)}, bf16[512,512]{1,0:T(8,128)(2,1)S(1)}, u32[]{:S(2)}, u32[]{:S(2)}) collective-permute-start(bf16[512,512]{1,0:T(8,128)(2,1)S(1)} %collective-permute-done.23.rest_4_), channel_id=1, source_target_pairs={{1,5},{2,6},{5,1},{6,2},{9,13},{10,14},{13,9},{14,10},{17,21},{18,... | collective-permute-start | bytes 1572872 | tf_op jit(solution)/shard_map/ppermute | solution.py:23
  124.6 3.8 %collective-permute-start.26 = (bf16[512,512]{1,0:T(8,128)(2,1)S(1)}, bf16[512,512]{1,0:T(8,128)(2,1)S(1)}, u32[]{:S(2)}, u32[]{:S(2)}) collective-permute-start(bf16[512,512]{1,0:T(8,128)(2,1)S(1)} %collective-permute-done.25.rest_6_), channel_id=1, source_target_pairs={{1,5},{2,6},{5,1},{6,2},{9,13},{10,14},{13,9},{14,10},{17,21},{18,... | collective-permute-start | bytes 1572872 | tf_op jit(solution)/shard_map/ppermute | solution.py:23
  131.2 5.2 %collective-permute-start.29 = (bf16[528,1024]{1,0:T(8,128)(2,1)S(1)}, bf16[528,1024]{1,0:T(8,128)(2,1)S(1)}, u32[]{:S(2)}, u32[]{:S(2)}) collective-permute-start(bf16[528,1024]{1,0:T(8,128)(2,1)S(1)} %get-tuple-element.34.refs_0_.rest_0_), channel_id=1, source_target_pairs={{1,9},{2,10},{5,13},{6,14},{9,1},{10,2},{13,5},{14,6},{17,25},{18,... | collective-permute-start | bytes 3244040 | tf_op jit(solution)/shard_map/ppermute | solution.py:23
  132.0 5.2 %collective-permute-start.27 = (bf16[528,1024]{1,0:T(8,128)(2,1)S(1)}, bf16[528,1024]{1,0:T(8,128)(2,1)S(1)}, u32[]{:S(2)}, u32[]{:S(2)}) collective-permute-start(bf16[528,1024]{1,0:T(8,128)(2,1)S(1)} %get-tuple-element.34.refs_0_.rest_0_), channel_id=1, source_target_pairs={{1,2},{2,1},{5,6},{6,5},{9,10},{10,9},{13,14},{14,13},{17,18},{18,... | collective-permute-start | bytes 3244040 | tf_op jit(solution)/shard_map/ppermute | solution.py:27
  132.7 7.5 %collective-permute-start.28 = (bf16[528,1024]{1,0:T(8,128)(2,1)S(1)}, bf16[528,1024]{1,0:T(8,128)(2,1)S(1)}, u32[]{:S(2)}, u32[]{:S(2)}) collective-permute-start(bf16[528,1024]{1,0:T(8,128)(2,1)S(1)} %get-tuple-element.34.refs_0_.rest_0_), channel_id=1, source_target_pairs={{1,5},{2,6},{5,1},{6,2},{9,13},{10,14},{13,9},{14,10},{17,21},{18,... | collective-permute-start | bytes 3244040 | tf_op jit(solution)/shard_map/ppermute | solution.py:23
  136.4 3.8 %collective-permute-start.30 = (bf16[528,1024]{1,0:T(8,128)(2,1)S(1)}, bf16[528,1024]{1,0:T(8,128)(2,1)S(1)}, u32[]{:S(2)}, u32[]{:S(2)}) collective-permute-start(bf16[528,1024]{1,0:T(8,128)(2,1)S(1)} %collective-permute-done.29.rest_2_), channel_id=1, source_target_pairs={{1,5},{2,6},{5,1},{6,2},{9,13},{10,14},{13,9},{14,10},{17,21},{18,... | collective-permute-start | bytes 3244040 | tf_op jit(solution)/shard_map/ppermute | solution.py:23
  143.1 88.0 %collective-permute-start.31 = (bf16[512,512]{1,0:T(8,128)(2,1)S(1)}, bf16[512,512]{1,0:T(8,128)(2,1)S(1)}, u32[]{:S(2)}, u32[]{:S(2)}) collective-permute-start(bf16[512,512]{1,0:T(8,128)(2,1)S(1)} %get-tuple-element.38), channel_id=1, source_target_pairs={{1,0},{2,3},{5,4},{6,7},{9,8},{10,11},{13,12},{14,15},{17,16},{18,... | collective-permute-start | bytes 1572872 | tf_op jit(solution)/shard_map/ppermute | solution.py:35
  145.1 85.5 %collective-permute-start.33 = (f32[1,512]{1,0:T(1,128)S(1)}, f32[1,512]{1,0:T(1,128)S(1)}, u32[]{:S(2)}, u32[]{:S(2)}) collective-permute-start(f32[1,512]{1,0:T(1,128)S(1)} %slice_add_fusion), channel_id=1, source_target_pairs={{1,0},{2,3},{5,4},{6,7},{9,8},{10,11},{13,12},{14,15},{17,16},{18,... | collective-permute-start | bytes 6152 | tf_op jit(solution)/shard_map/ppermute | solution.py:35
  (14 other events, 64.1 us)

commit v6 on v5

--- a/solution.py
+++ b/solution.py
@@ -6,7 +6,7 @@
 from jax.sharding import PartitionSpec as P
 
 EXTRA = 16
-VMEM = 24 * 1024 * 1024
+VMEM = 14 * 1024 * 1024
 NT = (((1,), (1,)), ((), ()))
 
 
@@ -92,71 +92,85 @@
     )(pivots, *extra, *operands.arrays)
 
 
-def product(left, right, added, form, size, share=None, turn=0):
+def product(left, halves, form, size, added=None, own=None, turn=0):
     count = left.shape[1] // size
     operands = Operands()
-    views = [[operands.add(view) for view in half] for half in right]
-    tall, wide = size + EXTRA, 2 * size
-    shapes = {
-        "joint": [(tall, wide)],
-        "both": [(tall, wide), (tall, size), (size, size)],
-        "split": [(size, size), (size, size)],
-    }[form]
+    views = [[operands.add(view) for view in half] for half in halves]
+    own_views = [operands.add(view) for view in own or []]
+    extra = [] if added is None else [added]
+    tall, wide = size + (EXTRA if extra else 0), size * len(halves)
+    shapes = [] if form == "apart" else [(tall, wide)]
+    if form != "joint":
+        shapes += [(size, size)] * (len(halves) - 1) + [(tall, size)]
     outs = [jax.ShapeDtypeStruct(shape, jnp.bfloat16) for shape in shapes]
-    outs.append(jax.ShapeDtypeStruct((EXTRA, size), jnp.float32))
-
-    def kernel(left_ref, added_ref, *rest):
-        refs = rest[: len(operands.arrays)]
-        results = rest[len(refs) :]
-
-        for half in range(2):
+    if extra:
+        outs.append(jax.ShapeDtypeStruct((EXTRA, size), jnp.float32))
+
+    def kernel(left_ref, *rest):
+        refs = rest[len(extra) : len(extra) + len(operands.arrays)]
+        results = rest[len(extra) + len(refs) :]
+        joint = None if form == "apart" else results[0]
+        single = [] if form == "joint" else results[len(shapes) - len(halves) : len(shapes)]
+
+        for i, half in enumerate(views):
             total = None
             for b in range(count):
                 part = jnp.dot(
                     left_ref[:, b * size : (b + 1) * size],
-                    read(refs, views[half][b], size),
+                    read(refs, half[b], size),
                     preferred_element_type=jnp.float32,
                 )
                 total = part if total is None else total + part
             total = total.astype(jnp.bfloat16)
-            if form != "split":
-                results[0][0:size, half * size : (half + 1) * size] = total
-            if form != "joint":
-                results[half + len(results) - 3][0:size, :] = total
+            if joint is not None:
+                joint[0:size, i * size : (i + 1) * size] = total
+            if single:
+                single[i][0:size, :] = total
+        if not extra:
+            return
 
         def pieces(b, k):
-            here = slice(k * share, (k + 1) * share)
-            own, end = (read(refs, views[half][b], size, slice(size, tall))[:, here] for half in (0, 1))
-            return jnp.concatenate([end, own, own, end], axis=1) * added_ref[...]
-
-        applied = added_ref[...] if share is None else pieces(0, turn + 1).astype(jnp.float32)
+            here = slice(k * (size // 4), (k + 1) * (size // 4))
+            near, end = (
+                read(refs, kind[b], size, slice(size, tall))[:, here] for kind in (own_views, views[-1])
+            )
+            return jnp.concatenate([end, near, near, end], axis=1) * rest[0][...]
+
+        applied = rest[0][...] if own is None else pieces(0, turn + 1).astype(jnp.float32)
         for b in range(count):
-            if share is None:
-                rows = read(refs, views[0][b], size, slice(size, tall))
+            if own is None:
+                rows = read(refs, views[-1][b], size, slice(size, tall))
             else:
                 rows = pieces(b, turn)
             applied = applied + lax.dot_general(
                 rows, left_ref[:, b * size : (b + 1) * size], NT, preferred_element_type=jnp.float32
             )
         results[-1][...] = applied
-        if form != "split":
-            results[0][size:tall, 0:size] = applied.astype(jnp.bfloat16)
-            results[0][size:tall, size:wide] = applied.astype(jnp.bfloat16)
-        if form == "both":
-            results[1][size:tall, :] = applied.astype(jnp.bfloat16)
+        applied = applied.astype(jnp.bfloat16)
+        if joint is not None:
+            for i in range(len(halves)):
+                joint[size:tall, i * size : (i + 1) * size] = applied
+        if single:
+            single[-1][size:tall, :] = applied
 
     return pl.pallas_call(
         kernel,
         out_shape=tuple(outs),
         compiler_params=pltpu.CompilerParams(vmem_limit_bytes=VMEM),
         cost_estimate=pl.CostEstimate(
-            flops=4 * size * size * size * count, bytes_accessed=24 * size * size, transcendentals=0
+            flops=2 * len(halves) * size * size * size * count,
+            bytes_accessed=12 * len(halves) * size * size,
+            transcendentals=0,
         ),
-    )(left, added, *operands.arrays)
+    )(left, *extra, *operands.arrays)
 
 
 def after(value, *others):
     return lax.optimization_barrier((value, *others))[0]
+
+
+def plain(*tiles):
+    return [(tile, None, 0) for tile in tiles]
 
 
 def shards(interval_blocks, interval_pivots, boundary_pivots, interval_residuals):
@@ -174,7 +188,8 @@
     ends_left = inward(lefts)
     lefts_other = swap_middle(lefts)
     rights_across = swap_rows(rights, 2)
-    end_upper, end_lower = inward(tiles[1]), inward(tiles[0])
+    end_lower = inward(tiles[0])
+    end_upper = inward(tiles[1])
     rights_beside = swap_rows(rights, 1)
 
     own = lax.dynamic_index_in_dim(boundary_pivots, position, 0, keepdims=True)
@@ -193,52 +208,65 @@
     def panel(turn, tiles, onto=None):
         return spread_columns(pivots[turn], tiles, size, count, onto)
 
-    ends_other = swap_middle(ends_left)
+    upper_panel, lower_panel = panel(2, [(0, (lefts, 1, 0))]), panel(0, [(0, (lefts, 0, 0))])
+    ends_other = swap_middle(after(ends_left, upper_panel, lower_panel))
     rights_last = swap_rows(rights_across, 1)
-    upper_panel, lower_panel = panel(2, [(0, (lefts, 1, 0))]), panel(0, [(0, (lefts, 0, 0))])
+    lower_panel = panel(0, [(1, (ends_left, 0, 0)), (2, (lefts_other, 0, 0))], lower_panel)
     upper_panel = panel(2, [(1, (ends_left, 1, 0)), (2, (lefts_other, 1, 0))], upper_panel)
-    end_upper = after(end_upper, upper_panel)
+    end_lower = after(end_lower, lower_panel, upper_panel)
+    lower_across = swap_rows(end_lower, 2)
+    lower_ends = [end_lower, swap_rows(end_lower, 1), lower_across, swap_rows(lower_across, 1)]
     upper_across = swap_rows(end_upper, 2)
-    lower_panel = panel(0, [(1, (ends_left, 0, 0)), (2, (lefts_other, 0, 0))], lower_panel)
-    end_lower = after(end_lower, lower_panel)
-    lower_across = swap_rows(end_lower, 2)
+    upper_ends = [end_upper, swap_rows(end_upper, 1), upper_across]
+    lower_panel = panel(0, [(3, (ends_other, 0, 0))], lower_panel)
     upper_panel = panel(2, [(3, (ends_other, 1, 0))], upper_panel)
-    lower_panel = panel(0, [(3, (ends_other, 0, 0))], lower_panel)
-
-    def first(turn, k, left, end, across):
-        ends = [end, swap_rows(end, 1), across, swap_rows(across, 1)]
-        right = [
-            [(tile, k, 0) for tile in (rights, rights_beside, rights_across, rights_last)],
-            [(tile, None, 0) for tile in ends],
-        ]
-        return product(left, right, held, "joint", size, share, turn)
-
-    upper, upper_vector = first(2, 1, upper_panel, end_upper, upper_across)
-    lower, _ = first(0, 0, lower_panel, end_lower, after(lower_across, upper))
-
-    def later(turn, left, added, right, form):
-        other = swap_middle(left)
-        partial = panel(turn, [(0, (left, None, 0)), (1, (left, None, size))])
+
+    def own_tiles(k):
+        return [(tile, k, 0) for tile in (rights, rights_beside, rights_across, rights_last)]
+
+    lower, _ = product(
+        lower_panel, [own_tiles(0), plain(*lower_ends)], "joint", size, held, own_tiles(0), 0
+    )
+    upper_panel = after(upper_panel, lower)
+    (upper_o,) = product(upper_panel, [own_tiles(1)], "apart", size)
+    upper_ends.append(swap_rows(after(upper_across, upper_o), 1))
+    upper_e, vector = product(
+        upper_panel, [plain(*upper_ends)], "apart", size, held, own_tiles(1), 2
+    )
+
+    def right_views(right, tie):
         parts = []
         for tile in right:
             beside, across = swap_rows(tile, 1), swap_rows(tile, 2)
-            parts.append([tile, beside, across, swap_rows(after(across, partial), 1)])
+            parts.append([tile, beside, across, swap_rows(after(across, *tie), 1)])
         if len(parts) == 1:
-            views = [[(tile, None, column) for tile in parts[0]] for column in (0, size)]
-        else:
-            views = [[(tile, None, 0) for tile in part] for part in parts]
-        moved = panel(turn, [(2, (other, None, 0)), (3, (other, None, size))], partial)
-        return product(moved, views, added, form, size)
-
-    whole, whole_o, whole_e, whole_vector = later(1, upper, upper_vector, [lower], "both")
+            return [[(tile, None, column) for tile in parts[0]] for column in (0, size)]
+        return [plain(*part) for part in parts]
+
+    other_o, other_e = swap_middle(upper_o), swap_middle(upper_e)
+    moved = panel(1, [(0, (upper_o, None, 0)), (1, (upper_e, None, 0))])
+    moved = panel(1, [(2, (other_o, None, 0))], moved)
+    views = right_views([lower], (moved, other_e))
+    moved = panel(1, [(3, (other_e, None, 0))], moved)
+    whole, whole_o, whole_e, vector = product(moved, views, "both", size, vector)
+
+    def left_panel(turn, left):
+        other = swap_middle(left)
+        partial = panel(turn, [(0, (left, None, 0)), (1, (left, None, size))])
+        return partial, panel(turn, [(2, (other, None, 0)), (3, (other, None, size))], partial)
+
     earlier = [from_behind(tile, "loop", 1) for tile in (whole_o, whole_e)]
-    halved, halved_vector = later(3, whole, whole_vector, earlier, "joint")
-    distant = from_behind(halved, "loop", 2)
-    reduced_o, reduced_e, applied = later(4, halved, halved_vector, [distant], "split")
+    partial, moved = left_panel(3, whole)
+    views = right_views(earlier, (partial,))
+    halved, vector = product(moved, views, "joint", size, vector)
+    partial, moved = left_panel(4, halved)
+    views = right_views([from_behind(halved, "loop", 2)], (partial,))
+    reduced_e, vector = product(moved, views[1:], "apart", size, vector)
+    (reduced_o,) = product(after(moved, reduced_e), views[:1], "apart", size)
 
     middle = (col == 1) | (col == 2)
-    block = jnp.where(middle, reduced_o, outward(reduced_e))
-    vector = applied[:1]
+    block = jnp.where(middle, reduced_o, outward(reduced_e)[:size])
+    vector = vector[:1]
     vector = vector + swap_middle(vector)
     vector = jnp.where(middle, vector, outward(vector))
     return (block[None], lax.dynamic_slice_in_dim(vector, col * share, share, 1))

time: 233 us -> 231 us (level)
  waiting for transfers between devices: 115 us -> 104 us
  Pallas kernels: 55.3 us -> 60.8 us
  local copies, waits for them, and re-layouts: 7.84 us -> 10.7 us
    ppermute x3, waiting for transfers between devices: 11 us -> 4.87 us  [inward(): return lax.ppermute(value, 'col', [(0, 1), (3, 2)])]
    ppermute x2, waiting for transfers between devices: 84.2 us -> 78.7 us  [outward(): return lax.ppermute(value, 'col', [(1, 0), (2, 3)])]
    pallas_call x12 -> x13, Pallas kernels: 37.2 us -> 40.6 us  [spread_columns(): pl.pallas_call(kernel, out_shape=jax.ShapeDtypeStruct((size, size * count...]
    unnamed x26 -> x32, local copies, waits for them, and re-layouts: 5.17 us -> 8 us
    ppermute x3, starting transfers between devices: 20.9 us -> 18.2 us  [inward(): return lax.ppermute(value, 'col', [(0, 1), (3, 2)])]
    pallas_call x5 -> x7, Pallas kernels: 18.1 us -> 20.2 us  [product(): pl.pallas_call(kernel, out_shape=tuple(outs), compiler_params=pltpu.Compi...]
    ppermute x6 -> x7, starting transfers between devices: 5.18 us -> 6.95 us  [swap_middle(): return lax.ppermute(value, 'col', [(1, 2), (2, 1)])]
  transfers between devices with their start and end apart: 34 -> 35, of which waited for: 4 -> 5; matrix products, arithmetic and copies ran while one was open for 1% -> 1% of each run, Pallas kernels for 18% -> 23%
where the time goes in v6:
time: 231 us; the launch traced here: 229 us
  waiting for transfers between devices  104 us (45%)
  Pallas kernels  60.8 us (26%)
  starting transfers between devices  48 us (21%)
  local copies, waits for them, and re-layouts  10.7 us (5%)
  other arithmetic  3.85 us (2%)
    ppermute x2, waiting for transfers between devices, outward(): return lax.ppermute(value, 'col', [(1, 0), (2, 3)])  78.7 us
    pallas_call x13, Pallas kernels, spread_columns(): pl.pallas_call(kernel, out_shape=jax.ShapeDtypeStruct((size, size * count...  40.6 us
    ppermute x2, waiting for transfers between devices, from_behind(): lax.ppermute(value, axis, [(i, (i + by) % devices) for i in range(devices)])  20.8 us
    pallas_call x7, Pallas kernels, product(): pl.pallas_call(kernel, out_shape=tuple(outs), compiler_params=pltpu.Compi...  20.2 us
    ppermute x3, starting transfers between devices, inward(): return lax.ppermute(value, 'col', [(0, 1), (3, 2)])  18.2 us
    ppermute x21, starting transfers between devices, swap_rows(): return lax.ppermute(value, ('row', 'col'), pairs)  18.2 us
    unnamed x32, local copies, waits for them, and re-layouts  8 us
    ppermute x7, starting transfers between devices, swap_middle(): return lax.ppermute(value, 'col', [(1, 2), (2, 1)])  6.95 us
  transfers between devices with their start and end apart: 35, of which 5 were waited for; matrix products, arithmetic and copies ran while one was open for 1% of the time, Pallas kernels for 23%

profile of v6, /device:TPU:0, one launch (start us, length us, event | category | flops | bytes accessed | tf_op | source)
XLA Modules:
  0.0 229.1 jit_solution(12374081307544192672)
XLA Ops:
  0.6 2.4 %slice.44.refs_0_ = bf16[2,512,512]{2,1,0:T(8,128)(2,1)} slice(bf16[4,512,512]{2,1,0:T(8,128)(2,1)} %bitcast.22), slice={[1:4:2], [0:512:1], [0:512:1]} | slice | bytes 2097152 | tf_op jit(solution)/shard_map/slice | solution.py:184
  3.1 6.0 %collective-permute-start = (bf16[2,512,512]{2,1,0:T(8,128)(2,1)}, bf16[2,512,512]{2,1,0:T(8,128)(2,1)}, u32[]{:S(2)}, u32[]{:S(2)}) collective-permute-start(bf16[2,512,512]{2,1,0:T(8,128)(2,1)} %slice.44.refs_0_), channel_id=1, source_target_pairs={{0,1},{3,2},{4,5},{7,6},{8,9},{11,10},{12,13},{15,14},{16,17},{19,... | collective-permute-start | bytes 3145736 | tf_op jit(solution)/shard_map/ppermute | solution.py:31
  9.1 1.6 collective-permute-start.1
  13.6 7.0 %collective-permute-start.6 = (bf16[528,512]{1,0:T(8,128)(2,1)}, bf16[528,512]{1,0:T(8,128)(2,1)}, u32[]{:S(2)}, u32[]{:S(2)}) collective-permute-start(bf16[528,512]{1,0:T(8,128)(2,1)} %get-tuple-element.60), channel_id=1, source_target_pairs={{0,1},{3,2},{4,5},{7,6},{8,9},{11,10},{12,13},{15,14},{16,17},{19,... | collective-permute-start | bytes 1622024 | tf_op jit(solution)/shard_map/ppermute | solution.py:31
  21.0 3.1 %shard_map.61.refs_0_ = bf16[512,2048]{1,0:T(8,128)(2,1)S(1)} custom-call(s32[4,512]{1,0:T(4,128)S(1)} %get-tuple-element.50.q_ref, bf16[2,512,512]{2,1,0:T(8,128)(2,1)} %slice.44.refs_0_), custom_call_target="tpu_custom_call" | custom-call | flops 1073741824 | bytes 2097152 | tf_op jit(solution)/shard_map/pallas_call | solution.py:83
  24.1 3.2 %shard_map.59.refs_0_ = bf16[512,2048]{1,0:T(8,128)(2,1)S(1)} custom-call(s32[4,512]{1,0:T(4,128)S(1)} %get-tuple-element.51.q_ref, bf16[2,512,512]{2,1,0:T(8,128)(2,1)} %slice.44.refs_0_), custom_call_target="tpu_custom_call" | custom-call | flops 1073741824 | bytes 2097152 | tf_op jit(solution)/shard_map/pallas_call | solution.py:83
  27.3 4.7 %collective-permute-done.refs_1_ = bf16[2,512,512]{2,1,0:T(8,128)(2,1)} collective-permute-done((bf16[2,512,512]{2,1,0:T(8,128)(2,1)}, bf16[2,512,512]{2,1,0:T(8,128)(2,1)}, u32[]{:S(2)}, u32[]{:S(2)}) %collective-permute-start) | collective-permute-done | bytes 1048608 | tf_op jit(solution)/shard_map/ppermute | solution.py:31
  32.0 5.2 %collective-permute-start.10 = (bf16[528,512]{1,0:T(8,128)(2,1)S(1)}, bf16[528,512]{1,0:T(8,128)(2,1)}, u32[]{:S(2)}, u32[]{:S(2)}) collective-permute-start(bf16[528,512]{1,0:T(8,128)(2,1)S(1)} %copy-done.11), channel_id=1, source_target_pairs={{0,1},{3,2},{4,5},{7,6},{8,9},{11,10},{12,13},{15,14},{16,17},{19,... | collective-permute-start | bytes 1622024 | tf_op jit(solution)/shard_map/ppermute | solution.py:31
  37.2 1.6 collective-permute-start.2
  38.9 4.5 %shard_map.63.refs_0_ = bf16[512,2048]{1,0:T(8,128)(2,1)S(1)} custom-call(s32[4,512]{1,0:T(4,128)S(1)} %get-tuple-element.50.q_ref, bf16[512,2048]{1,0:T(8,128)(2,1)S(1)} %shard_map.61.refs_0_, bf16[2,512,512]{2,1,0:T(8,128)(2,1)} %collective-permute-done.refs_1_, bf16[2,512,512]{2,1,0:T(8,128)(2,1)} %collective-permute-done.1.refs_2_), custom_call_target="tpu_custom_call" | custom-call | flops 2147483648 | bytes 2097152 | tf_op jit(solution)/shard_map/pallas_call | solution.py:83
  44.7 4.5 %shard_map.60.refs_0_ = bf16[512,2048]{1,0:T(8,128)(2,1)S(1)} custom-call(s32[4,512]{1,0:T(4,128)S(1)} %get-tuple-element.51.q_ref, bf16[512,2048]{1,0:T(8,128)(2,1)S(1)} %shard_map.59.refs_0_, bf16[2,512,512]{2,1,0:T(8,128)(2,1)} %collective-permute-done.refs_1_, bf16[2,512,512]{2,1,0:T(8,128)(2,1)} %collective-permute-done.1.refs_2_), custom_call_target="tpu_custom_call" | custom-call | flops 2147483648 | bytes 2097152 | tf_op jit(solution)/shard_map/pallas_call | solution.py:83
  52.1 1.7 collective-permute-start.5
  57.6 1.6 copy-done.9
  59.2 3.3 %shard_map.64.left_ref = bf16[512,2048]{1,0:T(8,128)(2,1)S(1)} custom-call(s32[4,512]{1,0:T(4,128)S(1)} %get-tuple-element.50.q_ref, bf16[512,2048]{1,0:T(8,128)(2,1)S(1)} %copy-done.9, bf16[2,512,512]{2,1,0:T(8,128)(2,1)} %collective-permute-done.2.refs_1_), custom_call_target="tpu_custom_call" | custom-call | flops 1073741824 | bytes 2097152 | tf_op jit(solution)/shard_map/pallas_call | solution.py:83
  62.5 3.1 %shard_map.62.left_ref = bf16[512,2048]{1,0:T(8,128)(2,1)S(1)} custom-call(s32[4,512]{1,0:T(4,128)S(1)} %get-tuple-element.51.q_ref, bf16[512,2048]{1,0:T(8,128)(2,1)S(1)} %copy-done.7, bf16[2,512,512]{2,1,0:T(8,128)(2,1)} %collective-permute-done.2.refs_1_), custom_call_target="tpu_custom_call" | custom-call | flops 1073741824 | bytes 2097152 | tf_op jit(solution)/shard_map/pallas_call | solution.py:83
  66.4 5.3 %shard_map.65 = (bf16[528,1024]{1,0:T(8,128)(2,1)S(1)}, f32[16,512]{1,0:T(8,128)}) custom-call(bf16[512,2048]{1,0:T(8,128)(2,1)S(1)} %shard_map.64.left_ref, bf16[16,512]{1,0:T(8,128)(2,1)S(1)} %iota.7.rest_0_, bf16[2,528,512]{2,1,0:T(8,128)(2,1)S(1)} %pad_maximum_fusion.rest_1_.rest_0_.rest_5_, ...), custom_call_target="tpu_custom_call" | custom-call | flops 2147483648 | bytes 6291456 | tf_op jit(solution)/shard_map/pallas_call | solution.py:156
  71.7 2.5 %shard_map.66.refs_0_ = bf16[512,512]{1,0:T(8,128)(2,1)S(1)} custom-call(bf16[512,2048]{1,0:T(8,128)(2,1)S(1)} %shard_map.62.left_ref, bf16[2,528,512]{2,1,0:T(8,128)(2,1)S(1)} %pad_maximum_fusion.rest_1_.rest_0_.rest_5_, bf16[2,528,512]{2,1,0:T(8,128)(2,1)S(1)} %collective-permute-done.3.rest_2_.rest_1_.rest_6_, ...), custom_call_target="tpu_custom_call" | custom-call | flops 1073741824 | bytes 3145728 | tf_op jit(solution)/shard_map/pallas_call | solution.py:156
  76.3 3.1 %shard_map.67 = (bf16[528,512]{1,0:T(8,128)(2,1)S(1)}, f32[16,512]{1,0:T(8,128)S(1)}) custom-call(bf16[512,2048]{1,0:T(8,128)(2,1)S(1)} %shard_map.62.left_ref, bf16[16,512]{1,0:T(8,128)(2,1)S(1)} %iota.7.rest_0_, bf16[528,512]{1,0:T(8,128)(2,1)} %collective-permute-done.10.rest_1_, bf16[528,512]{1,0:T(8,128)(2,1)S(1)} %collective-permute-done.11.rest_2_, ...), custom_call_target="tpu_custom_call" | custom-call | flops 1073741824 | bytes 3145728 | tf_op jit(solution)/shard_map/pallas_call | solution.py:156
  80.9 3.0 %shard_map.68.refs_0_ = bf16[512,2048]{1,0:T(8,128)(2,1)S(1)} custom-call(s32[4,512]{1,0:T(4,128)S(1)} %get-tuple-element.52.q_ref, bf16[512,512]{1,0:T(8,128)(2,1)S(1)} %shard_map.66.refs_0_, bf16[528,512]{1,0:T(8,128)(2,1)S(1)} %get-tuple-element.27.refs_1_), custom_call_target="tpu_custom_call" | custom-call | flops 2147483648 | bytes 2097152 | tf_op jit(solution)/shard_map/pallas_call | solution.py:83
  83.9 1.9 shard_map.69.refs_0_
  86.6 1.9 shard_map.70.left_ref
  88.5 2.8 %shard_map.71 = (bf16[528,1024]{1,0:T(8,128)(2,1)S(1)}, bf16[512,512]{1,0:T(8,128)(2,1)S(1)}, bf16[528,512]{1,0:T(8,128)(2,1)S(1)}, f32[16,512]{1,0:T(8,128)S(1)}) custom-call(bf16[512,2048]{1,0:T(8,128)(2,1)S(1)} %shard_map.70.left_ref, f32[16,512]{1,0:T(8,128)S(1)} %get-tuple-element.28.rest_0_, bf16[528,1024]{1,0:T(8,128)(2,1)S(1)} %get-tuple-element.24.rest_1_, ...), custom_call_target="tpu_custom_call" | custom-call | flops 2147483648 | bytes 6291456 | tf_op jit(solution)/shard_map/pallas_call | solution.py:156
  94.3 12.3 %collective-permute-done.24.rest_5_ = bf16[528,512]{1,0:T(8,128)(2,1)S(1)} collective-permute-done((bf16[528,512]{1,0:T(8,128)(2,1)S(1)}, bf16[528,512]{1,0:T(8,128)(2,1)S(1)}, u32[]{:S(2)}, u32[]{:S(2)}) %collective-permute-start.24) | collective-permute-done | bytes 540704 | tf_op jit(solution)/shard_map/ppermute | solution.py:17
  107.2 8.5 %collective-permute-done.20.rest_1_ = bf16[512,512]{1,0:T(8,128)(2,1)S(1)} collective-permute-done((bf16[512,512]{1,0:T(8,128)(2,1)S(1)}, bf16[512,512]{1,0:T(8,128)(2,1)S(1)}, u32[]{:S(2)}, u32[]{:S(2)}) %collective-permute-start.20) | collective-permute-done | bytes 524320 | tf_op jit(solution)/shard_map/ppermute | solution.py:17
  116.4 3.0 %shard_map.72.refs_0_ = bf16[512,2048]{1,0:T(8,128)(2,1)S(1)} custom-call(s32[4,512]{1,0:T(4,128)S(1)} %get-tuple-element.53.q_ref, bf16[528,1024]{1,0:T(8,128)(2,1)S(1)} %get-tuple-element.30.refs_0_), custom_call_target="tpu_custom_call" | custom-call | flops 2147483648 | bytes 2097152 | tf_op jit(solution)/shard_map/pallas_call | solution.py:83
  122.3 3.0 %shard_map.73.left_ref = bf16[512,2048]{1,0:T(8,128)(2,1)S(1)} custom-call(s32[4,512]{1,0:T(4,128)S(1)} %get-tuple-element.53.q_ref, bf16[512,2048]{1,0:T(8,128)(2,1)S(1)} %shard_map.72.refs_0_, bf16[528,1024]{1,0:T(8,128)(2,1)S(1)} %collective-permute-done.19.refs_1_), custom_call_target="tpu_custom_call" | custom-call | flops 2147483648 | bytes 2097152 | tf_op jit(solution)/shard_map/pallas_call | solution.py:83
  125.3 2.8 %shard_map.74 = (bf16[528,1024]{1,0:T(8,128)(2,1)S(1)}, f32[16,512]{1,0:T(8,128)S(1)}) custom-call(bf16[512,2048]{1,0:T(8,128)(2,1)S(1)} %shard_map.73.left_ref, f32[16,512]{1,0:T(8,128)S(1)} %get-tuple-element.31.rest_0_, bf16[512,512]{1,0:T(8,128)(2,1)S(1)} %collective-permute-done.20.rest_1_, bf16[512,512]{1,0:T(8,128)(2,1)S(1)} %collective-permute-done.21.rest_2_, ...), custom_call_target="tpu_custom_call" | custom-call | flops 2147483648 | bytes 6291456 | tf_op jit(solution)/shard_map/pallas_call | solution.py:156
  130.3 3.0 %shard_map.75.refs_0_ = bf16[512,2048]{1,0:T(8,128)(2,1)S(1)} custom-call(s32[4,512]{1,0:T(4,128)S(1)} %get-tuple-element.54.q_ref, bf16[528,1024]{1,0:T(8,128)(2,1)S(1)} %get-tuple-element.36.refs_0_.rest_1_.rest_0_), custom_call_target="tpu_custom_call" | custom-call | flops 2147483648 | bytes 2097152 | tf_op jit(solution)/shard_map/pallas_call | solution.py:83
  134.1 3.0 %shard_map.76.left_ref = bf16[512,2048]{1,0:T(8,128)(2,1)S(1)} custom-call(s32[4,512]{1,0:T(4,128)S(1)} %get-tuple-element.54.q_ref, bf16[512,2048]{1,0:T(8,128)(2,1)S(1)} %shard_map.75.refs_0_, bf16[528,1024]{1,0:T(8,128)(2,1)S(1)} %collective-permute-done.28.refs_1_), custom_call_target="tpu_custom_call" | custom-call | flops 2147483648 | bytes 2097152 | tf_op jit(solution)/shard_map/pallas_call | solution.py:83
  137.1 2.5 %shard_map.77 = (bf16[528,512]{1,0:T(8,128)(2,1)}, f32[16,512]{1,0:T(8,128)S(1)}) custom-call(bf16[512,2048]{1,0:T(8,128)(2,1)S(1)} %shard_map.76.left_ref, f32[16,512]{1,0:T(8,128)S(1)} %get-tuple-element.37.rest_0_, bf16[528,1024]{1,0:T(8,128)(2,1)S(1)} %get-tuple-element.36.refs_0_.rest_1_.rest_0_, ...), custom_call_target="tpu_custom_call" | custom-call | flops 1073741824 | bytes 3145728 | tf_op jit(solution)/shard_map/pallas_call | solution.py:156
  147.9 78.7 %collective-permute-done.34 = f32[1,512]{1,0:T(1,128)S(1)} collective-permute-done((f32[1,512]{1,0:T(1,128)S(1)}, f32[1,512]{1,0:T(1,128)S(1)}, u32[]{:S(2)}, u32[]{:S(2)}) %collective-permute-start.34) | collective-permute-done | bytes 2080 | tf_op jit(solution)/shard_map/ppermute | solution.py:35
  227.2 1.9 fusion
  (111 shorter events, 34.9 us)
Async XLA Ops:
  3.1 28.9 %collective-permute-start = (bf16[2,512,512]{2,1,0:T(8,128)(2,1)}, bf16[2,512,512]{2,1,0:T(8,128)(2,1)}, u32[]{:S(2)}, u32[]{:S(2)}) collective-permute-start(bf16[2,512,512]{2,1,0:T(8,128)(2,1)} %slice.44.refs_0_), channel_id=1, source_target_pairs={{0,1},{3,2},{4,5},{7,6},{8,9},{11,10},{12,13},{15,14},{16,17},{19,... | collective-permute-start | bytes 3145736 | tf_op jit(solution)/shard_map/ppermute | solution.py:31
  9.1 28.1 %collective-permute-start.1 = (bf16[2,512,512]{2,1,0:T(8,128)(2,1)}, bf16[2,512,512]{2,1,0:T(8,128)(2,1)}, u32[]{:S(2)}, u32[]{:S(2)}) collective-permute-start(bf16[2,512,512]{2,1,0:T(8,128)(2,1)} %slice.44.refs_0_), channel_id=1, source_target_pairs={{1,2},{2,1},{5,6},{6,5},{9,10},{10,9},{13,14},{14,13},{17,18},{18,... | collective-permute-start | bytes 3145736 | tf_op jit(solution)/shard_map/ppermute | solution.py:27
  12.1 40.0 %collective-permute-start.4 = (bf16[2,528,512]{2,1,0:T(8,128)(2,1)S(1)}, bf16[2,528,512]{2,1,0:T(8,128)(2,1)S(1)}, u32[]{:S(2)}, u32[]{:S(2)}) collective-permute-start(bf16[2,528,512]{2,1,0:T(8,128)(2,1)S(1)} %pad_maximum_fusion.rest_1_.rest_0_.rest_5_), channel_id=1, source_target_pairs={{1,9},{2,10},{5,13},{6,14},{9,1},{10,2},{13,5},{14,6},{17,25},{18,... | collective-permute-start | bytes 3244040 | tf_op jit(solution)/shard_map/ppermute | solution.py:23
  12.8 52.8 %collective-permute-start.3 = (bf16[2,528,512]{2,1,0:T(8,128)(2,1)S(1)}, bf16[2,528,512]{2,1,0:T(8,128)(2,1)S(1)}, u32[]{:S(2)}, u32[]{:S(2)}) collective-permute-start(bf16[2,528,512]{2,1,0:T(8,128)(2,1)S(1)} %pad_maximum_fusion.rest_1_.rest_0_.rest_5_), channel_id=1, source_target_pairs={{1,5},{2,6},{5,1},{6,2},{9,13},{10,14},{13,9},{14,10},{17,21},{18,... | collective-permute-start | bytes 3244040 | tf_op jit(solution)/shard_map/ppermute | solution.py:23
  13.6 37.1 %collective-permute-start.6 = (bf16[528,512]{1,0:T(8,128)(2,1)}, bf16[528,512]{1,0:T(8,128)(2,1)}, u32[]{:S(2)}, u32[]{:S(2)}) collective-permute-start(bf16[528,512]{1,0:T(8,128)(2,1)} %get-tuple-element.60), channel_id=1, source_target_pairs={{0,1},{3,2},{4,5},{7,6},{8,9},{11,10},{12,13},{15,14},{16,17},{19,... | collective-permute-start | bytes 1622024 | tf_op jit(solution)/shard_map/ppermute | solution.py:31
  32.0 21.9 %collective-permute-start.10 = (bf16[528,512]{1,0:T(8,128)(2,1)S(1)}, bf16[528,512]{1,0:T(8,128)(2,1)}, u32[]{:S(2)}, u32[]{:S(2)}) collective-permute-start(bf16[528,512]{1,0:T(8,128)(2,1)S(1)} %copy-done.11), channel_id=1, source_target_pairs={{0,1},{3,2},{4,5},{7,6},{8,9},{11,10},{12,13},{15,14},{16,17},{19,... | collective-permute-start | bytes 1622024 | tf_op jit(solution)/shard_map/ppermute | solution.py:31
  37.2 19.6 %collective-permute-start.2 = (bf16[2,512,512]{2,1,0:T(8,128)(2,1)}, bf16[2,512,512]{2,1,0:T(8,128)(2,1)}, u32[]{:S(2)}, u32[]{:S(2)}) collective-permute-start(bf16[2,512,512]{2,1,0:T(8,128)(2,1)} %collective-permute-done.refs_1_), channel_id=1, source_target_pairs={{1,2},{2,1},{5,6},{6,5},{9,10},{10,9},{13,14},{14,13},{17,18},{18,... | collective-permute-start | bytes 3145736 | tf_op jit(solution)/shard_map/ppermute | solution.py:27
  50.6 4.8 %collective-permute-start.8 = (bf16[528,512]{1,0:T(8,128)(2,1)}, bf16[528,512]{1,0:T(8,128)(2,1)}, u32[]{:S(2)}, u32[]{:S(2)}) collective-permute-start(bf16[528,512]{1,0:T(8,128)(2,1)} %collective-permute-done.6.rest_5_), channel_id=1, source_target_pairs={{1,9},{2,10},{5,13},{6,14},{9,1},{10,2},{13,5},{14,6},{17,25},{18,... | collective-permute-start | bytes 1622024 | tf_op jit(solution)/shard_map/ppermute | solution.py:23
  52.1 14.3 %collective-permute-start.5 = (bf16[2,528,512]{2,1,0:T(8,128)(2,1)S(1)}, bf16[2,528,512]{2,1,0:T(8,128)(2,1)}, u32[]{:S(2)}, u32[]{:S(2)}) collective-permute-start(bf16[2,528,512]{2,1,0:T(8,128)(2,1)S(1)} %collective-permute-done.4.rest_3_.rest_2_.rest_7_), channel_id=1, source_target_pairs={{1,5},{2,6},{5,1},{6,2},{9,13},{10,14},{13,9},{14,10},{17,21},{18,... | collective-permute-start | bytes 3244040 | tf_op jit(solution)/shard_map/ppermute | solution.py:23
  53.9 12.4 %collective-permute-start.7 = (bf16[528,512]{1,0:T(8,128)(2,1)}, bf16[528,512]{1,0:T(8,128)(2,1)}, u32[]{:S(2)}, u32[]{:S(2)}) collective-permute-start(bf16[528,512]{1,0:T(8,128)(2,1)} %collective-permute-done.6.rest_5_), channel_id=1, source_target_pairs={{1,5},{2,6},{5,1},{6,2},{9,13},{10,14},{13,9},{14,10},{17,21},{18,... | collective-permute-start | bytes 1622024 | tf_op jit(solution)/shard_map/ppermute | solution.py:23
  55.4 11.0 %collective-permute-start.9 = (bf16[528,512]{1,0:T(8,128)(2,1)}, bf16[528,512]{1,0:T(8,128)(2,1)}, u32[]{:S(2)}, u32[]{:S(2)}) collective-permute-start(bf16[528,512]{1,0:T(8,128)(2,1)} %collective-permute-done.8.rest_7_), channel_id=1, source_target_pairs={{1,5},{2,6},{5,1},{6,2},{9,13},{10,14},{13,9},{14,10},{17,21},{18,... | collective-permute-start | bytes 1622024 | tf_op jit(solution)/shard_map/ppermute | solution.py:23
  56.9 17.3 %collective-permute-start.12 = (bf16[528,512]{1,0:T(8,128)(2,1)}, bf16[528,512]{1,0:T(8,128)(2,1)S(1)}, u32[]{:S(2)}, u32[]{:S(2)}) collective-permute-start(bf16[528,512]{1,0:T(8,128)(2,1)} %collective-permute-done.10.rest_1_), channel_id=1, source_target_pairs={{1,9},{2,10},{5,13},{6,14},{9,1},{10,2},{13,5},{14,6},{17,25},{18,... | collective-permute-start | bytes 1622024 | tf_op jit(solution)/shard_map/ppermute | solution.py:23
  65.6 10.7 %collective-permute-start.11 = (bf16[528,512]{1,0:T(8,128)(2,1)}, bf16[528,512]{1,0:T(8,128)(2,1)S(1)}, u32[]{:S(2)}, u32[]{:S(2)}) collective-permute-start(bf16[528,512]{1,0:T(8,128)(2,1)} %collective-permute-done.10.rest_1_), channel_id=1, source_target_pairs={{1,5},{2,6},{5,1},{6,2},{9,13},{10,14},{13,9},{14,10},{17,21},{18,... | collective-permute-start | bytes 1622024 | tf_op jit(solution)/shard_map/ppermute | solution.py:23
  74.9 11.0 %collective-permute-start.17 = (bf16[528,1024]{1,0:T(8,128)(2,1)S(1)}, bf16[528,1024]{1,0:T(8,128)(2,1)S(1)}, u32[]{:S(2)}, u32[]{:S(2)}) collective-permute-start(bf16[528,1024]{1,0:T(8,128)(2,1)S(1)} %get-tuple-element.24.rest_1_), channel_id=1, source_target_pairs={{1,9},{2,10},{5,13},{6,14},{9,1},{10,2},{13,5},{14,6},{17,25},{18,... | collective-permute-start | bytes 3244040 | tf_op jit(solution)/shard_map/ppermute | solution.py:23
  75.6 8.3 %collective-permute-start.14 = (bf16[512,512]{1,0:T(8,128)(2,1)S(1)}, bf16[512,512]{1,0:T(8,128)(2,1)S(1)}, u32[]{:S(2)}, u32[]{:S(2)}) collective-permute-start(bf16[512,512]{1,0:T(8,128)(2,1)S(1)} %shard_map.66.refs_0_), channel_id=1, source_target_pairs={{1,2},{2,1},{5,6},{6,5},{9,10},{10,9},{13,14},{14,13},{17,18},{18,... | collective-permute-start | bytes 1572872 | tf_op jit(solution)/shard_map/ppermute | solution.py:27
  79.4 6.4 %collective-permute-start.15 = (bf16[528,512]{1,0:T(8,128)(2,1)S(1)}, bf16[528,512]{1,0:T(8,128)(2,1)S(1)}, u32[]{:S(2)}, u32[]{:S(2)}) collective-permute-start(bf16[528,512]{1,0:T(8,128)(2,1)S(1)} %get-tuple-element.27.refs_1_), channel_id=1, source_target_pairs={{1,2},{2,1},{5,6},{6,5},{9,10},{10,9},{13,14},{14,13},{17,18},{18,... | collective-permute-start | bytes 1622024 | tf_op jit(solution)/shard_map/ppermute | solution.py:27
  80.2 8.3 %collective-permute-start.16 = (bf16[528,1024]{1,0:T(8,128)(2,1)S(1)}, bf16[528,1024]{1,0:T(8,128)(2,1)S(1)}, u32[]{:S(2)}, u32[]{:S(2)}) collective-permute-start(bf16[528,1024]{1,0:T(8,128)(2,1)S(1)} %get-tuple-element.24.rest_1_), channel_id=1, source_target_pairs={{1,5},{2,6},{5,1},{6,2},{9,13},{10,14},{13,9},{14,10},{17,21},{18,... | collective-permute-start | bytes 3244040 | tf_op jit(solution)/shard_map/ppermute | solution.py:23
  91.3 15.2 %collective-permute-start.24 = (bf16[528,512]{1,0:T(8,128)(2,1)S(1)}, bf16[528,512]{1,0:T(8,128)(2,1)S(1)}, u32[]{:S(2)}, u32[]{:S(2)}) collective-permute-start(bf16[528,512]{1,0:T(8,128)(2,1)S(1)} %get-tuple-element.34), channel_id=1, source_target_pairs={{0,16},{16,0},{1,17},{17,1},{2,18},{18,2},{3,19},{19,3},{4,20},{20... | collective-permute-start | bytes 1622024 | tf_op jit(solution)/shard_map/ppermute | solution.py:17
  92.8 22.9 %collective-permute-start.20 = (bf16[512,512]{1,0:T(8,128)(2,1)S(1)}, bf16[512,512]{1,0:T(8,128)(2,1)S(1)}, u32[]{:S(2)}, u32[]{:S(2)}) collective-permute-start(bf16[512,512]{1,0:T(8,128)(2,1)S(1)} %get-tuple-element.32), channel_id=1, source_target_pairs={{0,16},{16,0},{1,17},{17,1},{2,18},{18,2},{3,19},{19,3},{4,20},{20... | collective-permute-start | bytes 1572872 | tf_op jit(solution)/shard_map/ppermute | solution.py:17
  93.4 28.9 %collective-permute-start.19 = (bf16[528,1024]{1,0:T(8,128)(2,1)S(1)}, bf16[528,1024]{1,0:T(8,128)(2,1)S(1)}, u32[]{:S(2)}, u32[]{:S(2)}) collective-permute-start(bf16[528,1024]{1,0:T(8,128)(2,1)S(1)} %get-tuple-element.30.refs_0_), channel_id=1, source_target_pairs={{1,2},{2,1},{5,6},{6,5},{9,10},{10,9},{13,14},{14,13},{17,18},{18,... | collective-permute-start | bytes 3244040 | tf_op jit(solution)/shard_map/ppermute | solution.py:27
  106.5 13.6 %collective-permute-start.26 = (bf16[528,512]{1,0:T(8,128)(2,1)S(1)}, bf16[528,512]{1,0:T(8,128)(2,1)S(1)}, u32[]{:S(2)}, u32[]{:S(2)}) collective-permute-start(bf16[528,512]{1,0:T(8,128)(2,1)S(1)} %collective-permute-done.24.rest_5_), channel_id=1, source_target_pairs={{1,9},{2,10},{5,13},{6,14},{9,1},{10,2},{13,5},{14,6},{17,25},{18,... | collective-permute-start | bytes 1622024 | tf_op jit(solution)/shard_map/ppermute | solution.py:23
  115.7 5.8 %collective-permute-start.22 = (bf16[512,512]{1,0:T(8,128)(2,1)S(1)}, bf16[512,512]{1,0:T(8,128)(2,1)S(1)}, u32[]{:S(2)}, u32[]{:S(2)}) collective-permute-start(bf16[512,512]{1,0:T(8,128)(2,1)S(1)} %collective-permute-done.20.rest_1_), channel_id=1, source_target_pairs={{1,9},{2,10},{5,13},{6,14},{9,1},{10,2},{13,5},{14,6},{17,25},{18,... | collective-permute-start | bytes 1572872 | tf_op jit(solution)/shard_map/ppermute | solution.py:23
  119.4 5.9 %collective-permute-start.25 = (bf16[528,512]{1,0:T(8,128)(2,1)S(1)}, bf16[528,512]{1,0:T(8,128)(2,1)S(1)}, u32[]{:S(2)}, u32[]{:S(2)}) collective-permute-start(bf16[528,512]{1,0:T(8,128)(2,1)S(1)} %collective-permute-done.24.rest_5_), channel_id=1, source_target_pairs={{1,5},{2,6},{5,1},{6,2},{9,13},{10,14},{13,9},{14,10},{17,21},{18,... | collective-permute-start | bytes 1622024 | tf_op jit(solution)/shard_map/ppermute | solution.py:23
  120.1 5.2 %collective-permute-start.27 = (bf16[528,512]{1,0:T(8,128)(2,1)S(1)}, bf16[528,512]{1,0:T(8,128)(2,1)S(1)}, u32[]{:S(2)}, u32[]{:S(2)}) collective-permute-start(bf16[528,512]{1,0:T(8,128)(2,1)S(1)} %collective-permute-done.26.rest_7_), channel_id=1, source_target_pairs={{1,5},{2,6},{5,1},{6,2},{9,13},{10,14},{13,9},{14,10},{17,21},{18,... | collective-permute-start | bytes 1622024 | tf_op jit(solution)/shard_map/ppermute | solution.py:23
  120.8 4.4 %collective-permute-start.21 = (bf16[512,512]{1,0:T(8,128)(2,1)S(1)}, bf16[512,512]{1,0:T(8,128)(2,1)S(1)}, u32[]{:S(2)}, u32[]{:S(2)}) collective-permute-start(bf16[512,512]{1,0:T(8,128)(2,1)S(1)} %collective-permute-done.20.rest_1_), channel_id=1, source_target_pairs={{1,5},{2,6},{5,1},{6,2},{9,13},{10,14},{13,9},{14,10},{17,21},{18,... | collective-permute-start | bytes 1572872 | tf_op jit(solution)/shard_map/ppermute | solution.py:23
  121.5 3.7 %collective-permute-start.23 = (bf16[512,512]{1,0:T(8,128)(2,1)S(1)}, bf16[512,512]{1,0:T(8,128)(2,1)S(1)}, u32[]{:S(2)}, u32[]{:S(2)}) collective-permute-start(bf16[512,512]{1,0:T(8,128)(2,1)S(1)} %collective-permute-done.22.rest_3_), channel_id=1, source_target_pairs={{1,5},{2,6},{5,1},{6,2},{9,13},{10,14},{13,9},{14,10},{17,21},{18,... | collective-permute-start | bytes 1572872 | tf_op jit(solution)/shard_map/ppermute | solution.py:23
  128.1 5.2 %collective-permute-start.30 = (bf16[528,1024]{1,0:T(8,128)(2,1)S(1)}, bf16[528,1024]{1,0:T(8,128)(2,1)S(1)}, u32[]{:S(2)}, u32[]{:S(2)}) collective-permute-start(bf16[528,1024]{1,0:T(8,128)(2,1)S(1)} %get-tuple-element.36.refs_0_.rest_1_.rest_0_), channel_id=1, source_target_pairs={{1,9},{2,10},{5,13},{6,14},{9,1},{10,2},{13,5},{14,6},{17,25},{18,... | collective-permute-start | bytes 3244040 | tf_op jit(solution)/shard_map/ppermute | solution.py:23
  128.8 5.2 %collective-permute-start.28 = (bf16[528,1024]{1,0:T(8,128)(2,1)S(1)}, bf16[528,1024]{1,0:T(8,128)(2,1)S(1)}, u32[]{:S(2)}, u32[]{:S(2)}) collective-permute-start(bf16[528,1024]{1,0:T(8,128)(2,1)S(1)} %get-tuple-element.36.refs_0_.rest_1_.rest_0_), channel_id=1, source_target_pairs={{1,2},{2,1},{5,6},{6,5},{9,10},{10,9},{13,14},{14,13},{17,18},{18,... | collective-permute-start | bytes 3244040 | tf_op jit(solution)/shard_map/ppermute | solution.py:27
  129.6 7.5 %collective-permute-start.29 = (bf16[528,1024]{1,0:T(8,128)(2,1)S(1)}, bf16[528,1024]{1,0:T(8,128)(2,1)S(1)}, u32[]{:S(2)}, u32[]{:S(2)}) collective-permute-start(bf16[528,1024]{1,0:T(8,128)(2,1)S(1)} %get-tuple-element.36.refs_0_.rest_1_.rest_0_), channel_id=1, source_target_pairs={{1,5},{2,6},{5,1},{6,2},{9,13},{10,14},{13,9},{14,10},{17,21},{18,... | collective-permute-start | bytes 3244040 | tf_op jit(solution)/shard_map/ppermute | solution.py:23
  133.3 3.8 %collective-permute-start.31 = (bf16[528,1024]{1,0:T(8,128)(2,1)S(1)}, bf16[528,1024]{1,0:T(8,128)(2,1)S(1)}, u32[]{:S(2)}, u32[]{:S(2)}) collective-permute-start(bf16[528,1024]{1,0:T(8,128)(2,1)S(1)} %collective-permute-done.30.rest_3_.rest_2_), channel_id=1, source_target_pairs={{1,5},{2,6},{5,1},{6,2},{9,13},{10,14},{13,9},{14,10},{17,21},{18,... | collective-permute-start | bytes 3244040 | tf_op jit(solution)/shard_map/ppermute | solution.py:23
  139.7 87.5 %collective-permute-start.32 = (bf16[528,512]{1,0:T(8,128)(2,1)}, bf16[528,512]{1,0:T(8,128)(2,1)}, u32[]{:S(2)}, u32[]{:S(2)}) collective-permute-start(bf16[528,512]{1,0:T(8,128)(2,1)} %get-tuple-element.39), channel_id=1, source_target_pairs={{1,0},{2,3},{5,4},{6,7},{9,8},{10,11},{13,12},{14,15},{17,16},{18,... | collective-permute-start | bytes 1622024 | tf_op jit(solution)/shard_map/ppermute | solution.py:35
  141.7 85.0 %collective-permute-start.34 = (f32[1,512]{1,0:T(1,128)S(1)}, f32[1,512]{1,0:T(1,128)S(1)}, u32[]{:S(2)}, u32[]{:S(2)}) collective-permute-start(f32[1,512]{1,0:T(1,128)S(1)} %slice_add_fusion), channel_id=1, source_target_pairs={{1,0},{2,3},{5,4},{6,7},{9,8},{10,11},{13,12},{14,15},{17,16},{18,... | collective-permute-start | bytes 6152 | tf_op jit(solution)/shard_map/ppermute | solution.py:35
  (18 other events, 68.6 us)

commit v7 on v6

--- a/solution.py
+++ b/solution.py
@@ -46,6 +46,10 @@
                 return i, lead, column
         self.arrays.append(array)
         return len(self.arrays) - 1, lead, column
+
+
+def near(arrays):
+    return [pltpu.with_memory_space_constraint(array, pltpu.VMEM) for array in arrays]
 
 
 def read(refs, view, size, rows=None):
@@ -82,14 +86,14 @@
 
     return pl.pallas_call(
         kernel,
-        out_shape=jax.ShapeDtypeStruct((size, size * count), jnp.bfloat16),
+        out_shape=pltpu.VMEM((size, size * count), jnp.bfloat16),
         compiler_params=pltpu.CompilerParams(vmem_limit_bytes=VMEM),
         cost_estimate=pl.CostEstimate(
             flops=2 * len(tiles) * size * size * size * count,
             bytes_accessed=8 * size * size,
             transcendentals=0,
         ),
-    )(pivots, *extra, *operands.arrays)
+    )(pivots, *near(extra), *near(operands.arrays))
 
 
 def product(left, halves, form, size, added=None, own=None, turn=0):
@@ -102,9 +106,9 @@
     shapes = [] if form == "apart" else [(tall, wide)]
     if form != "joint":
         shapes += [(size, size)] * (len(halves) - 1) + [(tall, size)]
-    outs = [jax.ShapeDtypeStruct(shape, jnp.bfloat16) for shape in shapes]
+    outs = [pltpu.VMEM(shape, jnp.bfloat16) for shape in shapes]
     if extra:
-        outs.append(jax.ShapeDtypeStruct((EXTRA, size), jnp.float32))
+        outs.append(pltpu.VMEM((EXTRA, size), jnp.float32))
 
     def kernel(left_ref, *rest):
         refs = rest[len(extra) : len(extra) + len(operands.arrays)]
@@ -162,7 +166,7 @@
             bytes_accessed=12 * len(halves) * size * size,
             transcendentals=0,
         ),
-    )(left, *extra, *operands.arrays)
+    )(*near([left]), *extra, *near(operands.arrays))
 
 
 def after(value, *others):
@@ -190,7 +194,6 @@
     rights_across = swap_rows(rights, 2)
     end_lower = inward(tiles[0])
     end_upper = inward(tiles[1])
-    rights_beside = swap_rows(rights, 1)
 
     own = lax.dynamic_index_in_dim(boundary_pivots, position, 0, keepdims=True)
     back = lax.dynamic_index_in_dim(
@@ -209,16 +212,20 @@
         return spread_columns(pivots[turn], tiles, size, count, onto)
 
     upper_panel, lower_panel = panel(2, [(0, (lefts, 1, 0))]), panel(0, [(0, (lefts, 0, 0))])
-    ends_other = swap_middle(after(ends_left, upper_panel, lower_panel))
+    ends_other = swap_middle(ends_left)
     rights_last = swap_rows(rights_across, 1)
+    rights_beside = swap_rows(after(rights, upper_panel, lower_panel), 1)
+    lower_across = swap_rows(end_lower, 2)
+    lower_panel = after(lower_panel, end_lower)
     lower_panel = panel(0, [(1, (ends_left, 0, 0)), (2, (lefts_other, 0, 0))], lower_panel)
+    upper_panel = after(upper_panel, end_lower)
     upper_panel = panel(2, [(1, (ends_left, 1, 0)), (2, (lefts_other, 1, 0))], upper_panel)
-    end_lower = after(end_lower, lower_panel, upper_panel)
-    lower_across = swap_rows(end_lower, 2)
-    lower_ends = [end_lower, swap_rows(end_lower, 1), lower_across, swap_rows(lower_across, 1)]
     upper_across = swap_rows(end_upper, 2)
     upper_ends = [end_upper, swap_rows(end_upper, 1), upper_across]
+    lower_panel = after(lower_panel, upper_panel, end_upper)
     lower_panel = panel(0, [(3, (ends_other, 0, 0))], lower_panel)
+    lower_last = swap_rows(after(lower_across, lower_panel), 1)
+    lower_ends = [end_lower, swap_rows(end_lower, 1), lower_across, lower_last]
     upper_panel = panel(2, [(3, (ends_other, 1, 0))], upper_panel)
 
     def own_tiles(k):

time: 231 us -> 232 us (level)
  waiting for transfers between devices: 104 us -> 114 us
  starting transfers between devices: 48 us -> 40.8 us
  Pallas kernels: 60.8 us -> 58.3 us
    ppermute x3, waiting for transfers between devices: 4.87 us -> 18.3 us  [inward(): return lax.ppermute(value, 'col', [(0, 1), (3, 2)])]
    ppermute x3, starting transfers between devices: 18.2 us -> 11.1 us  [inward(): return lax.ppermute(value, 'col', [(0, 1), (3, 2)])]
    pallas_call x13, Pallas kernels: 40.6 us -> 37.9 us  [spread_columns(): pl.pallas_call(kernel, out_shape=pltpu.VMEM((size, size * count), jnp.bfl...]
    ppermute x2, waiting for transfers between devices: 78.7 us -> 76.1 us  [outward(): return lax.ppermute(value, 'col', [(1, 0), (2, 3)])]
    unnamed x32 -> x34, local copies, waits for them, and re-layouts: 8 us -> 9.22 us
  transfers between devices with their start and end apart: 35 -> 35, of which waited for: 5 -> 5; matrix products, arithmetic and copies ran while one was open for 1% -> 1% of each run, Pallas kernels for 23% -> 22%
where the time goes in v7:
time: 232 us; the launch traced here: 230 us
  waiting for transfers between devices  114 us (49%)
  Pallas kernels  58.3 us (25%)
  starting transfers between devices  40.8 us (18%)
  local copies, waits for them, and re-layouts  11.9 us (5%)
  other arithmetic  3.68 us (2%)
    ppermute x2, waiting for transfers between devices, outward(): return lax.ppermute(value, 'col', [(1, 0), (2, 3)])  76.1 us
    pallas_call x13, Pallas kernels, spread_columns(): pl.pallas_call(kernel, out_shape=pltpu.VMEM((size, size * count), jnp.bfl...  37.9 us
    pallas_call x7, Pallas kernels, product(): pl.pallas_call(kernel, out_shape=tuple(outs), compiler_params=pltpu.Compi...  20.4 us
    ppermute x2, waiting for transfers between devices, from_behind(): lax.ppermute(value, axis, [(i, (i + by) % devices) for i in range(devices)])  19.6 us
    ppermute x21, starting transfers between devices, swap_rows(): return lax.ppermute(value, ('row', 'col'), pairs)  19 us
    ppermute x3, waiting for transfers between devices, inward(): return lax.ppermute(value, 'col', [(0, 1), (3, 2)])  18.3 us
    ppermute x3, starting transfers between devices, inward(): return lax.ppermute(value, 'col', [(0, 1), (3, 2)])  11.1 us
    unnamed x34, local copies, waits for them, and re-layouts  9.22 us
  transfers between devices with their start and end apart: 35, of which 5 were waited for; matrix products, arithmetic and copies ran while one was open for 1% of the time, Pallas kernels for 22%

profile of v7, /device:TPU:0, one launch (start us, length us, event | category | flops | bytes accessed | tf_op | source)
XLA Modules:
  0.0 230.2 jit_solution(1027454676225807422)
XLA Ops:
  0.6 2.4 %slice.44.refs_0_ = bf16[2,512,512]{2,1,0:T(8,128)(2,1)} slice(bf16[4,512,512]{2,1,0:T(8,128)(2,1)} %bitcast.22), slice={[1:4:2], [0:512:1], [0:512:1]} | slice | bytes 2097152 | tf_op jit(solution)/shard_map/slice | solution.py:188
  3.1 6.0 %collective-permute-start.1 = (bf16[2,512,512]{2,1,0:T(8,128)(2,1)}, bf16[2,512,512]{2,1,0:T(8,128)(2,1)}, u32[]{:S(2)}, u32[]{:S(2)}) collective-permute-start(bf16[2,512,512]{2,1,0:T(8,128)(2,1)} %slice.44.refs_0_), channel_id=1, source_target_pairs={{0,1},{3,2},{4,5},{7,6},{8,9},{11,10},{12,13},{15,14},{16,17},{19,... | collective-permute-start | bytes 3145736 | tf_op jit(solution)/shard_map/ppermute | solution.py:31
  9.1 1.6 collective-permute-start.2
  11.8 3.0 %collective-permute-start = (bf16[528,512]{1,0:T(8,128)(2,1)S(1)}, bf16[528,512]{1,0:T(8,128)(2,1)}, u32[]{:S(2)}, u32[]{:S(2)}) collective-permute-start(bf16[528,512]{1,0:T(8,128)(2,1)S(1)} %get-tuple-element.53), channel_id=1, source_target_pairs={{0,1},{3,2},{4,5},{7,6},{8,9},{11,10},{12,13},{15,14},{16,17},{19,... | collective-permute-start | bytes 1622024 | tf_op jit(solution)/shard_map/ppermute | solution.py:31
  14.8 2.1 collective-permute-start.4
  18.1 13.9 %collective-permute-done.1.refs_1_ = bf16[2,512,512]{2,1,0:T(8,128)(2,1)} collective-permute-done((bf16[2,512,512]{2,1,0:T(8,128)(2,1)}, bf16[2,512,512]{2,1,0:T(8,128)(2,1)}, u32[]{:S(2)}, u32[]{:S(2)}) %collective-permute-start.1) | collective-permute-done | bytes 1048608 | tf_op jit(solution)/shard_map/ppermute | solution.py:31
  32.8 3.1 %shard_map.62.refs_0_ = bf16[512,2048]{1,0:T(8,128)(2,1)S(1)} custom-call(s32[4,512]{1,0:T(4,128)S(1)} %get-tuple-element.56.q_ref, bf16[2,512,512]{2,1,0:T(8,128)(2,1)} %slice.44.refs_0_), custom_call_target="tpu_custom_call" | custom-call | flops 1073741824 | bytes 2097152 | tf_op jit(solution)/shard_map/pallas_call | solution.py:87
  36.0 3.1 %shard_map.59.refs_0_ = bf16[512,2048]{1,0:T(8,128)(2,1)S(1)} custom-call(s32[4,512]{1,0:T(4,128)S(1)} %get-tuple-element.57.q_ref, bf16[2,512,512]{2,1,0:T(8,128)(2,1)} %slice.44.refs_0_), custom_call_target="tpu_custom_call" | custom-call | flops 1073741824 | bytes 2097152 | tf_op jit(solution)/shard_map/pallas_call | solution.py:87
  39.1 4.4 %collective-permute-done.rest_5_ = bf16[528,512]{1,0:T(8,128)(2,1)} collective-permute-done((bf16[528,512]{1,0:T(8,128)(2,1)S(1)}, bf16[528,512]{1,0:T(8,128)(2,1)}, u32[]{:S(2)}, u32[]{:S(2)}) %collective-permute-start) | collective-permute-done | bytes 540704 | tf_op jit(solution)/shard_map/ppermute | solution.py:31
  45.8 1.7 collective-permute-start.7
  47.4 4.5 %shard_map.63.refs_0_ = bf16[512,2048]{1,0:T(8,128)(2,1)S(1)} custom-call(s32[4,512]{1,0:T(4,128)S(1)} %get-tuple-element.56.q_ref, bf16[512,2048]{1,0:T(8,128)(2,1)S(1)} %shard_map.62.refs_0_, bf16[2,512,512]{2,1,0:T(8,128)(2,1)} %collective-permute-done.1.refs_1_, bf16[2,512,512]{2,1,0:T(8,128)(2,1)} %collective-permute-done.2.refs_2_), custom_call_target="tpu_custom_call" | custom-call | flops 2147483648 | bytes 2097152 | tf_op jit(solution)/shard_map/pallas_call | solution.py:87
  52.0 4.5 %shard_map.60.refs_0_ = bf16[512,2048]{1,0:T(8,128)(2,1)S(1)} custom-call(s32[4,512]{1,0:T(4,128)S(1)} %get-tuple-element.57.q_ref, bf16[512,2048]{1,0:T(8,128)(2,1)S(1)} %shard_map.59.refs_0_, bf16[2,512,512]{2,1,0:T(8,128)(2,1)} %collective-permute-done.1.refs_1_, bf16[2,512,512]{2,1,0:T(8,128)(2,1)} %collective-permute-done.2.refs_2_), custom_call_target="tpu_custom_call" | custom-call | flops 2147483648 | bytes 2097152 | tf_op jit(solution)/shard_map/pallas_call | solution.py:87
  59.4 1.9 shard_map.64.left_ref
  66.8 1.6 copy-done.11
  68.4 1.9 shard_map.61.left_ref
  71.1 5.3 %shard_map.65 = (bf16[528,1024]{1,0:T(8,128)(2,1)S(1)}, f32[16,512]{1,0:T(8,128)}) custom-call(bf16[512,2048]{1,0:T(8,128)(2,1)S(1)} %copy-done.1, bf16[16,512]{1,0:T(8,128)(2,1)S(1)} %iota.7.rest_0_, bf16[2,528,512]{2,1,0:T(8,128)(2,1)S(1)} %pad_maximum_fusion.rest_1_.rest_0_.rest_5_, ...), custom_call_target="tpu_custom_call" | custom-call | flops 2147483648 | bytes 6291456 | tf_op jit(solution)/shard_map/pallas_call | solution.py:160
  76.3 2.5 %shard_map.66.refs_0_ = bf16[512,512]{1,0:T(8,128)(2,1)S(1)} custom-call(bf16[512,2048]{1,0:T(8,128)(2,1)S(1)} %shard_map.61.left_ref, bf16[2,528,512]{2,1,0:T(8,128)(2,1)S(1)} %pad_maximum_fusion.rest_1_.rest_0_.rest_5_, bf16[2,528,512]{2,1,0:T(8,128)(2,1)S(1)} %collective-permute-done.5.rest_2_.rest_1_.rest_6_, ...), custom_call_target="tpu_custom_call" | custom-call | flops 1073741824 | bytes 3145728 | tf_op jit(solution)/shard_map/pallas_call | solution.py:160
  81.0 3.3 %shard_map.67 = (bf16[528,512]{1,0:T(8,128)(2,1)S(1)}, f32[16,512]{1,0:T(8,128)S(1)}) custom-call(bf16[512,2048]{1,0:T(8,128)(2,1)S(1)} %shard_map.61.left_ref, bf16[16,512]{1,0:T(8,128)(2,1)S(1)} %iota.7.rest_0_, bf16[528,512]{1,0:T(8,128)(2,1)} %collective-permute-done.4.rest_1_, bf16[528,512]{1,0:T(8,128)(2,1)S(1)} %collective-permute-done.11.rest_2_, ...), custom_call_target="tpu_custom_call" | custom-call | flops 1073741824 | bytes 3145728 | tf_op jit(solution)/shard_map/pallas_call | solution.py:160
  85.7 3.0 %shard_map.68.refs_0_ = bf16[512,2048]{1,0:T(8,128)(2,1)S(1)} custom-call(s32[4,512]{1,0:T(4,128)S(1)} %get-tuple-element.58.q_ref, bf16[512,512]{1,0:T(8,128)(2,1)S(1)} %shard_map.66.refs_0_, bf16[528,512]{1,0:T(8,128)(2,1)S(1)} %get-tuple-element.33.refs_1_), custom_call_target="tpu_custom_call" | custom-call | flops 2147483648 | bytes 2097152 | tf_op jit(solution)/shard_map/pallas_call | solution.py:87
  88.7 1.9 shard_map.69.refs_0_
  91.4 1.9 shard_map.70.left_ref
  93.4 2.8 %shard_map.71 = (bf16[528,1024]{1,0:T(8,128)(2,1)S(1)}, bf16[512,512]{1,0:T(8,128)(2,1)S(1)}, bf16[528,512]{1,0:T(8,128)(2,1)S(1)}, f32[16,512]{1,0:T(8,128)S(1)}) custom-call(bf16[512,2048]{1,0:T(8,128)(2,1)S(1)} %shard_map.70.left_ref, f32[16,512]{1,0:T(8,128)S(1)} %get-tuple-element.34.rest_0_, bf16[528,1024]{1,0:T(8,128)(2,1)S(1)} %get-tuple-element.30.rest_1_, ...), custom_call_target="tpu_custom_call" | custom-call | flops 2147483648 | bytes 6291456 | tf_op jit(solution)/shard_map/pallas_call | solution.py:160
  99.1 12.3 %collective-permute-done.24.rest_5_ = bf16[528,512]{1,0:T(8,128)(2,1)S(1)} collective-permute-done((bf16[528,512]{1,0:T(8,128)(2,1)S(1)}, bf16[528,512]{1,0:T(8,128)(2,1)S(1)}, u32[]{:S(2)}, u32[]{:S(2)}) %collective-permute-start.24) | collective-permute-done | bytes 540704 | tf_op jit(solution)/shard_map/ppermute | solution.py:17
  112.1 7.4 %collective-permute-done.20.rest_1_ = bf16[512,512]{1,0:T(8,128)(2,1)S(1)} collective-permute-done((bf16[512,512]{1,0:T(8,128)(2,1)S(1)}, bf16[512,512]{1,0:T(8,128)(2,1)S(1)}, u32[]{:S(2)}, u32[]{:S(2)}) %collective-permute-start.20) | collective-permute-done | bytes 524320 | tf_op jit(solution)/shard_map/ppermute | solution.py:17
  120.1 3.0 %shard_map.72.refs_0_ = bf16[512,2048]{1,0:T(8,128)(2,1)S(1)} custom-call(s32[4,512]{1,0:T(4,128)S(1)} %get-tuple-element.59.q_ref, bf16[528,1024]{1,0:T(8,128)(2,1)S(1)} %get-tuple-element.36.refs_0_), custom_call_target="tpu_custom_call" | custom-call | flops 2147483648 | bytes 2097152 | tf_op jit(solution)/shard_map/pallas_call | solution.py:87
  126.0 3.0 %shard_map.73.left_ref = bf16[512,2048]{1,0:T(8,128)(2,1)S(1)} custom-call(s32[4,512]{1,0:T(4,128)S(1)} %get-tuple-element.59.q_ref, bf16[512,2048]{1,0:T(8,128)(2,1)S(1)} %shard_map.72.refs_0_, bf16[528,1024]{1,0:T(8,128)(2,1)S(1)} %collective-permute-done.19.refs_1_), custom_call_target="tpu_custom_call" | custom-call | flops 2147483648 | bytes 2097152 | tf_op jit(solution)/shard_map/pallas_call | solution.py:87
  129.0 2.8 %shard_map.74 = (bf16[528,1024]{1,0:T(8,128)(2,1)S(1)}, f32[16,512]{1,0:T(8,128)S(1)}) custom-call(bf16[512,2048]{1,0:T(8,128)(2,1)S(1)} %shard_map.73.left_ref, f32[16,512]{1,0:T(8,128)S(1)} %get-tuple-element.37.rest_0_, bf16[512,512]{1,0:T(8,128)(2,1)S(1)} %collective-permute-done.20.rest_1_, bf16[512,512]{1,0:T(8,128)(2,1)S(1)} %collective-permute-done.21.rest_2_, ...), custom_call_target="tpu_custom_call" | custom-call | flops 2147483648 | bytes 6291456 | tf_op jit(solution)/shard_map/pallas_call | solution.py:160
  134.0 3.0 %shard_map.75.refs_0_ = bf16[512,2048]{1,0:T(8,128)(2,1)S(1)} custom-call(s32[4,512]{1,0:T(4,128)S(1)} %get-tuple-element.60.q_ref, bf16[528,1024]{1,0:T(8,128)(2,1)S(1)} %get-tuple-element.42.refs_0_.rest_1_.rest_0_), custom_call_target="tpu_custom_call" | custom-call | flops 2147483648 | bytes 2097152 | tf_op jit(solution)/shard_map/pallas_call | solution.py:87
  137.8 3.0 %shard_map.76.left_ref = bf16[512,2048]{1,0:T(8,128)(2,1)S(1)} custom-call(s32[4,512]{1,0:T(4,128)S(1)} %get-tuple-element.60.q_ref, bf16[512,2048]{1,0:T(8,128)(2,1)S(1)} %shard_map.75.refs_0_, bf16[528,1024]{1,0:T(8,128)(2,1)S(1)} %collective-permute-done.28.refs_1_), custom_call_target="tpu_custom_call" | custom-call | flops 2147483648 | bytes 2097152 | tf_op jit(solution)/shard_map/pallas_call | solution.py:87
  140.9 2.5 %shard_map.77 = (bf16[528,512]{1,0:T(8,128)(2,1)}, f32[16,512]{1,0:T(8,128)S(1)}) custom-call(bf16[512,2048]{1,0:T(8,128)(2,1)S(1)} %shard_map.76.left_ref, f32[16,512]{1,0:T(8,128)S(1)} %get-tuple-element.43.rest_0_, bf16[528,1024]{1,0:T(8,128)(2,1)S(1)} %get-tuple-element.42.refs_0_.rest_1_.rest_0_, ...), custom_call_target="tpu_custom_call" | custom-call | flops 1073741824 | bytes 3145728 | tf_op jit(solution)/shard_map/pallas_call | solution.py:160
  151.7 76.1 %collective-permute-done.34 = f32[1,512]{1,0:T(1,128)S(1)} collective-permute-done((f32[1,512]{1,0:T(1,128)S(1)}, f32[1,512]{1,0:T(1,128)S(1)}, u32[]{:S(2)}, u32[]{:S(2)}) %collective-permute-start.34) | collective-permute-done | bytes 2080 | tf_op jit(solution)/shard_map/ppermute | solution.py:35
  228.3 1.9 fusion
  (113 shorter events, 37.4 us)
Async XLA Ops:
  3.1 28.9 %collective-permute-start.1 = (bf16[2,512,512]{2,1,0:T(8,128)(2,1)}, bf16[2,512,512]{2,1,0:T(8,128)(2,1)}, u32[]{:S(2)}, u32[]{:S(2)}) collective-permute-start(bf16[2,512,512]{2,1,0:T(8,128)(2,1)} %slice.44.refs_0_), channel_id=1, source_target_pairs={{0,1},{3,2},{4,5},{7,6},{8,9},{11,10},{12,13},{15,14},{16,17},{19,... | collective-permute-start | bytes 3145736 | tf_op jit(solution)/shard_map/ppermute | solution.py:31
  9.1 35.1 %collective-permute-start.2 = (bf16[2,512,512]{2,1,0:T(8,128)(2,1)}, bf16[2,512,512]{2,1,0:T(8,128)(2,1)}, u32[]{:S(2)}, u32[]{:S(2)}) collective-permute-start(bf16[2,512,512]{2,1,0:T(8,128)(2,1)} %slice.44.refs_0_), channel_id=1, source_target_pairs={{1,2},{2,1},{5,6},{6,5},{9,10},{10,9},{13,14},{14,13},{17,18},{18,... | collective-permute-start | bytes 3145736 | tf_op jit(solution)/shard_map/ppermute | solution.py:27
  11.8 31.7 %collective-permute-start = (bf16[528,512]{1,0:T(8,128)(2,1)S(1)}, bf16[528,512]{1,0:T(8,128)(2,1)}, u32[]{:S(2)}, u32[]{:S(2)}) collective-permute-start(bf16[528,512]{1,0:T(8,128)(2,1)S(1)} %get-tuple-element.53), channel_id=1, source_target_pairs={{0,1},{3,2},{4,5},{7,6},{8,9},{11,10},{12,13},{15,14},{16,17},{19,... | collective-permute-start | bytes 1622024 | tf_op jit(solution)/shard_map/ppermute | solution.py:31
  14.8 43.0 %collective-permute-start.4 = (bf16[528,512]{1,0:T(8,128)(2,1)}, bf16[528,512]{1,0:T(8,128)(2,1)}, u32[]{:S(2)}, u32[]{:S(2)}) collective-permute-start(bf16[528,512]{1,0:T(8,128)(2,1)} %get-tuple-element.65), channel_id=1, source_target_pairs={{0,1},{3,2},{4,5},{7,6},{8,9},{11,10},{12,13},{15,14},{16,17},{19,... | collective-permute-start | bytes 1622024 | tf_op jit(solution)/shard_map/ppermute | solution.py:31
  17.0 28.8 %collective-permute-start.6 = (bf16[2,528,512]{2,1,0:T(8,128)(2,1)S(1)}, bf16[2,528,512]{2,1,0:T(8,128)(2,1)S(1)}, u32[]{:S(2)}, u32[]{:S(2)}) collective-permute-start(bf16[2,528,512]{2,1,0:T(8,128)(2,1)S(1)} %pad_maximum_fusion.rest_1_.rest_0_.rest_5_), channel_id=1, source_target_pairs={{1,9},{2,10},{5,13},{6,14},{9,1},{10,2},{13,5},{14,6},{17,25},{18,... | collective-permute-start | bytes 3244040 | tf_op jit(solution)/shard_map/ppermute | solution.py:23
  32.0 27.3 %collective-permute-start.3 = (bf16[2,512,512]{2,1,0:T(8,128)(2,1)}, bf16[2,512,512]{2,1,0:T(8,128)(2,1)S(1)}, u32[]{:S(2)}, u32[]{:S(2)}) collective-permute-start(bf16[2,512,512]{2,1,0:T(8,128)(2,1)} %collective-permute-done.1.refs_1_), channel_id=1, source_target_pairs={{1,2},{2,1},{5,6},{6,5},{9,10},{10,9},{13,14},{14,13},{17,18},{18,... | collective-permute-start | bytes 3145736 | tf_op jit(solution)/shard_map/ppermute | solution.py:27
  43.5 26.8 %collective-permute-start.5 = (bf16[2,528,512]{2,1,0:T(8,128)(2,1)S(1)}, bf16[2,528,512]{2,1,0:T(8,128)(2,1)S(1)}, u32[]{:S(2)}, u32[]{:S(2)}) collective-permute-start(bf16[2,528,512]{2,1,0:T(8,128)(2,1)S(1)} %pad_maximum_fusion.rest_1_.rest_0_.rest_5_), channel_id=1, source_target_pairs={{1,5},{2,6},{5,1},{6,2},{9,13},{10,14},{13,9},{14,10},{17,21},{18,... | collective-permute-start | bytes 3244040 | tf_op jit(solution)/shard_map/ppermute | solution.py:23
  44.2 18.4 %collective-permute-start.9 = (bf16[528,512]{1,0:T(8,128)(2,1)}, bf16[528,512]{1,0:T(8,128)(2,1)}, u32[]{:S(2)}, u32[]{:S(2)}) collective-permute-start(bf16[528,512]{1,0:T(8,128)(2,1)} %collective-permute-done.rest_5_), channel_id=1, source_target_pairs={{1,9},{2,10},{5,13},{6,14},{9,1},{10,2},{13,5},{14,6},{17,25},{18,... | collective-permute-start | bytes 1622024 | tf_op jit(solution)/shard_map/ppermute | solution.py:23
  45.8 25.3 %collective-permute-start.7 = (bf16[2,528,512]{2,1,0:T(8,128)(2,1)S(1)}, bf16[2,528,512]{2,1,0:T(8,128)(2,1)}, u32[]{:S(2)}, u32[]{:S(2)}) collective-permute-start(bf16[2,528,512]{2,1,0:T(8,128)(2,1)S(1)} %collective-permute-done.6.rest_3_.rest_2_.rest_7_), channel_id=1, source_target_pairs={{1,5},{2,6},{5,1},{6,2},{9,13},{10,14},{13,9},{14,10},{17,21},{18,... | collective-permute-start | bytes 3244040 | tf_op jit(solution)/shard_map/ppermute | solution.py:23
  57.8 13.2 %collective-permute-start.8 = (bf16[528,512]{1,0:T(8,128)(2,1)}, bf16[528,512]{1,0:T(8,128)(2,1)}, u32[]{:S(2)}, u32[]{:S(2)}) collective-permute-start(bf16[528,512]{1,0:T(8,128)(2,1)} %collective-permute-done.rest_5_), channel_id=1, source_target_pairs={{1,5},{2,6},{5,1},{6,2},{9,13},{10,14},{13,9},{14,10},{17,21},{18,... | collective-permute-start | bytes 1622024 | tf_op jit(solution)/shard_map/ppermute | solution.py:23
  62.6 8.4 %collective-permute-start.10 = (bf16[528,512]{1,0:T(8,128)(2,1)}, bf16[528,512]{1,0:T(8,128)(2,1)}, u32[]{:S(2)}, u32[]{:S(2)}) collective-permute-start(bf16[528,512]{1,0:T(8,128)(2,1)} %collective-permute-done.9.rest_7_), channel_id=1, source_target_pairs={{1,5},{2,6},{5,1},{6,2},{9,13},{10,14},{13,9},{14,10},{17,21},{18,... | collective-permute-start | bytes 1622024 | tf_op jit(solution)/shard_map/ppermute | solution.py:23
  64.1 14.8 %collective-permute-start.12 = (bf16[528,512]{1,0:T(8,128)(2,1)}, bf16[528,512]{1,0:T(8,128)(2,1)}, u32[]{:S(2)}, u32[]{:S(2)}) collective-permute-start(bf16[528,512]{1,0:T(8,128)(2,1)} %collective-permute-done.4.rest_1_), channel_id=1, source_target_pairs={{1,9},{2,10},{5,13},{6,14},{9,1},{10,2},{13,5},{14,6},{17,25},{18,... | collective-permute-start | bytes 1622024 | tf_op jit(solution)/shard_map/ppermute | solution.py:23
  70.3 10.7 %collective-permute-start.11 = (bf16[528,512]{1,0:T(8,128)(2,1)}, bf16[528,512]{1,0:T(8,128)(2,1)S(1)}, u32[]{:S(2)}, u32[]{:S(2)}) collective-permute-start(bf16[528,512]{1,0:T(8,128)(2,1)} %collective-permute-done.4.rest_1_), channel_id=1, source_target_pairs={{1,5},{2,6},{5,1},{6,2},{9,13},{10,14},{13,9},{14,10},{17,21},{18,... | collective-permute-start | bytes 1622024 | tf_op jit(solution)/shard_map/ppermute | solution.py:23
  79.5 11.1 %collective-permute-start.17 = (bf16[528,1024]{1,0:T(8,128)(2,1)S(1)}, bf16[528,1024]{1,0:T(8,128)(2,1)S(1)}, u32[]{:S(2)}, u32[]{:S(2)}) collective-permute-start(bf16[528,1024]{1,0:T(8,128)(2,1)S(1)} %get-tuple-element.30.rest_1_), channel_id=1, source_target_pairs={{1,9},{2,10},{5,13},{6,14},{9,1},{10,2},{13,5},{14,6},{17,25},{18,... | collective-permute-start | bytes 3244040 | tf_op jit(solution)/shard_map/ppermute | solution.py:23
  80.3 8.5 %collective-permute-start.14 = (bf16[512,512]{1,0:T(8,128)(2,1)S(1)}, bf16[512,512]{1,0:T(8,128)(2,1)S(1)}, u32[]{:S(2)}, u32[]{:S(2)}) collective-permute-start(bf16[512,512]{1,0:T(8,128)(2,1)S(1)} %shard_map.66.refs_0_), channel_id=1, source_target_pairs={{1,2},{2,1},{5,6},{6,5},{9,10},{10,9},{13,14},{14,13},{17,18},{18,... | collective-permute-start | bytes 1572872 | tf_op jit(solution)/shard_map/ppermute | solution.py:27
  84.3 6.4 %collective-permute-start.15 = (bf16[528,512]{1,0:T(8,128)(2,1)S(1)}, bf16[528,512]{1,0:T(8,128)(2,1)S(1)}, u32[]{:S(2)}, u32[]{:S(2)}) collective-permute-start(bf16[528,512]{1,0:T(8,128)(2,1)S(1)} %get-tuple-element.33.refs_1_), channel_id=1, source_target_pairs={{1,2},{2,1},{5,6},{6,5},{9,10},{10,9},{13,14},{14,13},{17,18},{18,... | collective-permute-start | bytes 1622024 | tf_op jit(solution)/shard_map/ppermute | solution.py:27
  85.0 8.3 %collective-permute-start.16 = (bf16[528,1024]{1,0:T(8,128)(2,1)S(1)}, bf16[528,1024]{1,0:T(8,128)(2,1)S(1)}, u32[]{:S(2)}, u32[]{:S(2)}) collective-permute-start(bf16[528,1024]{1,0:T(8,128)(2,1)S(1)} %get-tuple-element.30.rest_1_), channel_id=1, source_target_pairs={{1,5},{2,6},{5,1},{6,2},{9,13},{10,14},{13,9},{14,10},{17,21},{18,... | collective-permute-start | bytes 3244040 | tf_op jit(solution)/shard_map/ppermute | solution.py:23
  96.2 15.2 %collective-permute-start.24 = (bf16[528,512]{1,0:T(8,128)(2,1)S(1)}, bf16[528,512]{1,0:T(8,128)(2,1)S(1)}, u32[]{:S(2)}, u32[]{:S(2)}) collective-permute-start(bf16[528,512]{1,0:T(8,128)(2,1)S(1)} %get-tuple-element.40), channel_id=1, source_target_pairs={{0,16},{16,0},{1,17},{17,1},{2,18},{18,2},{3,19},{19,3},{4,20},{20... | collective-permute-start | bytes 1622024 | tf_op jit(solution)/shard_map/ppermute | solution.py:17
  97.7 21.7 %collective-permute-start.20 = (bf16[512,512]{1,0:T(8,128)(2,1)S(1)}, bf16[512,512]{1,0:T(8,128)(2,1)S(1)}, u32[]{:S(2)}, u32[]{:S(2)}) collective-permute-start(bf16[512,512]{1,0:T(8,128)(2,1)S(1)} %get-tuple-element.38), channel_id=1, source_target_pairs={{0,16},{16,0},{1,17},{17,1},{2,18},{18,2},{3,19},{19,3},{4,20},{20... | collective-permute-start | bytes 1572872 | tf_op jit(solution)/shard_map/ppermute | solution.py:17
  98.2 27.8 %collective-permute-start.19 = (bf16[528,1024]{1,0:T(8,128)(2,1)S(1)}, bf16[528,1024]{1,0:T(8,128)(2,1)S(1)}, u32[]{:S(2)}, u32[]{:S(2)}) collective-permute-start(bf16[528,1024]{1,0:T(8,128)(2,1)S(1)} %get-tuple-element.36.refs_0_), channel_id=1, source_target_pairs={{1,2},{2,1},{5,6},{6,5},{9,10},{10,9},{13,14},{14,13},{17,18},{18,... | collective-permute-start | bytes 3244040 | tf_op jit(solution)/shard_map/ppermute | solution.py:27
  111.4 12.4 %collective-permute-start.26 = (bf16[528,512]{1,0:T(8,128)(2,1)S(1)}, bf16[528,512]{1,0:T(8,128)(2,1)S(1)}, u32[]{:S(2)}, u32[]{:S(2)}) collective-permute-start(bf16[528,512]{1,0:T(8,128)(2,1)S(1)} %collective-permute-done.24.rest_5_), channel_id=1, source_target_pairs={{1,9},{2,10},{5,13},{6,14},{9,1},{10,2},{13,5},{14,6},{17,25},{18,... | collective-permute-start | bytes 1622024 | tf_op jit(solution)/shard_map/ppermute | solution.py:23
  119.4 5.8 %collective-permute-start.22 = (bf16[512,512]{1,0:T(8,128)(2,1)S(1)}, bf16[512,512]{1,0:T(8,128)(2,1)S(1)}, u32[]{:S(2)}, u32[]{:S(2)}) collective-permute-start(bf16[512,512]{1,0:T(8,128)(2,1)S(1)} %collective-permute-done.20.rest_1_), channel_id=1, source_target_pairs={{1,9},{2,10},{5,13},{6,14},{9,1},{10,2},{13,5},{14,6},{17,25},{18,... | collective-permute-start | bytes 1572872 | tf_op jit(solution)/shard_map/ppermute | solution.py:23
  123.1 5.9 %collective-permute-start.25 = (bf16[528,512]{1,0:T(8,128)(2,1)S(1)}, bf16[528,512]{1,0:T(8,128)(2,1)S(1)}, u32[]{:S(2)}, u32[]{:S(2)}) collective-permute-start(bf16[528,512]{1,0:T(8,128)(2,1)S(1)} %collective-permute-done.24.rest_5_), channel_id=1, source_target_pairs={{1,5},{2,6},{5,1},{6,2},{9,13},{10,14},{13,9},{14,10},{17,21},{18,... | collective-permute-start | bytes 1622024 | tf_op jit(solution)/shard_map/ppermute | solution.py:23
  123.8 5.2 %collective-permute-start.27 = (bf16[528,512]{1,0:T(8,128)(2,1)S(1)}, bf16[528,512]{1,0:T(8,128)(2,1)S(1)}, u32[]{:S(2)}, u32[]{:S(2)}) collective-permute-start(bf16[528,512]{1,0:T(8,128)(2,1)S(1)} %collective-permute-done.26.rest_7_), channel_id=1, source_target_pairs={{1,5},{2,6},{5,1},{6,2},{9,13},{10,14},{13,9},{14,10},{17,21},{18,... | collective-permute-start | bytes 1622024 | tf_op jit(solution)/shard_map/ppermute | solution.py:23
  124.5 4.4 %collective-permute-start.21 = (bf16[512,512]{1,0:T(8,128)(2,1)S(1)}, bf16[512,512]{1,0:T(8,128)(2,1)S(1)}, u32[]{:S(2)}, u32[]{:S(2)}) collective-permute-start(bf16[512,512]{1,0:T(8,128)(2,1)S(1)} %collective-permute-done.20.rest_1_), channel_id=1, source_target_pairs={{1,5},{2,6},{5,1},{6,2},{9,13},{10,14},{13,9},{14,10},{17,21},{18,... | collective-permute-start | bytes 1572872 | tf_op jit(solution)/shard_map/ppermute | solution.py:23
  125.3 3.7 %collective-permute-start.23 = (bf16[512,512]{1,0:T(8,128)(2,1)S(1)}, bf16[512,512]{1,0:T(8,128)(2,1)S(1)}, u32[]{:S(2)}, u32[]{:S(2)}) collective-permute-start(bf16[512,512]{1,0:T(8,128)(2,1)S(1)} %collective-permute-done.22.rest_3_), channel_id=1, source_target_pairs={{1,5},{2,6},{5,1},{6,2},{9,13},{10,14},{13,9},{14,10},{17,21},{18,... | collective-permute-start | bytes 1572872 | tf_op jit(solution)/shard_map/ppermute | solution.py:23
  131.8 5.2 %collective-permute-start.30 = (bf16[528,1024]{1,0:T(8,128)(2,1)S(1)}, bf16[528,1024]{1,0:T(8,128)(2,1)S(1)}, u32[]{:S(2)}, u32[]{:S(2)}) collective-permute-start(bf16[528,1024]{1,0:T(8,128)(2,1)S(1)} %get-tuple-element.42.refs_0_.rest_1_.rest_0_), channel_id=1, source_target_pairs={{1,9},{2,10},{5,13},{6,14},{9,1},{10,2},{13,5},{14,6},{17,25},{18,... | collective-permute-start | bytes 3244040 | tf_op jit(solution)/shard_map/ppermute | solution.py:23
  132.6 5.2 %collective-permute-start.28 = (bf16[528,1024]{1,0:T(8,128)(2,1)S(1)}, bf16[528,1024]{1,0:T(8,128)(2,1)S(1)}, u32[]{:S(2)}, u32[]{:S(2)}) collective-permute-start(bf16[528,1024]{1,0:T(8,128)(2,1)S(1)} %get-tuple-element.42.refs_0_.rest_1_.rest_0_), channel_id=1, source_target_pairs={{1,2},{2,1},{5,6},{6,5},{9,10},{10,9},{13,14},{14,13},{17,18},{18,... | collective-permute-start | bytes 3244040 | tf_op jit(solution)/shard_map/ppermute | solution.py:27
  133.3 7.5 %collective-permute-start.29 = (bf16[528,1024]{1,0:T(8,128)(2,1)S(1)}, bf16[528,1024]{1,0:T(8,128)(2,1)S(1)}, u32[]{:S(2)}, u32[]{:S(2)}) collective-permute-start(bf16[528,1024]{1,0:T(8,128)(2,1)S(1)} %get-tuple-element.42.refs_0_.rest_1_.rest_0_), channel_id=1, source_target_pairs={{1,5},{2,6},{5,1},{6,2},{9,13},{10,14},{13,9},{14,10},{17,21},{18,... | collective-permute-start | bytes 3244040 | tf_op jit(solution)/shard_map/ppermute | solution.py:23
  137.1 3.8 %collective-permute-start.31 = (bf16[528,1024]{1,0:T(8,128)(2,1)S(1)}, bf16[528,1024]{1,0:T(8,128)(2,1)S(1)}, u32[]{:S(2)}, u32[]{:S(2)}) collective-permute-start(bf16[528,1024]{1,0:T(8,128)(2,1)S(1)} %collective-permute-done.30.rest_3_.rest_2_), channel_id=1, source_target_pairs={{1,5},{2,6},{5,1},{6,2},{9,13},{10,14},{13,9},{14,10},{17,21},{18,... | collective-permute-start | bytes 3244040 | tf_op jit(solution)/shard_map/ppermute | solution.py:23
  143.4 84.9 %collective-permute-start.32 = (bf16[528,512]{1,0:T(8,128)(2,1)}, bf16[528,512]{1,0:T(8,128)(2,1)}, u32[]{:S(2)}, u32[]{:S(2)}) collective-permute-start(bf16[528,512]{1,0:T(8,128)(2,1)} %get-tuple-element.45), channel_id=1, source_target_pairs={{1,0},{2,3},{5,4},{6,7},{9,8},{10,11},{13,12},{14,15},{17,16},{18,... | collective-permute-start | bytes 1622024 | tf_op jit(solution)/shard_map/ppermute | solution.py:35
  145.4 82.4 %collective-permute-start.34 = (f32[1,512]{1,0:T(1,128)S(1)}, f32[1,512]{1,0:T(1,128)S(1)}, u32[]{:S(2)}, u32[]{:S(2)}) collective-permute-start(f32[1,512]{1,0:T(1,128)S(1)} %slice_add_fusion), channel_id=1, source_target_pairs={{1,0},{2,3},{5,4},{6,7},{9,8},{10,11},{13,12},{14,15},{17,16},{18,... | collective-permute-start | bytes 6152 | tf_op jit(solution)/shard_map/ppermute | solution.py:35
  (19 other events, 47.9 us)

commit v8 on v6

--- a/solution.py
+++ b/solution.py
@@ -37,20 +37,45 @@
 
 class Operands:
     def __init__(self):
-        self.arrays = []
+        self.keys, self.arrays, self.specs = [], [], []
 
     def add(self, view):
-        array, lead, column = view
-        for i, known in enumerate(self.arrays):
-            if known is array:
-                return i, lead, column
+        array, which, column = view
+        part = which if isinstance(which, int) else None
+        for i, (known, known_part) in enumerate(self.keys):
+            if known is array and known_part == part:
+                return i, which, column
+        self.keys.append((array, part))
         self.arrays.append(array)
-        return len(self.arrays) - 1, lead, column
-
-
-def read(refs, view, size, rows=None):
-    which, lead, column = view
-    ref = refs[which] if lead is None else refs[which].at[lead]
+        if part is None:
+            self.specs.append(pl.BlockSpec(memory_space=pltpu.VMEM))
+        else:
+            self.specs.append(pl.BlockSpec(memory_space=pl.ANY))
+        return len(self.keys) - 1, which, column
+
+    def scratch(self):
+        parts = [array for array, part in self.keys if part is not None]
+        return [pltpu.VMEM(array.shape[1:], array.dtype) for array in parts] + [
+            pltpu.SemaphoreType.DMA((max(len(parts), 1),))
+        ]
+
+    def load(self, refs, scratch):
+        found, copies = [], []
+        for ref, (_, part) in zip(refs, self.keys):
+            if part is not None:
+                i = len(copies)
+                copies.append(pltpu.make_async_copy(ref.at[part], scratch[i], scratch[-1].at[i]))
+                copies[-1].start()
+                ref = scratch[i]
+            found.append(ref)
+        for copy in copies:
+            copy.wait()
+        return found
+
+
+def read(refs, view, size, rows=None, row=None):
+    i, which, column = view
+    ref = refs[i].at[row ^ which[0]] if isinstance(which, tuple) else refs[i]
     return ref[rows or slice(0, size), column : column + size]
 
 
@@ -71,18 +96,23 @@
     views = [(block, operands.add(view)) for block, view in tiles]
     extra = [] if onto is None else [onto]
 
-    def kernel(q_ref, *refs):
-        out = refs[-1]
+    def kernel(q_ref, *rest):
+        onto_ref, rest = rest[0], rest[len(extra) :]
+        refs, (out, *scratch) = rest[: len(operands.keys)], rest[len(operands.keys) :]
+        refs = operands.load(refs, scratch)
 
         @pl.loop(0, count)
         def _(n):
             here = pl.ds(pl.multiple_of(n * size, size), size)
-            moved = spread(refs[len(extra) :], views, q_ref, size, n).astype(out.dtype)
-            out[:, here] = moved if onto is None else moved + refs[0][:, here]
+            moved = spread(refs, views, q_ref, size, n).astype(out.dtype)
+            out[:, here] = moved if onto is None else moved + onto_ref[:, here]
 
     return pl.pallas_call(
         kernel,
         out_shape=jax.ShapeDtypeStruct((size, size * count), jnp.bfloat16),
+        in_specs=[pl.BlockSpec(memory_space=pltpu.VMEM)] * (1 + len(extra)) + operands.specs,
+        out_specs=pl.BlockSpec(memory_space=pltpu.VMEM),
+        scratch_shapes=operands.scratch(),
         compiler_params=pltpu.CompilerParams(vmem_limit_bytes=VMEM),
         cost_estimate=pl.CostEstimate(
             flops=2 * len(tiles) * size * size * size * count,
@@ -92,12 +122,13 @@
     )(pivots, *extra, *operands.arrays)
 
 
-def product(left, halves, form, size, added=None, own=None, turn=0):
+def product(left, halves, form, size, added=None, own=None, turn=0, row=None):
     count = left.shape[1] // size
     operands = Operands()
     views = [[operands.add(view) for view in half] for half in halves]
     own_views = [operands.add(view) for view in own or []]
     extra = [] if added is None else [added]
+    scalar = [] if row is None else [row.reshape(1)]
     tall, wide = size + (EXTRA if extra else 0), size * len(halves)
     shapes = [] if form == "apart" else [(tall, wide)]
     if form != "joint":
@@ -107,6 +138,9 @@
         outs.append(jax.ShapeDtypeStruct((EXTRA, size), jnp.float32))
 
     def kernel(left_ref, *rest):
+        here = None
+        if scalar:
+            here, rest = rest[0][0], rest[1:]
         refs = rest[len(extra) : len(extra) + len(operands.arrays)]
         results = rest[len(extra) + len(refs) :]
         joint = None if form == "apart" else results[0]
@@ -117,7 +151,7 @@
             for b in range(count):
                 part = jnp.dot(
                     left_ref[:, b * size : (b + 1) * size],
-                    read(refs, half[b], size),
+                    read(refs, half[b], size, row=here),
                     preferred_element_type=jnp.float32,
                 )
                 total = part if total is None else total + part
@@ -130,9 +164,10 @@
             return
 
         def pieces(b, k):
-            here = slice(k * (size // 4), (k + 1) * (size // 4))
+            lanes = slice(k * (size // 4), (k + 1) * (size // 4))
             near, end = (
-                read(refs, kind[b], size, slice(size, tall))[:, here] for kind in (own_views, views[-1])
+                read(refs, kind[b], size, slice(size, tall), here)[:, lanes]
+                for kind in (own_views, views[-1])
             )
             return jnp.concatenate([end, near, near, end], axis=1) * rest[0][...]
 
@@ -153,16 +188,20 @@
         if single:
             single[-1][size:tall, :] = applied
 
+    whole = pl.BlockSpec(memory_space=pltpu.VMEM)
+    specs = [pl.BlockSpec(memory_space=pltpu.SMEM)] * len(scalar) + [whole] * len(extra)
     return pl.pallas_call(
         kernel,
         out_shape=tuple(outs),
+        in_specs=[whole] + specs + operands.specs,
+        out_specs=(whole,) * len(outs),
         compiler_params=pltpu.CompilerParams(vmem_limit_bytes=VMEM),
         cost_estimate=pl.CostEstimate(
             flops=2 * len(halves) * size * size * size * count,
             bytes_accessed=12 * len(halves) * size * size,
             transcendentals=0,
         ),
-    )(left, *extra, *operands.arrays)
+    )(left, *scalar, *extra, *operands.arrays)
 
 
 def after(value, *others):
@@ -184,13 +223,11 @@
     lefts = blocks[1::2]
     riding = jnp.broadcast_to(interval_residuals[0].reshape(1, -1), (EXTRA, size))
     tiles = [jnp.concatenate([blocks[k], riding], axis=0) for k in (0, 2)]
-    rights = jnp.stack(tiles)
     ends_left = inward(lefts)
     lefts_other = swap_middle(lefts)
-    rights_across = swap_rows(rights, 2)
+    rights = [lax.all_gather(tile, "row", axis=0) for tile in tiles]
     end_lower = inward(tiles[0])
     end_upper = inward(tiles[1])
-    rights_beside = swap_rows(rights, 1)
 
     own = lax.dynamic_index_in_dim(boundary_pivots, position, 0, keepdims=True)
     back = lax.dynamic_index_in_dim(
@@ -210,7 +247,6 @@
 
     upper_panel, lower_panel = panel(2, [(0, (lefts, 1, 0))]), panel(0, [(0, (lefts, 0, 0))])
     ends_other = swap_middle(after(ends_left, upper_panel, lower_panel))
-    rights_last = swap_rows(rights_across, 1)
     lower_panel = panel(0, [(1, (ends_left, 0, 0)), (2, (lefts_other, 0, 0))], lower_panel)
     upper_panel = panel(2, [(1, (ends_left, 1, 0)), (2, (lefts_other, 1, 0))], upper_panel)
     end_lower = after(end_lower, lower_panel, upper_panel)
@@ -219,19 +255,19 @@
     upper_across = swap_rows(end_upper, 2)
     upper_ends = [end_upper, swap_rows(end_upper, 1), upper_across]
     lower_panel = panel(0, [(3, (ends_other, 0, 0))], lower_panel)
+
+    def own_tiles(k):
+        return [(rights[k], (b,), 0) for b in range(count)]
+
+    lower, _ = product(
+        lower_panel, [own_tiles(0), plain(*lower_ends)], "joint", size, held, own_tiles(0), 0, row
+    )
+    upper_panel = after(upper_panel, lower)
     upper_panel = panel(2, [(3, (ends_other, 1, 0))], upper_panel)
-
-    def own_tiles(k):
-        return [(tile, k, 0) for tile in (rights, rights_beside, rights_across, rights_last)]
-
-    lower, _ = product(
-        lower_panel, [own_tiles(0), plain(*lower_ends)], "joint", size, held, own_tiles(0), 0
-    )
-    upper_panel = after(upper_panel, lower)
-    (upper_o,) = product(upper_panel, [own_tiles(1)], "apart", size)
+    (upper_o,) = product(upper_panel, [own_tiles(1)], "apart", size, row=row)
     upper_ends.append(swap_rows(after(upper_across, upper_o), 1))
     upper_e, vector = product(
-        upper_panel, [plain(*upper_ends)], "apart", size, held, own_tiles(1), 2
+        upper_panel, [plain(*upper_ends)], "apart", size, held, own_tiles(1), 2, row
     )
 
     def right_views(right, tie):

time: 231 us -> 246 us (1.065)
  between operations: 1.39 us -> 14.8 us
  Pallas kernels: 60.8 us -> 53.6 us
  waiting for transfers between devices: 104 us -> 110 us
  local copies, waits for them, and re-layouts: 10.7 us -> 16.1 us
    ppermute x3, waiting for transfers between devices: 4.87 us -> 19.1 us  [inward(): return lax.ppermute(value, 'col', [(0, 1), (3, 2)])]
    ppermute x2, waiting for transfers between devices: 78.7 us -> 72 us  [outward(): return lax.ppermute(value, 'col', [(1, 0), (2, 3)])]
    unnamed x32 -> x42, local copies, waits for them, and re-layouts: 8 us -> 14.6 us
    pallas_call x13, Pallas kernels: 40.6 us -> 34.8 us  [spread_columns(): pl.pallas_call(kernel, out_shape=jax.ShapeDtypeStruct((size, size * count...]
    ppermute x2, waiting for transfers between devices: 20.8 us -> 18.1 us  [from_behind(): lax.ppermute(value, axis, [(i, (i + by) % devices) for i in range(devices)])]
    ppermute x21 -> x18, starting transfers between devices: 18.2 us -> 16.8 us  [swap_rows(): return lax.ppermute(value, ('row', 'col'), pairs)]
  transfers between devices with their start and end apart: 35 -> 34, of which waited for: 5 -> 5; matrix products, arithmetic and copies ran while one was open for 1% -> 0% of each run, Pallas kernels for 23% -> 19%
where the time goes in v8:
time: 246 us; the launch traced here: 244 us
  waiting for transfers between devices  110 us (45%)
  Pallas kernels  53.6 us (22%)
  starting transfers between devices  46.3 us (19%)
  local copies, waits for them, and re-layouts  16.1 us (7%)
  between operations  14.8 us (6%)
  other arithmetic  3.68 us (1%)
    ppermute x2, waiting for transfers between devices, outward(): return lax.ppermute(value, 'col', [(1, 0), (2, 3)])  72 us
    pallas_call x13, Pallas kernels, spread_columns(): pl.pallas_call(kernel, out_shape=jax.ShapeDtypeStruct((size, size * count...  34.8 us
    ppermute x3, starting transfers between devices, inward(): return lax.ppermute(value, 'col', [(0, 1), (3, 2)])  19.8 us
    ppermute x3, waiting for transfers between devices, inward(): return lax.ppermute(value, 'col', [(0, 1), (3, 2)])  19.1 us
    pallas_call x7, Pallas kernels, product(): pl.pallas_call(kernel, out_shape=tuple(outs), in_specs=[whole] + specs +...  18.8 us
    ppermute x2, waiting for transfers between devices, from_behind(): lax.ppermute(value, axis, [(i, (i + by) % devices) for i in range(devices)])  18.1 us
    ppermute x18, starting transfers between devices, swap_rows(): return lax.ppermute(value, ('row', 'col'), pairs)  16.8 us
    unnamed x42, local copies, waits for them, and re-layouts  14.6 us
  transfers between devices with their start and end apart: 34, of which 5 were waited for; matrix products, arithmetic and copies ran while one was open for 0% of the time, Pallas kernels for 19%

profile of v8, /device:TPU:0, one launch (start us, length us, event | category | flops | bytes accessed | tf_op | source)
XLA Modules:
  0.0 244.5 jit_solution(13326418593872945934)
XLA Ops:
  10.6 5.9 %collective-permute-start = (bf16[2,512,512]{2,1,0:T(8,128)(2,1)S(1)}, bf16[2,512,512]{2,1,0:T(8,128)(2,1)}, u32[]{:S(2)}, u32[]{:S(2)}) collective-permute-start(bf16[2,512,512]{2,1,0:T(8,128)(2,1)S(1)} %slice.44.rest_0_), channel_id=1, source_target_pairs={{0,1},{3,2},{4,5},{7,6},{8,9},{11,10},{12,13},{15,14},{16,17},{19,... | collective-permute-start | bytes 3145736 | tf_op jit(solution)/shard_map/ppermute | solution.py:31
  17.2 3.9 %collective-permute-start.3 = (bf16[528,512]{1,0:T(8,128)(2,1)}, bf16[528,512]{1,0:T(8,128)(2,1)}, u32[]{:S(2)}, u32[]{:S(2)}) collective-permute-start(bf16[528,512]{1,0:T(8,128)(2,1)} %get-tuple-element.56), channel_id=1, source_target_pairs={{0,1},{3,2},{4,5},{7,6},{8,9},{11,10},{12,13},{15,14},{16,17},{19,... | collective-permute-start | bytes 1622024 | tf_op jit(solution)/shard_map/ppermute | solution.py:31
  21.6 2.0 shard_map.59.rest_0_
  23.5 2.0 shard_map.61.rest_0_
  25.5 13.6 %collective-permute-done.rest_1_ = bf16[2,512,512]{2,1,0:T(8,128)(2,1)} collective-permute-done((bf16[2,512,512]{2,1,0:T(8,128)(2,1)S(1)}, bf16[2,512,512]{2,1,0:T(8,128)(2,1)}, u32[]{:S(2)}, u32[]{:S(2)}) %collective-permute-start) | collective-permute-done | bytes 1048608 | tf_op jit(solution)/shard_map/ppermute | solution.py:31
  39.8 4.1 %shard_map.60.rest_0_ = bf16[512,2048]{1,0:T(8,128)(2,1)S(1)} custom-call(s32[4,512]{1,0:T(4,128)S(1)} %get-tuple-element.47.q_ref, bf16[512,2048]{1,0:T(8,128)(2,1)S(1)} %shard_map.59.rest_0_, bf16[2,512,512]{2,1,0:T(8,128)(2,1)} %collective-permute-done.rest_1_, bf16[2,512,512]{2,1,0:T(8,128)(2,1)S(1)} %collective-permute-done.1.rest_2_), custom_call_target="tpu_custom_call" | custom-call | flops 2147483648 | bytes 2097152 | tf_op jit(solution)/shard_map/pallas_call | solution.py:110
  47.5 4.0 %shard_map.62.rest_0_ = bf16[512,2048]{1,0:T(8,128)(2,1)S(1)} custom-call(s32[4,512]{1,0:T(4,128)S(1)} %get-tuple-element.46.q_ref, bf16[512,2048]{1,0:T(8,128)(2,1)S(1)} %shard_map.61.rest_0_, bf16[2,512,512]{2,1,0:T(8,128)(2,1)} %collective-permute-done.rest_1_, bf16[2,512,512]{2,1,0:T(8,128)(2,1)S(1)} %copy-done.15), custom_call_target="tpu_custom_call" | custom-call | flops 2147483648 | bytes 2097152 | tf_op jit(solution)/shard_map/pallas_call | solution.py:110
  53.0 10.0 %collective-permute-start.7 = (bf16[528,512]{1,0:T(8,128)(2,1)}, bf16[528,512]{1,0:T(8,128)(2,1)}, u32[]{:S(2)}, u32[]{:S(2)}) collective-permute-start(bf16[528,512]{1,0:T(8,128)(2,1)} %get-tuple-element.55), channel_id=1, source_target_pairs={{0,1},{3,2},{4,5},{7,6},{8,9},{11,10},{12,13},{15,14},{16,17},{19,... | collective-permute-start | bytes 1622024 | tf_op jit(solution)/shard_map/ppermute | solution.py:31
  63.1 1.5 collective-permute-start.4
  66.0 5.5 %collective-permute-done.7.rest_2_ = bf16[528,512]{1,0:T(8,128)(2,1)} collective-permute-done((bf16[528,512]{1,0:T(8,128)(2,1)}, bf16[528,512]{1,0:T(8,128)(2,1)}, u32[]{:S(2)}, u32[]{:S(2)}) %collective-permute-start.7) | collective-permute-done | bytes 540704 | tf_op jit(solution)/shard_map/ppermute | solution.py:31
  74.5 2.0 shard_map.63.left_ref
  77.9 1.6 copy-done.10
  79.4 1.6 copy-done.11
  81.1 5.1 %shard_map.64 = (bf16[528,1024]{1,0:T(8,128)(2,1)S(1)}, f32[16,512]{1,0:T(8,128)}) custom-call(bf16[512,2048]{1,0:T(8,128)(2,1)S(1)} %copy-done.10, s32[1]{0:T(128)} %bitcast.6.rest_0_, bf16[16,512]{1,0:T(8,128)(2,1)S(1)} %iota.7.rest_1_, bf16[4,528,512]{2,1,0:T(8,128)(2,1)S(1)} %bitcast.23, bf16[528,512]{1,0:T(8,128)(2,1)} %collective-permute-done.3.rest_3_, ...), custom_call_target="tpu_custom_call" | custom-call | flops 2147483648 | bytes 6291456 | tf_op jit(solution)/shard_map/pallas_call | solution.py:193
  87.2 2.0 shard_map.65.left_ref
  89.2 1.6 copy-done
  94.2 3.1 %shard_map.67 = (bf16[528,512]{1,0:T(8,128)(2,1)S(1)}, f32[16,512]{1,0:T(8,128)S(1)}) custom-call(bf16[512,2048]{1,0:T(8,128)(2,1)S(1)} %shard_map.65.left_ref, s32[1]{0:T(128)} %bitcast.6.rest_0_, bf16[16,512]{1,0:T(8,128)(2,1)S(1)} %iota.7.rest_1_, bf16[528,512]{1,0:T(8,128)(2,1)} %collective-permute-done.7.rest_2_, ...), custom_call_target="tpu_custom_call" | custom-call | flops 1073741824 | bytes 3145728 | tf_op jit(solution)/shard_map/pallas_call | solution.py:193
  98.8 3.0 %shard_map.68.rest_0_ = bf16[512,2048]{1,0:T(8,128)(2,1)S(1)} custom-call(s32[4,512]{1,0:T(4,128)S(1)} %get-tuple-element.48.q_ref, bf16[512,512]{1,0:T(8,128)(2,1)S(1)} %shard_map.66.rest_0_, bf16[528,512]{1,0:T(8,128)(2,1)S(1)} %get-tuple-element.27.rest_1_), custom_call_target="tpu_custom_call" | custom-call | flops 2147483648 | bytes 2097152 | tf_op jit(solution)/shard_map/pallas_call | solution.py:110
  101.8 1.9 shard_map.69.rest_0_
  104.5 1.9 shard_map.70.left_ref
  106.4 2.8 %shard_map.71 = (bf16[528,1024]{1,0:T(8,128)(2,1)S(1)}, bf16[512,512]{1,0:T(8,128)(2,1)S(1)}, bf16[528,512]{1,0:T(8,128)(2,1)S(1)}, f32[16,512]{1,0:T(8,128)S(1)}) custom-call(bf16[512,2048]{1,0:T(8,128)(2,1)S(1)} %shard_map.70.left_ref, f32[16,512]{1,0:T(8,128)S(1)} %get-tuple-element.28.rest_0_, bf16[528,1024]{1,0:T(8,128)(2,1)S(1)} %copy-done.13, ...), custom_call_target="tpu_custom_call" | custom-call | flops 2147483648 | bytes 6291456 | tf_op jit(solution)/shard_map/pallas_call | solution.py:193
  109.2 1.5 collective-permute-start.21
  112.0 12.5 %collective-permute-done.21.rest_5_ = bf16[528,512]{1,0:T(8,128)(2,1)S(1)} collective-permute-done((bf16[528,512]{1,0:T(8,128)(2,1)S(1)}, bf16[528,512]{1,0:T(8,128)(2,1)S(1)}, u32[]{:S(2)}, u32[]{:S(2)}) %collective-permute-start.21) | collective-permute-done | bytes 540704 | tf_op jit(solution)/shard_map/ppermute | solution.py:17
  125.3 5.7 %collective-permute-done.17.rest_1_ = bf16[512,512]{1,0:T(8,128)(2,1)S(1)} collective-permute-done((bf16[512,512]{1,0:T(8,128)(2,1)S(1)}, bf16[512,512]{1,0:T(8,128)(2,1)S(1)}, u32[]{:S(2)}, u32[]{:S(2)}) %collective-permute-start.17) | collective-permute-done | bytes 524320 | tf_op jit(solution)/shard_map/ppermute | solution.py:17
  131.7 3.0 %shard_map.72.rest_0_ = bf16[512,2048]{1,0:T(8,128)(2,1)S(1)} custom-call(s32[4,512]{1,0:T(4,128)S(1)} %get-tuple-element.49.q_ref, bf16[528,1024]{1,0:T(8,128)(2,1)S(1)} %get-tuple-element.30.rest_0_), custom_call_target="tpu_custom_call" | custom-call | flops 2147483648 | bytes 2097152 | tf_op jit(solution)/shard_map/pallas_call | solution.py:110
  137.6 3.0 %shard_map.73.left_ref = bf16[512,2048]{1,0:T(8,128)(2,1)S(1)} custom-call(s32[4,512]{1,0:T(4,128)S(1)} %get-tuple-element.49.q_ref, bf16[512,2048]{1,0:T(8,128)(2,1)S(1)} %shard_map.72.rest_0_, bf16[528,1024]{1,0:T(8,128)(2,1)S(1)} %collective-permute-done.16.rest_1_), custom_call_target="tpu_custom_call" | custom-call | flops 2147483648 | bytes 2097152 | tf_op jit(solution)/shard_map/pallas_call | solution.py:110
  140.6 2.8 %shard_map.74 = (bf16[528,1024]{1,0:T(8,128)(2,1)S(1)}, f32[16,512]{1,0:T(8,128)S(1)}) custom-call(bf16[512,2048]{1,0:T(8,128)(2,1)S(1)} %shard_map.73.left_ref, f32[16,512]{1,0:T(8,128)S(1)} %get-tuple-element.31.rest_0_, bf16[512,512]{1,0:T(8,128)(2,1)S(1)} %collective-permute-done.17.rest_1_, bf16[512,512]{1,0:T(8,128)(2,1)S(1)} %collective-permute-done.18.rest_2_, ...), custom_call_target="tpu_custom_call" | custom-call | flops 2147483648 | bytes 6291456 | tf_op jit(solution)/shard_map/pallas_call | solution.py:193
  145.6 3.0 %shard_map.75.rest_0_ = bf16[512,2048]{1,0:T(8,128)(2,1)S(1)} custom-call(s32[4,512]{1,0:T(4,128)S(1)} %get-tuple-element.50.q_ref, bf16[528,1024]{1,0:T(8,128)(2,1)S(1)} %get-tuple-element.36.rest_0_.rest_1_), custom_call_target="tpu_custom_call" | custom-call | flops 2147483648 | bytes 2097152 | tf_op jit(solution)/shard_map/pallas_call | solution.py:110
  149.4 3.0 %shard_map.76.left_ref = bf16[512,2048]{1,0:T(8,128)(2,1)S(1)} custom-call(s32[4,512]{1,0:T(4,128)S(1)} %get-tuple-element.50.q_ref, bf16[512,2048]{1,0:T(8,128)(2,1)S(1)} %shard_map.75.rest_0_, bf16[528,1024]{1,0:T(8,128)(2,1)S(1)} %collective-permute-done.25.rest_1_), custom_call_target="tpu_custom_call" | custom-call | flops 2147483648 | bytes 2097152 | tf_op jit(solution)/shard_map/pallas_call | solution.py:110
  152.5 2.5 %shard_map.77 = (bf16[528,512]{1,0:T(8,128)(2,1)}, f32[16,512]{1,0:T(8,128)S(1)}) custom-call(bf16[512,2048]{1,0:T(8,128)(2,1)S(1)} %shard_map.76.left_ref, f32[16,512]{1,0:T(8,128)S(1)} %get-tuple-element.37.rest_0_, bf16[528,1024]{1,0:T(8,128)(2,1)S(1)} %get-tuple-element.36.rest_0_.rest_1_, bf16[528,1024]{1,0:T(8,128)(2,1)S(1)} %collective-permute-done.26.rest_2_.rest_1_, ...), custom_call_target="tpu_custom_call" | custom-call | flops 1073741824 | bytes 3145728 | tf_op jit(solution)/shard_map/pallas_call | solution.py:193
  163.3 72.0 %collective-permute-done.31 = f32[1,512]{1,0:T(1,128)S(1)} collective-permute-done((f32[1,512]{1,0:T(1,128)S(1)}, f32[1,512]{1,0:T(1,128)S(1)}, u32[]{:S(2)}, u32[]{:S(2)}) %collective-permute-start.31) | collective-permute-done | bytes 2080 | tf_op jit(solution)/shard_map/ppermute | solution.py:35
  235.8 1.9 fusion
  (120 shorter events, 39.9 us)
Async XLA Ops:
  7.2 70.7 %all-gather.5.cloned.1.call-start = ((), (), s32[]{:S(2)}) async-start(), calls=%async_computation | async-start | bytes 2703360 | tf_op jit(solution)/shard_map/all_gather | solution.py:228
  9.6 79.5 %all-gather.7.cloned.1.call-start = ((), (), s32[]{:S(2)}) async-start(), calls=%async_computation.1 | async-start | bytes 2703360 | tf_op jit(solution)/shard_map/all_gather | solution.py:228
  10.6 28.5 %collective-permute-start = (bf16[2,512,512]{2,1,0:T(8,128)(2,1)S(1)}, bf16[2,512,512]{2,1,0:T(8,128)(2,1)}, u32[]{:S(2)}, u32[]{:S(2)}) collective-permute-start(bf16[2,512,512]{2,1,0:T(8,128)(2,1)S(1)} %slice.44.rest_0_), channel_id=1, source_target_pairs={{0,1},{3,2},{4,5},{7,6},{8,9},{11,10},{12,13},{15,14},{16,17},{19,... | collective-permute-start | bytes 3145736 | tf_op jit(solution)/shard_map/ppermute | solution.py:31
  16.5 23.3 %collective-permute-start.1 = (bf16[2,512,512]{2,1,0:T(8,128)(2,1)S(1)}, bf16[2,512,512]{2,1,0:T(8,128)(2,1)S(1)}, u32[]{:S(2)}, u32[]{:S(2)}) collective-permute-start(bf16[2,512,512]{2,1,0:T(8,128)(2,1)S(1)} %slice.44.rest_0_), channel_id=1, source_target_pairs={{1,2},{2,1},{5,6},{6,5},{9,10},{10,9},{13,14},{14,13},{17,18},{18,... | collective-permute-start | bytes 3145736 | tf_op jit(solution)/shard_map/ppermute | solution.py:27
  17.2 34.3 %collective-permute-start.3 = (bf16[528,512]{1,0:T(8,128)(2,1)}, bf16[528,512]{1,0:T(8,128)(2,1)}, u32[]{:S(2)}, u32[]{:S(2)}) collective-permute-start(bf16[528,512]{1,0:T(8,128)(2,1)} %get-tuple-element.56), channel_id=1, source_target_pairs={{0,1},{3,2},{4,5},{7,6},{8,9},{11,10},{12,13},{15,14},{16,17},{19,... | collective-permute-start | bytes 1622024 | tf_op jit(solution)/shard_map/ppermute | solution.py:31
  39.0 35.4 %collective-permute-start.2 = (bf16[2,512,512]{2,1,0:T(8,128)(2,1)}, bf16[2,512,512]{2,1,0:T(8,128)(2,1)S(1)}, u32[]{:S(2)}, u32[]{:S(2)}) collective-permute-start(bf16[2,512,512]{2,1,0:T(8,128)(2,1)} %collective-permute-done.rest_1_), channel_id=1, source_target_pairs={{1,2},{2,1},{5,6},{6,5},{9,10},{10,9},{13,14},{14,13},{17,18},{18,... | collective-permute-start | bytes 3145736 | tf_op jit(solution)/shard_map/ppermute | solution.py:27
  51.5 13.0 %collective-permute-start.5 = (bf16[528,512]{1,0:T(8,128)(2,1)}, bf16[528,512]{1,0:T(8,128)(2,1)}, u32[]{:S(2)}, u32[]{:S(2)}) collective-permute-start(bf16[528,512]{1,0:T(8,128)(2,1)} %collective-permute-done.3.rest_3_), channel_id=1, source_target_pairs={{1,9},{2,10},{5,13},{6,14},{9,1},{10,2},{13,5},{14,6},{17,25},{18,... | collective-permute-start | bytes 1622024 | tf_op jit(solution)/shard_map/ppermute | solution.py:23
  53.0 18.5 %collective-permute-start.7 = (bf16[528,512]{1,0:T(8,128)(2,1)}, bf16[528,512]{1,0:T(8,128)(2,1)}, u32[]{:S(2)}, u32[]{:S(2)}) collective-permute-start(bf16[528,512]{1,0:T(8,128)(2,1)} %get-tuple-element.55), channel_id=1, source_target_pairs={{0,1},{3,2},{4,5},{7,6},{8,9},{11,10},{12,13},{15,14},{16,17},{19,... | collective-permute-start | bytes 1622024 | tf_op jit(solution)/shard_map/ppermute | solution.py:31
  63.1 14.8 %collective-permute-start.4 = (bf16[528,512]{1,0:T(8,128)(2,1)}, bf16[528,512]{1,0:T(8,128)(2,1)}, u32[]{:S(2)}, u32[]{:S(2)}) collective-permute-start(bf16[528,512]{1,0:T(8,128)(2,1)} %collective-permute-done.3.rest_3_), channel_id=1, source_target_pairs={{1,5},{2,6},{5,1},{6,2},{9,13},{10,14},{13,9},{14,10},{17,21},{18,... | collective-permute-start | bytes 1622024 | tf_op jit(solution)/shard_map/ppermute | solution.py:23
  64.5 13.3 %collective-permute-start.6 = (bf16[528,512]{1,0:T(8,128)(2,1)}, bf16[528,512]{1,0:T(8,128)(2,1)}, u32[]{:S(2)}, u32[]{:S(2)}) collective-permute-start(bf16[528,512]{1,0:T(8,128)(2,1)} %collective-permute-done.5.rest_5_), channel_id=1, source_target_pairs={{1,5},{2,6},{5,1},{6,2},{9,13},{10,14},{13,9},{14,10},{17,21},{18,... | collective-permute-start | bytes 1622024 | tf_op jit(solution)/shard_map/ppermute | solution.py:23
  71.5 20.5 %collective-permute-start.9 = (bf16[528,512]{1,0:T(8,128)(2,1)}, bf16[528,512]{1,0:T(8,128)(2,1)}, u32[]{:S(2)}, u32[]{:S(2)}) collective-permute-start(bf16[528,512]{1,0:T(8,128)(2,1)} %collective-permute-done.7.rest_2_), channel_id=1, source_target_pairs={{1,9},{2,10},{5,13},{6,14},{9,1},{10,2},{13,5},{14,6},{17,25},{18,... | collective-permute-start | bytes 1622024 | tf_op jit(solution)/shard_map/ppermute | solution.py:23
  73.0 21.2 %collective-permute-start.8 = (bf16[528,512]{1,0:T(8,128)(2,1)}, bf16[528,512]{1,0:T(8,128)(2,1)}, u32[]{:S(2)}, u32[]{:S(2)}) collective-permute-start(bf16[528,512]{1,0:T(8,128)(2,1)} %collective-permute-done.7.rest_2_), channel_id=1, source_target_pairs={{1,5},{2,6},{5,1},{6,2},{9,13},{10,14},{13,9},{14,10},{17,21},{18,... | collective-permute-start | bytes 1622024 | tf_op jit(solution)/shard_map/ppermute | solution.py:23
  92.8 11.0 %collective-permute-start.14 = (bf16[528,1024]{1,0:T(8,128)(2,1)S(1)}, bf16[528,1024]{1,0:T(8,128)(2,1)S(1)}, u32[]{:S(2)}, u32[]{:S(2)}) collective-permute-start(bf16[528,1024]{1,0:T(8,128)(2,1)S(1)} %copy-done.13), channel_id=1, source_target_pairs={{1,9},{2,10},{5,13},{6,14},{9,1},{10,2},{13,5},{14,6},{17,25},{18,... | collective-permute-start | bytes 3244040 | tf_op jit(solution)/shard_map/ppermute | solution.py:23
  93.5 8.3 %collective-permute-start.11 = (bf16[512,512]{1,0:T(8,128)(2,1)S(1)}, bf16[512,512]{1,0:T(8,128)(2,1)S(1)}, u32[]{:S(2)}, u32[]{:S(2)}) collective-permute-start(bf16[512,512]{1,0:T(8,128)(2,1)S(1)} %shard_map.66.rest_0_), channel_id=1, source_target_pairs={{1,2},{2,1},{5,6},{6,5},{9,10},{10,9},{13,14},{14,13},{17,18},{18,... | collective-permute-start | bytes 1572872 | tf_op jit(solution)/shard_map/ppermute | solution.py:27
  97.3 6.4 %collective-permute-start.12 = (bf16[528,512]{1,0:T(8,128)(2,1)S(1)}, bf16[528,512]{1,0:T(8,128)(2,1)S(1)}, u32[]{:S(2)}, u32[]{:S(2)}) collective-permute-start(bf16[528,512]{1,0:T(8,128)(2,1)S(1)} %get-tuple-element.27.rest_1_), channel_id=1, source_target_pairs={{1,2},{2,1},{5,6},{6,5},{9,10},{10,9},{13,14},{14,13},{17,18},{18,... | collective-permute-start | bytes 1622024 | tf_op jit(solution)/shard_map/ppermute | solution.py:27
  98.0 8.4 %collective-permute-start.13 = (bf16[528,1024]{1,0:T(8,128)(2,1)S(1)}, bf16[528,1024]{1,0:T(8,128)(2,1)S(1)}, u32[]{:S(2)}, u32[]{:S(2)}) collective-permute-start(bf16[528,1024]{1,0:T(8,128)(2,1)S(1)} %copy-done.13), channel_id=1, source_target_pairs={{1,5},{2,6},{5,1},{6,2},{9,13},{10,14},{13,9},{14,10},{17,21},{18,... | collective-permute-start | bytes 3244040 | tf_op jit(solution)/shard_map/ppermute | solution.py:23
  103.7 2.7 %collective-permute-start.15 = (bf16[528,1024]{1,0:T(8,128)(2,1)S(1)}, bf16[528,1024]{1,0:T(8,128)(2,1)S(1)}, u32[]{:S(2)}, u32[]{:S(2)}) collective-permute-start(bf16[528,1024]{1,0:T(8,128)(2,1)S(1)} %collective-permute-done.14.rest_3_), channel_id=1, source_target_pairs={{1,5},{2,6},{5,1},{6,2},{9,13},{10,14},{13,9},{14,10},{17,21},{18,... | collective-permute-start | bytes 3244040 | tf_op jit(solution)/shard_map/ppermute | solution.py:23
  109.2 15.2 %collective-permute-start.21 = (bf16[528,512]{1,0:T(8,128)(2,1)S(1)}, bf16[528,512]{1,0:T(8,128)(2,1)S(1)}, u32[]{:S(2)}, u32[]{:S(2)}) collective-permute-start(bf16[528,512]{1,0:T(8,128)(2,1)S(1)} %get-tuple-element.34), channel_id=1, source_target_pairs={{0,16},{16,0},{1,17},{17,1},{2,18},{18,2},{3,19},{19,3},{4,20},{20... | collective-permute-start | bytes 1622024 | tf_op jit(solution)/shard_map/ppermute | solution.py:17
  110.8 20.3 %collective-permute-start.17 = (bf16[512,512]{1,0:T(8,128)(2,1)S(1)}, bf16[512,512]{1,0:T(8,128)(2,1)S(1)}, u32[]{:S(2)}, u32[]{:S(2)}) collective-permute-start(bf16[512,512]{1,0:T(8,128)(2,1)S(1)} %get-tuple-element.32), channel_id=1, source_target_pairs={{0,16},{16,0},{1,17},{17,1},{2,18},{18,2},{3,19},{19,3},{4,20},{20... | collective-permute-start | bytes 1572872 | tf_op jit(solution)/shard_map/ppermute | solution.py:17
  111.3 26.3 %collective-permute-start.16 = (bf16[528,1024]{1,0:T(8,128)(2,1)S(1)}, bf16[528,1024]{1,0:T(8,128)(2,1)S(1)}, u32[]{:S(2)}, u32[]{:S(2)}) collective-permute-start(bf16[528,1024]{1,0:T(8,128)(2,1)S(1)} %get-tuple-element.30.rest_0_), channel_id=1, source_target_pairs={{1,2},{2,1},{5,6},{6,5},{9,10},{10,9},{13,14},{14,13},{17,18},{18,... | collective-permute-start | bytes 3244040 | tf_op jit(solution)/shard_map/ppermute | solution.py:27
  124.5 11.0 %collective-permute-start.23 = (bf16[528,512]{1,0:T(8,128)(2,1)S(1)}, bf16[528,512]{1,0:T(8,128)(2,1)S(1)}, u32[]{:S(2)}, u32[]{:S(2)}) collective-permute-start(bf16[528,512]{1,0:T(8,128)(2,1)S(1)} %collective-permute-done.21.rest_5_), channel_id=1, source_target_pairs={{1,9},{2,10},{5,13},{6,14},{9,1},{10,2},{13,5},{14,6},{17,25},{18,... | collective-permute-start | bytes 1622024 | tf_op jit(solution)/shard_map/ppermute | solution.py:23
  131.0 5.8 %collective-permute-start.19 = (bf16[512,512]{1,0:T(8,128)(2,1)S(1)}, bf16[512,512]{1,0:T(8,128)(2,1)S(1)}, u32[]{:S(2)}, u32[]{:S(2)}) collective-permute-start(bf16[512,512]{1,0:T(8,128)(2,1)S(1)} %collective-permute-done.17.rest_1_), channel_id=1, source_target_pairs={{1,9},{2,10},{5,13},{6,14},{9,1},{10,2},{13,5},{14,6},{17,25},{18,... | collective-permute-start | bytes 1572872 | tf_op jit(solution)/shard_map/ppermute | solution.py:23
  134.7 5.9 %collective-permute-start.22 = (bf16[528,512]{1,0:T(8,128)(2,1)S(1)}, bf16[528,512]{1,0:T(8,128)(2,1)S(1)}, u32[]{:S(2)}, u32[]{:S(2)}) collective-permute-start(bf16[528,512]{1,0:T(8,128)(2,1)S(1)} %collective-permute-done.21.rest_5_), channel_id=1, source_target_pairs={{1,5},{2,6},{5,1},{6,2},{9,13},{10,14},{13,9},{14,10},{17,21},{18,... | collective-permute-start | bytes 1622024 | tf_op jit(solution)/shard_map/ppermute | solution.py:23
  135.4 5.2 %collective-permute-start.24 = (bf16[528,512]{1,0:T(8,128)(2,1)S(1)}, bf16[528,512]{1,0:T(8,128)(2,1)S(1)}, u32[]{:S(2)}, u32[]{:S(2)}) collective-permute-start(bf16[528,512]{1,0:T(8,128)(2,1)S(1)} %collective-permute-done.23.rest_7_), channel_id=1, source_target_pairs={{1,5},{2,6},{5,1},{6,2},{9,13},{10,14},{13,9},{14,10},{17,21},{18,... | collective-permute-start | bytes 1622024 | tf_op jit(solution)/shard_map/ppermute | solution.py:23
  136.1 4.4 %collective-permute-start.18 = (bf16[512,512]{1,0:T(8,128)(2,1)S(1)}, bf16[512,512]{1,0:T(8,128)(2,1)S(1)}, u32[]{:S(2)}, u32[]{:S(2)}) collective-permute-start(bf16[512,512]{1,0:T(8,128)(2,1)S(1)} %collective-permute-done.17.rest_1_), channel_id=1, source_target_pairs={{1,5},{2,6},{5,1},{6,2},{9,13},{10,14},{13,9},{14,10},{17,21},{18,... | collective-permute-start | bytes 1572872 | tf_op jit(solution)/shard_map/ppermute | solution.py:23
  136.8 3.7 %collective-permute-start.20 = (bf16[512,512]{1,0:T(8,128)(2,1)S(1)}, bf16[512,512]{1,0:T(8,128)(2,1)S(1)}, u32[]{:S(2)}, u32[]{:S(2)}) collective-permute-start(bf16[512,512]{1,0:T(8,128)(2,1)S(1)} %collective-permute-done.19.rest_3_), channel_id=1, source_target_pairs={{1,5},{2,6},{5,1},{6,2},{9,13},{10,14},{13,9},{14,10},{17,21},{18,... | collective-permute-start | bytes 1572872 | tf_op jit(solution)/shard_map/ppermute | solution.py:23
  143.4 5.3 %collective-permute-start.27 = (bf16[528,1024]{1,0:T(8,128)(2,1)S(1)}, bf16[528,1024]{1,0:T(8,128)(2,1)S(1)}, u32[]{:S(2)}, u32[]{:S(2)}) collective-permute-start(bf16[528,1024]{1,0:T(8,128)(2,1)S(1)} %get-tuple-element.36.rest_0_.rest_1_), channel_id=1, source_target_pairs={{1,9},{2,10},{5,13},{6,14},{9,1},{10,2},{13,5},{14,6},{17,25},{18,... | collective-permute-start | bytes 3244040 | tf_op jit(solution)/shard_map/ppermute | solution.py:23
  144.2 5.3 %collective-permute-start.25 = (bf16[528,1024]{1,0:T(8,128)(2,1)S(1)}, bf16[528,1024]{1,0:T(8,128)(2,1)S(1)}, u32[]{:S(2)}, u32[]{:S(2)}) collective-permute-start(bf16[528,1024]{1,0:T(8,128)(2,1)S(1)} %get-tuple-element.36.rest_0_.rest_1_), channel_id=1, source_target_pairs={{1,2},{2,1},{5,6},{6,5},{9,10},{10,9},{13,14},{14,13},{17,18},{18,... | collective-permute-start | bytes 3244040 | tf_op jit(solution)/shard_map/ppermute | solution.py:27
  144.9 7.5 %collective-permute-start.26 = (bf16[528,1024]{1,0:T(8,128)(2,1)S(1)}, bf16[528,1024]{1,0:T(8,128)(2,1)S(1)}, u32[]{:S(2)}, u32[]{:S(2)}) collective-permute-start(bf16[528,1024]{1,0:T(8,128)(2,1)S(1)} %get-tuple-element.36.rest_0_.rest_1_), channel_id=1, source_target_pairs={{1,5},{2,6},{5,1},{6,2},{9,13},{10,14},{13,9},{14,10},{17,21},{18,... | collective-permute-start | bytes 3244040 | tf_op jit(solution)/shard_map/ppermute | solution.py:23
  148.7 3.8 %collective-permute-start.28 = (bf16[528,1024]{1,0:T(8,128)(2,1)S(1)}, bf16[528,1024]{1,0:T(8,128)(2,1)S(1)}, u32[]{:S(2)}, u32[]{:S(2)}) collective-permute-start(bf16[528,1024]{1,0:T(8,128)(2,1)S(1)} %collective-permute-done.27.rest_3_.rest_2_), channel_id=1, source_target_pairs={{1,5},{2,6},{5,1},{6,2},{9,13},{10,14},{13,9},{14,10},{17,21},{18,... | collective-permute-start | bytes 3244040 | tf_op jit(solution)/shard_map/ppermute | solution.py:23
  155.0 80.7 %collective-permute-start.29 = (bf16[528,512]{1,0:T(8,128)(2,1)}, bf16[528,512]{1,0:T(8,128)(2,1)}, u32[]{:S(2)}, u32[]{:S(2)}) collective-permute-start(bf16[528,512]{1,0:T(8,128)(2,1)} %get-tuple-element.39), channel_id=1, source_target_pairs={{1,0},{2,3},{5,4},{6,7},{9,8},{10,11},{13,12},{14,15},{17,16},{18,... | collective-permute-start | bytes 1622024 | tf_op jit(solution)/shard_map/ppermute | solution.py:35
  157.0 78.2 %collective-permute-start.31 = (f32[1,512]{1,0:T(1,128)S(1)}, f32[1,512]{1,0:T(1,128)S(1)}, u32[]{:S(2)}, u32[]{:S(2)}) collective-permute-start(f32[1,512]{1,0:T(1,128)S(1)} %slice_add_fusion), channel_id=1, source_target_pairs={{1,0},{2,3},{5,4},{6,7},{9,8},{10,11},{13,12},{14,15},{17,16},{18,... | collective-permute-start | bytes 6152 | tf_op jit(solution)/shard_map/ppermute | solution.py:35
  (22 other events, 60.8 us)
Sparse Core Ops, SparseCore 0:
  9.8 25.6 all-gather.4
  37.0 22.9 all-gather.6

commit v9 on v8

--- a/solution.py
+++ b/solution.py
@@ -7,6 +7,7 @@
 
 EXTRA = 16
 VMEM = 14 * 1024 * 1024
+TOKEN = jax.ShapeDtypeStruct((8, 128), jnp.float32)
 NT = (((1,), (1,)), ((), ()))
 
 
@@ -41,17 +42,16 @@
 
     def add(self, view):
         array, which, column = view
-        part = which if isinstance(which, int) else None
-        for i, (known, known_part) in enumerate(self.keys):
-            if known is array and known_part == part:
-                return i, which, column
-        self.keys.append((array, part))
+        for i, (known, part) in enumerate(self.keys):
+            if known is array and part == which:
+                return i, column
+        self.keys.append((array, which))
         self.arrays.append(array)
-        if part is None:
+        if which is None:
             self.specs.append(pl.BlockSpec(memory_space=pltpu.VMEM))
         else:
             self.specs.append(pl.BlockSpec(memory_space=pl.ANY))
-        return len(self.keys) - 1, which, column
+        return len(self.keys) - 1, column
 
     def scratch(self):
         parts = [array for array, part in self.keys if part is not None]
@@ -73,10 +73,9 @@
         return found
 
 
-def read(refs, view, size, rows=None, row=None):
-    i, which, column = view
-    ref = refs[i].at[row ^ which[0]] if isinstance(which, tuple) else refs[i]
-    return ref[rows or slice(0, size), column : column + size]
+def read(refs, view, size, rows=None):
+    i, column = view
+    return refs[i][rows or slice(0, size), column : column + size]
 
 
 def spread(refs, views, q_ref, size, n):
@@ -91,15 +90,16 @@
     return total
 
 
-def spread_columns(pivots, tiles, size, count, onto=None):
+def spread_columns(pivots, tiles, size, count, onto=None, wait=()):
     operands = Operands()
     views = [(block, operands.add(view)) for block, view in tiles]
     extra = [] if onto is None else [onto]
 
     def kernel(q_ref, *rest):
         onto_ref, rest = rest[0], rest[len(extra) :]
-        refs, (out, *scratch) = rest[: len(operands.keys)], rest[len(operands.keys) :]
-        refs = operands.load(refs, scratch)
+        token, out, *scratch = rest[len(operands.keys) + len(wait) :]
+        refs = operands.load(rest[: len(operands.keys)], scratch)
+        token[...] = jnp.zeros_like(token)
 
         @pl.loop(0, count)
         def _(n):
@@ -109,9 +109,11 @@
 
     return pl.pallas_call(
         kernel,
-        out_shape=jax.ShapeDtypeStruct((size, size * count), jnp.bfloat16),
-        in_specs=[pl.BlockSpec(memory_space=pltpu.VMEM)] * (1 + len(extra)) + operands.specs,
-        out_specs=pl.BlockSpec(memory_space=pltpu.VMEM),
+        out_shape=(TOKEN, jax.ShapeDtypeStruct((size, size * count), jnp.bfloat16)),
+        in_specs=[pl.BlockSpec(memory_space=pltpu.VMEM)] * (1 + len(extra))
+        + operands.specs
+        + [pl.BlockSpec(memory_space=pl.ANY)] * len(wait),
+        out_specs=(pl.BlockSpec(memory_space=pltpu.VMEM),) * 2,
         scratch_shapes=operands.scratch(),
         compiler_params=pltpu.CompilerParams(vmem_limit_bytes=VMEM),
         cost_estimate=pl.CostEstimate(
@@ -119,30 +121,29 @@
             bytes_accessed=8 * size * size,
             transcendentals=0,
         ),
-    )(pivots, *extra, *operands.arrays)
-
-
-def product(left, halves, form, size, added=None, own=None, turn=0, row=None):
+    )(pivots, *extra, *operands.arrays, *wait)
+
+
+def product(left, halves, form, size, added=None, own=None, turn=0, wait=()):
     count = left.shape[1] // size
     operands = Operands()
     views = [[operands.add(view) for view in half] for half in halves]
     own_views = [operands.add(view) for view in own or []]
     extra = [] if added is None else [added]
-    scalar = [] if row is None else [row.reshape(1)]
     tall, wide = size + (EXTRA if extra else 0), size * len(halves)
     shapes = [] if form == "apart" else [(tall, wide)]
     if form != "joint":
         shapes += [(size, size)] * (len(halves) - 1) + [(tall, size)]
-    outs = [jax.ShapeDtypeStruct(shape, jnp.bfloat16) for shape in shapes]
+    outs = [TOKEN] + [jax.ShapeDtypeStruct(shape, jnp.bfloat16) for shape in shapes]
     if extra:
         outs.append(jax.ShapeDtypeStruct((EXTRA, size), jnp.float32))
 
     def kernel(left_ref, *rest):
-        here = None
-        if scalar:
-            here, rest = rest[0][0], rest[1:]
-        refs = rest[len(extra) : len(extra) + len(operands.arrays)]
-        results = rest[len(extra) + len(refs) :]
+        refs = rest[len(extra) : len(extra) + len(operands.keys)]
+        token, *results = rest[len(extra) + len(refs) + len(wait) :]
+        results, scratch = results[: len(outs) - 1], results[len(outs) - 1 :]
+        refs = operands.load(refs, scratch)
+        token[...] = jnp.zeros_like(token)
         joint = None if form == "apart" else results[0]
         single = [] if form == "joint" else results[len(shapes) - len(halves) : len(shapes)]
 
@@ -151,7 +152,7 @@
             for b in range(count):
                 part = jnp.dot(
                     left_ref[:, b * size : (b + 1) * size],
-                    read(refs, half[b], size, row=here),
+                    read(refs, half[b], size),
                     preferred_element_type=jnp.float32,
                 )
                 total = part if total is None else total + part
@@ -166,7 +167,7 @@
         def pieces(b, k):
             lanes = slice(k * (size // 4), (k + 1) * (size // 4))
             near, end = (
-                read(refs, kind[b], size, slice(size, tall), here)[:, lanes]
+                read(refs, kind[b], size, slice(size, tall))[:, lanes]
                 for kind in (own_views, views[-1])
             )
             return jnp.concatenate([end, near, near, end], axis=1) * rest[0][...]
@@ -189,23 +190,24 @@
             single[-1][size:tall, :] = applied
 
     whole = pl.BlockSpec(memory_space=pltpu.VMEM)
-    specs = [pl.BlockSpec(memory_space=pltpu.SMEM)] * len(scalar) + [whole] * len(extra)
+    waits = [pl.BlockSpec(memory_space=pl.ANY)] * len(wait)
     return pl.pallas_call(
         kernel,
         out_shape=tuple(outs),
-        in_specs=[whole] + specs + operands.specs,
+        in_specs=[whole] * (1 + len(extra)) + operands.specs + waits,
         out_specs=(whole,) * len(outs),
+        scratch_shapes=operands.scratch(),
         compiler_params=pltpu.CompilerParams(vmem_limit_bytes=VMEM),
         cost_estimate=pl.CostEstimate(
             flops=2 * len(halves) * size * size * size * count,
             bytes_accessed=12 * len(halves) * size * size,
             transcendentals=0,
         ),
-    )(left, *scalar, *extra, *operands.arrays)
+    )(left, *extra, *operands.arrays, *wait)
 
 
 def after(value, *others):
-    return lax.optimization_barrier((value, *others))[0]
+    return lax.optimization_barrier((value, *others))
 
 
 def plain(*tiles):
@@ -225,9 +227,11 @@
     tiles = [jnp.concatenate([blocks[k], riding], axis=0) for k in (0, 2)]
     ends_left = inward(lefts)
     lefts_other = swap_middle(lefts)
-    rights = [lax.all_gather(tile, "row", axis=0) for tile in tiles]
+    rights = jnp.stack(tiles)
+    rights_across = swap_rows(rights, 2)
     end_lower = inward(tiles[0])
     end_upper = inward(tiles[1])
+    rights_beside = swap_rows(rights, 1)
 
     own = lax.dynamic_index_in_dim(boundary_pivots, position, 0, keepdims=True)
     back = lax.dynamic_index_in_dim(
@@ -242,63 +246,72 @@
     places = lax.broadcasted_iota(jnp.int32, (EXTRA, size), 1)
     held = ((places < 2 * share) == (col == 1)).astype(jnp.bfloat16)
 
-    def panel(turn, tiles, onto=None):
-        return spread_columns(pivots[turn], tiles, size, count, onto)
-
-    upper_panel, lower_panel = panel(2, [(0, (lefts, 1, 0))]), panel(0, [(0, (lefts, 0, 0))])
-    ends_other = swap_middle(after(ends_left, upper_panel, lower_panel))
-    lower_panel = panel(0, [(1, (ends_left, 0, 0)), (2, (lefts_other, 0, 0))], lower_panel)
-    upper_panel = panel(2, [(1, (ends_left, 1, 0)), (2, (lefts_other, 1, 0))], upper_panel)
-    end_lower = after(end_lower, lower_panel, upper_panel)
+    def panel(turn, tiles, onto=None, wait=()):
+        return spread_columns(pivots[turn], tiles, size, count, onto, wait)
+
+    lower_done, lower_panel = panel(0, [(0, (lefts, 0, 0))])
+    upper_done, upper_panel = panel(2, [(0, (lefts, 1, 0))])
+    tied, *seen = after(ends_left, lower_done, upper_done)
+    ends_other = swap_middle(tied)
+    rights_last = swap_rows(rights_across, 1)
+    lower_done, lower_panel = panel(
+        0, [(1, (ends_left, 0, 0)), (2, (lefts_other, 0, 0))], lower_panel, seen
+    )
+    upper_done, upper_panel = panel(
+        2, [(1, (ends_left, 1, 0)), (2, (lefts_other, 1, 0))], upper_panel
+    )
+    end_lower, *seen = after(end_lower, lower_done, upper_done)
     lower_across = swap_rows(end_lower, 2)
     lower_ends = [end_lower, swap_rows(end_lower, 1), lower_across, swap_rows(lower_across, 1)]
     upper_across = swap_rows(end_upper, 2)
     upper_ends = [end_upper, swap_rows(end_upper, 1), upper_across]
-    lower_panel = panel(0, [(3, (ends_other, 0, 0))], lower_panel)
 
     def own_tiles(k):
-        return [(rights[k], (b,), 0) for b in range(count)]
-
-    lower, _ = product(
-        lower_panel, [own_tiles(0), plain(*lower_ends)], "joint", size, held, own_tiles(0), 0, row
-    )
-    upper_panel = after(upper_panel, lower)
-    upper_panel = panel(2, [(3, (ends_other, 1, 0))], upper_panel)
-    (upper_o,) = product(upper_panel, [own_tiles(1)], "apart", size, row=row)
-    upper_ends.append(swap_rows(after(upper_across, upper_o), 1))
-    upper_e, vector = product(
-        upper_panel, [plain(*upper_ends)], "apart", size, held, own_tiles(1), 2, row
+        return [(tile, k, 0) for tile in (rights, rights_beside, rights_across, rights_last)]
+
+    _, lower_panel = panel(0, [(3, (ends_other, 0, 0))], lower_panel, seen)
+    lower_done, lower, _ = product(
+        lower_panel, [own_tiles(0), plain(*lower_ends)], "joint", size, held, own_tiles(0), 0
+    )
+    _, upper_panel = panel(2, [(3, (ends_other, 1, 0))], upper_panel, [lower_done])
+    upper_done, upper_o = product(upper_panel, [own_tiles(1)], "apart", size)
+    tied, seen = after(upper_across, upper_done)
+    upper_ends.append(swap_rows(tied, 1))
+    _, upper_e, vector = product(
+        upper_panel, [plain(*upper_ends)], "apart", size, held, own_tiles(1), 2, [seen]
     )
 
     def right_views(right, tie):
-        parts = []
+        parts, seen = [], []
         for tile in right:
             beside, across = swap_rows(tile, 1), swap_rows(tile, 2)
-            parts.append([tile, beside, across, swap_rows(after(across, *tie), 1)])
+            tied, token, *_ = after(across, *tie)
+            parts.append([tile, beside, across, swap_rows(tied, 1)])
+            seen.append(token)
         if len(parts) == 1:
-            return [[(tile, None, column) for tile in parts[0]] for column in (0, size)]
-        return [plain(*part) for part in parts]
+            return [[(tile, None, column) for tile in parts[0]] for column in (0, size)], seen
+        return [plain(*part) for part in parts], seen
 
     other_o, other_e = swap_middle(upper_o), swap_middle(upper_e)
-    moved = panel(1, [(0, (upper_o, None, 0)), (1, (upper_e, None, 0))])
-    moved = panel(1, [(2, (other_o, None, 0))], moved)
-    views = right_views([lower], (moved, other_e))
-    moved = panel(1, [(3, (other_e, None, 0))], moved)
-    whole, whole_o, whole_e, vector = product(moved, views, "both", size, vector)
+    _, moved = panel(1, [(0, (upper_o, None, 0)), (1, (upper_e, None, 0))])
+    done, moved = panel(1, [(2, (other_o, None, 0))], moved)
+    views, seen = right_views([lower], (done, other_e))
+    _, moved = panel(1, [(3, (other_e, None, 0))], moved)
+    _, whole, whole_o, whole_e, vector = product(moved, views, "both", size, vector, wait=seen)
 
     def left_panel(turn, left):
         other = swap_middle(left)
-        partial = panel(turn, [(0, (left, None, 0)), (1, (left, None, size))])
-        return partial, panel(turn, [(2, (other, None, 0)), (3, (other, None, size))], partial)
+        done, moved = panel(turn, [(0, (left, None, 0)), (1, (left, None, size))])
+        return done, panel(turn, [(2, (other, None, 0)), (3, (other, None, size))], moved)[1]
 
     earlier = [from_behind(tile, "loop", 1) for tile in (whole_o, whole_e)]
-    partial, moved = left_panel(3, whole)
-    views = right_views(earlier, (partial,))
-    halved, vector = product(moved, views, "joint", size, vector)
-    partial, moved = left_panel(4, halved)
-    views = right_views([from_behind(halved, "loop", 2)], (partial,))
-    reduced_e, vector = product(moved, views[1:], "apart", size, vector)
-    (reduced_o,) = product(after(moved, reduced_e), views[:1], "apart", size)
+    done, moved = left_panel(3, whole)
+    views, seen = right_views(earlier, (done,))
+    _, halved, vector = product(moved, views, "joint", size, vector, wait=seen)
+    done, moved = left_panel(4, halved)
+    views, seen = right_views([from_behind(halved, "loop", 2)], (done,))
+    done, reduced_e, vector = product(moved, views[1:], "apart", size, vector, wait=seen)
+    _, reduced_o = product(moved, views[:1], "apart", size, wait=[done])
 
     middle = (col == 1) | (col == 2)
     block = jnp.where(middle, reduced_o, outward(reduced_e)[:size])

time: 246 us -> 233 us (0.947)
  between operations: 14.8 us -> 1.46 us
  Pallas kernels: 53.6 us -> 64.2 us
  waiting for transfers between devices: 110 us -> 103 us
  local copies, waits for them, and re-layouts: 16.1 us -> 10.7 us
    ppermute x3, waiting for transfers between devices: 19.1 us -> 5.81 us  [inward(): return lax.ppermute(value, 'col', [(0, 1), (3, 2)])]
    pallas_call x20, Pallas kernels: 53.6 us -> 64.2 us  [the longest x13 40 us: spread_columns(): pl.pallas_call(kernel, out_shape=(TOKEN, jax.ShapeDtypeStruct((size, size...]
    unnamed x42 -> x32, local copies, waits for them, and re-layouts: 14.6 us -> 8.01 us
    ppermute x2, waiting for transfers between devices: 72 us -> 76.2 us  [outward(): return lax.ppermute(value, 'col', [(1, 0), (2, 3)])]
    ppermute x2, waiting for transfers between devices: 18.1 us -> 20.9 us  [from_behind(): lax.ppermute(value, axis, [(i, (i + by) % devices) for i in range(devices)])]
    ppermute x18 -> x21, starting transfers between devices: 16.8 us -> 18.3 us  [swap_rows(): return lax.ppermute(value, ('row', 'col'), pairs)]
  transfers between devices with their start and end apart: 34 -> 35, of which waited for: 5 -> 5; matrix products, arithmetic and copies ran while one was open for 0% -> 1% of each run, Pallas kernels for 19% -> 24%
where the time goes in v9:
time: 233 us; the launch traced here: 231 us
  waiting for transfers between devices  103 us (44%)
  Pallas kernels  64.2 us (28%)
  starting transfers between devices  48 us (21%)
  local copies, waits for them, and re-layouts  10.7 us (5%)
  other arithmetic  3.84 us (2%)
    ppermute x2, waiting for transfers between devices, outward(): return lax.ppermute(value, 'col', [(1, 0), (2, 3)])  76.2 us
    pallas_call x13, Pallas kernels, spread_columns(): pl.pallas_call(kernel, out_shape=(TOKEN, jax.ShapeDtypeStruct((size, size...  40 us
    pallas_call x7, Pallas kernels, product(): pl.pallas_call(kernel, out_shape=tuple(outs), in_specs=[whole] * (1 + len...  24.2 us
    ppermute x2, waiting for transfers between devices, from_behind(): lax.ppermute(value, axis, [(i, (i + by) % devices) for i in range(devices)])  20.9 us
    ppermute x21, starting transfers between devices, swap_rows(): return lax.ppermute(value, ('row', 'col'), pairs)  18.3 us
    ppermute x3, starting transfers between devices, inward(): return lax.ppermute(value, 'col', [(0, 1), (3, 2)])  18.2 us
    unnamed x32, local copies, waits for them, and re-layouts  8.01 us
    ppermute x7, starting transfers between devices, swap_middle(): return lax.ppermute(value, 'col', [(1, 2), (2, 1)])  6.78 us
  transfers between devices with their start and end apart: 35, of which 5 were waited for; matrix products, arithmetic and copies ran while one was open for 1% of the time, Pallas kernels for 24%

profile of v9, /device:TPU:0, one launch (start us, length us, event | category | flops | bytes accessed | tf_op | source)
XLA Modules:
  0.0 231.2 jit_solution(16135468297540271803)
XLA Ops:
  0.6 2.5 %slice.44.rest_0_ = bf16[2,512,512]{2,1,0:T(8,128)(2,1)} slice(bf16[4,512,512]{2,1,0:T(8,128)(2,1)} %bitcast.22), slice={[1:4:2], [0:512:1], [0:512:1]} | slice | bytes 2097152 | tf_op jit(solution)/shard_map/slice | solution.py:225
  3.1 6.1 %collective-permute-start = (bf16[2,512,512]{2,1,0:T(8,128)(2,1)}, bf16[2,512,512]{2,1,0:T(8,128)(2,1)}, u32[]{:S(2)}, u32[]{:S(2)}) collective-permute-start(bf16[2,512,512]{2,1,0:T(8,128)(2,1)} %slice.44.rest_0_), channel_id=1, source_target_pairs={{0,1},{3,2},{4,5},{7,6},{8,9},{11,10},{12,13},{15,14},{16,17},{19,... | collective-permute-start | bytes 3145736 | tf_op jit(solution)/shard_map/ppermute | solution.py:32
  9.2 1.6 collective-permute-start.1
  13.6 6.9 %collective-permute-start.3 = (bf16[528,512]{1,0:T(8,128)(2,1)}, bf16[528,512]{1,0:T(8,128)(2,1)}, u32[]{:S(2)}, u32[]{:S(2)}) collective-permute-start(bf16[528,512]{1,0:T(8,128)(2,1)} %get-tuple-element.123), channel_id=1, source_target_pairs={{0,1},{3,2},{4,5},{7,6},{8,9},{11,10},{12,13},{15,14},{16,17},{19,... | collective-permute-start | bytes 1622024 | tf_op jit(solution)/shard_map/ppermute | solution.py:32
  21.0 3.0 %shard_map.59 = (f32[8,128]{1,0:T(8,128)S(1)}, bf16[512,2048]{1,0:T(8,128)(2,1)S(1)}) custom-call(s32[4,512]{1,0:T(4,128)S(1)} %get-tuple-element.115.q_ref, bf16[2,512,512]{2,1,0:T(8,128)(2,1)} %slice.44.rest_0_), custom_call_target="tpu_custom_call" | custom-call | flops 1073741824 | bytes 2097152 | tf_op jit(solution)/shard_map/pallas_call | solution.py:110
  24.0 3.0 %shard_map.61 = (f32[8,128]{1,0:T(8,128)S(1)}, bf16[512,2048]{1,0:T(8,128)(2,1)S(1)}) custom-call(s32[4,512]{1,0:T(4,128)S(1)} %get-tuple-element.114.q_ref, bf16[2,512,512]{2,1,0:T(8,128)(2,1)} %slice.44.rest_0_), custom_call_target="tpu_custom_call" | custom-call | flops 1073741824 | bytes 2097152 | tf_op jit(solution)/shard_map/pallas_call | solution.py:110
  27.0 5.0 %collective-permute-done.rest_1_ = bf16[2,512,512]{2,1,0:T(8,128)(2,1)} collective-permute-done((bf16[2,512,512]{2,1,0:T(8,128)(2,1)}, bf16[2,512,512]{2,1,0:T(8,128)(2,1)}, u32[]{:S(2)}, u32[]{:S(2)}) %collective-permute-start) | collective-permute-done | bytes 1048608 | tf_op jit(solution)/shard_map/ppermute | solution.py:32
  32.0 5.2 %collective-permute-start.10 = (bf16[528,512]{1,0:T(8,128)(2,1)S(1)}, bf16[528,512]{1,0:T(8,128)(2,1)}, u32[]{:S(2)}, u32[]{:S(2)}) collective-permute-start(bf16[528,512]{1,0:T(8,128)(2,1)S(1)} %copy-done.11), channel_id=1, source_target_pairs={{0,1},{3,2},{4,5},{7,6},{8,9},{11,10},{12,13},{15,14},{16,17},{19,... | collective-permute-start | bytes 1622024 | tf_op jit(solution)/shard_map/ppermute | solution.py:32
  37.3 1.7 collective-permute-start.2
  38.9 4.2 %shard_map.60 = (f32[8,128]{1,0:T(8,128)S(1)}, bf16[512,2048]{1,0:T(8,128)(2,1)S(1)}) custom-call(s32[4,512]{1,0:T(4,128)S(1)} %get-tuple-element.115.q_ref, bf16[512,2048]{1,0:T(8,128)(2,1)S(1)} %get-tuple-element.54.rest_0_, bf16[2,512,512]{2,1,0:T(8,128)(2,1)} %collective-permute-done.rest_1_, bf16[2,512,512]{2,1,0:T(8,128)(2,1)} %collective-permute-done.1.rest_2_), custom_call_target="tpu_custom_call" | custom-call | flops 2147483648 | bytes 2097152 | tf_op jit(solution)/shard_map/pallas_call | solution.py:110
  44.5 4.2 %shard_map.62 = (f32[8,128]{1,0:T(8,128)S(1)}, bf16[512,2048]{1,0:T(8,128)(2,1)S(1)}) custom-call(s32[4,512]{1,0:T(4,128)S(1)} %get-tuple-element.114.q_ref, bf16[512,2048]{1,0:T(8,128)(2,1)S(1)} %get-tuple-element.59.rest_0_, bf16[2,512,512]{2,1,0:T(8,128)(2,1)} %collective-permute-done.rest_1_, bf16[2,512,512]{2,1,0:T(8,128)(2,1)} %collective-permute-done.1.rest_2_, ...), custom_call_target="tpu_custom_call" | custom-call | flops 2147483648 | bytes 2097152 | tf_op jit(solution)/shard_map/pallas_call | solution.py:110
  51.5 1.7 collective-permute-start.6
  59.2 3.1 %shard_map.63 = (f32[8,128]{1,0:T(8,128)}, bf16[512,2048]{1,0:T(8,128)(2,1)S(1)}) custom-call(s32[4,512]{1,0:T(4,128)S(1)} %get-tuple-element.114.q_ref, bf16[512,2048]{1,0:T(8,128)(2,1)S(1)} %copy-done.7, bf16[2,512,512]{2,1,0:T(8,128)(2,1)} %collective-permute-done.2.rest_1_, f32[8,128]{1,0:T(8,128)S(1)} %get-tuple-element.65.rest_2_, ...), custom_call_target="tpu_custom_call" | custom-call | flops 1073741824 | bytes 2097152 | tf_op jit(solution)/shard_map/pallas_call | solution.py:110
  63.0 6.4 %shard_map.64 = (f32[8,128]{1,0:T(8,128)S(1)}, bf16[528,1024]{1,0:T(8,128)(2,1)S(1)}, f32[16,512]{1,0:T(8,128)}) custom-call(bf16[512,2048]{1,0:T(8,128)(2,1)S(1)} %get-tuple-element.67.left_ref, bf16[16,512]{1,0:T(8,128)(2,1)S(1)} %iota.7.rest_0_, bf16[2,528,512]{2,1,0:T(8,128)(2,1)S(1)} %pad_maximum_fusion.rest_1_.rest_0_.rest_5_, ...), custom_call_target="tpu_custom_call" | custom-call | flops 2147483648 | bytes 6291456 | tf_op jit(solution)/shard_map/pallas_call | solution.py:194
  69.5 3.1 %shard_map.65 = (f32[8,128]{1,0:T(8,128)}, bf16[512,2048]{1,0:T(8,128)(2,1)S(1)}) custom-call(s32[4,512]{1,0:T(4,128)S(1)} %get-tuple-element.115.q_ref, bf16[512,2048]{1,0:T(8,128)(2,1)S(1)} %copy-done.9, bf16[2,512,512]{2,1,0:T(8,128)(2,1)} %collective-permute-done.2.rest_1_, f32[8,128]{1,0:T(8,128)S(1)} %get-tuple-element.69.rest_2_), custom_call_target="tpu_custom_call" | custom-call | flops 1073741824 | bytes 2097152 | tf_op jit(solution)/shard_map/pallas_call | solution.py:110
  72.5 2.5 %shard_map.66 = (f32[8,128]{1,0:T(8,128)S(1)}, bf16[512,512]{1,0:T(8,128)(2,1)S(1)}) custom-call(bf16[512,2048]{1,0:T(8,128)(2,1)S(1)} %get-tuple-element.70.left_ref, bf16[2,528,512]{2,1,0:T(8,128)(2,1)S(1)} %pad_maximum_fusion.rest_1_.rest_0_.rest_5_, bf16[2,528,512]{2,1,0:T(8,128)(2,1)S(1)} %collective-permute-done.4.rest_2_.rest_1_.rest_6_, ...), custom_call_target="tpu_custom_call" | custom-call | flops 1073741824 | bytes 3145728 | tf_op jit(solution)/shard_map/pallas_call | solution.py:194
  77.2 4.5 %shard_map.67 = (f32[8,128]{1,0:T(8,128)}, bf16[528,512]{1,0:T(8,128)(2,1)S(1)}, f32[16,512]{1,0:T(8,128)S(1)}) custom-call(bf16[512,2048]{1,0:T(8,128)(2,1)S(1)} %get-tuple-element.70.left_ref, bf16[16,512]{1,0:T(8,128)(2,1)S(1)} %iota.7.rest_0_, bf16[528,512]{1,0:T(8,128)(2,1)} %collective-permute-done.10.rest_1_, ...), custom_call_target="tpu_custom_call" | custom-call | flops 1073741824 | bytes 3145728 | tf_op jit(solution)/shard_map/pallas_call | solution.py:194
  83.2 3.0 %shard_map.68 = (f32[8,128]{1,0:T(8,128)}, bf16[512,2048]{1,0:T(8,128)(2,1)S(1)}) custom-call(s32[4,512]{1,0:T(4,128)S(1)} %get-tuple-element.116.q_ref, bf16[512,512]{1,0:T(8,128)(2,1)S(1)} %get-tuple-element.71.rest_0_, bf16[528,512]{1,0:T(8,128)(2,1)S(1)} %get-tuple-element.75.rest_1_), custom_call_target="tpu_custom_call" | custom-call | flops 2147483648 | bytes 2097152 | tf_op jit(solution)/shard_map/pallas_call | solution.py:110
  86.2 1.9 shard_map.69
  89.1 2.5 %shard_map.70 = (f32[8,128]{1,0:T(8,128)}, bf16[512,2048]{1,0:T(8,128)(2,1)S(1)}) custom-call(s32[4,512]{1,0:T(4,128)S(1)} %get-tuple-element.116.q_ref, bf16[512,2048]{1,0:T(8,128)(2,1)S(1)} %get-tuple-element.77.rest_0_, bf16[528,512]{1,0:T(8,128)(2,1)S(1)} %collective-permute-done.15.rest_1_), custom_call_target="tpu_custom_call" | custom-call | flops 1073741824 | bytes 2097152 | tf_op jit(solution)/shard_map/pallas_call | solution.py:110
  91.6 3.2 %shard_map.71 = (f32[8,128]{1,0:T(8,128)}, bf16[528,1024]{1,0:T(8,128)(2,1)S(1)}, bf16[512,512]{1,0:T(8,128)(2,1)S(1)}, bf16[528,512]{1,0:T(8,128)(2,1)S(1)}, f32[16,512]{1,0:T(8,128)S(1)}) custom-call(bf16[512,2048]{1,0:T(8,128)(2,1)S(1)} %get-tuple-element.78.left_ref, f32[16,512]{1,0:T(8,128)S(1)} %get-tuple-element.79.rest_0_, ...), custom_call_target="tpu_custom_call" | custom-call | flops 2147483648 | bytes 6291456 | tf_op jit(solution)/shard_map/pallas_call | solution.py:194
  97.6 12.5 %collective-permute-done.24.rest_5_ = bf16[528,512]{1,0:T(8,128)(2,1)S(1)} collective-permute-done((bf16[528,512]{1,0:T(8,128)(2,1)S(1)}, bf16[528,512]{1,0:T(8,128)(2,1)S(1)}, u32[]{:S(2)}, u32[]{:S(2)}) %collective-permute-start.24) | collective-permute-done | bytes 540704 | tf_op jit(solution)/shard_map/ppermute | solution.py:18
  110.8 8.5 %collective-permute-done.20.rest_1_ = bf16[512,512]{1,0:T(8,128)(2,1)S(1)} collective-permute-done((bf16[512,512]{1,0:T(8,128)(2,1)S(1)}, bf16[512,512]{1,0:T(8,128)(2,1)S(1)}, u32[]{:S(2)}, u32[]{:S(2)}) %collective-permute-start.20) | collective-permute-done | bytes 524320 | tf_op jit(solution)/shard_map/ppermute | solution.py:18
  120.0 3.0 %shard_map.72 = (f32[8,128]{1,0:T(8,128)S(1)}, bf16[512,2048]{1,0:T(8,128)(2,1)S(1)}) custom-call(s32[4,512]{1,0:T(4,128)S(1)} %get-tuple-element.117.q_ref, bf16[528,1024]{1,0:T(8,128)(2,1)S(1)} %get-tuple-element.84.rest_0_), custom_call_target="tpu_custom_call" | custom-call | flops 2147483648 | bytes 2097152 | tf_op jit(solution)/shard_map/pallas_call | solution.py:110
  125.8 3.0 %shard_map.73 = (f32[8,128]{1,0:T(8,128)}, bf16[512,2048]{1,0:T(8,128)(2,1)S(1)}) custom-call(s32[4,512]{1,0:T(4,128)S(1)} %get-tuple-element.117.q_ref, bf16[512,2048]{1,0:T(8,128)(2,1)S(1)} %get-tuple-element.85.rest_0_, bf16[528,1024]{1,0:T(8,128)(2,1)S(1)} %collective-permute-done.19.rest_1_), custom_call_target="tpu_custom_call" | custom-call | flops 2147483648 | bytes 2097152 | tf_op jit(solution)/shard_map/pallas_call | solution.py:110
  128.9 3.2 %shard_map.74 = (f32[8,128]{1,0:T(8,128)}, bf16[528,1024]{1,0:T(8,128)(2,1)S(1)}, f32[16,512]{1,0:T(8,128)S(1)}) custom-call(bf16[512,2048]{1,0:T(8,128)(2,1)S(1)} %get-tuple-element.86.left_ref, f32[16,512]{1,0:T(8,128)S(1)} %get-tuple-element.87.rest_0_, bf16[512,512]{1,0:T(8,128)(2,1)S(1)} %collective-permute-done.20.rest_1_, ...), custom_call_target="tpu_custom_call" | custom-call | flops 2147483648 | bytes 6291456 | tf_op jit(solution)/shard_map/pallas_call | solution.py:194
  134.3 3.0 %shard_map.75 = (f32[8,128]{1,0:T(8,128)S(1)}, bf16[512,2048]{1,0:T(8,128)(2,1)S(1)}) custom-call(s32[4,512]{1,0:T(4,128)S(1)} %get-tuple-element.118.q_ref, bf16[528,1024]{1,0:T(8,128)(2,1)S(1)} %get-tuple-element.95.rest_0_.rest_1_), custom_call_target="tpu_custom_call" | custom-call | flops 2147483648 | bytes 2097152 | tf_op jit(solution)/shard_map/pallas_call | solution.py:110
  138.1 3.0 %shard_map.76 = (f32[8,128]{1,0:T(8,128)}, bf16[512,2048]{1,0:T(8,128)(2,1)S(1)}) custom-call(s32[4,512]{1,0:T(4,128)S(1)} %get-tuple-element.118.q_ref, bf16[512,2048]{1,0:T(8,128)(2,1)S(1)} %get-tuple-element.96.rest_0_, bf16[528,1024]{1,0:T(8,128)(2,1)S(1)} %collective-permute-done.28.rest_1_), custom_call_target="tpu_custom_call" | custom-call | flops 2147483648 | bytes 2097152 | tf_op jit(solution)/shard_map/pallas_call | solution.py:110
  141.2 2.6 %shard_map.77 = (f32[8,128]{1,0:T(8,128)S(1)}, bf16[528,512]{1,0:T(8,128)(2,1)}, f32[16,512]{1,0:T(8,128)S(1)}) custom-call(bf16[512,2048]{1,0:T(8,128)(2,1)S(1)} %get-tuple-element.97.left_ref, f32[16,512]{1,0:T(8,128)S(1)} %get-tuple-element.100.rest_0_, bf16[528,1024]{1,0:T(8,128)(2,1)S(1)} %get-tuple-element.95.rest_0_.rest_1_, ...), custom_call_target="tpu_custom_call" | custom-call | flops 1073741824 | bytes 3145728 | tf_op jit(solution)/shard_map/pallas_call | solution.py:194
  150.8 1.8 shard_map.78
  152.6 76.2 %collective-permute-done.34 = f32[1,512]{1,0:T(1,128)S(1)} collective-permute-done((f32[1,512]{1,0:T(1,128)S(1)}, f32[1,512]{1,0:T(1,128)S(1)}, u32[]{:S(2)}, u32[]{:S(2)}) %collective-permute-start.34) | collective-permute-done | bytes 2080 | tf_op jit(solution)/shard_map/ppermute | solution.py:36
  229.3 1.9 fusion
  (111 shorter events, 35.8 us)
Async XLA Ops:
  3.1 28.9 %collective-permute-start = (bf16[2,512,512]{2,1,0:T(8,128)(2,1)}, bf16[2,512,512]{2,1,0:T(8,128)(2,1)}, u32[]{:S(2)}, u32[]{:S(2)}) collective-permute-start(bf16[2,512,512]{2,1,0:T(8,128)(2,1)} %slice.44.rest_0_), channel_id=1, source_target_pairs={{0,1},{3,2},{4,5},{7,6},{8,9},{11,10},{12,13},{15,14},{16,17},{19,... | collective-permute-start | bytes 3145736 | tf_op jit(solution)/shard_map/ppermute | solution.py:32
  9.2 28.1 %collective-permute-start.1 = (bf16[2,512,512]{2,1,0:T(8,128)(2,1)}, bf16[2,512,512]{2,1,0:T(8,128)(2,1)}, u32[]{:S(2)}, u32[]{:S(2)}) collective-permute-start(bf16[2,512,512]{2,1,0:T(8,128)(2,1)} %slice.44.rest_0_), channel_id=1, source_target_pairs={{1,2},{2,1},{5,6},{6,5},{9,10},{10,9},{13,14},{14,13},{17,18},{18,... | collective-permute-start | bytes 3145736 | tf_op jit(solution)/shard_map/ppermute | solution.py:28
  12.1 50.1 %collective-permute-start.4 = (bf16[2,528,512]{2,1,0:T(8,128)(2,1)S(1)}, bf16[2,528,512]{2,1,0:T(8,128)(2,1)S(1)}, u32[]{:S(2)}, u32[]{:S(2)}) collective-permute-start(bf16[2,528,512]{2,1,0:T(8,128)(2,1)S(1)} %pad_maximum_fusion.rest_1_.rest_0_.rest_5_), channel_id=1, source_target_pairs={{1,5},{2,6},{5,1},{6,2},{9,13},{10,14},{13,9},{14,10},{17,21},{18,... | collective-permute-start | bytes 3244040 | tf_op jit(solution)/shard_map/ppermute | solution.py:24
  12.9 38.6 %collective-permute-start.5 = (bf16[2,528,512]{2,1,0:T(8,128)(2,1)S(1)}, bf16[2,528,512]{2,1,0:T(8,128)(2,1)S(1)}, u32[]{:S(2)}, u32[]{:S(2)}) collective-permute-start(bf16[2,528,512]{2,1,0:T(8,128)(2,1)S(1)} %pad_maximum_fusion.rest_1_.rest_0_.rest_5_), channel_id=1, source_target_pairs={{1,9},{2,10},{5,13},{6,14},{9,1},{10,2},{13,5},{14,6},{17,25},{18,... | collective-permute-start | bytes 3244040 | tf_op jit(solution)/shard_map/ppermute | solution.py:24
  13.6 36.4 %collective-permute-start.3 = (bf16[528,512]{1,0:T(8,128)(2,1)}, bf16[528,512]{1,0:T(8,128)(2,1)}, u32[]{:S(2)}, u32[]{:S(2)}) collective-permute-start(bf16[528,512]{1,0:T(8,128)(2,1)} %get-tuple-element.123), channel_id=1, source_target_pairs={{0,1},{3,2},{4,5},{7,6},{8,9},{11,10},{12,13},{15,14},{16,17},{19,... | collective-permute-start | bytes 1622024 | tf_op jit(solution)/shard_map/ppermute | solution.py:32
  32.0 21.9 %collective-permute-start.10 = (bf16[528,512]{1,0:T(8,128)(2,1)S(1)}, bf16[528,512]{1,0:T(8,128)(2,1)}, u32[]{:S(2)}, u32[]{:S(2)}) collective-permute-start(bf16[528,512]{1,0:T(8,128)(2,1)S(1)} %copy-done.11), channel_id=1, source_target_pairs={{0,1},{3,2},{4,5},{7,6},{8,9},{11,10},{12,13},{15,14},{16,17},{19,... | collective-permute-start | bytes 1622024 | tf_op jit(solution)/shard_map/ppermute | solution.py:32
  37.3 19.6 %collective-permute-start.2 = (bf16[2,512,512]{2,1,0:T(8,128)(2,1)}, bf16[2,512,512]{2,1,0:T(8,128)(2,1)}, u32[]{:S(2)}, u32[]{:S(2)}) collective-permute-start(bf16[2,512,512]{2,1,0:T(8,128)(2,1)} %collective-permute-done.rest_1_), channel_id=1, source_target_pairs={{1,2},{2,1},{5,6},{6,5},{9,10},{10,9},{13,14},{14,13},{17,18},{18,... | collective-permute-start | bytes 3145736 | tf_op jit(solution)/shard_map/ppermute | solution.py:28
  50.0 5.4 %collective-permute-start.8 = (bf16[528,512]{1,0:T(8,128)(2,1)}, bf16[528,512]{1,0:T(8,128)(2,1)}, u32[]{:S(2)}, u32[]{:S(2)}) collective-permute-start(bf16[528,512]{1,0:T(8,128)(2,1)} %collective-permute-done.3.rest_5_), channel_id=1, source_target_pairs={{1,9},{2,10},{5,13},{6,14},{9,1},{10,2},{13,5},{14,6},{17,25},{18,... | collective-permute-start | bytes 1622024 | tf_op jit(solution)/shard_map/ppermute | solution.py:24
  51.5 11.5 %collective-permute-start.6 = (bf16[2,528,512]{2,1,0:T(8,128)(2,1)S(1)}, bf16[2,528,512]{2,1,0:T(8,128)(2,1)}, u32[]{:S(2)}, u32[]{:S(2)}) collective-permute-start(bf16[2,528,512]{2,1,0:T(8,128)(2,1)S(1)} %collective-permute-done.5.rest_3_.rest_2_.rest_7_), channel_id=1, source_target_pairs={{1,5},{2,6},{5,1},{6,2},{9,13},{10,14},{13,9},{14,10},{17,21},{18,... | collective-permute-start | bytes 3244040 | tf_op jit(solution)/shard_map/ppermute | solution.py:24
  53.9 9.0 %collective-permute-start.7 = (bf16[528,512]{1,0:T(8,128)(2,1)}, bf16[528,512]{1,0:T(8,128)(2,1)}, u32[]{:S(2)}, u32[]{:S(2)}) collective-permute-start(bf16[528,512]{1,0:T(8,128)(2,1)} %collective-permute-done.3.rest_5_), channel_id=1, source_target_pairs={{1,5},{2,6},{5,1},{6,2},{9,13},{10,14},{13,9},{14,10},{17,21},{18,... | collective-permute-start | bytes 1622024 | tf_op jit(solution)/shard_map/ppermute | solution.py:24
  55.4 7.6 %collective-permute-start.9 = (bf16[528,512]{1,0:T(8,128)(2,1)}, bf16[528,512]{1,0:T(8,128)(2,1)}, u32[]{:S(2)}, u32[]{:S(2)}) collective-permute-start(bf16[528,512]{1,0:T(8,128)(2,1)} %collective-permute-done.8.rest_7_), channel_id=1, source_target_pairs={{1,5},{2,6},{5,1},{6,2},{9,13},{10,14},{13,9},{14,10},{17,21},{18,... | collective-permute-start | bytes 1622024 | tf_op jit(solution)/shard_map/ppermute | solution.py:24
  56.9 18.2 %collective-permute-start.12 = (bf16[528,512]{1,0:T(8,128)(2,1)}, bf16[528,512]{1,0:T(8,128)(2,1)S(1)}, u32[]{:S(2)}, u32[]{:S(2)}) collective-permute-start(bf16[528,512]{1,0:T(8,128)(2,1)} %collective-permute-done.10.rest_1_), channel_id=1, source_target_pairs={{1,9},{2,10},{5,13},{6,14},{9,1},{10,2},{13,5},{14,6},{17,25},{18,... | collective-permute-start | bytes 1622024 | tf_op jit(solution)/shard_map/ppermute | solution.py:24
  62.3 14.9 %collective-permute-start.11 = (bf16[528,512]{1,0:T(8,128)(2,1)}, bf16[528,512]{1,0:T(8,128)(2,1)S(1)}, u32[]{:S(2)}, u32[]{:S(2)}) collective-permute-start(bf16[528,512]{1,0:T(8,128)(2,1)} %collective-permute-done.10.rest_1_), channel_id=1, source_target_pairs={{1,5},{2,6},{5,1},{6,2},{9,13},{10,14},{13,9},{14,10},{17,21},{18,... | collective-permute-start | bytes 1622024 | tf_op jit(solution)/shard_map/ppermute | solution.py:24
  75.8 12.3 %collective-permute-start.17 = (bf16[528,1024]{1,0:T(8,128)(2,1)S(1)}, bf16[528,1024]{1,0:T(8,128)(2,1)S(1)}, u32[]{:S(2)}, u32[]{:S(2)}) collective-permute-start(bf16[528,1024]{1,0:T(8,128)(2,1)S(1)} %get-tuple-element.80.rest_1_), channel_id=1, source_target_pairs={{1,9},{2,10},{5,13},{6,14},{9,1},{10,2},{13,5},{14,6},{17,25},{18,... | collective-permute-start | bytes 3244040 | tf_op jit(solution)/shard_map/ppermute | solution.py:24
  76.5 9.7 %collective-permute-start.14 = (bf16[512,512]{1,0:T(8,128)(2,1)S(1)}, bf16[512,512]{1,0:T(8,128)(2,1)S(1)}, u32[]{:S(2)}, u32[]{:S(2)}) collective-permute-start(bf16[512,512]{1,0:T(8,128)(2,1)S(1)} %get-tuple-element.71.rest_0_), channel_id=1, source_target_pairs={{1,2},{2,1},{5,6},{6,5},{9,10},{10,9},{13,14},{14,13},{17,18},{18,... | collective-permute-start | bytes 1572872 | tf_op jit(solution)/shard_map/ppermute | solution.py:28
  81.7 6.4 %collective-permute-start.15 = (bf16[528,512]{1,0:T(8,128)(2,1)S(1)}, bf16[528,512]{1,0:T(8,128)(2,1)S(1)}, u32[]{:S(2)}, u32[]{:S(2)}) collective-permute-start(bf16[528,512]{1,0:T(8,128)(2,1)S(1)} %get-tuple-element.75.rest_1_), channel_id=1, source_target_pairs={{1,2},{2,1},{5,6},{6,5},{9,10},{10,9},{13,14},{14,13},{17,18},{18,... | collective-permute-start | bytes 1622024 | tf_op jit(solution)/shard_map/ppermute | solution.py:28
  82.4 9.2 %collective-permute-start.16 = (bf16[528,1024]{1,0:T(8,128)(2,1)S(1)}, bf16[528,1024]{1,0:T(8,128)(2,1)S(1)}, u32[]{:S(2)}, u32[]{:S(2)}) collective-permute-start(bf16[528,1024]{1,0:T(8,128)(2,1)S(1)} %get-tuple-element.80.rest_1_), channel_id=1, source_target_pairs={{1,5},{2,6},{5,1},{6,2},{9,13},{10,14},{13,9},{14,10},{17,21},{18,... | collective-permute-start | bytes 3244040 | tf_op jit(solution)/shard_map/ppermute | solution.py:24
  94.8 15.3 %collective-permute-start.24 = (bf16[528,512]{1,0:T(8,128)(2,1)S(1)}, bf16[528,512]{1,0:T(8,128)(2,1)S(1)}, u32[]{:S(2)}, u32[]{:S(2)}) collective-permute-start(bf16[528,512]{1,0:T(8,128)(2,1)S(1)} %get-tuple-element.91), channel_id=1, source_target_pairs={{0,16},{16,0},{1,17},{17,1},{2,18},{18,2},{3,19},{19,3},{4,20},{20... | collective-permute-start | bytes 1622024 | tf_op jit(solution)/shard_map/ppermute | solution.py:18
  96.4 22.9 %collective-permute-start.20 = (bf16[512,512]{1,0:T(8,128)(2,1)S(1)}, bf16[512,512]{1,0:T(8,128)(2,1)S(1)}, u32[]{:S(2)}, u32[]{:S(2)}) collective-permute-start(bf16[512,512]{1,0:T(8,128)(2,1)S(1)} %get-tuple-element.88), channel_id=1, source_target_pairs={{0,16},{16,0},{1,17},{17,1},{2,18},{18,2},{3,19},{19,3},{4,20},{20... | collective-permute-start | bytes 1572872 | tf_op jit(solution)/shard_map/ppermute | solution.py:18
  96.9 28.9 %collective-permute-start.19 = (bf16[528,1024]{1,0:T(8,128)(2,1)S(1)}, bf16[528,1024]{1,0:T(8,128)(2,1)S(1)}, u32[]{:S(2)}, u32[]{:S(2)}) collective-permute-start(bf16[528,1024]{1,0:T(8,128)(2,1)S(1)} %get-tuple-element.84.rest_0_), channel_id=1, source_target_pairs={{1,2},{2,1},{5,6},{6,5},{9,10},{10,9},{13,14},{14,13},{17,18},{18,... | collective-permute-start | bytes 3244040 | tf_op jit(solution)/shard_map/ppermute | solution.py:28
  110.1 13.6 %collective-permute-start.26 = (bf16[528,512]{1,0:T(8,128)(2,1)S(1)}, bf16[528,512]{1,0:T(8,128)(2,1)S(1)}, u32[]{:S(2)}, u32[]{:S(2)}) collective-permute-start(bf16[528,512]{1,0:T(8,128)(2,1)S(1)} %collective-permute-done.24.rest_5_), channel_id=1, source_target_pairs={{1,9},{2,10},{5,13},{6,14},{9,1},{10,2},{13,5},{14,6},{17,25},{18,... | collective-permute-start | bytes 1622024 | tf_op jit(solution)/shard_map/ppermute | solution.py:24
  119.3 5.8 %collective-permute-start.22 = (bf16[512,512]{1,0:T(8,128)(2,1)S(1)}, bf16[512,512]{1,0:T(8,128)(2,1)S(1)}, u32[]{:S(2)}, u32[]{:S(2)}) collective-permute-start(bf16[512,512]{1,0:T(8,128)(2,1)S(1)} %collective-permute-done.20.rest_1_), channel_id=1, source_target_pairs={{1,9},{2,10},{5,13},{6,14},{9,1},{10,2},{13,5},{14,6},{17,25},{18,... | collective-permute-start | bytes 1572872 | tf_op jit(solution)/shard_map/ppermute | solution.py:24
  123.0 5.9 %collective-permute-start.25 = (bf16[528,512]{1,0:T(8,128)(2,1)S(1)}, bf16[528,512]{1,0:T(8,128)(2,1)S(1)}, u32[]{:S(2)}, u32[]{:S(2)}) collective-permute-start(bf16[528,512]{1,0:T(8,128)(2,1)S(1)} %collective-permute-done.24.rest_5_), channel_id=1, source_target_pairs={{1,5},{2,6},{5,1},{6,2},{9,13},{10,14},{13,9},{14,10},{17,21},{18,... | collective-permute-start | bytes 1622024 | tf_op jit(solution)/shard_map/ppermute | solution.py:24
  123.7 5.2 %collective-permute-start.27 = (bf16[528,512]{1,0:T(8,128)(2,1)S(1)}, bf16[528,512]{1,0:T(8,128)(2,1)S(1)}, u32[]{:S(2)}, u32[]{:S(2)}) collective-permute-start(bf16[528,512]{1,0:T(8,128)(2,1)S(1)} %collective-permute-done.26.rest_7_), channel_id=1, source_target_pairs={{1,5},{2,6},{5,1},{6,2},{9,13},{10,14},{13,9},{14,10},{17,21},{18,... | collective-permute-start | bytes 1622024 | tf_op jit(solution)/shard_map/ppermute | solution.py:24
  124.4 4.5 %collective-permute-start.21 = (bf16[512,512]{1,0:T(8,128)(2,1)S(1)}, bf16[512,512]{1,0:T(8,128)(2,1)S(1)}, u32[]{:S(2)}, u32[]{:S(2)}) collective-permute-start(bf16[512,512]{1,0:T(8,128)(2,1)S(1)} %collective-permute-done.20.rest_1_), channel_id=1, source_target_pairs={{1,5},{2,6},{5,1},{6,2},{9,13},{10,14},{13,9},{14,10},{17,21},{18,... | collective-permute-start | bytes 1572872 | tf_op jit(solution)/shard_map/ppermute | solution.py:24
  125.1 3.8 %collective-permute-start.23 = (bf16[512,512]{1,0:T(8,128)(2,1)S(1)}, bf16[512,512]{1,0:T(8,128)(2,1)S(1)}, u32[]{:S(2)}, u32[]{:S(2)}) collective-permute-start(bf16[512,512]{1,0:T(8,128)(2,1)S(1)} %collective-permute-done.22.rest_3_), channel_id=1, source_target_pairs={{1,5},{2,6},{5,1},{6,2},{9,13},{10,14},{13,9},{14,10},{17,21},{18,... | collective-permute-start | bytes 1572872 | tf_op jit(solution)/shard_map/ppermute | solution.py:24
  132.1 5.2 %collective-permute-start.30 = (bf16[528,1024]{1,0:T(8,128)(2,1)S(1)}, bf16[528,1024]{1,0:T(8,128)(2,1)S(1)}, u32[]{:S(2)}, u32[]{:S(2)}) collective-permute-start(bf16[528,1024]{1,0:T(8,128)(2,1)S(1)} %get-tuple-element.95.rest_0_.rest_1_), channel_id=1, source_target_pairs={{1,9},{2,10},{5,13},{6,14},{9,1},{10,2},{13,5},{14,6},{17,25},{18,... | collective-permute-start | bytes 3244040 | tf_op jit(solution)/shard_map/ppermute | solution.py:24
  132.9 5.3 %collective-permute-start.28 = (bf16[528,1024]{1,0:T(8,128)(2,1)S(1)}, bf16[528,1024]{1,0:T(8,128)(2,1)S(1)}, u32[]{:S(2)}, u32[]{:S(2)}) collective-permute-start(bf16[528,1024]{1,0:T(8,128)(2,1)S(1)} %get-tuple-element.95.rest_0_.rest_1_), channel_id=1, source_target_pairs={{1,2},{2,1},{5,6},{6,5},{9,10},{10,9},{13,14},{14,13},{17,18},{18,... | collective-permute-start | bytes 3244040 | tf_op jit(solution)/shard_map/ppermute | solution.py:28
  133.6 7.5 %collective-permute-start.29 = (bf16[528,1024]{1,0:T(8,128)(2,1)S(1)}, bf16[528,1024]{1,0:T(8,128)(2,1)S(1)}, u32[]{:S(2)}, u32[]{:S(2)}) collective-permute-start(bf16[528,1024]{1,0:T(8,128)(2,1)S(1)} %get-tuple-element.95.rest_0_.rest_1_), channel_id=1, source_target_pairs={{1,5},{2,6},{5,1},{6,2},{9,13},{10,14},{13,9},{14,10},{17,21},{18,... | collective-permute-start | bytes 3244040 | tf_op jit(solution)/shard_map/ppermute | solution.py:24
  137.4 3.8 %collective-permute-start.31 = (bf16[528,1024]{1,0:T(8,128)(2,1)S(1)}, bf16[528,1024]{1,0:T(8,128)(2,1)S(1)}, u32[]{:S(2)}, u32[]{:S(2)}) collective-permute-start(bf16[528,1024]{1,0:T(8,128)(2,1)S(1)} %collective-permute-done.30.rest_3_.rest_2_), channel_id=1, source_target_pairs={{1,5},{2,6},{5,1},{6,2},{9,13},{10,14},{13,9},{14,10},{17,21},{18,... | collective-permute-start | bytes 3244040 | tf_op jit(solution)/shard_map/ppermute | solution.py:24
  143.8 85.5 %collective-permute-start.32 = (bf16[528,512]{1,0:T(8,128)(2,1)}, bf16[528,512]{1,0:T(8,128)(2,1)}, u32[]{:S(2)}, u32[]{:S(2)}) collective-permute-start(bf16[528,512]{1,0:T(8,128)(2,1)} %get-tuple-element.104), channel_id=1, source_target_pairs={{1,0},{2,3},{5,4},{6,7},{9,8},{10,11},{13,12},{14,15},{17,16},{18,... | collective-permute-start | bytes 1622024 | tf_op jit(solution)/shard_map/ppermute | solution.py:36
  145.8 83.0 %collective-permute-start.34 = (f32[1,512]{1,0:T(1,128)S(1)}, f32[1,512]{1,0:T(1,128)S(1)}, u32[]{:S(2)}, u32[]{:S(2)}) collective-permute-start(f32[1,512]{1,0:T(1,128)S(1)} %slice_add_fusion), channel_id=1, source_target_pairs={{1,0},{2,3},{5,4},{6,7},{9,8},{10,11},{13,12},{14,15},{17,16},{18,... | collective-permute-start | bytes 6152 | tf_op jit(solution)/shard_map/ppermute | solution.py:36
  (18 other events, 72.9 us)

commit v10 on v6

--- a/solution.py
+++ b/solution.py
@@ -202,8 +202,9 @@
         lax.dynamic_index_in_dim(pivots, col ^ flip, 1, keepdims=True) for flip in (0, 1, 3, 2)
     ]
     pivots = jnp.concatenate(order, axis=1)
-    places = lax.broadcasted_iota(jnp.int32, (EXTRA, size), 1)
+    places = lax.broadcasted_iota(jnp.int32, (1, size), 1)
     held = ((places < 2 * share) == (col == 1)).astype(jnp.bfloat16)
+    held, *pivots = lax.optimization_barrier((held, *(pivots[turn] for turn in range(5))))
 
     def panel(turn, tiles, onto=None):
         return spread_columns(pivots[turn], tiles, size, count, onto)
@@ -266,7 +267,7 @@
 
     middle = (col == 1) | (col == 2)
     block = jnp.where(middle, reduced_o, outward(reduced_e)[:size])
-    vector = vector[:1]
+    vector = after(vector, reduced_o)[:1]
     vector = vector + swap_middle(vector)
     vector = jnp.where(middle, vector, outward(vector))
     return (block[None], lax.dynamic_slice_in_dim(vector, col * share, share, 1))

time: 231 us -> 221 us (0.957)
  waiting for transfers between devices: 104 us -> 116 us
  local copies, waits for them, and re-layouts: 10.7 us -> 2.67 us
  Pallas kernels: 60.8 us -> 54 us
  starting transfers between devices: 48 us -> 42.9 us
    unnamed x32 -> x12, local copies, waits for them, and re-layouts: 8 us -> 0.03 us
    ppermute x3, waiting for transfers between devices: 4.87 us -> 11 us  [inward(): return lax.ppermute(value, 'col', [(0, 1), (3, 2)])]
    ppermute x2, waiting for transfers between devices: 78.7 us -> 84.4 us  [outward(): return lax.ppermute(value, 'col', [(1, 0), (2, 3)])]
    pallas_call x7, Pallas kernels: 20.2 us -> 16 us  [product(): pl.pallas_call(kernel, out_shape=tuple(outs), compiler_params=pltpu.Compi...]
    ppermute x21, starting transfers between devices: 18.2 us -> 15.1 us  [swap_rows(): return lax.ppermute(value, ('row', 'col'), pairs)]
    pallas_call x13, Pallas kernels: 40.6 us -> 38 us  [spread_columns(): pl.pallas_call(kernel, out_shape=jax.ShapeDtypeStruct((size, size * count...]
  transfers between devices with their start and end apart: 35 -> 35, of which waited for: 5 -> 5; matrix products, arithmetic and copies ran while one was open for 1% -> 1% of each run, Pallas kernels for 23% -> 21%
where the time goes in v10:
time: 221 us; the launch traced here: 220 us
  waiting for transfers between devices  116 us (52%)
  Pallas kernels  54 us (24%)
  starting transfers between devices  42.9 us (19%)
  other arithmetic  2.8 us (1%)
  local copies, waits for them, and re-layouts  2.67 us (1%)
    ppermute x2, waiting for transfers between devices, outward(): return lax.ppermute(value, 'col', [(1, 0), (2, 3)])  84.4 us
    pallas_call x13, Pallas kernels, spread_columns(): pl.pallas_call(kernel, out_shape=jax.ShapeDtypeStruct((size, size * count...  38 us
    ppermute x2, waiting for transfers between devices, from_behind(): lax.ppermute(value, axis, [(i, (i + by) % devices) for i in range(devices)])  20.9 us
    ppermute x3, starting transfers between devices, inward(): return lax.ppermute(value, 'col', [(0, 1), (3, 2)])  17.3 us
    pallas_call x7, Pallas kernels, product(): pl.pallas_call(kernel, out_shape=tuple(outs), compiler_params=pltpu.Compi...  16 us
    ppermute x21, starting transfers between devices, swap_rows(): return lax.ppermute(value, ('row', 'col'), pairs)  15.1 us
    ppermute x3, waiting for transfers between devices, inward(): return lax.ppermute(value, 'col', [(0, 1), (3, 2)])  11 us
    ppermute x7, starting transfers between devices, swap_middle(): return lax.ppermute(value, 'col', [(1, 2), (2, 1)])  5.89 us
  transfers between devices with their start and end apart: 35, of which 5 were waited for; matrix products, arithmetic and copies ran while one was open for 1% of the time, Pallas kernels for 21%

profile of v10, /device:TPU:0, one launch (start us, length us, event | category | flops | bytes accessed | tf_op | source)
XLA Modules:
  0.0 220.1 jit_solution(17174657797368576944)
XLA Ops:
  0.6 2.4 %slice.37.refs_0_ = bf16[2,512,512]{2,1,0:T(8,128)(2,1)} slice(bf16[4,512,512]{2,1,0:T(8,128)(2,1)} %bitcast.22), slice={[1:4:2], [0:512:1], [0:512:1]} | slice | bytes 2097152 | tf_op jit(solution)/shard_map/slice | solution.py:184
  3.1 6.0 %collective-permute-start = (bf16[2,512,512]{2,1,0:T(8,128)(2,1)}, bf16[2,512,512]{2,1,0:T(8,128)(2,1)}, u32[]{:S(2)}, u32[]{:S(2)}) collective-permute-start(bf16[2,512,512]{2,1,0:T(8,128)(2,1)} %slice.37.refs_0_), channel_id=1, source_target_pairs={{0,1},{3,2},{4,5},{7,6},{8,9},{11,10},{12,13},{15,14},{16,17},{19,... | collective-permute-start | bytes 3145736 | tf_op jit(solution)/shard_map/ppermute | solution.py:31
  9.1 1.6 collective-permute-start.1
  13.6 6.9 %collective-permute-start.6 = (bf16[528,512]{1,0:T(8,128)(2,1)}, bf16[528,512]{1,0:T(8,128)(2,1)}, u32[]{:S(2)}, u32[]{:S(2)}) collective-permute-start(bf16[528,512]{1,0:T(8,128)(2,1)} %get-tuple-element.74), channel_id=1, source_target_pairs={{0,1},{3,2},{4,5},{7,6},{8,9},{11,10},{12,13},{15,14},{16,17},{19,... | collective-permute-start | bytes 1622024 | tf_op jit(solution)/shard_map/ppermute | solution.py:31
  20.9 3.1 %shard_map.61.refs_0_ = bf16[512,2048]{1,0:T(8,128)(2,1)S(1)} custom-call(s32[4,512]{1,0:T(4,128)S(1)} %get-tuple-element.33.q_ref, bf16[2,512,512]{2,1,0:T(8,128)(2,1)} %slice.37.refs_0_), custom_call_target="tpu_custom_call" | custom-call | flops 1073741824 | bytes 2097152 | tf_op jit(solution)/shard_map/pallas_call | solution.py:83
  24.0 3.2 %shard_map.59.refs_0_ = bf16[512,2048]{1,0:T(8,128)(2,1)S(1)} custom-call(s32[4,512]{1,0:T(4,128)S(1)} %get-tuple-element.32.q_ref, bf16[2,512,512]{2,1,0:T(8,128)(2,1)} %slice.37.refs_0_), custom_call_target="tpu_custom_call" | custom-call | flops 1073741824 | bytes 2097152 | tf_op jit(solution)/shard_map/pallas_call | solution.py:83
  27.2 4.8 %collective-permute-done.refs_1_ = bf16[2,512,512]{2,1,0:T(8,128)(2,1)} collective-permute-done((bf16[2,512,512]{2,1,0:T(8,128)(2,1)}, bf16[2,512,512]{2,1,0:T(8,128)(2,1)}, u32[]{:S(2)}, u32[]{:S(2)}) %collective-permute-start) | collective-permute-done | bytes 1048608 | tf_op jit(solution)/shard_map/ppermute | solution.py:31
  32.0 4.4 %collective-permute-start.10 = (bf16[528,512]{1,0:T(8,128)(2,1)S(1)}, bf16[528,512]{1,0:T(8,128)(2,1)S(1)}, u32[]{:S(2)}, u32[]{:S(2)}) collective-permute-start(bf16[528,512]{1,0:T(8,128)(2,1)S(1)} %copy-done.1), channel_id=1, source_target_pairs={{0,1},{3,2},{4,5},{7,6},{8,9},{11,10},{12,13},{15,14},{16,17},{19,... | collective-permute-start | bytes 1622024 | tf_op jit(solution)/shard_map/ppermute | solution.py:31
  37.1 4.5 %shard_map.63.refs_0_ = bf16[512,2048]{1,0:T(8,128)(2,1)S(1)} custom-call(s32[4,512]{1,0:T(4,128)S(1)} %get-tuple-element.33.q_ref, bf16[512,2048]{1,0:T(8,128)(2,1)S(1)} %shard_map.61.refs_0_, bf16[2,512,512]{2,1,0:T(8,128)(2,1)} %collective-permute-done.refs_1_, bf16[2,512,512]{2,1,0:T(8,128)(2,1)} %collective-permute-done.1.refs_2_), custom_call_target="tpu_custom_call" | custom-call | flops 2147483648 | bytes 2097152 | tf_op jit(solution)/shard_map/pallas_call | solution.py:83
  41.7 4.5 %shard_map.60.refs_0_ = bf16[512,2048]{1,0:T(8,128)(2,1)S(1)} custom-call(s32[4,512]{1,0:T(4,128)S(1)} %get-tuple-element.32.q_ref, bf16[512,2048]{1,0:T(8,128)(2,1)S(1)} %shard_map.59.refs_0_, bf16[2,512,512]{2,1,0:T(8,128)(2,1)} %collective-permute-done.refs_1_, bf16[2,512,512]{2,1,0:T(8,128)(2,1)} %collective-permute-done.1.refs_2_), custom_call_target="tpu_custom_call" | custom-call | flops 2147483648 | bytes 2097152 | tf_op jit(solution)/shard_map/pallas_call | solution.py:83
  47.7 6.2 %collective-permute-done.10.rest_1_ = bf16[528,512]{1,0:T(8,128)(2,1)S(1)} collective-permute-done((bf16[528,512]{1,0:T(8,128)(2,1)S(1)}, bf16[528,512]{1,0:T(8,128)(2,1)S(1)}, u32[]{:S(2)}, u32[]{:S(2)}) %collective-permute-start.10) | collective-permute-done | bytes 540704 | tf_op jit(solution)/shard_map/ppermute | solution.py:31
  56.0 1.9 shard_map.64.left_ref
  57.9 1.9 shard_map.62.left_ref
  60.6 4.5 %shard_map.65 = (bf16[528,1024]{1,0:T(8,128)(2,1)S(1)}, f32[16,512]{1,0:T(8,128)}) custom-call(bf16[512,2048]{1,0:T(8,128)(2,1)S(1)} %shard_map.64.left_ref, bf16[1,512]{1,0:T(2,128)(2,1)S(1)} %compare_convert_fusion.rest_0_, bf16[2,528,512]{2,1,0:T(8,128)(2,1)S(1)} %pad_maximum_fusion.rest_1_.rest_0_.rest_5_, ...), custom_call_target="tpu_custom_call" | custom-call | flops 2147483648 | bytes 6291456 | tf_op jit(solution)/shard_map/pallas_call | solution.py:156
  65.1 1.2 shard_map.66.refs_0_
  68.5 1.7 shard_map.67
  71.7 3.0 %shard_map.68.refs_0_ = bf16[512,2048]{1,0:T(8,128)(2,1)S(1)} custom-call(s32[4,512]{1,0:T(4,128)S(1)} %get-tuple-element.31.q_ref, bf16[512,512]{1,0:T(8,128)(2,1)S(1)} %shard_map.66.refs_0_, bf16[528,512]{1,0:T(8,128)(2,1)S(1)} %get-tuple-element.40.refs_1_), custom_call_target="tpu_custom_call" | custom-call | flops 2147483648 | bytes 2097152 | tf_op jit(solution)/shard_map/pallas_call | solution.py:83
  74.7 1.9 shard_map.69.refs_0_
  77.5 1.9 shard_map.70.left_ref
  79.5 2.8 %shard_map.71 = (bf16[528,1024]{1,0:T(8,128)(2,1)S(1)}, bf16[512,512]{1,0:T(8,128)(2,1)S(1)}, bf16[528,512]{1,0:T(8,128)(2,1)S(1)}, f32[16,512]{1,0:T(8,128)S(1)}) custom-call(bf16[512,2048]{1,0:T(8,128)(2,1)S(1)} %shard_map.70.left_ref, f32[16,512]{1,0:T(8,128)S(1)} %get-tuple-element.41.rest_0_, bf16[528,1024]{1,0:T(8,128)(2,1)S(1)} %get-tuple-element.37.rest_1_, ...), custom_call_target="tpu_custom_call" | custom-call | flops 2147483648 | bytes 6291456 | tf_op jit(solution)/shard_map/pallas_call | solution.py:156
  82.3 1.5 collective-permute-start.24
  85.1 12.5 %collective-permute-done.24.rest_5_ = bf16[528,512]{1,0:T(8,128)(2,1)S(1)} collective-permute-done((bf16[528,512]{1,0:T(8,128)(2,1)S(1)}, bf16[528,512]{1,0:T(8,128)(2,1)S(1)}, u32[]{:S(2)}, u32[]{:S(2)}) %collective-permute-start.24) | collective-permute-done | bytes 540704 | tf_op jit(solution)/shard_map/ppermute | solution.py:17
  98.2 8.5 %collective-permute-done.20.rest_1_ = bf16[512,512]{1,0:T(8,128)(2,1)S(1)} collective-permute-done((bf16[512,512]{1,0:T(8,128)(2,1)S(1)}, bf16[512,512]{1,0:T(8,128)(2,1)S(1)}, u32[]{:S(2)}, u32[]{:S(2)}) %collective-permute-start.20) | collective-permute-done | bytes 524320 | tf_op jit(solution)/shard_map/ppermute | solution.py:17
  107.4 3.0 %shard_map.72.refs_0_ = bf16[512,2048]{1,0:T(8,128)(2,1)S(1)} custom-call(s32[4,512]{1,0:T(4,128)S(1)} %get-tuple-element.30.q_ref, bf16[528,1024]{1,0:T(8,128)(2,1)S(1)} %get-tuple-element.43.refs_0_), custom_call_target="tpu_custom_call" | custom-call | flops 2147483648 | bytes 2097152 | tf_op jit(solution)/shard_map/pallas_call | solution.py:83
  113.2 3.0 %shard_map.73.left_ref = bf16[512,2048]{1,0:T(8,128)(2,1)S(1)} custom-call(s32[4,512]{1,0:T(4,128)S(1)} %get-tuple-element.30.q_ref, bf16[512,2048]{1,0:T(8,128)(2,1)S(1)} %shard_map.72.refs_0_, bf16[528,1024]{1,0:T(8,128)(2,1)S(1)} %collective-permute-done.19.refs_1_), custom_call_target="tpu_custom_call" | custom-call | flops 2147483648 | bytes 2097152 | tf_op jit(solution)/shard_map/pallas_call | solution.py:83
  116.3 2.8 %shard_map.74 = (bf16[528,1024]{1,0:T(8,128)(2,1)S(1)}, f32[16,512]{1,0:T(8,128)S(1)}) custom-call(bf16[512,2048]{1,0:T(8,128)(2,1)S(1)} %shard_map.73.left_ref, f32[16,512]{1,0:T(8,128)S(1)} %get-tuple-element.44.rest_0_, bf16[512,512]{1,0:T(8,128)(2,1)S(1)} %collective-permute-done.20.rest_1_, bf16[512,512]{1,0:T(8,128)(2,1)S(1)} %collective-permute-done.21.rest_2_, ...), custom_call_target="tpu_custom_call" | custom-call | flops 2147483648 | bytes 6291456 | tf_op jit(solution)/shard_map/pallas_call | solution.py:156
  121.3 3.0 %shard_map.75.refs_0_ = bf16[512,2048]{1,0:T(8,128)(2,1)S(1)} custom-call(s32[4,512]{1,0:T(4,128)S(1)} %get-tuple-element.29.q_ref, bf16[528,1024]{1,0:T(8,128)(2,1)S(1)} %get-tuple-element.49.refs_0_.rest_1_.rest_0_), custom_call_target="tpu_custom_call" | custom-call | flops 2147483648 | bytes 2097152 | tf_op jit(solution)/shard_map/pallas_call | solution.py:83
  125.0 3.0 %shard_map.76.left_ref = bf16[512,2048]{1,0:T(8,128)(2,1)S(1)} custom-call(s32[4,512]{1,0:T(4,128)S(1)} %get-tuple-element.29.q_ref, bf16[512,2048]{1,0:T(8,128)(2,1)S(1)} %shard_map.75.refs_0_, bf16[528,1024]{1,0:T(8,128)(2,1)S(1)} %collective-permute-done.28.refs_1_), custom_call_target="tpu_custom_call" | custom-call | flops 2147483648 | bytes 2097152 | tf_op jit(solution)/shard_map/pallas_call | solution.py:83
  128.1 1.7 shard_map.77
  129.8 1.3 collective-permute-start.32
  133.1 1.3 collective-permute-start.34
  134.4 84.4 %collective-permute-done.34 = f32[1,512]{1,0:T(1,128)S(1)} collective-permute-done((f32[1,512]{1,0:T(1,128)S(1)}, f32[1,512]{1,0:T(1,128)S(1)}, u32[]{:S(2)}, u32[]{:S(2)}) %collective-permute-start.34) | collective-permute-done | bytes 2080 | tf_op jit(solution)/shard_map/ppermute | solution.py:35
  (90 shorter events, 24.2 us)
Async XLA Ops:
  3.1 28.9 %collective-permute-start = (bf16[2,512,512]{2,1,0:T(8,128)(2,1)}, bf16[2,512,512]{2,1,0:T(8,128)(2,1)}, u32[]{:S(2)}, u32[]{:S(2)}) collective-permute-start(bf16[2,512,512]{2,1,0:T(8,128)(2,1)} %slice.37.refs_0_), channel_id=1, source_target_pairs={{0,1},{3,2},{4,5},{7,6},{8,9},{11,10},{12,13},{15,14},{16,17},{19,... | collective-permute-start | bytes 3145736 | tf_op jit(solution)/shard_map/ppermute | solution.py:31
  9.1 27.3 %collective-permute-start.1 = (bf16[2,512,512]{2,1,0:T(8,128)(2,1)}, bf16[2,512,512]{2,1,0:T(8,128)(2,1)}, u32[]{:S(2)}, u32[]{:S(2)}) collective-permute-start(bf16[2,512,512]{2,1,0:T(8,128)(2,1)} %slice.37.refs_0_), channel_id=1, source_target_pairs={{1,2},{2,1},{5,6},{6,5},{9,10},{10,9},{13,14},{14,13},{17,18},{18,... | collective-permute-start | bytes 3145736 | tf_op jit(solution)/shard_map/ppermute | solution.py:27
  12.1 34.9 %collective-permute-start.4 = (bf16[2,528,512]{2,1,0:T(8,128)(2,1)S(1)}, bf16[2,528,512]{2,1,0:T(8,128)(2,1)S(1)}, u32[]{:S(2)}, u32[]{:S(2)}) collective-permute-start(bf16[2,528,512]{2,1,0:T(8,128)(2,1)S(1)} %pad_maximum_fusion.rest_1_.rest_0_.rest_5_), channel_id=1, source_target_pairs={{1,9},{2,10},{5,13},{6,14},{9,1},{10,2},{13,5},{14,6},{17,25},{18,... | collective-permute-start | bytes 3244040 | tf_op jit(solution)/shard_map/ppermute | solution.py:23
  12.8 47.0 %collective-permute-start.3 = (bf16[2,528,512]{2,1,0:T(8,128)(2,1)S(1)}, bf16[2,528,512]{2,1,0:T(8,128)(2,1)S(1)}, u32[]{:S(2)}, u32[]{:S(2)}) collective-permute-start(bf16[2,528,512]{2,1,0:T(8,128)(2,1)S(1)} %pad_maximum_fusion.rest_1_.rest_0_.rest_5_), channel_id=1, source_target_pairs={{1,5},{2,6},{5,1},{6,2},{9,13},{10,14},{13,9},{14,10},{17,21},{18,... | collective-permute-start | bytes 3244040 | tf_op jit(solution)/shard_map/ppermute | solution.py:23
  13.6 32.7 %collective-permute-start.6 = (bf16[528,512]{1,0:T(8,128)(2,1)}, bf16[528,512]{1,0:T(8,128)(2,1)}, u32[]{:S(2)}, u32[]{:S(2)}) collective-permute-start(bf16[528,512]{1,0:T(8,128)(2,1)} %get-tuple-element.74), channel_id=1, source_target_pairs={{0,1},{3,2},{4,5},{7,6},{8,9},{11,10},{12,13},{15,14},{16,17},{19,... | collective-permute-start | bytes 1622024 | tf_op jit(solution)/shard_map/ppermute | solution.py:31
  32.0 21.9 %collective-permute-start.10 = (bf16[528,512]{1,0:T(8,128)(2,1)S(1)}, bf16[528,512]{1,0:T(8,128)(2,1)S(1)}, u32[]{:S(2)}, u32[]{:S(2)}) collective-permute-start(bf16[528,512]{1,0:T(8,128)(2,1)S(1)} %copy-done.1), channel_id=1, source_target_pairs={{0,1},{3,2},{4,5},{7,6},{8,9},{11,10},{12,13},{15,14},{16,17},{19,... | collective-permute-start | bytes 1622024 | tf_op jit(solution)/shard_map/ppermute | solution.py:31
  36.4 18.9 %collective-permute-start.2 = (bf16[2,512,512]{2,1,0:T(8,128)(2,1)}, bf16[2,512,512]{2,1,0:T(8,128)(2,1)S(1)}, u32[]{:S(2)}, u32[]{:S(2)}) collective-permute-start(bf16[2,512,512]{2,1,0:T(8,128)(2,1)} %collective-permute-done.refs_1_), channel_id=1, source_target_pairs={{1,2},{2,1},{5,6},{6,5},{9,10},{10,9},{13,14},{14,13},{17,18},{18,... | collective-permute-start | bytes 3145736 | tf_op jit(solution)/shard_map/ppermute | solution.py:27
  46.2 8.4 %collective-permute-start.8 = (bf16[528,512]{1,0:T(8,128)(2,1)}, bf16[528,512]{1,0:T(8,128)(2,1)S(1)}, u32[]{:S(2)}, u32[]{:S(2)}) collective-permute-start(bf16[528,512]{1,0:T(8,128)(2,1)} %collective-permute-done.6.rest_5_), channel_id=1, source_target_pairs={{1,9},{2,10},{5,13},{6,14},{9,1},{10,2},{13,5},{14,6},{17,25},{18,... | collective-permute-start | bytes 1622024 | tf_op jit(solution)/shard_map/ppermute | solution.py:23
  46.9 13.6 %collective-permute-start.5 = (bf16[2,528,512]{2,1,0:T(8,128)(2,1)S(1)}, bf16[2,528,512]{2,1,0:T(8,128)(2,1)S(1)}, u32[]{:S(2)}, u32[]{:S(2)}) collective-permute-start(bf16[2,528,512]{2,1,0:T(8,128)(2,1)S(1)} %collective-permute-done.4.rest_3_.rest_2_.rest_7_), channel_id=1, source_target_pairs={{1,5},{2,6},{5,1},{6,2},{9,13},{10,14},{13,9},{14,10},{17,21},{18,... | collective-permute-start | bytes 3244040 | tf_op jit(solution)/shard_map/ppermute | solution.py:23
  53.9 6.7 %collective-permute-start.7 = (bf16[528,512]{1,0:T(8,128)(2,1)}, bf16[528,512]{1,0:T(8,128)(2,1)S(1)}, u32[]{:S(2)}, u32[]{:S(2)}) collective-permute-start(bf16[528,512]{1,0:T(8,128)(2,1)} %collective-permute-done.6.rest_5_), channel_id=1, source_target_pairs={{1,5},{2,6},{5,1},{6,2},{9,13},{10,14},{13,9},{14,10},{17,21},{18,... | collective-permute-start | bytes 1622024 | tf_op jit(solution)/shard_map/ppermute | solution.py:23
  54.6 6.0 %collective-permute-start.9 = (bf16[528,512]{1,0:T(8,128)(2,1)S(1)}, bf16[528,512]{1,0:T(8,128)(2,1)S(1)}, u32[]{:S(2)}, u32[]{:S(2)}) collective-permute-start(bf16[528,512]{1,0:T(8,128)(2,1)S(1)} %collective-permute-done.8.rest_7_), channel_id=1, source_target_pairs={{1,5},{2,6},{5,1},{6,2},{9,13},{10,14},{13,9},{14,10},{17,21},{18,... | collective-permute-start | bytes 1622024 | tf_op jit(solution)/shard_map/ppermute | solution.py:23
  55.3 11.0 %collective-permute-start.12 = (bf16[528,512]{1,0:T(8,128)(2,1)S(1)}, bf16[528,512]{1,0:T(8,128)(2,1)S(1)}, u32[]{:S(2)}, u32[]{:S(2)}) collective-permute-start(bf16[528,512]{1,0:T(8,128)(2,1)S(1)} %collective-permute-done.10.rest_1_), channel_id=1, source_target_pairs={{1,9},{2,10},{5,13},{6,14},{9,1},{10,2},{13,5},{14,6},{17,25},{18,... | collective-permute-start | bytes 1622024 | tf_op jit(solution)/shard_map/ppermute | solution.py:23
  59.9 8.6 %collective-permute-start.11 = (bf16[528,512]{1,0:T(8,128)(2,1)S(1)}, bf16[528,512]{1,0:T(8,128)(2,1)S(1)}, u32[]{:S(2)}, u32[]{:S(2)}) collective-permute-start(bf16[528,512]{1,0:T(8,128)(2,1)S(1)} %collective-permute-done.10.rest_1_), channel_id=1, source_target_pairs={{1,5},{2,6},{5,1},{6,2},{9,13},{10,14},{13,9},{14,10},{17,21},{18,... | collective-permute-start | bytes 1622024 | tf_op jit(solution)/shard_map/ppermute | solution.py:23
  67.1 9.6 %collective-permute-start.17 = (bf16[528,1024]{1,0:T(8,128)(2,1)S(1)}, bf16[528,1024]{1,0:T(8,128)(2,1)S(1)}, u32[]{:S(2)}, u32[]{:S(2)}) collective-permute-start(bf16[528,1024]{1,0:T(8,128)(2,1)S(1)} %get-tuple-element.37.rest_1_), channel_id=1, source_target_pairs={{1,9},{2,10},{5,13},{6,14},{9,1},{10,2},{13,5},{14,6},{17,25},{18,... | collective-permute-start | bytes 3244040 | tf_op jit(solution)/shard_map/ppermute | solution.py:23
  67.8 6.9 %collective-permute-start.14 = (bf16[512,512]{1,0:T(8,128)(2,1)S(1)}, bf16[512,512]{1,0:T(8,128)(2,1)S(1)}, u32[]{:S(2)}, u32[]{:S(2)}) collective-permute-start(bf16[512,512]{1,0:T(8,128)(2,1)S(1)} %shard_map.66.refs_0_), channel_id=1, source_target_pairs={{1,2},{2,1},{5,6},{6,5},{9,10},{10,9},{13,14},{14,13},{17,18},{18,... | collective-permute-start | bytes 1572872 | tf_op jit(solution)/shard_map/ppermute | solution.py:27
  70.2 6.4 %collective-permute-start.15 = (bf16[528,512]{1,0:T(8,128)(2,1)S(1)}, bf16[528,512]{1,0:T(8,128)(2,1)S(1)}, u32[]{:S(2)}, u32[]{:S(2)}) collective-permute-start(bf16[528,512]{1,0:T(8,128)(2,1)S(1)} %get-tuple-element.40.refs_1_), channel_id=1, source_target_pairs={{1,2},{2,1},{5,6},{6,5},{9,10},{10,9},{13,14},{14,13},{17,18},{18,... | collective-permute-start | bytes 1622024 | tf_op jit(solution)/shard_map/ppermute | solution.py:27
  70.9 8.5 %collective-permute-start.16 = (bf16[528,1024]{1,0:T(8,128)(2,1)S(1)}, bf16[528,1024]{1,0:T(8,128)(2,1)S(1)}, u32[]{:S(2)}, u32[]{:S(2)}) collective-permute-start(bf16[528,1024]{1,0:T(8,128)(2,1)S(1)} %get-tuple-element.37.rest_1_), channel_id=1, source_target_pairs={{1,5},{2,6},{5,1},{6,2},{9,13},{10,14},{13,9},{14,10},{17,21},{18,... | collective-permute-start | bytes 3244040 | tf_op jit(solution)/shard_map/ppermute | solution.py:23
  82.3 15.2 %collective-permute-start.24 = (bf16[528,512]{1,0:T(8,128)(2,1)S(1)}, bf16[528,512]{1,0:T(8,128)(2,1)S(1)}, u32[]{:S(2)}, u32[]{:S(2)}) collective-permute-start(bf16[528,512]{1,0:T(8,128)(2,1)S(1)} %get-tuple-element.47), channel_id=1, source_target_pairs={{0,16},{16,0},{1,17},{17,1},{2,18},{18,2},{3,19},{19,3},{4,20},{20... | collective-permute-start | bytes 1622024 | tf_op jit(solution)/shard_map/ppermute | solution.py:17
  83.8 22.9 %collective-permute-start.20 = (bf16[512,512]{1,0:T(8,128)(2,1)S(1)}, bf16[512,512]{1,0:T(8,128)(2,1)S(1)}, u32[]{:S(2)}, u32[]{:S(2)}) collective-permute-start(bf16[512,512]{1,0:T(8,128)(2,1)S(1)} %get-tuple-element.45), channel_id=1, source_target_pairs={{0,16},{16,0},{1,17},{17,1},{2,18},{18,2},{3,19},{19,3},{4,20},{20... | collective-permute-start | bytes 1572872 | tf_op jit(solution)/shard_map/ppermute | solution.py:17
  84.3 28.9 %collective-permute-start.19 = (bf16[528,1024]{1,0:T(8,128)(2,1)S(1)}, bf16[528,1024]{1,0:T(8,128)(2,1)S(1)}, u32[]{:S(2)}, u32[]{:S(2)}) collective-permute-start(bf16[528,1024]{1,0:T(8,128)(2,1)S(1)} %get-tuple-element.43.refs_0_), channel_id=1, source_target_pairs={{1,2},{2,1},{5,6},{6,5},{9,10},{10,9},{13,14},{14,13},{17,18},{18,... | collective-permute-start | bytes 3244040 | tf_op jit(solution)/shard_map/ppermute | solution.py:27
  97.5 13.6 %collective-permute-start.26 = (bf16[528,512]{1,0:T(8,128)(2,1)S(1)}, bf16[528,512]{1,0:T(8,128)(2,1)S(1)}, u32[]{:S(2)}, u32[]{:S(2)}) collective-permute-start(bf16[528,512]{1,0:T(8,128)(2,1)S(1)} %collective-permute-done.24.rest_5_), channel_id=1, source_target_pairs={{1,9},{2,10},{5,13},{6,14},{9,1},{10,2},{13,5},{14,6},{17,25},{18,... | collective-permute-start | bytes 1622024 | tf_op jit(solution)/shard_map/ppermute | solution.py:23
  106.7 5.8 %collective-permute-start.22 = (bf16[512,512]{1,0:T(8,128)(2,1)S(1)}, bf16[512,512]{1,0:T(8,128)(2,1)S(1)}, u32[]{:S(2)}, u32[]{:S(2)}) collective-permute-start(bf16[512,512]{1,0:T(8,128)(2,1)S(1)} %collective-permute-done.20.rest_1_), channel_id=1, source_target_pairs={{1,9},{2,10},{5,13},{6,14},{9,1},{10,2},{13,5},{14,6},{17,25},{18,... | collective-permute-start | bytes 1572872 | tf_op jit(solution)/shard_map/ppermute | solution.py:23
  110.4 5.9 %collective-permute-start.25 = (bf16[528,512]{1,0:T(8,128)(2,1)S(1)}, bf16[528,512]{1,0:T(8,128)(2,1)S(1)}, u32[]{:S(2)}, u32[]{:S(2)}) collective-permute-start(bf16[528,512]{1,0:T(8,128)(2,1)S(1)} %collective-permute-done.24.rest_5_), channel_id=1, source_target_pairs={{1,5},{2,6},{5,1},{6,2},{9,13},{10,14},{13,9},{14,10},{17,21},{18,... | collective-permute-start | bytes 1622024 | tf_op jit(solution)/shard_map/ppermute | solution.py:23
  111.1 5.2 %collective-permute-start.27 = (bf16[528,512]{1,0:T(8,128)(2,1)S(1)}, bf16[528,512]{1,0:T(8,128)(2,1)S(1)}, u32[]{:S(2)}, u32[]{:S(2)}) collective-permute-start(bf16[528,512]{1,0:T(8,128)(2,1)S(1)} %collective-permute-done.26.rest_7_), channel_id=1, source_target_pairs={{1,5},{2,6},{5,1},{6,2},{9,13},{10,14},{13,9},{14,10},{17,21},{18,... | collective-permute-start | bytes 1622024 | tf_op jit(solution)/shard_map/ppermute | solution.py:23
  111.8 4.4 %collective-permute-start.21 = (bf16[512,512]{1,0:T(8,128)(2,1)S(1)}, bf16[512,512]{1,0:T(8,128)(2,1)S(1)}, u32[]{:S(2)}, u32[]{:S(2)}) collective-permute-start(bf16[512,512]{1,0:T(8,128)(2,1)S(1)} %collective-permute-done.20.rest_1_), channel_id=1, source_target_pairs={{1,5},{2,6},{5,1},{6,2},{9,13},{10,14},{13,9},{14,10},{17,21},{18,... | collective-permute-start | bytes 1572872 | tf_op jit(solution)/shard_map/ppermute | solution.py:23
  112.5 3.7 %collective-permute-start.23 = (bf16[512,512]{1,0:T(8,128)(2,1)S(1)}, bf16[512,512]{1,0:T(8,128)(2,1)S(1)}, u32[]{:S(2)}, u32[]{:S(2)}) collective-permute-start(bf16[512,512]{1,0:T(8,128)(2,1)S(1)} %collective-permute-done.22.rest_3_), channel_id=1, source_target_pairs={{1,5},{2,6},{5,1},{6,2},{9,13},{10,14},{13,9},{14,10},{17,21},{18,... | collective-permute-start | bytes 1572872 | tf_op jit(solution)/shard_map/ppermute | solution.py:23
  119.0 5.2 %collective-permute-start.30 = (bf16[528,1024]{1,0:T(8,128)(2,1)S(1)}, bf16[528,1024]{1,0:T(8,128)(2,1)S(1)}, u32[]{:S(2)}, u32[]{:S(2)}) collective-permute-start(bf16[528,1024]{1,0:T(8,128)(2,1)S(1)} %get-tuple-element.49.refs_0_.rest_1_.rest_0_), channel_id=1, source_target_pairs={{1,9},{2,10},{5,13},{6,14},{9,1},{10,2},{13,5},{14,6},{17,25},{18,... | collective-permute-start | bytes 3244040 | tf_op jit(solution)/shard_map/ppermute | solution.py:23
  119.8 5.2 %collective-permute-start.28 = (bf16[528,1024]{1,0:T(8,128)(2,1)S(1)}, bf16[528,1024]{1,0:T(8,128)(2,1)S(1)}, u32[]{:S(2)}, u32[]{:S(2)}) collective-permute-start(bf16[528,1024]{1,0:T(8,128)(2,1)S(1)} %get-tuple-element.49.refs_0_.rest_1_.rest_0_), channel_id=1, source_target_pairs={{1,2},{2,1},{5,6},{6,5},{9,10},{10,9},{13,14},{14,13},{17,18},{18,... | collective-permute-start | bytes 3244040 | tf_op jit(solution)/shard_map/ppermute | solution.py:27
  120.5 7.5 %collective-permute-start.29 = (bf16[528,1024]{1,0:T(8,128)(2,1)S(1)}, bf16[528,1024]{1,0:T(8,128)(2,1)S(1)}, u32[]{:S(2)}, u32[]{:S(2)}) collective-permute-start(bf16[528,1024]{1,0:T(8,128)(2,1)S(1)} %get-tuple-element.49.refs_0_.rest_1_.rest_0_), channel_id=1, source_target_pairs={{1,5},{2,6},{5,1},{6,2},{9,13},{10,14},{13,9},{14,10},{17,21},{18,... | collective-permute-start | bytes 3244040 | tf_op jit(solution)/shard_map/ppermute | solution.py:23
  124.3 3.8 %collective-permute-start.31 = (bf16[528,1024]{1,0:T(8,128)(2,1)S(1)}, bf16[528,1024]{1,0:T(8,128)(2,1)S(1)}, u32[]{:S(2)}, u32[]{:S(2)}) collective-permute-start(bf16[528,1024]{1,0:T(8,128)(2,1)S(1)} %collective-permute-done.30.rest_3_.rest_2_), channel_id=1, source_target_pairs={{1,5},{2,6},{5,1},{6,2},{9,13},{10,14},{13,9},{14,10},{17,21},{18,... | collective-permute-start | bytes 3244040 | tf_op jit(solution)/shard_map/ppermute | solution.py:23
  129.8 89.5 %collective-permute-start.32 = (bf16[528,512]{1,0:T(8,128)(2,1)S(1)}, bf16[528,512]{1,0:T(8,128)(2,1)S(1)}, u32[]{:S(2)}, u32[]{:S(2)}) collective-permute-start(bf16[528,512]{1,0:T(8,128)(2,1)S(1)} %get-tuple-element.52), channel_id=1, source_target_pairs={{1,0},{2,3},{5,4},{6,7},{9,8},{10,11},{13,12},{14,15},{17,16},{18,... | collective-permute-start | bytes 1622024 | tf_op jit(solution)/shard_map/ppermute | solution.py:35
  133.1 85.7 %collective-permute-start.34 = (f32[1,512]{1,0:T(1,128)S(1)}, f32[1,512]{1,0:T(1,128)S(1)}, u32[]{:S(2)}, u32[]{:S(2)}) collective-permute-start(f32[1,512]{1,0:T(1,128)S(1)} %slice_add_fusion), channel_id=1, source_target_pairs={{1,0},{2,3},{5,4},{6,7},{9,8},{10,11},{13,12},{14,15},{17,16},{18,... | collective-permute-start | bytes 6152 | tf_op jit(solution)/shard_map/ppermute | solution.py:35
  (8 other events, 48.5 us)

commit v11 on v10

--- a/solution.py
+++ b/solution.py
@@ -181,17 +181,6 @@
     position = lax.axis_index("loop")
     positions = lax.axis_size("loop")
 
-    lefts = blocks[1::2]
-    riding = jnp.broadcast_to(interval_residuals[0].reshape(1, -1), (EXTRA, size))
-    tiles = [jnp.concatenate([blocks[k], riding], axis=0) for k in (0, 2)]
-    rights = jnp.stack(tiles)
-    ends_left = inward(lefts)
-    lefts_other = swap_middle(lefts)
-    rights_across = swap_rows(rights, 2)
-    end_lower = inward(tiles[0])
-    end_upper = inward(tiles[1])
-    rights_beside = swap_rows(rights, 1)
-
     own = lax.dynamic_index_in_dim(boundary_pivots, position, 0, keepdims=True)
     back = lax.dynamic_index_in_dim(
         boundary_pivots, (position + positions - 1) % positions, 0, keepdims=True
@@ -204,7 +193,21 @@
     pivots = jnp.concatenate(order, axis=1)
     places = lax.broadcasted_iota(jnp.int32, (1, size), 1)
     held = ((places < 2 * share) == (col == 1)).astype(jnp.bfloat16)
-    held, *pivots = lax.optimization_barrier((held, *(pivots[turn] for turn in range(5))))
+    pivots = [pivots[turn] for turn in range(5)]
+
+    lefts = blocks[1::2]
+    riding = jnp.broadcast_to(interval_residuals[0].reshape(1, -1), (EXTRA, size))
+    tiles = [jnp.concatenate([blocks[k], riding], axis=0) for k in (0, 2)]
+    rights = jnp.stack(tiles)
+    lefts, rights, tiles, held, pivots = lax.optimization_barrier(
+        (lefts, rights, tiles, held, pivots)
+    )
+    ends_left = inward(lefts)
+    lefts_other = swap_middle(lefts)
+    rights_across = swap_rows(rights, 2)
+    end_lower = inward(tiles[0])
+    end_upper = inward(tiles[1])
+    rights_beside = swap_rows(rights, 1)
 
     def panel(turn, tiles, onto=None):
         return spread_columns(pivots[turn], tiles, size, count, onto)

time: 221 us -> 221 us (level)
  waiting for transfers between devices: 116 us -> 123 us
  Pallas kernels: 54 us -> 47.3 us
    ppermute x3, waiting for transfers between devices: 11 us -> 19 us  [inward(): return lax.ppermute(value, 'col', [(0, 1), (3, 2)])]
    pallas_call x13, Pallas kernels: 38 us -> 32.4 us  [spread_columns(): pl.pallas_call(kernel, out_shape=jax.ShapeDtypeStruct((size, size * count...]
    slice x1, local copies, waits for them, and re-layouts: 2.41 us -> 0.07 us  [shards(): lefts = blocks[1::2]]
  transfers between devices with their start and end apart: 35 -> 35, of which waited for: 5 -> 6; matrix products, arithmetic and copies ran while one was open for 1% -> 0% of each run, Pallas kernels for 21% -> 18%
where the time goes in v11:
time: 221 us; the launch traced here: 220 us
  waiting for transfers between devices  123 us (56%)
  Pallas kernels  47.3 us (21%)
  starting transfers between devices  42 us (19%)
  local copies, waits for them, and re-layouts  3.17 us (1%)
  other arithmetic  2.55 us (1%)
    ppermute x2, waiting for transfers between devices, outward(): return lax.ppermute(value, 'col', [(1, 0), (2, 3)])  83.1 us
    pallas_call x13, Pallas kernels, spread_columns(): pl.pallas_call(kernel, out_shape=jax.ShapeDtypeStruct((size, size * count...  32.4 us
    ppermute x2, waiting for transfers between devices, from_behind(): lax.ppermute(value, axis, [(i, (i + by) % devices) for i in range(devices)])  20.9 us
    ppermute x3, waiting for transfers between devices, inward(): return lax.ppermute(value, 'col', [(0, 1), (3, 2)])  19 us
    ppermute x3, starting transfers between devices, inward(): return lax.ppermute(value, 'col', [(0, 1), (3, 2)])  17.3 us
    ppermute x21, starting transfers between devices, swap_rows(): return lax.ppermute(value, ('row', 'col'), pairs)  15.1 us
    pallas_call x7, Pallas kernels, product(): pl.pallas_call(kernel, out_shape=tuple(outs), compiler_params=pltpu.Compi...  14.9 us
    ppermute x7, starting transfers between devices, swap_middle(): return lax.ppermute(value, 'col', [(1, 2), (2, 1)])  4.98 us
  transfers between devices with their start and end apart: 35, of which 6 were waited for; matrix products, arithmetic and copies ran while one was open for 0% of the time, Pallas kernels for 18%

profile of v11, /device:TPU:0, one launch (start us, length us, event | category | flops | bytes accessed | tf_op | source)
XLA Modules:
  0.0 219.6 jit_solution(13976260632483954640)
XLA Ops:
  2.7 1.4 slice_bitcast_fusion.1
  5.1 5.0 %collective-permute-start = (bf16[2,512,512]{2,1,0:T(8,128)(2,1)S(1)}, bf16[2,512,512]{2,1,0:T(8,128)(2,1)S(1)}, u32[]{:S(2)}, u32[]{:S(2)}) collective-permute-start(bf16[2,512,512]{2,1,0:T(8,128)(2,1)S(1)} %slice.32.refs_0_), channel_id=1, source_target_pairs={{0,1},{3,2},{4,5},{7,6},{8,9},{11,10},{12,13},{15,14},{16,17},{19,... | collective-permute-start | bytes 3145736 | tf_op jit(solution)/shard_map/ppermute | solution.py:31
  12.3 7.9 %collective-permute-start.6 = (bf16[528,512]{1,0:T(8,128)(2,1)S(1)}, bf16[528,512]{1,0:T(8,128)(2,1)S(1)}, u32[]{:S(2)}, u32[]{:S(2)}) collective-permute-start(bf16[528,512]{1,0:T(8,128)(2,1)S(1)} %get-tuple-element.42), channel_id=1, source_target_pairs={{0,1},{3,2},{4,5},{7,6},{8,9},{11,10},{12,13},{15,14},{16,17},{19,... | collective-permute-start | bytes 1622024 | tf_op jit(solution)/shard_map/ppermute | solution.py:31
  20.3 1.9 shard_map.61.refs_0_
  22.2 1.9 shard_map.59.refs_0_
  24.1 9.5 %collective-permute-done.refs_1_ = bf16[2,512,512]{2,1,0:T(8,128)(2,1)S(1)} collective-permute-done((bf16[2,512,512]{2,1,0:T(8,128)(2,1)S(1)}, bf16[2,512,512]{2,1,0:T(8,128)(2,1)S(1)}, u32[]{:S(2)}, u32[]{:S(2)}) %collective-permute-start) | collective-permute-done | bytes 1048608 | tf_op jit(solution)/shard_map/ppermute | solution.py:31
  33.6 4.4 %collective-permute-start.10 = (bf16[528,512]{1,0:T(8,128)(2,1)S(1)}, bf16[528,512]{1,0:T(8,128)(2,1)S(1)}, u32[]{:S(2)}, u32[]{:S(2)}) collective-permute-start(bf16[528,512]{1,0:T(8,128)(2,1)S(1)} %get-tuple-element.46), channel_id=1, source_target_pairs={{0,1},{3,2},{4,5},{7,6},{8,9},{11,10},{12,13},{15,14},{16,17},{19,... | collective-permute-start | bytes 1622024 | tf_op jit(solution)/shard_map/ppermute | solution.py:31
  38.8 3.0 %shard_map.63.refs_0_ = bf16[512,2048]{1,0:T(8,128)(2,1)S(1)} custom-call(s32[4,512]{1,0:T(4,128)S(1)} %get-tuple-element.38.q_ref, bf16[512,2048]{1,0:T(8,128)(2,1)S(1)} %shard_map.61.refs_0_, bf16[2,512,512]{2,1,0:T(8,128)(2,1)S(1)} %collective-permute-done.refs_1_, bf16[2,512,512]{2,1,0:T(8,128)(2,1)S(1)} %collective-permute-done.1.refs_2_), custom_call_target="tpu_custom_call" | custom-call | flops 2147483648 | bytes 2097152 | tf_op jit(solution)/shard_map/pallas_call | solution.py:83
  41.8 3.0 %shard_map.60.refs_0_ = bf16[512,2048]{1,0:T(8,128)(2,1)S(1)} custom-call(s32[4,512]{1,0:T(4,128)S(1)} %get-tuple-element.36.q_ref, bf16[512,2048]{1,0:T(8,128)(2,1)S(1)} %shard_map.59.refs_0_, bf16[2,512,512]{2,1,0:T(8,128)(2,1)S(1)} %collective-permute-done.refs_1_, bf16[2,512,512]{2,1,0:T(8,128)(2,1)S(1)} %collective-permute-done.1.refs_2_), custom_call_target="tpu_custom_call" | custom-call | flops 2147483648 | bytes 2097152 | tf_op jit(solution)/shard_map/pallas_call | solution.py:83
  46.6 9.0 %collective-permute-done.10.rest_1_ = bf16[528,512]{1,0:T(8,128)(2,1)S(1)} collective-permute-done((bf16[528,512]{1,0:T(8,128)(2,1)S(1)}, bf16[528,512]{1,0:T(8,128)(2,1)S(1)}, u32[]{:S(2)}, u32[]{:S(2)}) %collective-permute-start.10) | collective-permute-done | bytes 540704 | tf_op jit(solution)/shard_map/ppermute | solution.py:31
  57.8 1.9 shard_map.64.left_ref
  59.7 1.9 shard_map.62.left_ref
  62.3 3.4 %shard_map.65 = (bf16[528,1024]{1,0:T(8,128)(2,1)S(1)}, f32[16,512]{1,0:T(8,128)}) custom-call(bf16[512,2048]{1,0:T(8,128)(2,1)S(1)} %shard_map.64.left_ref, bf16[1,512]{1,0:T(2,128)(2,1)S(1)} %compare_convert_fusion.rest_0_, bf16[2,528,512]{2,1,0:T(8,128)(2,1)S(1)} %pad_maximum_fusion.rest_1_.rest_0_.rest_5_, ...), custom_call_target="tpu_custom_call" | custom-call | flops 2147483648 | bytes 6291456 | tf_op jit(solution)/shard_map/pallas_call | solution.py:156
  65.8 1.2 shard_map.66.refs_0_
  69.2 1.7 shard_map.67
  72.4 3.0 %shard_map.68.refs_0_ = bf16[512,2048]{1,0:T(8,128)(2,1)S(1)} custom-call(s32[4,512]{1,0:T(4,128)S(1)} %get-tuple-element.35.q_ref, bf16[512,512]{1,0:T(8,128)(2,1)S(1)} %shard_map.66.refs_0_, bf16[528,512]{1,0:T(8,128)(2,1)S(1)} %get-tuple-element.48.refs_1_), custom_call_target="tpu_custom_call" | custom-call | flops 2147483648 | bytes 2097152 | tf_op jit(solution)/shard_map/pallas_call | solution.py:83
  75.4 1.9 shard_map.69.refs_0_
  78.2 1.9 shard_map.70.left_ref
  80.2 2.8 %shard_map.71 = (bf16[528,1024]{1,0:T(8,128)(2,1)S(1)}, bf16[512,512]{1,0:T(8,128)(2,1)S(1)}, bf16[528,512]{1,0:T(8,128)(2,1)S(1)}, f32[16,512]{1,0:T(8,128)S(1)}) custom-call(bf16[512,2048]{1,0:T(8,128)(2,1)S(1)} %shard_map.70.left_ref, f32[16,512]{1,0:T(8,128)S(1)} %get-tuple-element.49.rest_0_, bf16[528,1024]{1,0:T(8,128)(2,1)S(1)} %get-tuple-element.44.rest_1_, ...), custom_call_target="tpu_custom_call" | custom-call | flops 2147483648 | bytes 6291456 | tf_op jit(solution)/shard_map/pallas_call | solution.py:156
  83.0 1.5 collective-permute-start.24
  85.8 12.5 %collective-permute-done.24.rest_5_ = bf16[528,512]{1,0:T(8,128)(2,1)S(1)} collective-permute-done((bf16[528,512]{1,0:T(8,128)(2,1)S(1)}, bf16[528,512]{1,0:T(8,128)(2,1)S(1)}, u32[]{:S(2)}, u32[]{:S(2)}) %collective-permute-start.24) | collective-permute-done | bytes 540704 | tf_op jit(solution)/shard_map/ppermute | solution.py:17
  98.9 8.5 %collective-permute-done.20.rest_1_ = bf16[512,512]{1,0:T(8,128)(2,1)S(1)} collective-permute-done((bf16[512,512]{1,0:T(8,128)(2,1)S(1)}, bf16[512,512]{1,0:T(8,128)(2,1)S(1)}, u32[]{:S(2)}, u32[]{:S(2)}) %collective-permute-start.20) | collective-permute-done | bytes 524320 | tf_op jit(solution)/shard_map/ppermute | solution.py:17
  108.1 3.0 %shard_map.72.refs_0_ = bf16[512,2048]{1,0:T(8,128)(2,1)S(1)} custom-call(s32[4,512]{1,0:T(4,128)S(1)} %get-tuple-element.34.q_ref, bf16[528,1024]{1,0:T(8,128)(2,1)S(1)} %get-tuple-element.51.refs_0_), custom_call_target="tpu_custom_call" | custom-call | flops 2147483648 | bytes 2097152 | tf_op jit(solution)/shard_map/pallas_call | solution.py:83
  113.9 3.0 %shard_map.73.left_ref = bf16[512,2048]{1,0:T(8,128)(2,1)S(1)} custom-call(s32[4,512]{1,0:T(4,128)S(1)} %get-tuple-element.34.q_ref, bf16[512,2048]{1,0:T(8,128)(2,1)S(1)} %shard_map.72.refs_0_, bf16[528,1024]{1,0:T(8,128)(2,1)S(1)} %collective-permute-done.19.refs_1_), custom_call_target="tpu_custom_call" | custom-call | flops 2147483648 | bytes 2097152 | tf_op jit(solution)/shard_map/pallas_call | solution.py:83
  117.0 2.8 %shard_map.74 = (bf16[528,1024]{1,0:T(8,128)(2,1)S(1)}, f32[16,512]{1,0:T(8,128)S(1)}) custom-call(bf16[512,2048]{1,0:T(8,128)(2,1)S(1)} %shard_map.73.left_ref, f32[16,512]{1,0:T(8,128)S(1)} %get-tuple-element.52.rest_0_, bf16[512,512]{1,0:T(8,128)(2,1)S(1)} %collective-permute-done.20.rest_1_, bf16[512,512]{1,0:T(8,128)(2,1)S(1)} %collective-permute-done.21.rest_2_, ...), custom_call_target="tpu_custom_call" | custom-call | flops 2147483648 | bytes 6291456 | tf_op jit(solution)/shard_map/pallas_call | solution.py:156
  122.0 3.0 %shard_map.75.refs_0_ = bf16[512,2048]{1,0:T(8,128)(2,1)S(1)} custom-call(s32[4,512]{1,0:T(4,128)S(1)} %get-tuple-element.33.q_ref, bf16[528,1024]{1,0:T(8,128)(2,1)S(1)} %get-tuple-element.57.refs_0_.rest_1_.rest_0_), custom_call_target="tpu_custom_call" | custom-call | flops 2147483648 | bytes 2097152 | tf_op jit(solution)/shard_map/pallas_call | solution.py:83
  125.8 3.0 %shard_map.76.left_ref = bf16[512,2048]{1,0:T(8,128)(2,1)S(1)} custom-call(s32[4,512]{1,0:T(4,128)S(1)} %get-tuple-element.33.q_ref, bf16[512,2048]{1,0:T(8,128)(2,1)S(1)} %shard_map.75.refs_0_, bf16[528,1024]{1,0:T(8,128)(2,1)S(1)} %collective-permute-done.28.refs_1_), custom_call_target="tpu_custom_call" | custom-call | flops 2147483648 | bytes 2097152 | tf_op jit(solution)/shard_map/pallas_call | solution.py:83
  128.8 1.7 shard_map.77
  130.5 1.3 collective-permute-start.32
  131.8 1.2 shard_map.78
  133.8 1.3 collective-permute-start.34
  135.1 83.1 %collective-permute-done.34 = f32[1,512]{1,0:T(1,128)S(1)} collective-permute-done((f32[1,512]{1,0:T(1,128)S(1)}, f32[1,512]{1,0:T(1,128)S(1)}, u32[]{:S(2)}, u32[]{:S(2)}) %collective-permute-start.34) | collective-permute-done | bytes 2080 | tf_op jit(solution)/shard_map/ppermute | solution.py:35
  (84 shorter events, 25.4 us)
Async XLA Ops:
  5.1 28.5 %collective-permute-start = (bf16[2,512,512]{2,1,0:T(8,128)(2,1)S(1)}, bf16[2,512,512]{2,1,0:T(8,128)(2,1)S(1)}, u32[]{:S(2)}, u32[]{:S(2)}) collective-permute-start(bf16[2,512,512]{2,1,0:T(8,128)(2,1)S(1)} %slice.32.refs_0_), channel_id=1, source_target_pairs={{0,1},{3,2},{4,5},{7,6},{8,9},{11,10},{12,13},{15,14},{16,17},{19,... | collective-permute-start | bytes 3145736 | tf_op jit(solution)/shard_map/ppermute | solution.py:31
  10.1 27.9 %collective-permute-start.1 = (bf16[2,512,512]{2,1,0:T(8,128)(2,1)S(1)}, bf16[2,512,512]{2,1,0:T(8,128)(2,1)S(1)}, u32[]{:S(2)}, u32[]{:S(2)}) collective-permute-start(bf16[2,512,512]{2,1,0:T(8,128)(2,1)S(1)} %slice.32.refs_0_), channel_id=1, source_target_pairs={{1,2},{2,1},{5,6},{6,5},{9,10},{10,9},{13,14},{14,13},{17,18},{18,... | collective-permute-start | bytes 3145736 | tf_op jit(solution)/shard_map/ppermute | solution.py:27
  10.9 35.0 %collective-permute-start.4 = (bf16[2,528,512]{2,1,0:T(8,128)(2,1)S(1)}, bf16[2,528,512]{2,1,0:T(8,128)(2,1)S(1)}, u32[]{:S(2)}, u32[]{:S(2)}) collective-permute-start(bf16[2,528,512]{2,1,0:T(8,128)(2,1)S(1)} %pad_maximum_fusion.rest_1_.rest_0_.rest_5_), channel_id=1, source_target_pairs={{1,9},{2,10},{5,13},{6,14},{9,1},{10,2},{13,5},{14,6},{17,25},{18,... | collective-permute-start | bytes 3244040 | tf_op jit(solution)/shard_map/ppermute | solution.py:23
  11.6 50.0 %collective-permute-start.3 = (bf16[2,528,512]{2,1,0:T(8,128)(2,1)S(1)}, bf16[2,528,512]{2,1,0:T(8,128)(2,1)S(1)}, u32[]{:S(2)}, u32[]{:S(2)}) collective-permute-start(bf16[2,528,512]{2,1,0:T(8,128)(2,1)S(1)} %pad_maximum_fusion.rest_1_.rest_0_.rest_5_), channel_id=1, source_target_pairs={{1,5},{2,6},{5,1},{6,2},{9,13},{10,14},{13,9},{14,10},{17,21},{18,... | collective-permute-start | bytes 3244040 | tf_op jit(solution)/shard_map/ppermute | solution.py:23
  12.3 32.9 %collective-permute-start.6 = (bf16[528,512]{1,0:T(8,128)(2,1)S(1)}, bf16[528,512]{1,0:T(8,128)(2,1)S(1)}, u32[]{:S(2)}, u32[]{:S(2)}) collective-permute-start(bf16[528,512]{1,0:T(8,128)(2,1)S(1)} %get-tuple-element.42), channel_id=1, source_target_pairs={{0,1},{3,2},{4,5},{7,6},{8,9},{11,10},{12,13},{15,14},{16,17},{19,... | collective-permute-start | bytes 1622024 | tf_op jit(solution)/shard_map/ppermute | solution.py:31
  33.6 22.0 %collective-permute-start.10 = (bf16[528,512]{1,0:T(8,128)(2,1)S(1)}, bf16[528,512]{1,0:T(8,128)(2,1)S(1)}, u32[]{:S(2)}, u32[]{:S(2)}) collective-permute-start(bf16[528,512]{1,0:T(8,128)(2,1)S(1)} %get-tuple-element.46), channel_id=1, source_target_pairs={{0,1},{3,2},{4,5},{7,6},{8,9},{11,10},{12,13},{15,14},{16,17},{19,... | collective-permute-start | bytes 1622024 | tf_op jit(solution)/shard_map/ppermute | solution.py:31
  38.0 19.0 %collective-permute-start.2 = (bf16[2,512,512]{2,1,0:T(8,128)(2,1)S(1)}, bf16[2,512,512]{2,1,0:T(8,128)(2,1)S(1)}, u32[]{:S(2)}, u32[]{:S(2)}) collective-permute-start(bf16[2,512,512]{2,1,0:T(8,128)(2,1)S(1)} %collective-permute-done.refs_1_), channel_id=1, source_target_pairs={{1,2},{2,1},{5,6},{6,5},{9,10},{10,9},{13,14},{14,13},{17,18},{18,... | collective-permute-start | bytes 3145736 | tf_op jit(solution)/shard_map/ppermute | solution.py:27
  45.2 11.1 %collective-permute-start.8 = (bf16[528,512]{1,0:T(8,128)(2,1)S(1)}, bf16[528,512]{1,0:T(8,128)(2,1)S(1)}, u32[]{:S(2)}, u32[]{:S(2)}) collective-permute-start(bf16[528,512]{1,0:T(8,128)(2,1)S(1)} %collective-permute-done.6.rest_5_), channel_id=1, source_target_pairs={{1,9},{2,10},{5,13},{6,14},{9,1},{10,2},{13,5},{14,6},{17,25},{18,... | collective-permute-start | bytes 1622024 | tf_op jit(solution)/shard_map/ppermute | solution.py:23
  45.9 16.4 %collective-permute-start.5 = (bf16[2,528,512]{2,1,0:T(8,128)(2,1)S(1)}, bf16[2,528,512]{2,1,0:T(8,128)(2,1)S(1)}, u32[]{:S(2)}, u32[]{:S(2)}) collective-permute-start(bf16[2,528,512]{2,1,0:T(8,128)(2,1)S(1)} %collective-permute-done.4.rest_3_.rest_2_.rest_7_), channel_id=1, source_target_pairs={{1,5},{2,6},{5,1},{6,2},{9,13},{10,14},{13,9},{14,10},{17,21},{18,... | collective-permute-start | bytes 3244040 | tf_op jit(solution)/shard_map/ppermute | solution.py:23
  55.6 6.7 %collective-permute-start.7 = (bf16[528,512]{1,0:T(8,128)(2,1)S(1)}, bf16[528,512]{1,0:T(8,128)(2,1)S(1)}, u32[]{:S(2)}, u32[]{:S(2)}) collective-permute-start(bf16[528,512]{1,0:T(8,128)(2,1)S(1)} %collective-permute-done.6.rest_5_), channel_id=1, source_target_pairs={{1,5},{2,6},{5,1},{6,2},{9,13},{10,14},{13,9},{14,10},{17,21},{18,... | collective-permute-start | bytes 1622024 | tf_op jit(solution)/shard_map/ppermute | solution.py:23
  56.3 6.0 %collective-permute-start.9 = (bf16[528,512]{1,0:T(8,128)(2,1)S(1)}, bf16[528,512]{1,0:T(8,128)(2,1)S(1)}, u32[]{:S(2)}, u32[]{:S(2)}) collective-permute-start(bf16[528,512]{1,0:T(8,128)(2,1)S(1)} %collective-permute-done.8.rest_7_), channel_id=1, source_target_pairs={{1,5},{2,6},{5,1},{6,2},{9,13},{10,14},{13,9},{14,10},{17,21},{18,... | collective-permute-start | bytes 1622024 | tf_op jit(solution)/shard_map/ppermute | solution.py:23
  57.1 10.0 %collective-permute-start.12 = (bf16[528,512]{1,0:T(8,128)(2,1)S(1)}, bf16[528,512]{1,0:T(8,128)(2,1)S(1)}, u32[]{:S(2)}, u32[]{:S(2)}) collective-permute-start(bf16[528,512]{1,0:T(8,128)(2,1)S(1)} %collective-permute-done.10.rest_1_), channel_id=1, source_target_pairs={{1,9},{2,10},{5,13},{6,14},{9,1},{10,2},{13,5},{14,6},{17,25},{18,... | collective-permute-start | bytes 1622024 | tf_op jit(solution)/shard_map/ppermute | solution.py:23
  61.6 7.6 %collective-permute-start.11 = (bf16[528,512]{1,0:T(8,128)(2,1)S(1)}, bf16[528,512]{1,0:T(8,128)(2,1)S(1)}, u32[]{:S(2)}, u32[]{:S(2)}) collective-permute-start(bf16[528,512]{1,0:T(8,128)(2,1)S(1)} %collective-permute-done.10.rest_1_), channel_id=1, source_target_pairs={{1,5},{2,6},{5,1},{6,2},{9,13},{10,14},{13,9},{14,10},{17,21},{18,... | collective-permute-start | bytes 1622024 | tf_op jit(solution)/shard_map/ppermute | solution.py:23
  67.7 9.6 %collective-permute-start.17 = (bf16[528,1024]{1,0:T(8,128)(2,1)S(1)}, bf16[528,1024]{1,0:T(8,128)(2,1)S(1)}, u32[]{:S(2)}, u32[]{:S(2)}) collective-permute-start(bf16[528,1024]{1,0:T(8,128)(2,1)S(1)} %get-tuple-element.44.rest_1_), channel_id=1, source_target_pairs={{1,9},{2,10},{5,13},{6,14},{9,1},{10,2},{13,5},{14,6},{17,25},{18,... | collective-permute-start | bytes 3244040 | tf_op jit(solution)/shard_map/ppermute | solution.py:23
  68.5 6.9 %collective-permute-start.14 = (bf16[512,512]{1,0:T(8,128)(2,1)S(1)}, bf16[512,512]{1,0:T(8,128)(2,1)S(1)}, u32[]{:S(2)}, u32[]{:S(2)}) collective-permute-start(bf16[512,512]{1,0:T(8,128)(2,1)S(1)} %shard_map.66.refs_0_), channel_id=1, source_target_pairs={{1,2},{2,1},{5,6},{6,5},{9,10},{10,9},{13,14},{14,13},{17,18},{18,... | collective-permute-start | bytes 1572872 | tf_op jit(solution)/shard_map/ppermute | solution.py:27
  70.9 6.4 %collective-permute-start.15 = (bf16[528,512]{1,0:T(8,128)(2,1)S(1)}, bf16[528,512]{1,0:T(8,128)(2,1)S(1)}, u32[]{:S(2)}, u32[]{:S(2)}) collective-permute-start(bf16[528,512]{1,0:T(8,128)(2,1)S(1)} %get-tuple-element.48.refs_1_), channel_id=1, source_target_pairs={{1,2},{2,1},{5,6},{6,5},{9,10},{10,9},{13,14},{14,13},{17,18},{18,... | collective-permute-start | bytes 1622024 | tf_op jit(solution)/shard_map/ppermute | solution.py:27
  71.6 8.5 %collective-permute-start.16 = (bf16[528,1024]{1,0:T(8,128)(2,1)S(1)}, bf16[528,1024]{1,0:T(8,128)(2,1)S(1)}, u32[]{:S(2)}, u32[]{:S(2)}) collective-permute-start(bf16[528,1024]{1,0:T(8,128)(2,1)S(1)} %get-tuple-element.44.rest_1_), channel_id=1, source_target_pairs={{1,5},{2,6},{5,1},{6,2},{9,13},{10,14},{13,9},{14,10},{17,21},{18,... | collective-permute-start | bytes 3244040 | tf_op jit(solution)/shard_map/ppermute | solution.py:23
  83.0 15.2 %collective-permute-start.24 = (bf16[528,512]{1,0:T(8,128)(2,1)S(1)}, bf16[528,512]{1,0:T(8,128)(2,1)S(1)}, u32[]{:S(2)}, u32[]{:S(2)}) collective-permute-start(bf16[528,512]{1,0:T(8,128)(2,1)S(1)} %get-tuple-element.55), channel_id=1, source_target_pairs={{0,16},{16,0},{1,17},{17,1},{2,18},{18,2},{3,19},{19,3},{4,20},{20... | collective-permute-start | bytes 1622024 | tf_op jit(solution)/shard_map/ppermute | solution.py:17
  84.5 22.9 %collective-permute-start.20 = (bf16[512,512]{1,0:T(8,128)(2,1)S(1)}, bf16[512,512]{1,0:T(8,128)(2,1)S(1)}, u32[]{:S(2)}, u32[]{:S(2)}) collective-permute-start(bf16[512,512]{1,0:T(8,128)(2,1)S(1)} %get-tuple-element.53), channel_id=1, source_target_pairs={{0,16},{16,0},{1,17},{17,1},{2,18},{18,2},{3,19},{19,3},{4,20},{20... | collective-permute-start | bytes 1572872 | tf_op jit(solution)/shard_map/ppermute | solution.py:17
  85.0 28.9 %collective-permute-start.19 = (bf16[528,1024]{1,0:T(8,128)(2,1)S(1)}, bf16[528,1024]{1,0:T(8,128)(2,1)S(1)}, u32[]{:S(2)}, u32[]{:S(2)}) collective-permute-start(bf16[528,1024]{1,0:T(8,128)(2,1)S(1)} %get-tuple-element.51.refs_0_), channel_id=1, source_target_pairs={{1,2},{2,1},{5,6},{6,5},{9,10},{10,9},{13,14},{14,13},{17,18},{18,... | collective-permute-start | bytes 3244040 | tf_op jit(solution)/shard_map/ppermute | solution.py:27
  98.2 13.6 %collective-permute-start.26 = (bf16[528,512]{1,0:T(8,128)(2,1)S(1)}, bf16[528,512]{1,0:T(8,128)(2,1)S(1)}, u32[]{:S(2)}, u32[]{:S(2)}) collective-permute-start(bf16[528,512]{1,0:T(8,128)(2,1)S(1)} %collective-permute-done.24.rest_5_), channel_id=1, source_target_pairs={{1,9},{2,10},{5,13},{6,14},{9,1},{10,2},{13,5},{14,6},{17,25},{18,... | collective-permute-start | bytes 1622024 | tf_op jit(solution)/shard_map/ppermute | solution.py:23
  107.4 5.8 %collective-permute-start.22 = (bf16[512,512]{1,0:T(8,128)(2,1)S(1)}, bf16[512,512]{1,0:T(8,128)(2,1)S(1)}, u32[]{:S(2)}, u32[]{:S(2)}) collective-permute-start(bf16[512,512]{1,0:T(8,128)(2,1)S(1)} %collective-permute-done.20.rest_1_), channel_id=1, source_target_pairs={{1,9},{2,10},{5,13},{6,14},{9,1},{10,2},{13,5},{14,6},{17,25},{18,... | collective-permute-start | bytes 1572872 | tf_op jit(solution)/shard_map/ppermute | solution.py:23
  111.1 5.9 %collective-permute-start.25 = (bf16[528,512]{1,0:T(8,128)(2,1)S(1)}, bf16[528,512]{1,0:T(8,128)(2,1)S(1)}, u32[]{:S(2)}, u32[]{:S(2)}) collective-permute-start(bf16[528,512]{1,0:T(8,128)(2,1)S(1)} %collective-permute-done.24.rest_5_), channel_id=1, source_target_pairs={{1,5},{2,6},{5,1},{6,2},{9,13},{10,14},{13,9},{14,10},{17,21},{18,... | collective-permute-start | bytes 1622024 | tf_op jit(solution)/shard_map/ppermute | solution.py:23
  111.8 5.2 %collective-permute-start.27 = (bf16[528,512]{1,0:T(8,128)(2,1)S(1)}, bf16[528,512]{1,0:T(8,128)(2,1)S(1)}, u32[]{:S(2)}, u32[]{:S(2)}) collective-permute-start(bf16[528,512]{1,0:T(8,128)(2,1)S(1)} %collective-permute-done.26.rest_7_), channel_id=1, source_target_pairs={{1,5},{2,6},{5,1},{6,2},{9,13},{10,14},{13,9},{14,10},{17,21},{18,... | collective-permute-start | bytes 1622024 | tf_op jit(solution)/shard_map/ppermute | solution.py:23
  112.5 4.4 %collective-permute-start.21 = (bf16[512,512]{1,0:T(8,128)(2,1)S(1)}, bf16[512,512]{1,0:T(8,128)(2,1)S(1)}, u32[]{:S(2)}, u32[]{:S(2)}) collective-permute-start(bf16[512,512]{1,0:T(8,128)(2,1)S(1)} %collective-permute-done.20.rest_1_), channel_id=1, source_target_pairs={{1,5},{2,6},{5,1},{6,2},{9,13},{10,14},{13,9},{14,10},{17,21},{18,... | collective-permute-start | bytes 1572872 | tf_op jit(solution)/shard_map/ppermute | solution.py:23
  113.2 3.7 %collective-permute-start.23 = (bf16[512,512]{1,0:T(8,128)(2,1)S(1)}, bf16[512,512]{1,0:T(8,128)(2,1)S(1)}, u32[]{:S(2)}, u32[]{:S(2)}) collective-permute-start(bf16[512,512]{1,0:T(8,128)(2,1)S(1)} %collective-permute-done.22.rest_3_), channel_id=1, source_target_pairs={{1,5},{2,6},{5,1},{6,2},{9,13},{10,14},{13,9},{14,10},{17,21},{18,... | collective-permute-start | bytes 1572872 | tf_op jit(solution)/shard_map/ppermute | solution.py:23
  119.8 5.2 %collective-permute-start.30 = (bf16[528,1024]{1,0:T(8,128)(2,1)S(1)}, bf16[528,1024]{1,0:T(8,128)(2,1)S(1)}, u32[]{:S(2)}, u32[]{:S(2)}) collective-permute-start(bf16[528,1024]{1,0:T(8,128)(2,1)S(1)} %get-tuple-element.57.refs_0_.rest_1_.rest_0_), channel_id=1, source_target_pairs={{1,9},{2,10},{5,13},{6,14},{9,1},{10,2},{13,5},{14,6},{17,25},{18,... | collective-permute-start | bytes 3244040 | tf_op jit(solution)/shard_map/ppermute | solution.py:23
  120.5 5.2 %collective-permute-start.28 = (bf16[528,1024]{1,0:T(8,128)(2,1)S(1)}, bf16[528,1024]{1,0:T(8,128)(2,1)S(1)}, u32[]{:S(2)}, u32[]{:S(2)}) collective-permute-start(bf16[528,1024]{1,0:T(8,128)(2,1)S(1)} %get-tuple-element.57.refs_0_.rest_1_.rest_0_), channel_id=1, source_target_pairs={{1,2},{2,1},{5,6},{6,5},{9,10},{10,9},{13,14},{14,13},{17,18},{18,... | collective-permute-start | bytes 3244040 | tf_op jit(solution)/shard_map/ppermute | solution.py:27
  121.3 7.5 %collective-permute-start.29 = (bf16[528,1024]{1,0:T(8,128)(2,1)S(1)}, bf16[528,1024]{1,0:T(8,128)(2,1)S(1)}, u32[]{:S(2)}, u32[]{:S(2)}) collective-permute-start(bf16[528,1024]{1,0:T(8,128)(2,1)S(1)} %get-tuple-element.57.refs_0_.rest_1_.rest_0_), channel_id=1, source_target_pairs={{1,5},{2,6},{5,1},{6,2},{9,13},{10,14},{13,9},{14,10},{17,21},{18,... | collective-permute-start | bytes 3244040 | tf_op jit(solution)/shard_map/ppermute | solution.py:23
  125.0 3.8 %collective-permute-start.31 = (bf16[528,1024]{1,0:T(8,128)(2,1)S(1)}, bf16[528,1024]{1,0:T(8,128)(2,1)S(1)}, u32[]{:S(2)}, u32[]{:S(2)}) collective-permute-start(bf16[528,1024]{1,0:T(8,128)(2,1)S(1)} %collective-permute-done.30.rest_3_.rest_2_), channel_id=1, source_target_pairs={{1,5},{2,6},{5,1},{6,2},{9,13},{10,14},{13,9},{14,10},{17,21},{18,... | collective-permute-start | bytes 3244040 | tf_op jit(solution)/shard_map/ppermute | solution.py:23
  130.5 88.2 %collective-permute-start.32 = (bf16[528,512]{1,0:T(8,128)(2,1)S(1)}, bf16[528,512]{1,0:T(8,128)(2,1)S(1)}, u32[]{:S(2)}, u32[]{:S(2)}) collective-permute-start(bf16[528,512]{1,0:T(8,128)(2,1)S(1)} %get-tuple-element.60), channel_id=1, source_target_pairs={{1,0},{2,3},{5,4},{6,7},{9,8},{10,11},{13,12},{14,15},{17,16},{18,... | collective-permute-start | bytes 1622024 | tf_op jit(solution)/shard_map/ppermute | solution.py:35
  133.8 84.4 %collective-permute-start.34 = (f32[1,512]{1,0:T(1,128)S(1)}, f32[1,512]{1,0:T(1,128)S(1)}, u32[]{:S(2)}, u32[]{:S(2)}) collective-permute-start(f32[1,512]{1,0:T(1,128)S(1)} %slice_add_fusion), channel_id=1, source_target_pairs={{1,0},{2,3},{5,4},{6,7},{9,8},{10,11},{13,12},{14,15},{17,16},{18,... | collective-permute-start | bytes 6152 | tf_op jit(solution)/shard_map/ppermute | solution.py:35
  (5 other events, 8.4 us)

commit v12 on v11

--- a/solution.py
+++ b/solution.py
@@ -254,19 +254,29 @@
     moved = panel(1, [(3, (other_e, None, 0))], moved)
     whole, whole_o, whole_e, vector = product(moved, views, "both", size, vector)
 
-    def left_panel(turn, left):
-        other = swap_middle(left)
-        partial = panel(turn, [(0, (left, None, 0)), (1, (left, None, size))])
-        return partial, panel(turn, [(2, (other, None, 0)), (3, (other, None, size))], partial)
-
-    earlier = [from_behind(tile, "loop", 1) for tile in (whole_o, whole_e)]
-    partial, moved = left_panel(3, whole)
-    views = right_views(earlier, (partial,))
-    halved, vector = product(moved, views, "joint", size, vector)
-    partial, moved = left_panel(4, halved)
-    views = right_views([from_behind(halved, "loop", 2)], (partial,))
-    reduced_e, vector = product(moved, views[1:], "apart", size, vector)
-    (reduced_o,) = product(after(moved, reduced_e), views[:1], "apart", size)
+    def tile_row(tile, across, last_tie):
+        return plain(tile, swap_rows(tile, 1), across, swap_rows(after(across, last_tie), 1))
+
+    earlier_e, earlier_o = from_behind(whole_e, "loop", 1), from_behind(whole_o, "loop", 1)
+    other = swap_middle(whole)
+    across_e, across_o = swap_rows(earlier_e, 2), swap_rows(earlier_o, 2)
+    partial = panel(3, [(0, (whole, None, 0)), (1, (whole, None, size))])
+    views = tile_row(earlier_e, across_e, partial)
+    moved = panel(3, [(2, (other, None, 0)), (3, (other, None, size))], partial)
+    views_o = tile_row(earlier_o, across_o, moved)
+    halved_e, vector = product(moved, [views], "apart", size, vector)
+    (halved_o,) = product(after(moved, halved_e), [views_o], "apart", size)
+
+    distant_e, distant_o = from_behind(halved_e, "loop", 2), from_behind(halved_o, "loop", 2)
+    other_e, across_e = swap_middle(halved_e), swap_rows(distant_e, 2)
+    other_o, across_o = swap_middle(halved_o), swap_rows(distant_o, 2)
+    partial = panel(4, [(0, (halved_o, None, 0)), (1, (halved_e, None, 0))])
+    views = tile_row(distant_e, across_e, partial)
+    partial = panel(4, [(3, (other_e, None, 0))], partial)
+    views_o = tile_row(distant_o, across_o, partial)
+    moved = panel(4, [(2, (other_o, None, 0))], partial)
+    reduced_e, vector = product(moved, [views], "apart", size, vector)
+    (reduced_o,) = product(after(moved, reduced_e), [views_o], "apart", size)
 
     middle = (col == 1) | (col == 2)
     block = jnp.where(middle, reduced_o, outward(reduced_e)[:size])

time: 221 us -> 215 us (0.973)
  waiting for transfers between devices: 123 us -> 114 us
  starting transfers between devices: 42 us -> 44.7 us
    ppermute x2, waiting for transfers between devices: 83.1 us -> 73.8 us  [outward(): return lax.ppermute(value, 'col', [(1, 0), (2, 3)])]
    ppermute x21 -> x24, starting transfers between devices: 15.1 us -> 17 us  [swap_rows(): return lax.ppermute(value, ('row', 'col'), pairs)]
    pallas_call x13 -> x14, Pallas kernels: 32.4 us -> 33.2 us  [spread_columns(): pl.pallas_call(kernel, out_shape=jax.ShapeDtypeStruct((size, size * count...]
    ppermute x7 -> x8, starting transfers between devices: 4.98 us -> 5.63 us  [swap_middle(): return lax.ppermute(value, 'col', [(1, 2), (2, 1)])]
    pallas_call x7 -> x8, Pallas kernels: 14.9 us -> 15.1 us  [product(): pl.pallas_call(kernel, out_shape=tuple(outs), compiler_params=pltpu.Compi...]
  transfers between devices with their start and end apart: 35 -> 39, of which waited for: 6 -> 6; matrix products, arithmetic and copies ran while one was open for 0% -> 0% of each run, Pallas kernels for 18% -> 21%
where the time goes in v12:
time: 215 us; the launch traced here: 214 us
  waiting for transfers between devices  114 us (53%)
  Pallas kernels  48.3 us (22%)
  starting transfers between devices  44.7 us (21%)
  local copies, waits for them, and re-layouts  3.17 us (1%)
  other arithmetic  2.55 us (1%)
    ppermute x2, waiting for transfers between devices, outward(): return lax.ppermute(value, 'col', [(1, 0), (2, 3)])  73.8 us
    pallas_call x14, Pallas kernels, spread_columns(): pl.pallas_call(kernel, out_shape=jax.ShapeDtypeStruct((size, size * count...  33.2 us
    ppermute x2, waiting for transfers between devices, from_behind(): lax.ppermute(value, axis, [(i, (i + by) % devices) for i in range(devices)])  20.9 us
    ppermute x3, waiting for transfers between devices, inward(): return lax.ppermute(value, 'col', [(0, 1), (3, 2)])  19 us
    ppermute x3, starting transfers between devices, inward(): return lax.ppermute(value, 'col', [(0, 1), (3, 2)])  17.3 us
    ppermute x24, starting transfers between devices, swap_rows(): return lax.ppermute(value, ('row', 'col'), pairs)  17 us
    pallas_call x8, Pallas kernels, product(): pl.pallas_call(kernel, out_shape=tuple(outs), compiler_params=pltpu.Compi...  15.1 us
    ppermute x8, starting transfers between devices, swap_middle(): return lax.ppermute(value, 'col', [(1, 2), (2, 1)])  5.63 us
  transfers between devices with their start and end apart: 39, of which 6 were waited for; matrix products, arithmetic and copies ran while one was open for 0% of the time, Pallas kernels for 21%

profile of v12, /device:TPU:0, one launch (start us, length us, event | category | flops | bytes accessed | tf_op | source)
XLA Modules:
  0.0 214.0 jit_solution(5891147923878494289)
XLA Ops:
  2.7 1.4 slice_bitcast_fusion.1
  5.1 5.0 %collective-permute-start = (bf16[2,512,512]{2,1,0:T(8,128)(2,1)S(1)}, bf16[2,512,512]{2,1,0:T(8,128)(2,1)S(1)}, u32[]{:S(2)}, u32[]{:S(2)}) collective-permute-start(bf16[2,512,512]{2,1,0:T(8,128)(2,1)S(1)} %slice.32.refs_0_), channel_id=1, source_target_pairs={{0,1},{3,2},{4,5},{7,6},{8,9},{11,10},{12,13},{15,14},{16,17},{19,... | collective-permute-start | bytes 3145736 | tf_op jit(solution)/shard_map/ppermute | solution.py:31
  12.3 7.9 %collective-permute-start.6 = (bf16[528,512]{1,0:T(8,128)(2,1)S(1)}, bf16[528,512]{1,0:T(8,128)(2,1)S(1)}, u32[]{:S(2)}, u32[]{:S(2)}) collective-permute-start(bf16[528,512]{1,0:T(8,128)(2,1)S(1)} %get-tuple-element.44), channel_id=1, source_target_pairs={{0,1},{3,2},{4,5},{7,6},{8,9},{11,10},{12,13},{15,14},{16,17},{19,... | collective-permute-start | bytes 1622024 | tf_op jit(solution)/shard_map/ppermute | solution.py:31
  20.3 1.9 shard_map.61.refs_0_
  22.2 1.9 shard_map.59.refs_0_
  24.1 9.5 %collective-permute-done.refs_1_ = bf16[2,512,512]{2,1,0:T(8,128)(2,1)S(1)} collective-permute-done((bf16[2,512,512]{2,1,0:T(8,128)(2,1)S(1)}, bf16[2,512,512]{2,1,0:T(8,128)(2,1)S(1)}, u32[]{:S(2)}, u32[]{:S(2)}) %collective-permute-start) | collective-permute-done | bytes 1048608 | tf_op jit(solution)/shard_map/ppermute | solution.py:31
  33.6 4.4 %collective-permute-start.10 = (bf16[528,512]{1,0:T(8,128)(2,1)S(1)}, bf16[528,512]{1,0:T(8,128)(2,1)S(1)}, u32[]{:S(2)}, u32[]{:S(2)}) collective-permute-start(bf16[528,512]{1,0:T(8,128)(2,1)S(1)} %get-tuple-element.48), channel_id=1, source_target_pairs={{0,1},{3,2},{4,5},{7,6},{8,9},{11,10},{12,13},{15,14},{16,17},{19,... | collective-permute-start | bytes 1622024 | tf_op jit(solution)/shard_map/ppermute | solution.py:31
  38.8 3.0 %shard_map.63.refs_0_ = bf16[512,2048]{1,0:T(8,128)(2,1)S(1)} custom-call(s32[4,512]{1,0:T(4,128)S(1)} %get-tuple-element.40.q_ref, bf16[512,2048]{1,0:T(8,128)(2,1)S(1)} %shard_map.61.refs_0_, bf16[2,512,512]{2,1,0:T(8,128)(2,1)S(1)} %collective-permute-done.refs_1_, bf16[2,512,512]{2,1,0:T(8,128)(2,1)S(1)} %collective-permute-done.1.refs_2_), custom_call_target="tpu_custom_call" | custom-call | flops 2147483648 | bytes 2097152 | tf_op jit(solution)/shard_map/pallas_call | solution.py:83
  41.8 3.0 %shard_map.60.refs_0_ = bf16[512,2048]{1,0:T(8,128)(2,1)S(1)} custom-call(s32[4,512]{1,0:T(4,128)S(1)} %get-tuple-element.38.q_ref, bf16[512,2048]{1,0:T(8,128)(2,1)S(1)} %shard_map.59.refs_0_, bf16[2,512,512]{2,1,0:T(8,128)(2,1)S(1)} %collective-permute-done.refs_1_, bf16[2,512,512]{2,1,0:T(8,128)(2,1)S(1)} %collective-permute-done.1.refs_2_), custom_call_target="tpu_custom_call" | custom-call | flops 2147483648 | bytes 2097152 | tf_op jit(solution)/shard_map/pallas_call | solution.py:83
  46.6 9.0 %collective-permute-done.10.rest_1_ = bf16[528,512]{1,0:T(8,128)(2,1)S(1)} collective-permute-done((bf16[528,512]{1,0:T(8,128)(2,1)S(1)}, bf16[528,512]{1,0:T(8,128)(2,1)S(1)}, u32[]{:S(2)}, u32[]{:S(2)}) %collective-permute-start.10) | collective-permute-done | bytes 540704 | tf_op jit(solution)/shard_map/ppermute | solution.py:31
  57.8 1.9 shard_map.64.left_ref
  59.7 1.9 shard_map.62.left_ref
  62.3 3.4 %shard_map.65 = (bf16[528,1024]{1,0:T(8,128)(2,1)S(1)}, f32[16,512]{1,0:T(8,128)}) custom-call(bf16[512,2048]{1,0:T(8,128)(2,1)S(1)} %shard_map.64.left_ref, bf16[1,512]{1,0:T(2,128)(2,1)S(1)} %compare_convert_fusion.rest_0_, bf16[2,528,512]{2,1,0:T(8,128)(2,1)S(1)} %pad_maximum_fusion.rest_1_.rest_0_.rest_5_, ...), custom_call_target="tpu_custom_call" | custom-call | flops 2147483648 | bytes 6291456 | tf_op jit(solution)/shard_map/pallas_call | solution.py:156
  69.2 1.7 shard_map.67
  72.4 3.0 %shard_map.68.refs_0_ = bf16[512,2048]{1,0:T(8,128)(2,1)S(1)} custom-call(s32[4,512]{1,0:T(4,128)S(1)} %get-tuple-element.37.q_ref, bf16[512,512]{1,0:T(8,128)(2,1)S(1)} %shard_map.66.refs_0_, bf16[528,512]{1,0:T(8,128)(2,1)S(1)} %get-tuple-element.50.refs_1_), custom_call_target="tpu_custom_call" | custom-call | flops 2147483648 | bytes 2097152 | tf_op jit(solution)/shard_map/pallas_call | solution.py:83
  75.4 1.9 shard_map.69.refs_0_
  78.2 1.9 shard_map.70.left_ref
  80.2 2.8 %shard_map.71 = (bf16[528,1024]{1,0:T(8,128)(2,1)S(1)}, bf16[512,512]{1,0:T(8,128)(2,1)S(1)}, bf16[528,512]{1,0:T(8,128)(2,1)S(1)}, f32[16,512]{1,0:T(8,128)S(1)}) custom-call(bf16[512,2048]{1,0:T(8,128)(2,1)S(1)} %shard_map.70.left_ref, f32[16,512]{1,0:T(8,128)S(1)} %get-tuple-element.51.rest_0_, bf16[528,1024]{1,0:T(8,128)(2,1)S(1)} %get-tuple-element.46.rest_1_, ...), custom_call_target="tpu_custom_call" | custom-call | flops 2147483648 | bytes 6291456 | tf_op jit(solution)/shard_map/pallas_call | solution.py:156
  83.0 1.5 collective-permute-start.20
  85.8 12.4 %collective-permute-done.20.rest_1_ = bf16[528,512]{1,0:T(8,128)(2,1)S(1)} collective-permute-done((bf16[528,512]{1,0:T(8,128)(2,1)S(1)}, bf16[528,512]{1,0:T(8,128)(2,1)S(1)}, u32[]{:S(2)}, u32[]{:S(2)}) %collective-permute-start.20) | collective-permute-done | bytes 540704 | tf_op jit(solution)/shard_map/ppermute | solution.py:17
  98.9 8.5 %collective-permute-done.24.rest_0_ = bf16[512,512]{1,0:T(8,128)(2,1)S(1)} collective-permute-done((bf16[512,512]{1,0:T(8,128)(2,1)S(1)}, bf16[512,512]{1,0:T(8,128)(2,1)S(1)}, u32[]{:S(2)}, u32[]{:S(2)}) %collective-permute-start.24) | collective-permute-done | bytes 524320 | tf_op jit(solution)/shard_map/ppermute | solution.py:17
  108.1 3.0 %shard_map.72.refs_0_ = bf16[512,2048]{1,0:T(8,128)(2,1)S(1)} custom-call(s32[4,512]{1,0:T(4,128)S(1)} %get-tuple-element.36.q_ref, bf16[528,1024]{1,0:T(8,128)(2,1)S(1)} %get-tuple-element.53.refs_0_), custom_call_target="tpu_custom_call" | custom-call | flops 2147483648 | bytes 2097152 | tf_op jit(solution)/shard_map/pallas_call | solution.py:83
  113.2 3.0 %shard_map.73.left_ref = bf16[512,2048]{1,0:T(8,128)(2,1)S(1)} custom-call(s32[4,512]{1,0:T(4,128)S(1)} %get-tuple-element.36.q_ref, bf16[512,2048]{1,0:T(8,128)(2,1)S(1)} %shard_map.72.refs_0_, bf16[528,1024]{1,0:T(8,128)(2,1)S(1)} %collective-permute-done.19.refs_1_), custom_call_target="tpu_custom_call" | custom-call | flops 2147483648 | bytes 2097152 | tf_op jit(solution)/shard_map/pallas_call | solution.py:83
  116.9 1.7 shard_map.74
  120.1 1.2 shard_map.75.refs_0_.rest_0_
  123.5 3.0 %shard_map.76.refs_0_ = bf16[512,2048]{1,0:T(8,128)(2,1)S(1)} custom-call(s32[4,512]{1,0:T(4,128)S(1)} %get-tuple-element.35.q_ref, bf16[512,512]{1,0:T(8,128)(2,1)S(1)} %shard_map.75.refs_0_.rest_0_, bf16[528,512]{1,0:T(8,128)(2,1)S(1)} %get-tuple-element.57.refs_1_.rest_1_), custom_call_target="tpu_custom_call" | custom-call | flops 2147483648 | bytes 2097152 | tf_op jit(solution)/shard_map/pallas_call | solution.py:83
  127.9 1.9 shard_map.77.refs_0_
  130.5 1.9 shard_map.78.left_ref
  132.5 1.7 shard_map.79
  134.1 1.3 collective-permute-start.36
  137.4 1.3 collective-permute-start.38
  138.8 73.8 %collective-permute-done.38 = f32[1,512]{1,0:T(1,128)S(1)} collective-permute-done((f32[1,512]{1,0:T(1,128)S(1)}, f32[1,512]{1,0:T(1,128)S(1)}, u32[]{:S(2)}, u32[]{:S(2)}) %collective-permute-start.38) | collective-permute-done | bytes 2080 | tf_op jit(solution)/shard_map/ppermute | solution.py:35
  (94 shorter events, 30.6 us)
Async XLA Ops:
  5.1 28.5 %collective-permute-start = (bf16[2,512,512]{2,1,0:T(8,128)(2,1)S(1)}, bf16[2,512,512]{2,1,0:T(8,128)(2,1)S(1)}, u32[]{:S(2)}, u32[]{:S(2)}) collective-permute-start(bf16[2,512,512]{2,1,0:T(8,128)(2,1)S(1)} %slice.32.refs_0_), channel_id=1, source_target_pairs={{0,1},{3,2},{4,5},{7,6},{8,9},{11,10},{12,13},{15,14},{16,17},{19,... | collective-permute-start | bytes 3145736 | tf_op jit(solution)/shard_map/ppermute | solution.py:31
  10.1 27.9 %collective-permute-start.1 = (bf16[2,512,512]{2,1,0:T(8,128)(2,1)S(1)}, bf16[2,512,512]{2,1,0:T(8,128)(2,1)S(1)}, u32[]{:S(2)}, u32[]{:S(2)}) collective-permute-start(bf16[2,512,512]{2,1,0:T(8,128)(2,1)S(1)} %slice.32.refs_0_), channel_id=1, source_target_pairs={{1,2},{2,1},{5,6},{6,5},{9,10},{10,9},{13,14},{14,13},{17,18},{18,... | collective-permute-start | bytes 3145736 | tf_op jit(solution)/shard_map/ppermute | solution.py:27
  10.9 35.0 %collective-permute-start.4 = (bf16[2,528,512]{2,1,0:T(8,128)(2,1)S(1)}, bf16[2,528,512]{2,1,0:T(8,128)(2,1)S(1)}, u32[]{:S(2)}, u32[]{:S(2)}) collective-permute-start(bf16[2,528,512]{2,1,0:T(8,128)(2,1)S(1)} %pad_maximum_fusion.rest_1_.rest_0_.rest_5_), channel_id=1, source_target_pairs={{1,9},{2,10},{5,13},{6,14},{9,1},{10,2},{13,5},{14,6},{17,25},{18,... | collective-permute-start | bytes 3244040 | tf_op jit(solution)/shard_map/ppermute | solution.py:23
  11.6 50.0 %collective-permute-start.3 = (bf16[2,528,512]{2,1,0:T(8,128)(2,1)S(1)}, bf16[2,528,512]{2,1,0:T(8,128)(2,1)S(1)}, u32[]{:S(2)}, u32[]{:S(2)}) collective-permute-start(bf16[2,528,512]{2,1,0:T(8,128)(2,1)S(1)} %pad_maximum_fusion.rest_1_.rest_0_.rest_5_), channel_id=1, source_target_pairs={{1,5},{2,6},{5,1},{6,2},{9,13},{10,14},{13,9},{14,10},{17,21},{18,... | collective-permute-start | bytes 3244040 | tf_op jit(solution)/shard_map/ppermute | solution.py:23
  12.3 32.9 %collective-permute-start.6 = (bf16[528,512]{1,0:T(8,128)(2,1)S(1)}, bf16[528,512]{1,0:T(8,128)(2,1)S(1)}, u32[]{:S(2)}, u32[]{:S(2)}) collective-permute-start(bf16[528,512]{1,0:T(8,128)(2,1)S(1)} %get-tuple-element.44), channel_id=1, source_target_pairs={{0,1},{3,2},{4,5},{7,6},{8,9},{11,10},{12,13},{15,14},{16,17},{19,... | collective-permute-start | bytes 1622024 | tf_op jit(solution)/shard_map/ppermute | solution.py:31
  33.6 22.0 %collective-permute-start.10 = (bf16[528,512]{1,0:T(8,128)(2,1)S(1)}, bf16[528,512]{1,0:T(8,128)(2,1)S(1)}, u32[]{:S(2)}, u32[]{:S(2)}) collective-permute-start(bf16[528,512]{1,0:T(8,128)(2,1)S(1)} %get-tuple-element.48), channel_id=1, source_target_pairs={{0,1},{3,2},{4,5},{7,6},{8,9},{11,10},{12,13},{15,14},{16,17},{19,... | collective-permute-start | bytes 1622024 | tf_op jit(solution)/shard_map/ppermute | solution.py:31
  38.0 19.0 %collective-permute-start.2 = (bf16[2,512,512]{2,1,0:T(8,128)(2,1)S(1)}, bf16[2,512,512]{2,1,0:T(8,128)(2,1)S(1)}, u32[]{:S(2)}, u32[]{:S(2)}) collective-permute-start(bf16[2,512,512]{2,1,0:T(8,128)(2,1)S(1)} %collective-permute-done.refs_1_), channel_id=1, source_target_pairs={{1,2},{2,1},{5,6},{6,5},{9,10},{10,9},{13,14},{14,13},{17,18},{18,... | collective-permute-start | bytes 3145736 | tf_op jit(solution)/shard_map/ppermute | solution.py:27
  45.2 11.1 %collective-permute-start.8 = (bf16[528,512]{1,0:T(8,128)(2,1)S(1)}, bf16[528,512]{1,0:T(8,128)(2,1)S(1)}, u32[]{:S(2)}, u32[]{:S(2)}) collective-permute-start(bf16[528,512]{1,0:T(8,128)(2,1)S(1)} %collective-permute-done.6.rest_5_), channel_id=1, source_target_pairs={{1,9},{2,10},{5,13},{6,14},{9,1},{10,2},{13,5},{14,6},{17,25},{18,... | collective-permute-start | bytes 1622024 | tf_op jit(solution)/shard_map/ppermute | solution.py:23
  45.9 16.4 %collective-permute-start.5 = (bf16[2,528,512]{2,1,0:T(8,128)(2,1)S(1)}, bf16[2,528,512]{2,1,0:T(8,128)(2,1)S(1)}, u32[]{:S(2)}, u32[]{:S(2)}) collective-permute-start(bf16[2,528,512]{2,1,0:T(8,128)(2,1)S(1)} %collective-permute-done.4.rest_3_.rest_2_.rest_7_), channel_id=1, source_target_pairs={{1,5},{2,6},{5,1},{6,2},{9,13},{10,14},{13,9},{14,10},{17,21},{18,... | collective-permute-start | bytes 3244040 | tf_op jit(solution)/shard_map/ppermute | solution.py:23
  55.6 6.7 %collective-permute-start.7 = (bf16[528,512]{1,0:T(8,128)(2,1)S(1)}, bf16[528,512]{1,0:T(8,128)(2,1)S(1)}, u32[]{:S(2)}, u32[]{:S(2)}) collective-permute-start(bf16[528,512]{1,0:T(8,128)(2,1)S(1)} %collective-permute-done.6.rest_5_), channel_id=1, source_target_pairs={{1,5},{2,6},{5,1},{6,2},{9,13},{10,14},{13,9},{14,10},{17,21},{18,... | collective-permute-start | bytes 1622024 | tf_op jit(solution)/shard_map/ppermute | solution.py:23
  56.3 6.0 %collective-permute-start.9 = (bf16[528,512]{1,0:T(8,128)(2,1)S(1)}, bf16[528,512]{1,0:T(8,128)(2,1)S(1)}, u32[]{:S(2)}, u32[]{:S(2)}) collective-permute-start(bf16[528,512]{1,0:T(8,128)(2,1)S(1)} %collective-permute-done.8.rest_7_), channel_id=1, source_target_pairs={{1,5},{2,6},{5,1},{6,2},{9,13},{10,14},{13,9},{14,10},{17,21},{18,... | collective-permute-start | bytes 1622024 | tf_op jit(solution)/shard_map/ppermute | solution.py:23
  57.1 10.0 %collective-permute-start.12 = (bf16[528,512]{1,0:T(8,128)(2,1)S(1)}, bf16[528,512]{1,0:T(8,128)(2,1)S(1)}, u32[]{:S(2)}, u32[]{:S(2)}) collective-permute-start(bf16[528,512]{1,0:T(8,128)(2,1)S(1)} %collective-permute-done.10.rest_1_), channel_id=1, source_target_pairs={{1,9},{2,10},{5,13},{6,14},{9,1},{10,2},{13,5},{14,6},{17,25},{18,... | collective-permute-start | bytes 1622024 | tf_op jit(solution)/shard_map/ppermute | solution.py:23
  61.6 7.6 %collective-permute-start.11 = (bf16[528,512]{1,0:T(8,128)(2,1)S(1)}, bf16[528,512]{1,0:T(8,128)(2,1)S(1)}, u32[]{:S(2)}, u32[]{:S(2)}) collective-permute-start(bf16[528,512]{1,0:T(8,128)(2,1)S(1)} %collective-permute-done.10.rest_1_), channel_id=1, source_target_pairs={{1,5},{2,6},{5,1},{6,2},{9,13},{10,14},{13,9},{14,10},{17,21},{18,... | collective-permute-start | bytes 1622024 | tf_op jit(solution)/shard_map/ppermute | solution.py:23
  67.7 9.6 %collective-permute-start.17 = (bf16[528,1024]{1,0:T(8,128)(2,1)S(1)}, bf16[528,1024]{1,0:T(8,128)(2,1)S(1)}, u32[]{:S(2)}, u32[]{:S(2)}) collective-permute-start(bf16[528,1024]{1,0:T(8,128)(2,1)S(1)} %get-tuple-element.46.rest_1_), channel_id=1, source_target_pairs={{1,9},{2,10},{5,13},{6,14},{9,1},{10,2},{13,5},{14,6},{17,25},{18,... | collective-permute-start | bytes 3244040 | tf_op jit(solution)/shard_map/ppermute | solution.py:23
  68.5 6.9 %collective-permute-start.14 = (bf16[512,512]{1,0:T(8,128)(2,1)S(1)}, bf16[512,512]{1,0:T(8,128)(2,1)S(1)}, u32[]{:S(2)}, u32[]{:S(2)}) collective-permute-start(bf16[512,512]{1,0:T(8,128)(2,1)S(1)} %shard_map.66.refs_0_), channel_id=1, source_target_pairs={{1,2},{2,1},{5,6},{6,5},{9,10},{10,9},{13,14},{14,13},{17,18},{18,... | collective-permute-start | bytes 1572872 | tf_op jit(solution)/shard_map/ppermute | solution.py:27
  70.9 6.4 %collective-permute-start.15 = (bf16[528,512]{1,0:T(8,128)(2,1)S(1)}, bf16[528,512]{1,0:T(8,128)(2,1)S(1)}, u32[]{:S(2)}, u32[]{:S(2)}) collective-permute-start(bf16[528,512]{1,0:T(8,128)(2,1)S(1)} %get-tuple-element.50.refs_1_), channel_id=1, source_target_pairs={{1,2},{2,1},{5,6},{6,5},{9,10},{10,9},{13,14},{14,13},{17,18},{18,... | collective-permute-start | bytes 1622024 | tf_op jit(solution)/shard_map/ppermute | solution.py:27
  71.6 8.5 %collective-permute-start.16 = (bf16[528,1024]{1,0:T(8,128)(2,1)S(1)}, bf16[528,1024]{1,0:T(8,128)(2,1)S(1)}, u32[]{:S(2)}, u32[]{:S(2)}) collective-permute-start(bf16[528,1024]{1,0:T(8,128)(2,1)S(1)} %get-tuple-element.46.rest_1_), channel_id=1, source_target_pairs={{1,5},{2,6},{5,1},{6,2},{9,13},{10,14},{13,9},{14,10},{17,21},{18,... | collective-permute-start | bytes 3244040 | tf_op jit(solution)/shard_map/ppermute | solution.py:23
  83.0 15.2 %collective-permute-start.20 = (bf16[528,512]{1,0:T(8,128)(2,1)S(1)}, bf16[528,512]{1,0:T(8,128)(2,1)S(1)}, u32[]{:S(2)}, u32[]{:S(2)}) collective-permute-start(bf16[528,512]{1,0:T(8,128)(2,1)S(1)} %get-tuple-element.55), channel_id=1, source_target_pairs={{0,16},{16,0},{1,17},{17,1},{2,18},{18,2},{3,19},{19,3},{4,20},{20... | collective-permute-start | bytes 1622024 | tf_op jit(solution)/shard_map/ppermute | solution.py:17
  84.5 28.7 %collective-permute-start.19 = (bf16[528,1024]{1,0:T(8,128)(2,1)S(1)}, bf16[528,1024]{1,0:T(8,128)(2,1)S(1)}, u32[]{:S(2)}, u32[]{:S(2)}) collective-permute-start(bf16[528,1024]{1,0:T(8,128)(2,1)S(1)} %get-tuple-element.53.refs_0_), channel_id=1, source_target_pairs={{1,2},{2,1},{5,6},{6,5},{9,10},{10,9},{13,14},{14,13},{17,18},{18,... | collective-permute-start | bytes 3244040 | tf_op jit(solution)/shard_map/ppermute | solution.py:27
  85.2 22.2 %collective-permute-start.24 = (bf16[512,512]{1,0:T(8,128)(2,1)S(1)}, bf16[512,512]{1,0:T(8,128)(2,1)S(1)}, u32[]{:S(2)}, u32[]{:S(2)}) collective-permute-start(bf16[512,512]{1,0:T(8,128)(2,1)S(1)} %get-tuple-element.59), channel_id=1, source_target_pairs={{0,16},{16,0},{1,17},{17,1},{2,18},{18,2},{3,19},{19,3},{4,20},{20... | collective-permute-start | bytes 1572872 | tf_op jit(solution)/shard_map/ppermute | solution.py:17
  98.2 13.6 %collective-permute-start.22 = (bf16[528,512]{1,0:T(8,128)(2,1)S(1)}, bf16[528,512]{1,0:T(8,128)(2,1)S(1)}, u32[]{:S(2)}, u32[]{:S(2)}) collective-permute-start(bf16[528,512]{1,0:T(8,128)(2,1)S(1)} %collective-permute-done.20.rest_1_), channel_id=1, source_target_pairs={{1,9},{2,10},{5,13},{6,14},{9,1},{10,2},{13,5},{14,6},{17,25},{18,... | collective-permute-start | bytes 1622024 | tf_op jit(solution)/shard_map/ppermute | solution.py:23
  107.4 8.8 %collective-permute-start.26 = (bf16[512,512]{1,0:T(8,128)(2,1)S(1)}, bf16[512,512]{1,0:T(8,128)(2,1)S(1)}, u32[]{:S(2)}, u32[]{:S(2)}) collective-permute-start(bf16[512,512]{1,0:T(8,128)(2,1)S(1)} %collective-permute-done.24.rest_0_), channel_id=1, source_target_pairs={{1,9},{2,10},{5,13},{6,14},{9,1},{10,2},{13,5},{14,6},{17,25},{18,... | collective-permute-start | bytes 1572872 | tf_op jit(solution)/shard_map/ppermute | solution.py:23
  112.5 7.6 %collective-permute-start.25 = (bf16[512,512]{1,0:T(8,128)(2,1)S(1)}, bf16[512,512]{1,0:T(8,128)(2,1)S(1)}, u32[]{:S(2)}, u32[]{:S(2)}) collective-permute-start(bf16[512,512]{1,0:T(8,128)(2,1)S(1)} %collective-permute-done.24.rest_0_), channel_id=1, source_target_pairs={{1,5},{2,6},{5,1},{6,2},{9,13},{10,14},{13,9},{14,10},{17,21},{18,... | collective-permute-start | bytes 1572872 | tf_op jit(solution)/shard_map/ppermute | solution.py:23
  118.6 7.8 %collective-permute-start.31 = (bf16[528,512]{1,0:T(8,128)(2,1)S(1)}, bf16[528,512]{1,0:T(8,128)(2,1)S(1)}, u32[]{:S(2)}, u32[]{:S(2)}) collective-permute-start(bf16[528,512]{1,0:T(8,128)(2,1)S(1)} %get-tuple-element.57.refs_1_.rest_1_), channel_id=1, source_target_pairs={{1,9},{2,10},{5,13},{6,14},{9,1},{10,2},{13,5},{14,6},{17,25},{18,... | collective-permute-start | bytes 1622024 | tf_op jit(solution)/shard_map/ppermute | solution.py:23
  119.4 7.8 %collective-permute-start.28 = (bf16[528,512]{1,0:T(8,128)(2,1)S(1)}, bf16[528,512]{1,0:T(8,128)(2,1)S(1)}, u32[]{:S(2)}, u32[]{:S(2)}) collective-permute-start(bf16[528,512]{1,0:T(8,128)(2,1)S(1)} %get-tuple-element.57.refs_1_.rest_1_), channel_id=1, source_target_pairs={{1,2},{2,1},{5,6},{6,5},{9,10},{10,9},{13,14},{14,13},{17,18},{18,... | collective-permute-start | bytes 1622024 | tf_op jit(solution)/shard_map/ppermute | solution.py:27
  121.3 8.4 %collective-permute-start.34 = (bf16[512,512]{1,0:T(8,128)(2,1)S(1)}, bf16[512,512]{1,0:T(8,128)(2,1)S(1)}, u32[]{:S(2)}, u32[]{:S(2)}) collective-permute-start(bf16[512,512]{1,0:T(8,128)(2,1)S(1)} %shard_map.75.refs_0_.rest_0_), channel_id=1, source_target_pairs={{1,9},{2,10},{5,13},{6,14},{9,1},{10,2},{13,5},{14,6},{17,25},{18,... | collective-permute-start | bytes 1572872 | tf_op jit(solution)/shard_map/ppermute | solution.py:23
  122.0 8.5 %collective-permute-start.29 = (bf16[512,512]{1,0:T(8,128)(2,1)S(1)}, bf16[512,512]{1,0:T(8,128)(2,1)S(1)}, u32[]{:S(2)}, u32[]{:S(2)}) collective-permute-start(bf16[512,512]{1,0:T(8,128)(2,1)S(1)} %shard_map.75.refs_0_.rest_0_), channel_id=1, source_target_pairs={{1,2},{2,1},{5,6},{6,5},{9,10},{10,9},{13,14},{14,13},{17,18},{18,... | collective-permute-start | bytes 1572872 | tf_op jit(solution)/shard_map/ppermute | solution.py:27
  122.7 9.7 %collective-permute-start.30 = (bf16[528,512]{1,0:T(8,128)(2,1)S(1)}, bf16[528,512]{1,0:T(8,128)(2,1)S(1)}, u32[]{:S(2)}, u32[]{:S(2)}) collective-permute-start(bf16[528,512]{1,0:T(8,128)(2,1)S(1)} %get-tuple-element.57.refs_1_.rest_1_), channel_id=1, source_target_pairs={{1,5},{2,6},{5,1},{6,2},{9,13},{10,14},{13,9},{14,10},{17,21},{18,... | collective-permute-start | bytes 1622024 | tf_op jit(solution)/shard_map/ppermute | solution.py:23
  126.5 6.0 %collective-permute-start.32 = (bf16[528,512]{1,0:T(8,128)(2,1)S(1)}, bf16[528,512]{1,0:T(8,128)(2,1)S(1)}, u32[]{:S(2)}, u32[]{:S(2)}) collective-permute-start(bf16[528,512]{1,0:T(8,128)(2,1)S(1)} %collective-permute-done.31.rest_3_), channel_id=1, source_target_pairs={{1,5},{2,6},{5,1},{6,2},{9,13},{10,14},{13,9},{14,10},{17,21},{18,... | collective-permute-start | bytes 1622024 | tf_op jit(solution)/shard_map/ppermute | solution.py:23
  127.2 8.3 %collective-permute-start.33 = (bf16[512,512]{1,0:T(8,128)(2,1)S(1)}, bf16[512,512]{1,0:T(8,128)(2,1)S(1)}, u32[]{:S(2)}, u32[]{:S(2)}) collective-permute-start(bf16[512,512]{1,0:T(8,128)(2,1)S(1)} %shard_map.75.refs_0_.rest_0_), channel_id=1, source_target_pairs={{1,5},{2,6},{5,1},{6,2},{9,13},{10,14},{13,9},{14,10},{17,21},{18,... | collective-permute-start | bytes 1572872 | tf_op jit(solution)/shard_map/ppermute | solution.py:23
  134.1 79.0 %collective-permute-start.36 = (bf16[528,512]{1,0:T(8,128)(2,1)S(1)}, bf16[528,512]{1,0:T(8,128)(2,1)S(1)}, u32[]{:S(2)}, u32[]{:S(2)}) collective-permute-start(bf16[528,512]{1,0:T(8,128)(2,1)S(1)} %get-tuple-element.63), channel_id=1, source_target_pairs={{1,0},{2,3},{5,4},{6,7},{9,8},{10,11},{13,12},{14,15},{17,16},{18,... | collective-permute-start | bytes 1622024 | tf_op jit(solution)/shard_map/ppermute | solution.py:35
  137.4 75.2 %collective-permute-start.38 = (f32[1,512]{1,0:T(1,128)S(1)}, f32[1,512]{1,0:T(1,128)S(1)}, u32[]{:S(2)}, u32[]{:S(2)}) collective-permute-start(f32[1,512]{1,0:T(1,128)S(1)} %slice_add_fusion), channel_id=1, source_target_pairs={{1,0},{2,3},{5,4},{6,7},{9,8},{10,11},{13,12},{14,15},{17,16},{18,... | collective-permute-start | bytes 6152 | tf_op jit(solution)/shard_map/ppermute | solution.py:35
  (9 other events, 28.9 us)

commit v13 on v12

--- a/solution.py
+++ b/solution.py
@@ -66,7 +66,7 @@
     return total
 
 
-def spread_columns(pivots, tiles, size, count, onto=None):
+def spread_columns(pivots, tiles, size, count, onto=None, weight=1):
     operands = Operands()
     views = [(block, operands.add(view)) for block, view in tiles]
     extra = [] if onto is None else [onto]
@@ -85,33 +85,29 @@
         out_shape=jax.ShapeDtypeStruct((size, size * count), jnp.bfloat16),
         compiler_params=pltpu.CompilerParams(vmem_limit_bytes=VMEM),
         cost_estimate=pl.CostEstimate(
-            flops=2 * len(tiles) * size * size * size * count,
-            bytes_accessed=8 * size * size,
+            flops=2 * weight * len(tiles) * size * size * size * count,
+            bytes_accessed=8 * weight * size * size,
             transcendentals=0,
         ),
     )(pivots, *extra, *operands.arrays)
 
 
-def product(left, halves, form, size, added=None, own=None, turn=0):
+def product(left, halves, form, size, added=None, own=None, turn=0, weight=1):
     count = left.shape[1] // size
     operands = Operands()
     views = [[operands.add(view) for view in half] for half in halves]
     own_views = [operands.add(view) for view in own or []]
     extra = [] if added is None else [added]
     tall, wide = size + (EXTRA if extra else 0), size * len(halves)
-    shapes = [] if form == "apart" else [(tall, wide)]
-    if form != "joint":
-        shapes += [(size, size)] * (len(halves) - 1) + [(tall, size)]
-    outs = [jax.ShapeDtypeStruct(shape, jnp.bfloat16) for shape in shapes]
+    kind = jnp.float32 if form == "open" else jnp.bfloat16
+    shapes = {"joint": [(tall, wide)], "apart": [(tall, size)], "open": [(size, size)]}[form]
+    outs = [jax.ShapeDtypeStruct(shape, kind) for shape in shapes]
     if extra:
         outs.append(jax.ShapeDtypeStruct((EXTRA, size), jnp.float32))
 
     def kernel(left_ref, *rest):
         refs = rest[len(extra) : len(extra) + len(operands.arrays)]
         results = rest[len(extra) + len(refs) :]
-        joint = None if form == "apart" else results[0]
-        single = [] if form == "joint" else results[len(shapes) - len(halves) : len(shapes)]
-
         for i, half in enumerate(views):
             total = None
             for b in range(count):
@@ -121,11 +117,7 @@
                     preferred_element_type=jnp.float32,
                 )
                 total = part if total is None else total + part
-            total = total.astype(jnp.bfloat16)
-            if joint is not None:
-                joint[0:size, i * size : (i + 1) * size] = total
-            if single:
-                single[i][0:size, :] = total
+            results[0][0:size, i * size : (i + 1) * size] = total.astype(kind)
         if not extra:
             return
 
@@ -146,23 +138,93 @@
                 rows, left_ref[:, b * size : (b + 1) * size], NT, preferred_element_type=jnp.float32
             )
         results[-1][...] = applied
-        applied = applied.astype(jnp.bfloat16)
-        if joint is not None:
+        if form != "open":
             for i in range(len(halves)):
-                joint[size:tall, i * size : (i + 1) * size] = applied
-        if single:
-            single[-1][size:tall, :] = applied
+                results[0][size:tall, i * size : (i + 1) * size] = applied.astype(kind)
 
     return pl.pallas_call(
         kernel,
         out_shape=tuple(outs),
         compiler_params=pltpu.CompilerParams(vmem_limit_bytes=VMEM),
         cost_estimate=pl.CostEstimate(
-            flops=2 * len(halves) * size * size * size * count,
-            bytes_accessed=12 * len(halves) * size * size,
+            flops=2 * weight * len(halves) * size * size * size * count,
+            bytes_accessed=12 * weight * len(halves) * size * size,
             transcendentals=0,
         ),
     )(left, *extra, *operands.arrays)
+
+
+def call(kernel, flops, outs, *operands):
+    return pl.pallas_call(
+        kernel,
+        out_shape=outs,
+        compiler_params=pltpu.CompilerParams(vmem_limit_bytes=VMEM),
+        cost_estimate=pl.CostEstimate(flops=flops, bytes_accessed=1 << 20, transcendentals=0),
+    )(*operands)
+
+
+def early(value, weight=20):
+    def kernel(value_ref, out):
+        del value_ref, out
+
+    return pl.pallas_call(
+        kernel,
+        out_shape=jax.ShapeDtypeStruct(value.shape, value.dtype),
+        in_specs=[pl.BlockSpec(memory_space=pl.ANY)],
+        out_specs=pl.BlockSpec(memory_space=pl.ANY),
+        input_output_aliases={0: 0},
+        cost_estimate=pl.CostEstimate(flops=weight << 30, bytes_accessed=0, transcendentals=0),
+    )(value)
+
+
+def beside_each_other(left, right):
+    size = left.shape[1]
+
+    def kernel(left_ref, right_ref, out):
+        out[:, 0:size] = left_ref[0:size, :]
+        out[:, size : 2 * size] = right_ref[0:size, :]
+
+    return call(kernel, 1, jax.ShapeDtypeStruct((size, 2 * size), left.dtype), left, right)
+
+
+def pick_rows(pivots, block, tiles):
+    size = tiles[0].shape[1]
+
+    def kernel(q_ref, *refs):
+        out = refs[-1]
+        rows, places = None, None
+        named = jnp.transpose(jnp.broadcast_to(q_ref[block : block + 1, :], (size, size)))
+        for b, ref in enumerate(refs[:-1]):
+            at = lax.broadcasted_iota(jnp.int32, (size, size), 1) + b * size
+            hot = jnp.where(at == named, 1.0, 0.0).astype(jnp.bfloat16)
+            part = jnp.dot(hot, ref[0:size, :], preferred_element_type=jnp.float32)
+            rows = part if rows is None else rows + part
+            part = lax.dot_general(
+                ref[size : size + EXTRA, :], hot, NT, preferred_element_type=jnp.float32
+            )
+            places = part if places is None else places + part
+        out[0:size, :] = rows.astype(out.dtype)
+        out[size : size + EXTRA, :] = places.astype(out.dtype)
+
+    flops = 2 * size * size * size * len(tiles)
+    return call(kernel, flops, jax.ShapeDtypeStruct(tiles[0].shape, tiles[0].dtype), pivots, *tiles)
+
+
+def finish(left, picked, base, applied):
+    size = left.shape[1]
+
+    def kernel(left_ref, picked_ref, base_ref, applied_ref, out, vector):
+        part = jnp.dot(left_ref[...], picked_ref[0:size, :], preferred_element_type=jnp.float32)
+        out[...] = (base_ref[...] + part).astype(out.dtype)
+        vector[...] = applied_ref[...] + lax.dot_general(
+            picked_ref[size : size + EXTRA, :], left_ref[...], NT, preferred_element_type=jnp.float32
+        )
+
+    outs = (
+        jax.ShapeDtypeStruct((size, size), jnp.bfloat16),
+        jax.ShapeDtypeStruct(applied.shape, applied.dtype),
+    )
+    return call(kernel, 2 * size * size * size, outs, left, picked, base, applied)
 
 
 def after(value, *others):
@@ -209,8 +271,8 @@
     end_upper = inward(tiles[1])
     rights_beside = swap_rows(rights, 1)
 
-    def panel(turn, tiles, onto=None):
-        return spread_columns(pivots[turn], tiles, size, count, onto)
+    def panel(turn, tiles, onto=None, weight=1):
+        return spread_columns(pivots[turn], tiles, size, count, onto, weight)
 
     upper_panel, lower_panel = panel(2, [(0, (lefts, 1, 0))]), panel(0, [(0, (lefts, 0, 0))])
     ends_other = swap_middle(after(ends_left, upper_panel, lower_panel))
@@ -252,10 +314,12 @@
     moved = panel(1, [(2, (other_o, None, 0))], moved)
     views = right_views([lower], (moved, other_e))
     moved = panel(1, [(3, (other_e, None, 0))], moved)
-    whole, whole_o, whole_e, vector = product(moved, views, "both", size, vector)
-
-    def tile_row(tile, across, last_tie):
-        return plain(tile, swap_rows(tile, 1), across, swap_rows(after(across, last_tie), 1))
+    whole_e, vector = product(moved, views[1:], "apart", size, vector)
+    (whole_o,) = product(after(moved, whole_e), views[:1], "apart", size)
+    whole = beside_each_other(whole_o, whole_e)
+
+    def tile_row(tile, across, *last_ties):
+        return plain(tile, swap_rows(tile, 1), across, swap_rows(after(across, *last_ties), 1))
 
     earlier_e, earlier_o = from_behind(whole_e, "loop", 1), from_behind(whole_o, "loop", 1)
     other = swap_middle(whole)
@@ -268,18 +332,21 @@
     (halved_o,) = product(after(moved, halved_e), [views_o], "apart", size)
 
     distant_e, distant_o = from_behind(halved_e, "loop", 2), from_behind(halved_o, "loop", 2)
-    other_e, across_e = swap_middle(halved_e), swap_rows(distant_e, 2)
+    other_e, across_e = early(swap_middle(halved_e)), early(swap_rows(distant_e, 2))
     other_o, across_o = swap_middle(halved_o), swap_rows(distant_o, 2)
     partial = panel(4, [(0, (halved_o, None, 0)), (1, (halved_e, None, 0))])
     views = tile_row(distant_e, across_e, partial)
     partial = panel(4, [(3, (other_e, None, 0))], partial)
-    views_o = tile_row(distant_o, across_o, partial)
-    moved = panel(4, [(2, (other_o, None, 0))], partial)
-    reduced_e, vector = product(moved, [views], "apart", size, vector)
-    (reduced_o,) = product(after(moved, reduced_e), [views_o], "apart", size)
+    base, applied = product(partial, [views], "open", size, vector)
+    picked = pick_rows(pivots[4], 2, [view[0] for view in views])
+    views_o = tile_row(distant_o, across_o, base, picked)
+    other_o = early(after(other_o, base, picked))
+    reduced_e, vector = finish(other_o, picked, base, applied)
+    moved = panel(4, [(2, (other_o, None, 0))], after(partial, reduced_e), 0)
+    (reduced_o,) = product(moved, [views_o], "apart", size, weight=0)
 
     middle = (col == 1) | (col == 2)
-    block = jnp.where(middle, reduced_o, outward(reduced_e)[:size])
+    block = jnp.where(middle, reduced_o, outward(reduced_e))
     vector = after(vector, reduced_o)[:1]
     vector = vector + swap_middle(vector)
     vector = jnp.where(middle, vector, outward(vector))

time: 215 us -> 226 us (1.051)
  waiting for transfers between devices: 114 us -> 102 us
  local copies, waits for them, and re-layouts: 3.17 us -> 12.4 us
  Pallas kernels: 48.3 us -> 56.8 us
  starting transfers between devices: 44.7 us -> 48.5 us
    ppermute x2, waiting for transfers between devices: 73.8 us -> 63.1 us  [outward(): return lax.ppermute(value, 'col', [(1, 0), (2, 3)])]
    unnamed x6 -> x32, local copies, waits for them, and re-layouts: 0.73 us -> 9.98 us
    ppermute x24, starting transfers between devices: 17 us -> 20.9 us  [swap_rows(): return lax.ppermute(value, ('row', 'col'), pairs)]
    pallas_call x0 -> x6, Pallas kernels: none -> 3.7 us  [the longest x3 3.7 us: call(): pl.pallas_call(kernel, out_shape=outs, compiler_params=pltpu.CompilerPara...]
    pallas_call x8 -> x9, Pallas kernels: 15.1 us -> 18.7 us  [product(): pl.pallas_call(kernel, out_shape=tuple(outs), compiler_params=pltpu.Compi...]
  transfers between devices with their start and end apart: 39 -> 39, of which waited for: 6 -> 6; matrix products, arithmetic and copies ran while one was open for 0% -> 1% of each run, Pallas kernels for 21% -> 25%
where the time goes in v13:
time: 226 us; the launch traced here: 224 us
  waiting for transfers between devices  102 us (45%)
  Pallas kernels  56.8 us (25%)
  starting transfers between devices  48.5 us (21%)
  local copies, waits for them, and re-layouts  12.4 us (5%)
  other arithmetic  3.65 us (2%)
    ppermute x2, waiting for transfers between devices, outward(): return lax.ppermute(value, 'col', [(1, 0), (2, 3)])  63.1 us
    pallas_call x14, Pallas kernels, spread_columns(): pl.pallas_call(kernel, out_shape=jax.ShapeDtypeStruct((size, size * count...  34.3 us
    ppermute x24, starting transfers between devices, swap_rows(): return lax.ppermute(value, ('row', 'col'), pairs)  20.9 us
    ppermute x2, waiting for transfers between devices, from_behind(): lax.ppermute(value, axis, [(i, (i + by) % devices) for i in range(devices)])  19.5 us
    ppermute x3, waiting for transfers between devices, inward(): return lax.ppermute(value, 'col', [(0, 1), (3, 2)])  19 us
    pallas_call x9, Pallas kernels, product(): pl.pallas_call(kernel, out_shape=tuple(outs), compiler_params=pltpu.Compi...  18.7 us
    ppermute x3, starting transfers between devices, inward(): return lax.ppermute(value, 'col', [(0, 1), (3, 2)])  17.3 us
    unnamed x32, local copies, waits for them, and re-layouts  9.98 us
  transfers between devices with their start and end apart: 39, of which 6 were waited for; matrix products, arithmetic and copies ran while one was open for 1% of the time, Pallas kernels for 25%

profile of v13, /device:TPU:0, one launch (start us, length us, event | category | flops | bytes accessed | tf_op | source)
XLA Modules:
  0.0 224.4 jit_solution(4070679403574762101)
XLA Ops:
  4.4 5.0 %collective-permute-start = (bf16[2,512,512]{2,1,0:T(8,128)(2,1)S(1)}, bf16[2,512,512]{2,1,0:T(8,128)(2,1)S(1)}, u32[]{:S(2)}, u32[]{:S(2)}) collective-permute-start(bf16[2,512,512]{2,1,0:T(8,128)(2,1)S(1)} %slice.29.refs_0_), channel_id=1, source_target_pairs={{0,1},{3,2},{4,5},{7,6},{8,9},{11,10},{12,13},{15,14},{16,17},{19,... | collective-permute-start | bytes 3145736 | tf_op jit(solution)/shard_map/ppermute | solution.py:31
  11.6 7.9 %collective-permute-start.6 = (bf16[528,512]{1,0:T(8,128)(2,1)S(1)}, bf16[528,512]{1,0:T(8,128)(2,1)S(1)}, u32[]{:S(2)}, u32[]{:S(2)}) collective-permute-start(bf16[528,512]{1,0:T(8,128)(2,1)S(1)} %get-tuple-element.46), channel_id=1, source_target_pairs={{0,1},{3,2},{4,5},{7,6},{8,9},{11,10},{12,13},{15,14},{16,17},{19,... | collective-permute-start | bytes 1622024 | tf_op jit(solution)/shard_map/ppermute | solution.py:31
  19.6 1.9 shard_map.61.refs_0_
  21.5 1.9 shard_map.59.refs_0_
  23.4 9.5 %collective-permute-done.refs_1_ = bf16[2,512,512]{2,1,0:T(8,128)(2,1)S(1)} collective-permute-done((bf16[2,512,512]{2,1,0:T(8,128)(2,1)S(1)}, bf16[2,512,512]{2,1,0:T(8,128)(2,1)S(1)}, u32[]{:S(2)}, u32[]{:S(2)}) %collective-permute-start) | collective-permute-done | bytes 1048608 | tf_op jit(solution)/shard_map/ppermute | solution.py:31
  32.9 4.4 %collective-permute-start.10 = (bf16[528,512]{1,0:T(8,128)(2,1)S(1)}, bf16[528,512]{1,0:T(8,128)(2,1)S(1)}, u32[]{:S(2)}, u32[]{:S(2)}) collective-permute-start(bf16[528,512]{1,0:T(8,128)(2,1)S(1)} %get-tuple-element.50), channel_id=1, source_target_pairs={{0,1},{3,2},{4,5},{7,6},{8,9},{11,10},{12,13},{15,14},{16,17},{19,... | collective-permute-start | bytes 1622024 | tf_op jit(solution)/shard_map/ppermute | solution.py:31
  38.1 3.0 %shard_map.63.refs_0_ = bf16[512,2048]{1,0:T(8,128)(2,1)S(1)} custom-call(s32[4,512]{1,0:T(4,128)S(1)} %get-tuple-element.42.q_ref, bf16[512,2048]{1,0:T(8,128)(2,1)S(1)} %shard_map.61.refs_0_, bf16[2,512,512]{2,1,0:T(8,128)(2,1)S(1)} %collective-permute-done.refs_1_, bf16[2,512,512]{2,1,0:T(8,128)(2,1)S(1)} %collective-permute-done.1.refs_2_), custom_call_target="tpu_custom_call" | custom-call | flops 2147483648 | bytes 2097152 | tf_op jit(solution)/shard_map/pallas_call | solution.py:83
  41.1 3.0 %shard_map.60.refs_0_ = bf16[512,2048]{1,0:T(8,128)(2,1)S(1)} custom-call(s32[4,512]{1,0:T(4,128)S(1)} %get-tuple-element.40.q_ref, bf16[512,2048]{1,0:T(8,128)(2,1)S(1)} %shard_map.59.refs_0_, bf16[2,512,512]{2,1,0:T(8,128)(2,1)S(1)} %collective-permute-done.refs_1_, bf16[2,512,512]{2,1,0:T(8,128)(2,1)S(1)} %collective-permute-done.1.refs_2_), custom_call_target="tpu_custom_call" | custom-call | flops 2147483648 | bytes 2097152 | tf_op jit(solution)/shard_map/pallas_call | solution.py:83
  45.9 9.0 %collective-permute-done.10.rest_1_ = bf16[528,512]{1,0:T(8,128)(2,1)S(1)} collective-permute-done((bf16[528,512]{1,0:T(8,128)(2,1)S(1)}, bf16[528,512]{1,0:T(8,128)(2,1)S(1)}, u32[]{:S(2)}, u32[]{:S(2)}) %collective-permute-start.10) | collective-permute-done | bytes 540704 | tf_op jit(solution)/shard_map/ppermute | solution.py:31
  57.1 1.9 shard_map.64.left_ref
  59.0 1.9 shard_map.62.left_ref
  61.6 3.4 %shard_map.65 = (bf16[528,1024]{1,0:T(8,128)(2,1)S(1)}, f32[16,512]{1,0:T(8,128)}) custom-call(bf16[512,2048]{1,0:T(8,128)(2,1)S(1)} %shard_map.64.left_ref, bf16[1,512]{1,0:T(2,128)(2,1)S(1)} %compare_convert_fusion.rest_0_, bf16[2,528,512]{2,1,0:T(8,128)(2,1)S(1)} %pad_maximum_fusion.rest_1_.rest_0_.rest_5_, ...), custom_call_target="tpu_custom_call" | custom-call | flops 2147483648 | bytes 6291456 | tf_op jit(solution)/shard_map/pallas_call | solution.py:145
  68.5 1.7 shard_map.67
  71.7 3.0 %shard_map.68.refs_0_ = bf16[512,2048]{1,0:T(8,128)(2,1)S(1)} custom-call(s32[4,512]{1,0:T(4,128)S(1)} %get-tuple-element.39.q_ref, bf16[512,512]{1,0:T(8,128)(2,1)S(1)} %shard_map.66.refs_0_, bf16[528,512]{1,0:T(8,128)(2,1)S(1)} %get-tuple-element.52.refs_1_), custom_call_target="tpu_custom_call" | custom-call | flops 2147483648 | bytes 2097152 | tf_op jit(solution)/shard_map/pallas_call | solution.py:83
  74.7 1.9 shard_map.69.refs_0_
  77.5 1.9 shard_map.70.left_ref
  79.5 1.7 shard_map.71
  81.2 1.5 collective-permute-start.20
  85.4 11.0 %collective-permute-done.20.rest_1_ = bf16[528,512]{1,0:T(8,128)(2,1)S(1)} collective-permute-done((bf16[528,512]{1,0:T(8,128)(2,1)S(1)}, bf16[528,512]{1,0:T(8,128)(2,1)S(1)}, u32[]{:S(2)}, u32[]{:S(2)}) %collective-permute-start.20) | collective-permute-done | bytes 540704 | tf_op jit(solution)/shard_map/ppermute | solution.py:17
  97.1 8.5 %collective-permute-done.24.rest_0_ = bf16[512,512]{1,0:T(8,128)(2,1)S(1)} collective-permute-done((bf16[512,512]{1,0:T(8,128)(2,1)S(1)}, bf16[512,512]{1,0:T(8,128)(2,1)S(1)}, u32[]{:S(2)}, u32[]{:S(2)}) %collective-permute-start.24) | collective-permute-done | bytes 524320 | tf_op jit(solution)/shard_map/ppermute | solution.py:17
  106.3 3.0 %shard_map.74.refs_0_ = bf16[512,2048]{1,0:T(8,128)(2,1)S(1)} custom-call(s32[4,512]{1,0:T(4,128)S(1)} %get-tuple-element.38.q_ref, bf16[512,1024]{1,0:T(8,128)(2,1)S(1)} %shard_map.73.refs_0_), custom_call_target="tpu_custom_call" | custom-call | flops 2147483648 | bytes 2097152 | tf_op jit(solution)/shard_map/pallas_call | solution.py:83
  111.4 3.0 %shard_map.75.left_ref = bf16[512,2048]{1,0:T(8,128)(2,1)S(1)} custom-call(s32[4,512]{1,0:T(4,128)S(1)} %get-tuple-element.38.q_ref, bf16[512,2048]{1,0:T(8,128)(2,1)S(1)} %shard_map.74.refs_0_, bf16[512,1024]{1,0:T(8,128)(2,1)S(1)} %collective-permute-done.19.refs_1_), custom_call_target="tpu_custom_call" | custom-call | flops 2147483648 | bytes 2097152 | tf_op jit(solution)/shard_map/pallas_call | solution.py:83
  115.1 2.5 %shard_map.76 = (bf16[528,512]{1,0:T(8,128)(2,1)}, f32[16,512]{1,0:T(8,128)S(1)}) custom-call(bf16[512,2048]{1,0:T(8,128)(2,1)S(1)} %shard_map.75.left_ref, f32[16,512]{1,0:T(8,128)S(1)} %get-tuple-element.57.rest_0_, bf16[528,512]{1,0:T(8,128)(2,1)S(1)} %collective-permute-done.20.rest_1_, bf16[528,512]{1,0:T(8,128)(2,1)S(1)} %collective-permute-done.21.rest_2_, ...), custom_call_target="tpu_custom_call" | custom-call | flops 1073741824 | bytes 3145728 | tf_op jit(solution)/shard_map/pallas_call | solution.py:145
  124.0 4.0 %shard_map.78.refs_0_ = bf16[512,2048]{1,0:T(8,128)(2,1)S(1)} custom-call(s32[4,512]{1,0:T(4,128)S(1)} %get-tuple-element.37.q_ref, bf16[512,512]{1,0:T(8,128)(2,1)S(1)} %shard_map.77.refs_0_.rest_0_, bf16[528,512]{1,0:T(8,128)(2,1)} %get-tuple-element.59.refs_1_.rest_1_.refs_0_), custom_call_target="tpu_custom_call" | custom-call | flops 2147483648 | bytes 2097152 | tf_op jit(solution)/shard_map/pallas_call | solution.py:83
  132.3 1.6 copy-done.1
  135.0 1.9 shard_map.80.left_ref.refs_0_
  136.9 3.1 %shard_map.83.picked_ref = bf16[528,512]{1,0:T(8,128)(2,1)S(1)} custom-call(s32[4,512]{1,0:T(4,128)S(1)} %get-tuple-element.37.q_ref, bf16[528,512]{1,0:T(8,128)(2,1)} %get-tuple-element.59.refs_1_.rest_1_.refs_0_, bf16[528,512]{1,0:T(8,128)(2,1)} %collective-permute-done.30.rest_2_.refs_1_, bf16[528,512]{1,0:T(8,128)(2,1)S(1)} %copy-done.12, ...), custom_call_target="tpu_custom_call" | custom-call | flops 1073741824 | bytes 1048576 | tf_op jit(solution)/shard_map/pallas_call | solution.py:158
  140.8 3.1 %shard_map.82 = (f32[512,512]{1,0:T(8,128)S(1)}, f32[16,512]{1,0:T(8,128)S(1)}) custom-call(bf16[512,2048]{1,0:T(8,128)(2,1)S(1)} %shard_map.80.left_ref.refs_0_, f32[16,512]{1,0:T(8,128)S(1)} %get-tuple-element.62.rest_0_, bf16[528,512]{1,0:T(8,128)(2,1)} %get-tuple-element.59.refs_1_.rest_1_.refs_0_, ...), custom_call_target="tpu_custom_call" | custom-call | flops 1073741824 | bytes 3145728 | tf_op jit(solution)/shard_map/pallas_call | solution.py:145
  152.3 1.9 shard_map.86.left_ref
  154.3 2.6 %shard_map.87 = bf16[512,512]{1,0:T(8,128)(2,1)S(1)} custom-call(bf16[512,2048]{1,0:T(8,128)(2,1)S(1)} %shard_map.86.left_ref, bf16[512,512]{1,0:T(8,128)(2,1)S(1)} %shard_map.77.refs_0_.rest_0_, bf16[512,512]{1,0:T(8,128)(2,1)} %collective-permute-done.33.rest_1_, bf16[512,512]{1,0:T(8,128)(2,1)} %collective-permute-done.34.rest_2_, ...), custom_call_target="tpu_custom_call" | custom-call | tf_op jit(solution)/shard_map/pallas_call | solution.py:145
  158.9 63.1 %collective-permute-done.36 = bf16[512,512]{1,0:T(8,128)(2,1)} collective-permute-done((bf16[512,512]{1,0:T(8,128)(2,1)S(1)}, bf16[512,512]{1,0:T(8,128)(2,1)}, u32[]{:S(2)}, u32[]{:S(2)}) %collective-permute-start.36) | collective-permute-done | bytes 524320 | tf_op jit(solution)/shard_map/ppermute | solution.py:35
  222.0 1.9 select_bitcast_fusion
  (127 shorter events, 47.0 us)
Async XLA Ops:
  4.4 28.5 %collective-permute-start = (bf16[2,512,512]{2,1,0:T(8,128)(2,1)S(1)}, bf16[2,512,512]{2,1,0:T(8,128)(2,1)S(1)}, u32[]{:S(2)}, u32[]{:S(2)}) collective-permute-start(bf16[2,512,512]{2,1,0:T(8,128)(2,1)S(1)} %slice.29.refs_0_), channel_id=1, source_target_pairs={{0,1},{3,2},{4,5},{7,6},{8,9},{11,10},{12,13},{15,14},{16,17},{19,... | collective-permute-start | bytes 3145736 | tf_op jit(solution)/shard_map/ppermute | solution.py:31
  9.4 27.9 %collective-permute-start.1 = (bf16[2,512,512]{2,1,0:T(8,128)(2,1)S(1)}, bf16[2,512,512]{2,1,0:T(8,128)(2,1)S(1)}, u32[]{:S(2)}, u32[]{:S(2)}) collective-permute-start(bf16[2,512,512]{2,1,0:T(8,128)(2,1)S(1)} %slice.29.refs_0_), channel_id=1, source_target_pairs={{1,2},{2,1},{5,6},{6,5},{9,10},{10,9},{13,14},{14,13},{17,18},{18,... | collective-permute-start | bytes 3145736 | tf_op jit(solution)/shard_map/ppermute | solution.py:27
  10.2 35.0 %collective-permute-start.4 = (bf16[2,528,512]{2,1,0:T(8,128)(2,1)S(1)}, bf16[2,528,512]{2,1,0:T(8,128)(2,1)S(1)}, u32[]{:S(2)}, u32[]{:S(2)}) collective-permute-start(bf16[2,528,512]{2,1,0:T(8,128)(2,1)S(1)} %pad_maximum_fusion.rest_1_.rest_0_.rest_5_), channel_id=1, source_target_pairs={{1,9},{2,10},{5,13},{6,14},{9,1},{10,2},{13,5},{14,6},{17,25},{18,... | collective-permute-start | bytes 3244040 | tf_op jit(solution)/shard_map/ppermute | solution.py:23
  10.9 50.0 %collective-permute-start.3 = (bf16[2,528,512]{2,1,0:T(8,128)(2,1)S(1)}, bf16[2,528,512]{2,1,0:T(8,128)(2,1)S(1)}, u32[]{:S(2)}, u32[]{:S(2)}) collective-permute-start(bf16[2,528,512]{2,1,0:T(8,128)(2,1)S(1)} %pad_maximum_fusion.rest_1_.rest_0_.rest_5_), channel_id=1, source_target_pairs={{1,5},{2,6},{5,1},{6,2},{9,13},{10,14},{13,9},{14,10},{17,21},{18,... | collective-permute-start | bytes 3244040 | tf_op jit(solution)/shard_map/ppermute | solution.py:23
  11.6 32.9 %collective-permute-start.6 = (bf16[528,512]{1,0:T(8,128)(2,1)S(1)}, bf16[528,512]{1,0:T(8,128)(2,1)S(1)}, u32[]{:S(2)}, u32[]{:S(2)}) collective-permute-start(bf16[528,512]{1,0:T(8,128)(2,1)S(1)} %get-tuple-element.46), channel_id=1, source_target_pairs={{0,1},{3,2},{4,5},{7,6},{8,9},{11,10},{12,13},{15,14},{16,17},{19,... | collective-permute-start | bytes 1622024 | tf_op jit(solution)/shard_map/ppermute | solution.py:31
  32.9 22.0 %collective-permute-start.10 = (bf16[528,512]{1,0:T(8,128)(2,1)S(1)}, bf16[528,512]{1,0:T(8,128)(2,1)S(1)}, u32[]{:S(2)}, u32[]{:S(2)}) collective-permute-start(bf16[528,512]{1,0:T(8,128)(2,1)S(1)} %get-tuple-element.50), channel_id=1, source_target_pairs={{0,1},{3,2},{4,5},{7,6},{8,9},{11,10},{12,13},{15,14},{16,17},{19,... | collective-permute-start | bytes 1622024 | tf_op jit(solution)/shard_map/ppermute | solution.py:31
  37.3 19.0 %collective-permute-start.2 = (bf16[2,512,512]{2,1,0:T(8,128)(2,1)S(1)}, bf16[2,512,512]{2,1,0:T(8,128)(2,1)S(1)}, u32[]{:S(2)}, u32[]{:S(2)}) collective-permute-start(bf16[2,512,512]{2,1,0:T(8,128)(2,1)S(1)} %collective-permute-done.refs_1_), channel_id=1, source_target_pairs={{1,2},{2,1},{5,6},{6,5},{9,10},{10,9},{13,14},{14,13},{17,18},{18,... | collective-permute-start | bytes 3145736 | tf_op jit(solution)/shard_map/ppermute | solution.py:27
  44.5 11.1 %collective-permute-start.8 = (bf16[528,512]{1,0:T(8,128)(2,1)S(1)}, bf16[528,512]{1,0:T(8,128)(2,1)S(1)}, u32[]{:S(2)}, u32[]{:S(2)}) collective-permute-start(bf16[528,512]{1,0:T(8,128)(2,1)S(1)} %collective-permute-done.6.rest_5_), channel_id=1, source_target_pairs={{1,9},{2,10},{5,13},{6,14},{9,1},{10,2},{13,5},{14,6},{17,25},{18,... | collective-permute-start | bytes 1622024 | tf_op jit(solution)/shard_map/ppermute | solution.py:23
  45.2 16.4 %collective-permute-start.5 = (bf16[2,528,512]{2,1,0:T(8,128)(2,1)S(1)}, bf16[2,528,512]{2,1,0:T(8,128)(2,1)S(1)}, u32[]{:S(2)}, u32[]{:S(2)}) collective-permute-start(bf16[2,528,512]{2,1,0:T(8,128)(2,1)S(1)} %collective-permute-done.4.rest_3_.rest_2_.rest_7_), channel_id=1, source_target_pairs={{1,5},{2,6},{5,1},{6,2},{9,13},{10,14},{13,9},{14,10},{17,21},{18,... | collective-permute-start | bytes 3244040 | tf_op jit(solution)/shard_map/ppermute | solution.py:23
  54.9 6.7 %collective-permute-start.7 = (bf16[528,512]{1,0:T(8,128)(2,1)S(1)}, bf16[528,512]{1,0:T(8,128)(2,1)S(1)}, u32[]{:S(2)}, u32[]{:S(2)}) collective-permute-start(bf16[528,512]{1,0:T(8,128)(2,1)S(1)} %collective-permute-done.6.rest_5_), channel_id=1, source_target_pairs={{1,5},{2,6},{5,1},{6,2},{9,13},{10,14},{13,9},{14,10},{17,21},{18,... | collective-permute-start | bytes 1622024 | tf_op jit(solution)/shard_map/ppermute | solution.py:23
  56.4 10.0 %collective-permute-start.12 = (bf16[528,512]{1,0:T(8,128)(2,1)S(1)}, bf16[528,512]{1,0:T(8,128)(2,1)S(1)}, u32[]{:S(2)}, u32[]{:S(2)}) collective-permute-start(bf16[528,512]{1,0:T(8,128)(2,1)S(1)} %collective-permute-done.10.rest_1_), channel_id=1, source_target_pairs={{1,9},{2,10},{5,13},{6,14},{9,1},{10,2},{13,5},{14,6},{17,25},{18,... | collective-permute-start | bytes 1622024 | tf_op jit(solution)/shard_map/ppermute | solution.py:23
  60.9 7.6 %collective-permute-start.11 = (bf16[528,512]{1,0:T(8,128)(2,1)S(1)}, bf16[528,512]{1,0:T(8,128)(2,1)S(1)}, u32[]{:S(2)}, u32[]{:S(2)}) collective-permute-start(bf16[528,512]{1,0:T(8,128)(2,1)S(1)} %collective-permute-done.10.rest_1_), channel_id=1, source_target_pairs={{1,5},{2,6},{5,1},{6,2},{9,13},{10,14},{13,9},{14,10},{17,21},{18,... | collective-permute-start | bytes 1622024 | tf_op jit(solution)/shard_map/ppermute | solution.py:23
  67.0 9.6 %collective-permute-start.17 = (bf16[528,1024]{1,0:T(8,128)(2,1)S(1)}, bf16[528,1024]{1,0:T(8,128)(2,1)S(1)}, u32[]{:S(2)}, u32[]{:S(2)}) collective-permute-start(bf16[528,1024]{1,0:T(8,128)(2,1)S(1)} %get-tuple-element.48.rest_1_.rest_0_), channel_id=1, source_target_pairs={{1,9},{2,10},{5,13},{6,14},{9,1},{10,2},{13,5},{14,6},{17,25},{18,... | collective-permute-start | bytes 3244040 | tf_op jit(solution)/shard_map/ppermute | solution.py:23
  67.8 6.9 %collective-permute-start.14 = (bf16[512,512]{1,0:T(8,128)(2,1)S(1)}, bf16[512,512]{1,0:T(8,128)(2,1)S(1)}, u32[]{:S(2)}, u32[]{:S(2)}) collective-permute-start(bf16[512,512]{1,0:T(8,128)(2,1)S(1)} %shard_map.66.refs_0_), channel_id=1, source_target_pairs={{1,2},{2,1},{5,6},{6,5},{9,10},{10,9},{13,14},{14,13},{17,18},{18,... | collective-permute-start | bytes 1572872 | tf_op jit(solution)/shard_map/ppermute | solution.py:27
  70.2 6.4 %collective-permute-start.15 = (bf16[528,512]{1,0:T(8,128)(2,1)S(1)}, bf16[528,512]{1,0:T(8,128)(2,1)S(1)}, u32[]{:S(2)}, u32[]{:S(2)}) collective-permute-start(bf16[528,512]{1,0:T(8,128)(2,1)S(1)} %get-tuple-element.52.refs_1_), channel_id=1, source_target_pairs={{1,2},{2,1},{5,6},{6,5},{9,10},{10,9},{13,14},{14,13},{17,18},{18,... | collective-permute-start | bytes 1622024 | tf_op jit(solution)/shard_map/ppermute | solution.py:27
  70.9 8.5 %collective-permute-start.16 = (bf16[528,1024]{1,0:T(8,128)(2,1)S(1)}, bf16[528,1024]{1,0:T(8,128)(2,1)S(1)}, u32[]{:S(2)}, u32[]{:S(2)}) collective-permute-start(bf16[528,1024]{1,0:T(8,128)(2,1)S(1)} %get-tuple-element.48.rest_1_.rest_0_), channel_id=1, source_target_pairs={{1,5},{2,6},{5,1},{6,2},{9,13},{10,14},{13,9},{14,10},{17,21},{18,... | collective-permute-start | bytes 3244040 | tf_op jit(solution)/shard_map/ppermute | solution.py:23
  81.2 15.2 %collective-permute-start.20 = (bf16[528,512]{1,0:T(8,128)(2,1)S(1)}, bf16[528,512]{1,0:T(8,128)(2,1)S(1)}, u32[]{:S(2)}, u32[]{:S(2)}) collective-permute-start(bf16[528,512]{1,0:T(8,128)(2,1)S(1)} %get-tuple-element.55.right_ref), channel_id=1, source_target_pairs={{0,16},{16,0},{1,17},{17,1},{2,18},{18,2},{3,19},{19,3},{4,20},{20... | collective-permute-start | bytes 1622024 | tf_op jit(solution)/shard_map/ppermute | solution.py:17
  84.0 27.4 %collective-permute-start.19 = (bf16[512,1024]{1,0:T(8,128)(2,1)S(1)}, bf16[512,1024]{1,0:T(8,128)(2,1)S(1)}, u32[]{:S(2)}, u32[]{:S(2)}) collective-permute-start(bf16[512,1024]{1,0:T(8,128)(2,1)S(1)} %shard_map.73.refs_0_), channel_id=1, source_target_pairs={{1,2},{2,1},{5,6},{6,5},{9,10},{10,9},{13,14},{14,13},{17,18},{18,... | collective-permute-start | bytes 3145736 | tf_op jit(solution)/shard_map/ppermute | solution.py:27
  84.8 20.8 %collective-permute-start.24 = (bf16[512,512]{1,0:T(8,128)(2,1)S(1)}, bf16[512,512]{1,0:T(8,128)(2,1)S(1)}, u32[]{:S(2)}, u32[]{:S(2)}) collective-permute-start(bf16[512,512]{1,0:T(8,128)(2,1)S(1)} %shard_map.72.left_ref), channel_id=1, source_target_pairs={{0,16},{16,0},{1,17},{17,1},{2,18},{18,2},{3,19},{19,3},{4,20},{20... | collective-permute-start | bytes 1572872 | tf_op jit(solution)/shard_map/ppermute | solution.py:17
  96.4 13.6 %collective-permute-start.22 = (bf16[528,512]{1,0:T(8,128)(2,1)S(1)}, bf16[528,512]{1,0:T(8,128)(2,1)S(1)}, u32[]{:S(2)}, u32[]{:S(2)}) collective-permute-start(bf16[528,512]{1,0:T(8,128)(2,1)S(1)} %collective-permute-done.20.rest_1_), channel_id=1, source_target_pairs={{1,9},{2,10},{5,13},{6,14},{9,1},{10,2},{13,5},{14,6},{17,25},{18,... | collective-permute-start | bytes 1622024 | tf_op jit(solution)/shard_map/ppermute | solution.py:23
  105.6 8.8 %collective-permute-start.26 = (bf16[512,512]{1,0:T(8,128)(2,1)S(1)}, bf16[512,512]{1,0:T(8,128)(2,1)S(1)}, u32[]{:S(2)}, u32[]{:S(2)}) collective-permute-start(bf16[512,512]{1,0:T(8,128)(2,1)S(1)} %collective-permute-done.24.rest_0_), channel_id=1, source_target_pairs={{1,9},{2,10},{5,13},{6,14},{9,1},{10,2},{13,5},{14,6},{17,25},{18,... | collective-permute-start | bytes 1572872 | tf_op jit(solution)/shard_map/ppermute | solution.py:23
  110.7 9.8 %collective-permute-start.25 = (bf16[512,512]{1,0:T(8,128)(2,1)S(1)}, bf16[512,512]{1,0:T(8,128)(2,1)S(1)}, u32[]{:S(2)}, u32[]{:S(2)}) collective-permute-start(bf16[512,512]{1,0:T(8,128)(2,1)S(1)} %collective-permute-done.24.rest_0_), channel_id=1, source_target_pairs={{1,5},{2,6},{5,1},{6,2},{9,13},{10,14},{13,9},{14,10},{17,21},{18,... | collective-permute-start | bytes 1572872 | tf_op jit(solution)/shard_map/ppermute | solution.py:23
  114.4 6.1 %collective-permute-start.27 = (bf16[512,512]{1,0:T(8,128)(2,1)S(1)}, bf16[512,512]{1,0:T(8,128)(2,1)S(1)}, u32[]{:S(2)}, u32[]{:S(2)}) collective-permute-start(bf16[512,512]{1,0:T(8,128)(2,1)S(1)} %collective-permute-done.26.rest_2_), channel_id=1, source_target_pairs={{1,5},{2,6},{5,1},{6,2},{9,13},{10,14},{13,9},{14,10},{17,21},{18,... | collective-permute-start | bytes 1572872 | tf_op jit(solution)/shard_map/ppermute | solution.py:23
  117.7 11.7 %collective-permute-start.31 = (bf16[528,512]{1,0:T(8,128)(2,1)}, bf16[528,512]{1,0:T(8,128)(2,1)S(1)}, u32[]{:S(2)}, u32[]{:S(2)}) collective-permute-start(bf16[528,512]{1,0:T(8,128)(2,1)} %get-tuple-element.59.refs_1_.rest_1_.refs_0_), channel_id=1, source_target_pairs={{1,9},{2,10},{5,13},{6,14},{9,1},{10,2},{13,5},{14,6},{17,25},{18,... | collective-permute-start | bytes 1622024 | tf_op jit(solution)/shard_map/ppermute | solution.py:23
  118.4 18.5 %collective-permute-start.30 = (bf16[528,512]{1,0:T(8,128)(2,1)}, bf16[528,512]{1,0:T(8,128)(2,1)}, u32[]{:S(2)}, u32[]{:S(2)}) collective-permute-start(bf16[528,512]{1,0:T(8,128)(2,1)} %get-tuple-element.59.refs_1_.rest_1_.refs_0_), channel_id=1, source_target_pairs={{1,5},{2,6},{5,1},{6,2},{9,13},{10,14},{13,9},{14,10},{17,21},{18,... | collective-permute-start | bytes 1622024 | tf_op jit(solution)/shard_map/ppermute | solution.py:23
  119.8 11.0 %collective-permute-start.28 = (bf16[528,512]{1,0:T(8,128)(2,1)}, bf16[528,512]{1,0:T(8,128)(2,1)S(1)}, u32[]{:S(2)}, u32[]{:S(2)}) collective-permute-start(bf16[528,512]{1,0:T(8,128)(2,1)} %get-tuple-element.59.refs_1_.rest_1_.refs_0_), channel_id=1, source_target_pairs={{1,2},{2,1},{5,6},{6,5},{9,10},{10,9},{13,14},{14,13},{17,18},{18,... | collective-permute-start | bytes 1622024 | tf_op jit(solution)/shard_map/ppermute | solution.py:27
  121.8 23.1 %collective-permute-start.34 = (bf16[512,512]{1,0:T(8,128)(2,1)S(1)}, bf16[512,512]{1,0:T(8,128)(2,1)}, u32[]{:S(2)}, u32[]{:S(2)}) collective-permute-start(bf16[512,512]{1,0:T(8,128)(2,1)S(1)} %shard_map.77.refs_0_.rest_0_), channel_id=1, source_target_pairs={{1,9},{2,10},{5,13},{6,14},{9,1},{10,2},{13,5},{14,6},{17,25},{18,... | collective-permute-start | bytes 1572872 | tf_op jit(solution)/shard_map/ppermute | solution.py:23
  123.3 23.1 %collective-permute-start.29 = (bf16[512,512]{1,0:T(8,128)(2,1)S(1)}, bf16[512,512]{1,0:T(8,128)(2,1)S(1)}, u32[]{:S(2)}, u32[]{:S(2)}) collective-permute-start(bf16[512,512]{1,0:T(8,128)(2,1)S(1)} %shard_map.77.refs_0_.rest_0_), channel_id=1, source_target_pairs={{1,2},{2,1},{5,6},{6,5},{9,10},{10,9},{13,14},{14,13},{17,18},{18,... | collective-permute-start | bytes 1572872 | tf_op jit(solution)/shard_map/ppermute | solution.py:27
  129.4 24.9 %collective-permute-start.33 = (bf16[512,512]{1,0:T(8,128)(2,1)S(1)}, bf16[512,512]{1,0:T(8,128)(2,1)}, u32[]{:S(2)}, u32[]{:S(2)}) collective-permute-start(bf16[512,512]{1,0:T(8,128)(2,1)S(1)} %shard_map.77.refs_0_.rest_0_), channel_id=1, source_target_pairs={{1,5},{2,6},{5,1},{6,2},{9,13},{10,14},{13,9},{14,10},{17,21},{18,... | collective-permute-start | bytes 1572872 | tf_op jit(solution)/shard_map/ppermute | solution.py:23
  144.9 9.3 %collective-permute-start.35 = (bf16[512,512]{1,0:T(8,128)(2,1)}, bf16[512,512]{1,0:T(8,128)(2,1)}, u32[]{:S(2)}, u32[]{:S(2)}) collective-permute-start(bf16[512,512]{1,0:T(8,128)(2,1)} %collective-permute-done.34.rest_2_), channel_id=1, source_target_pairs={{1,5},{2,6},{5,1},{6,2},{9,13},{10,14},{13,9},{14,10},{17,21},{18,... | collective-permute-start | bytes 1572872 | tf_op jit(solution)/shard_map/ppermute | solution.py:23
  151.0 71.0 %collective-permute-start.36 = (bf16[512,512]{1,0:T(8,128)(2,1)S(1)}, bf16[512,512]{1,0:T(8,128)(2,1)}, u32[]{:S(2)}, u32[]{:S(2)}) collective-permute-start(bf16[512,512]{1,0:T(8,128)(2,1)S(1)} %get-tuple-element.67), channel_id=1, source_target_pairs={{1,0},{2,3},{5,4},{6,7},{9,8},{10,11},{13,12},{14,15},{17,16},{18,... | collective-permute-start | bytes 1572872 | tf_op jit(solution)/shard_map/ppermute | solution.py:35
  157.6 66.4 %collective-permute-start.38 = (f32[1,512]{1,0:T(1,128)S(1)}, f32[1,512]{1,0:T(1,128)S(1)}, u32[]{:S(2)}, u32[]{:S(2)}) collective-permute-start(f32[1,512]{1,0:T(1,128)S(1)} %slice_add_fusion), channel_id=1, source_target_pairs={{1,0},{2,3},{5,4},{6,7},{9,8},{10,11},{13,12},{14,15},{17,16},{18,... | collective-permute-start | bytes 6152 | tf_op jit(solution)/shard_map/ppermute | solution.py:35
  (22 other events, 50.1 us)

commit v14 on v13

--- a/solution.py
+++ b/solution.py
@@ -173,6 +173,7 @@
         in_specs=[pl.BlockSpec(memory_space=pl.ANY)],
         out_specs=pl.BlockSpec(memory_space=pl.ANY),
         input_output_aliases={0: 0},
+        compiler_params=pltpu.CompilerParams(vmem_limit_bytes=1024 * 1024),
         cost_estimate=pl.CostEstimate(flops=weight << 30, bytes_accessed=0, transcendentals=0),
     )(value)
 

time: 226 us -> 212 us (0.938)
  local copies, waits for them, and re-layouts: 12.4 us -> 2.41 us
  waiting for transfers between devices: 102 us -> 109 us
  Pallas kernels: 56.8 us -> 50.7 us
  starting transfers between devices: 48.5 us -> 44.7 us
    unnamed x32 -> x6, local copies, waits for them, and re-layouts: 9.98 us -> 0.03 us
    ppermute x2, waiting for transfers between devices: 63.1 us -> 70.5 us  [outward(): return lax.ppermute(value, 'col', [(1, 0), (2, 3)])]
    ppermute x24, starting transfers between devices: 20.9 us -> 17.1 us  [swap_rows(): return lax.ppermute(value, ('row', 'col'), pairs)]
    pallas_call x9, Pallas kernels: 18.7 us -> 15.2 us  [product(): pl.pallas_call(kernel, out_shape=tuple(outs), compiler_params=pltpu.Compi...]
  transfers between devices with their start and end apart: 39 -> 39, of which waited for: 6 -> 6; matrix products, arithmetic and copies ran while one was open for 1% -> 0% of each run, Pallas kernels for 25% -> 23%
where the time goes in v14:
time: 212 us; the launch traced here: 211 us
  waiting for transfers between devices  109 us (51%)
  Pallas kernels  50.7 us (24%)
  starting transfers between devices  44.7 us (21%)
  other arithmetic  2.56 us (1%)
  local copies, waits for them, and re-layouts  2.41 us (1%)
    ppermute x2, waiting for transfers between devices, outward(): return lax.ppermute(value, 'col', [(1, 0), (2, 3)])  70.5 us
    pallas_call x14, Pallas kernels, spread_columns(): pl.pallas_call(kernel, out_shape=jax.ShapeDtypeStruct((size, size * count...  33.2 us
    ppermute x2, waiting for transfers between devices, from_behind(): lax.ppermute(value, axis, [(i, (i + by) % devices) for i in range(devices)])  19.5 us
    ppermute x3, waiting for transfers between devices, inward(): return lax.ppermute(value, 'col', [(0, 1), (3, 2)])  19 us
    ppermute x3, starting transfers between devices, inward(): return lax.ppermute(value, 'col', [(0, 1), (3, 2)])  17.3 us
    ppermute x24, starting transfers between devices, swap_rows(): return lax.ppermute(value, ('row', 'col'), pairs)  17.1 us
    pallas_call x9, Pallas kernels, product(): pl.pallas_call(kernel, out_shape=tuple(outs), compiler_params=pltpu.Compi...  15.2 us
    ppermute x8, starting transfers between devices, swap_middle(): return lax.ppermute(value, 'col', [(1, 2), (2, 1)])  5.64 us
  transfers between devices with their start and end apart: 39, of which 6 were waited for; matrix products, arithmetic and copies ran while one was open for 0% of the time, Pallas kernels for 23%

profile of v14, /device:TPU:0, one launch (start us, length us, event | category | flops | bytes accessed | tf_op | source)
XLA Modules:
  0.0 211.1 jit_solution(3463397628299368141)
XLA Ops:
  2.8 1.3 slice_bitcast_fusion.1
  4.4 5.0 %collective-permute-start = (bf16[2,512,512]{2,1,0:T(8,128)(2,1)S(1)}, bf16[2,512,512]{2,1,0:T(8,128)(2,1)S(1)}, u32[]{:S(2)}, u32[]{:S(2)}) collective-permute-start(bf16[2,512,512]{2,1,0:T(8,128)(2,1)S(1)} %slice.29.refs_0_), channel_id=1, source_target_pairs={{0,1},{3,2},{4,5},{7,6},{8,9},{11,10},{12,13},{15,14},{16,17},{19,... | collective-permute-start | bytes 3145736 | tf_op jit(solution)/shard_map/ppermute | solution.py:31
  11.6 7.9 %collective-permute-start.6 = (bf16[528,512]{1,0:T(8,128)(2,1)S(1)}, bf16[528,512]{1,0:T(8,128)(2,1)S(1)}, u32[]{:S(2)}, u32[]{:S(2)}) collective-permute-start(bf16[528,512]{1,0:T(8,128)(2,1)S(1)} %get-tuple-element.46), channel_id=1, source_target_pairs={{0,1},{3,2},{4,5},{7,6},{8,9},{11,10},{12,13},{15,14},{16,17},{19,... | collective-permute-start | bytes 1622024 | tf_op jit(solution)/shard_map/ppermute | solution.py:31
  19.5 1.9 shard_map.61.refs_0_
  21.4 1.9 shard_map.59.refs_0_
  23.3 9.5 %collective-permute-done.refs_1_ = bf16[2,512,512]{2,1,0:T(8,128)(2,1)S(1)} collective-permute-done((bf16[2,512,512]{2,1,0:T(8,128)(2,1)S(1)}, bf16[2,512,512]{2,1,0:T(8,128)(2,1)S(1)}, u32[]{:S(2)}, u32[]{:S(2)}) %collective-permute-start) | collective-permute-done | bytes 1048608 | tf_op jit(solution)/shard_map/ppermute | solution.py:31
  32.9 4.4 %collective-permute-start.10 = (bf16[528,512]{1,0:T(8,128)(2,1)S(1)}, bf16[528,512]{1,0:T(8,128)(2,1)S(1)}, u32[]{:S(2)}, u32[]{:S(2)}) collective-permute-start(bf16[528,512]{1,0:T(8,128)(2,1)S(1)} %get-tuple-element.50), channel_id=1, source_target_pairs={{0,1},{3,2},{4,5},{7,6},{8,9},{11,10},{12,13},{15,14},{16,17},{19,... | collective-permute-start | bytes 1622024 | tf_op jit(solution)/shard_map/ppermute | solution.py:31
  38.1 3.0 %shard_map.63.refs_0_ = bf16[512,2048]{1,0:T(8,128)(2,1)S(1)} custom-call(s32[4,512]{1,0:T(4,128)S(1)} %get-tuple-element.42.q_ref, bf16[512,2048]{1,0:T(8,128)(2,1)S(1)} %shard_map.61.refs_0_, bf16[2,512,512]{2,1,0:T(8,128)(2,1)S(1)} %collective-permute-done.refs_1_, bf16[2,512,512]{2,1,0:T(8,128)(2,1)S(1)} %collective-permute-done.1.refs_2_), custom_call_target="tpu_custom_call" | custom-call | flops 2147483648 | bytes 2097152 | tf_op jit(solution)/shard_map/pallas_call | solution.py:83
  41.1 3.0 %shard_map.60.refs_0_ = bf16[512,2048]{1,0:T(8,128)(2,1)S(1)} custom-call(s32[4,512]{1,0:T(4,128)S(1)} %get-tuple-element.40.q_ref, bf16[512,2048]{1,0:T(8,128)(2,1)S(1)} %shard_map.59.refs_0_, bf16[2,512,512]{2,1,0:T(8,128)(2,1)S(1)} %collective-permute-done.refs_1_, bf16[2,512,512]{2,1,0:T(8,128)(2,1)S(1)} %collective-permute-done.1.refs_2_), custom_call_target="tpu_custom_call" | custom-call | flops 2147483648 | bytes 2097152 | tf_op jit(solution)/shard_map/pallas_call | solution.py:83
  45.9 9.0 %collective-permute-done.10.rest_1_ = bf16[528,512]{1,0:T(8,128)(2,1)S(1)} collective-permute-done((bf16[528,512]{1,0:T(8,128)(2,1)S(1)}, bf16[528,512]{1,0:T(8,128)(2,1)S(1)}, u32[]{:S(2)}, u32[]{:S(2)}) %collective-permute-start.10) | collective-permute-done | bytes 540704 | tf_op jit(solution)/shard_map/ppermute | solution.py:31
  57.0 1.9 shard_map.64.left_ref
  59.0 1.9 shard_map.62.left_ref
  61.6 3.4 %shard_map.65 = (bf16[528,1024]{1,0:T(8,128)(2,1)S(1)}, f32[16,512]{1,0:T(8,128)}) custom-call(bf16[512,2048]{1,0:T(8,128)(2,1)S(1)} %shard_map.64.left_ref, bf16[1,512]{1,0:T(2,128)(2,1)S(1)} %compare_convert_fusion.rest_0_, bf16[2,528,512]{2,1,0:T(8,128)(2,1)S(1)} %pad_maximum_fusion.rest_1_.rest_0_.rest_5_, ...), custom_call_target="tpu_custom_call" | custom-call | flops 2147483648 | bytes 6291456 | tf_op jit(solution)/shard_map/pallas_call | solution.py:145
  68.5 1.7 shard_map.67
  71.6 3.0 %shard_map.68.refs_0_ = bf16[512,2048]{1,0:T(8,128)(2,1)S(1)} custom-call(s32[4,512]{1,0:T(4,128)S(1)} %get-tuple-element.39.q_ref, bf16[512,512]{1,0:T(8,128)(2,1)S(1)} %shard_map.66.refs_0_, bf16[528,512]{1,0:T(8,128)(2,1)S(1)} %get-tuple-element.52.refs_1_), custom_call_target="tpu_custom_call" | custom-call | flops 2147483648 | bytes 2097152 | tf_op jit(solution)/shard_map/pallas_call | solution.py:83
  74.6 1.9 shard_map.69.refs_0_
  77.5 1.9 shard_map.70.left_ref
  79.4 1.7 shard_map.71
  81.2 1.5 collective-permute-start.20
  85.4 11.0 %collective-permute-done.20.rest_1_ = bf16[528,512]{1,0:T(8,128)(2,1)S(1)} collective-permute-done((bf16[528,512]{1,0:T(8,128)(2,1)S(1)}, bf16[528,512]{1,0:T(8,128)(2,1)S(1)}, u32[]{:S(2)}, u32[]{:S(2)}) %collective-permute-start.20) | collective-permute-done | bytes 540704 | tf_op jit(solution)/shard_map/ppermute | solution.py:17
  97.1 8.5 %collective-permute-done.24.rest_0_ = bf16[512,512]{1,0:T(8,128)(2,1)S(1)} collective-permute-done((bf16[512,512]{1,0:T(8,128)(2,1)S(1)}, bf16[512,512]{1,0:T(8,128)(2,1)S(1)}, u32[]{:S(2)}, u32[]{:S(2)}) %collective-permute-start.24) | collective-permute-done | bytes 524320 | tf_op jit(solution)/shard_map/ppermute | solution.py:17
  106.3 3.0 %shard_map.74.refs_0_ = bf16[512,2048]{1,0:T(8,128)(2,1)S(1)} custom-call(s32[4,512]{1,0:T(4,128)S(1)} %get-tuple-element.38.q_ref, bf16[512,1024]{1,0:T(8,128)(2,1)S(1)} %shard_map.73.refs_0_), custom_call_target="tpu_custom_call" | custom-call | flops 2147483648 | bytes 2097152 | tf_op jit(solution)/shard_map/pallas_call | solution.py:83
  111.4 3.0 %shard_map.75.left_ref = bf16[512,2048]{1,0:T(8,128)(2,1)S(1)} custom-call(s32[4,512]{1,0:T(4,128)S(1)} %get-tuple-element.38.q_ref, bf16[512,2048]{1,0:T(8,128)(2,1)S(1)} %shard_map.74.refs_0_, bf16[512,1024]{1,0:T(8,128)(2,1)S(1)} %collective-permute-done.19.refs_1_), custom_call_target="tpu_custom_call" | custom-call | flops 2147483648 | bytes 2097152 | tf_op jit(solution)/shard_map/pallas_call | solution.py:83
  115.1 1.7 shard_map.76
  121.6 3.0 %shard_map.78.refs_0_ = bf16[512,2048]{1,0:T(8,128)(2,1)S(1)} custom-call(s32[4,512]{1,0:T(4,128)S(1)} %get-tuple-element.37.q_ref, bf16[512,512]{1,0:T(8,128)(2,1)S(1)} %shard_map.77.refs_0_.rest_0_, bf16[528,512]{1,0:T(8,128)(2,1)S(1)} %get-tuple-element.59.refs_1_.rest_1_.refs_0_), custom_call_target="tpu_custom_call" | custom-call | flops 2147483648 | bytes 2097152 | tf_op jit(solution)/shard_map/pallas_call | solution.py:83
  126.1 1.9 shard_map.80.left_ref.refs_0_
  128.0 1.7 shard_map.83.picked_ref
  129.8 1.7 shard_map.82
  132.7 1.3 collective-permute-start.36
  134.0 1.9 shard_map.86.left_ref
  137.9 1.3 collective-permute-start.38
  139.2 70.5 %collective-permute-done.36 = bf16[512,512]{1,0:T(8,128)(2,1)S(1)} collective-permute-done((bf16[512,512]{1,0:T(8,128)(2,1)S(1)}, bf16[512,512]{1,0:T(8,128)(2,1)S(1)}, u32[]{:S(2)}, u32[]{:S(2)}) %collective-permute-start.36) | collective-permute-done | bytes 524320 | tf_op jit(solution)/shard_map/ppermute | solution.py:35
  (101 shorter events, 33.1 us)
Async XLA Ops:
  4.4 28.5 %collective-permute-start = (bf16[2,512,512]{2,1,0:T(8,128)(2,1)S(1)}, bf16[2,512,512]{2,1,0:T(8,128)(2,1)S(1)}, u32[]{:S(2)}, u32[]{:S(2)}) collective-permute-start(bf16[2,512,512]{2,1,0:T(8,128)(2,1)S(1)} %slice.29.refs_0_), channel_id=1, source_target_pairs={{0,1},{3,2},{4,5},{7,6},{8,9},{11,10},{12,13},{15,14},{16,17},{19,... | collective-permute-start | bytes 3145736 | tf_op jit(solution)/shard_map/ppermute | solution.py:31
  9.4 27.9 %collective-permute-start.1 = (bf16[2,512,512]{2,1,0:T(8,128)(2,1)S(1)}, bf16[2,512,512]{2,1,0:T(8,128)(2,1)S(1)}, u32[]{:S(2)}, u32[]{:S(2)}) collective-permute-start(bf16[2,512,512]{2,1,0:T(8,128)(2,1)S(1)} %slice.29.refs_0_), channel_id=1, source_target_pairs={{1,2},{2,1},{5,6},{6,5},{9,10},{10,9},{13,14},{14,13},{17,18},{18,... | collective-permute-start | bytes 3145736 | tf_op jit(solution)/shard_map/ppermute | solution.py:27
  10.1 35.0 %collective-permute-start.4 = (bf16[2,528,512]{2,1,0:T(8,128)(2,1)S(1)}, bf16[2,528,512]{2,1,0:T(8,128)(2,1)S(1)}, u32[]{:S(2)}, u32[]{:S(2)}) collective-permute-start(bf16[2,528,512]{2,1,0:T(8,128)(2,1)S(1)} %pad_maximum_fusion.rest_1_.rest_0_.rest_5_), channel_id=1, source_target_pairs={{1,9},{2,10},{5,13},{6,14},{9,1},{10,2},{13,5},{14,6},{17,25},{18,... | collective-permute-start | bytes 3244040 | tf_op jit(solution)/shard_map/ppermute | solution.py:23
  10.9 50.0 %collective-permute-start.3 = (bf16[2,528,512]{2,1,0:T(8,128)(2,1)S(1)}, bf16[2,528,512]{2,1,0:T(8,128)(2,1)S(1)}, u32[]{:S(2)}, u32[]{:S(2)}) collective-permute-start(bf16[2,528,512]{2,1,0:T(8,128)(2,1)S(1)} %pad_maximum_fusion.rest_1_.rest_0_.rest_5_), channel_id=1, source_target_pairs={{1,5},{2,6},{5,1},{6,2},{9,13},{10,14},{13,9},{14,10},{17,21},{18,... | collective-permute-start | bytes 3244040 | tf_op jit(solution)/shard_map/ppermute | solution.py:23
  11.6 32.9 %collective-permute-start.6 = (bf16[528,512]{1,0:T(8,128)(2,1)S(1)}, bf16[528,512]{1,0:T(8,128)(2,1)S(1)}, u32[]{:S(2)}, u32[]{:S(2)}) collective-permute-start(bf16[528,512]{1,0:T(8,128)(2,1)S(1)} %get-tuple-element.46), channel_id=1, source_target_pairs={{0,1},{3,2},{4,5},{7,6},{8,9},{11,10},{12,13},{15,14},{16,17},{19,... | collective-permute-start | bytes 1622024 | tf_op jit(solution)/shard_map/ppermute | solution.py:31
  32.9 22.0 %collective-permute-start.10 = (bf16[528,512]{1,0:T(8,128)(2,1)S(1)}, bf16[528,512]{1,0:T(8,128)(2,1)S(1)}, u32[]{:S(2)}, u32[]{:S(2)}) collective-permute-start(bf16[528,512]{1,0:T(8,128)(2,1)S(1)} %get-tuple-element.50), channel_id=1, source_target_pairs={{0,1},{3,2},{4,5},{7,6},{8,9},{11,10},{12,13},{15,14},{16,17},{19,... | collective-permute-start | bytes 1622024 | tf_op jit(solution)/shard_map/ppermute | solution.py:31
  37.3 19.0 %collective-permute-start.2 = (bf16[2,512,512]{2,1,0:T(8,128)(2,1)S(1)}, bf16[2,512,512]{2,1,0:T(8,128)(2,1)S(1)}, u32[]{:S(2)}, u32[]{:S(2)}) collective-permute-start(bf16[2,512,512]{2,1,0:T(8,128)(2,1)S(1)} %collective-permute-done.refs_1_), channel_id=1, source_target_pairs={{1,2},{2,1},{5,6},{6,5},{9,10},{10,9},{13,14},{14,13},{17,18},{18,... | collective-permute-start | bytes 3145736 | tf_op jit(solution)/shard_map/ppermute | solution.py:27
  44.5 11.1 %collective-permute-start.8 = (bf16[528,512]{1,0:T(8,128)(2,1)S(1)}, bf16[528,512]{1,0:T(8,128)(2,1)S(1)}, u32[]{:S(2)}, u32[]{:S(2)}) collective-permute-start(bf16[528,512]{1,0:T(8,128)(2,1)S(1)} %collective-permute-done.6.rest_5_), channel_id=1, source_target_pairs={{1,9},{2,10},{5,13},{6,14},{9,1},{10,2},{13,5},{14,6},{17,25},{18,... | collective-permute-start | bytes 1622024 | tf_op jit(solution)/shard_map/ppermute | solution.py:23
  45.2 16.4 %collective-permute-start.5 = (bf16[2,528,512]{2,1,0:T(8,128)(2,1)S(1)}, bf16[2,528,512]{2,1,0:T(8,128)(2,1)S(1)}, u32[]{:S(2)}, u32[]{:S(2)}) collective-permute-start(bf16[2,528,512]{2,1,0:T(8,128)(2,1)S(1)} %collective-permute-done.4.rest_3_.rest_2_.rest_7_), channel_id=1, source_target_pairs={{1,5},{2,6},{5,1},{6,2},{9,13},{10,14},{13,9},{14,10},{17,21},{18,... | collective-permute-start | bytes 3244040 | tf_op jit(solution)/shard_map/ppermute | solution.py:23
  54.9 6.7 %collective-permute-start.7 = (bf16[528,512]{1,0:T(8,128)(2,1)S(1)}, bf16[528,512]{1,0:T(8,128)(2,1)S(1)}, u32[]{:S(2)}, u32[]{:S(2)}) collective-permute-start(bf16[528,512]{1,0:T(8,128)(2,1)S(1)} %collective-permute-done.6.rest_5_), channel_id=1, source_target_pairs={{1,5},{2,6},{5,1},{6,2},{9,13},{10,14},{13,9},{14,10},{17,21},{18,... | collective-permute-start | bytes 1622024 | tf_op jit(solution)/shard_map/ppermute | solution.py:23
  55.6 6.0 %collective-permute-start.9 = (bf16[528,512]{1,0:T(8,128)(2,1)S(1)}, bf16[528,512]{1,0:T(8,128)(2,1)S(1)}, u32[]{:S(2)}, u32[]{:S(2)}) collective-permute-start(bf16[528,512]{1,0:T(8,128)(2,1)S(1)} %collective-permute-done.8.rest_7_), channel_id=1, source_target_pairs={{1,5},{2,6},{5,1},{6,2},{9,13},{10,14},{13,9},{14,10},{17,21},{18,... | collective-permute-start | bytes 1622024 | tf_op jit(solution)/shard_map/ppermute | solution.py:23
  56.3 10.0 %collective-permute-start.12 = (bf16[528,512]{1,0:T(8,128)(2,1)S(1)}, bf16[528,512]{1,0:T(8,128)(2,1)S(1)}, u32[]{:S(2)}, u32[]{:S(2)}) collective-permute-start(bf16[528,512]{1,0:T(8,128)(2,1)S(1)} %collective-permute-done.10.rest_1_), channel_id=1, source_target_pairs={{1,9},{2,10},{5,13},{6,14},{9,1},{10,2},{13,5},{14,6},{17,25},{18,... | collective-permute-start | bytes 1622024 | tf_op jit(solution)/shard_map/ppermute | solution.py:23
  60.9 7.6 %collective-permute-start.11 = (bf16[528,512]{1,0:T(8,128)(2,1)S(1)}, bf16[528,512]{1,0:T(8,128)(2,1)S(1)}, u32[]{:S(2)}, u32[]{:S(2)}) collective-permute-start(bf16[528,512]{1,0:T(8,128)(2,1)S(1)} %collective-permute-done.10.rest_1_), channel_id=1, source_target_pairs={{1,5},{2,6},{5,1},{6,2},{9,13},{10,14},{13,9},{14,10},{17,21},{18,... | collective-permute-start | bytes 1622024 | tf_op jit(solution)/shard_map/ppermute | solution.py:23
  67.0 9.6 %collective-permute-start.17 = (bf16[528,1024]{1,0:T(8,128)(2,1)S(1)}, bf16[528,1024]{1,0:T(8,128)(2,1)S(1)}, u32[]{:S(2)}, u32[]{:S(2)}) collective-permute-start(bf16[528,1024]{1,0:T(8,128)(2,1)S(1)} %get-tuple-element.48.rest_1_.rest_0_), channel_id=1, source_target_pairs={{1,9},{2,10},{5,13},{6,14},{9,1},{10,2},{13,5},{14,6},{17,25},{18,... | collective-permute-start | bytes 3244040 | tf_op jit(solution)/shard_map/ppermute | solution.py:23
  67.8 6.9 %collective-permute-start.14 = (bf16[512,512]{1,0:T(8,128)(2,1)S(1)}, bf16[512,512]{1,0:T(8,128)(2,1)S(1)}, u32[]{:S(2)}, u32[]{:S(2)}) collective-permute-start(bf16[512,512]{1,0:T(8,128)(2,1)S(1)} %shard_map.66.refs_0_), channel_id=1, source_target_pairs={{1,2},{2,1},{5,6},{6,5},{9,10},{10,9},{13,14},{14,13},{17,18},{18,... | collective-permute-start | bytes 1572872 | tf_op jit(solution)/shard_map/ppermute | solution.py:27
  70.2 6.4 %collective-permute-start.15 = (bf16[528,512]{1,0:T(8,128)(2,1)S(1)}, bf16[528,512]{1,0:T(8,128)(2,1)S(1)}, u32[]{:S(2)}, u32[]{:S(2)}) collective-permute-start(bf16[528,512]{1,0:T(8,128)(2,1)S(1)} %get-tuple-element.52.refs_1_), channel_id=1, source_target_pairs={{1,2},{2,1},{5,6},{6,5},{9,10},{10,9},{13,14},{14,13},{17,18},{18,... | collective-permute-start | bytes 1622024 | tf_op jit(solution)/shard_map/ppermute | solution.py:27
  70.9 8.5 %collective-permute-start.16 = (bf16[528,1024]{1,0:T(8,128)(2,1)S(1)}, bf16[528,1024]{1,0:T(8,128)(2,1)S(1)}, u32[]{:S(2)}, u32[]{:S(2)}) collective-permute-start(bf16[528,1024]{1,0:T(8,128)(2,1)S(1)} %get-tuple-element.48.rest_1_.rest_0_), channel_id=1, source_target_pairs={{1,5},{2,6},{5,1},{6,2},{9,13},{10,14},{13,9},{14,10},{17,21},{18,... | collective-permute-start | bytes 3244040 | tf_op jit(solution)/shard_map/ppermute | solution.py:23
  81.2 15.2 %collective-permute-start.20 = (bf16[528,512]{1,0:T(8,128)(2,1)S(1)}, bf16[528,512]{1,0:T(8,128)(2,1)S(1)}, u32[]{:S(2)}, u32[]{:S(2)}) collective-permute-start(bf16[528,512]{1,0:T(8,128)(2,1)S(1)} %get-tuple-element.55.right_ref), channel_id=1, source_target_pairs={{0,16},{16,0},{1,17},{17,1},{2,18},{18,2},{3,19},{19,3},{4,20},{20... | collective-permute-start | bytes 1622024 | tf_op jit(solution)/shard_map/ppermute | solution.py:17
  84.0 27.4 %collective-permute-start.19 = (bf16[512,1024]{1,0:T(8,128)(2,1)S(1)}, bf16[512,1024]{1,0:T(8,128)(2,1)S(1)}, u32[]{:S(2)}, u32[]{:S(2)}) collective-permute-start(bf16[512,1024]{1,0:T(8,128)(2,1)S(1)} %shard_map.73.refs_0_), channel_id=1, source_target_pairs={{1,2},{2,1},{5,6},{6,5},{9,10},{10,9},{13,14},{14,13},{17,18},{18,... | collective-permute-start | bytes 3145736 | tf_op jit(solution)/shard_map/ppermute | solution.py:27
  84.8 20.8 %collective-permute-start.24 = (bf16[512,512]{1,0:T(8,128)(2,1)S(1)}, bf16[512,512]{1,0:T(8,128)(2,1)S(1)}, u32[]{:S(2)}, u32[]{:S(2)}) collective-permute-start(bf16[512,512]{1,0:T(8,128)(2,1)S(1)} %shard_map.72.left_ref), channel_id=1, source_target_pairs={{0,16},{16,0},{1,17},{17,1},{2,18},{18,2},{3,19},{19,3},{4,20},{20... | collective-permute-start | bytes 1572872 | tf_op jit(solution)/shard_map/ppermute | solution.py:17
  96.4 13.6 %collective-permute-start.22 = (bf16[528,512]{1,0:T(8,128)(2,1)S(1)}, bf16[528,512]{1,0:T(8,128)(2,1)S(1)}, u32[]{:S(2)}, u32[]{:S(2)}) collective-permute-start(bf16[528,512]{1,0:T(8,128)(2,1)S(1)} %collective-permute-done.20.rest_1_), channel_id=1, source_target_pairs={{1,9},{2,10},{5,13},{6,14},{9,1},{10,2},{13,5},{14,6},{17,25},{18,... | collective-permute-start | bytes 1622024 | tf_op jit(solution)/shard_map/ppermute | solution.py:23
  105.6 8.8 %collective-permute-start.26 = (bf16[512,512]{1,0:T(8,128)(2,1)S(1)}, bf16[512,512]{1,0:T(8,128)(2,1)S(1)}, u32[]{:S(2)}, u32[]{:S(2)}) collective-permute-start(bf16[512,512]{1,0:T(8,128)(2,1)S(1)} %collective-permute-done.24.rest_0_), channel_id=1, source_target_pairs={{1,9},{2,10},{5,13},{6,14},{9,1},{10,2},{13,5},{14,6},{17,25},{18,... | collective-permute-start | bytes 1572872 | tf_op jit(solution)/shard_map/ppermute | solution.py:23
  109.3 5.8 %collective-permute-start.21 = (bf16[528,512]{1,0:T(8,128)(2,1)S(1)}, bf16[528,512]{1,0:T(8,128)(2,1)S(1)}, u32[]{:S(2)}, u32[]{:S(2)}) collective-permute-start(bf16[528,512]{1,0:T(8,128)(2,1)S(1)} %collective-permute-done.20.rest_1_), channel_id=1, source_target_pairs={{1,5},{2,6},{5,1},{6,2},{9,13},{10,14},{13,9},{14,10},{17,21},{18,... | collective-permute-start | bytes 1622024 | tf_op jit(solution)/shard_map/ppermute | solution.py:23
  110.7 8.3 %collective-permute-start.25 = (bf16[512,512]{1,0:T(8,128)(2,1)S(1)}, bf16[512,512]{1,0:T(8,128)(2,1)S(1)}, u32[]{:S(2)}, u32[]{:S(2)}) collective-permute-start(bf16[512,512]{1,0:T(8,128)(2,1)S(1)} %collective-permute-done.24.rest_0_), channel_id=1, source_target_pairs={{1,5},{2,6},{5,1},{6,2},{9,13},{10,14},{13,9},{14,10},{17,21},{18,... | collective-permute-start | bytes 1572872 | tf_op jit(solution)/shard_map/ppermute | solution.py:23
  116.8 7.8 %collective-permute-start.31 = (bf16[528,512]{1,0:T(8,128)(2,1)S(1)}, bf16[528,512]{1,0:T(8,128)(2,1)S(1)}, u32[]{:S(2)}, u32[]{:S(2)}) collective-permute-start(bf16[528,512]{1,0:T(8,128)(2,1)S(1)} %get-tuple-element.59.refs_1_.rest_1_.refs_0_), channel_id=1, source_target_pairs={{1,9},{2,10},{5,13},{6,14},{9,1},{10,2},{13,5},{14,6},{17,25},{18,... | collective-permute-start | bytes 1622024 | tf_op jit(solution)/shard_map/ppermute | solution.py:23
  117.5 10.4 %collective-permute-start.30 = (bf16[528,512]{1,0:T(8,128)(2,1)S(1)}, bf16[528,512]{1,0:T(8,128)(2,1)S(1)}, u32[]{:S(2)}, u32[]{:S(2)}) collective-permute-start(bf16[528,512]{1,0:T(8,128)(2,1)S(1)} %get-tuple-element.59.refs_1_.rest_1_.refs_0_), channel_id=1, source_target_pairs={{1,5},{2,6},{5,1},{6,2},{9,13},{10,14},{13,9},{14,10},{17,21},{18,... | collective-permute-start | bytes 1622024 | tf_op jit(solution)/shard_map/ppermute | solution.py:23
  118.3 7.1 %collective-permute-start.28 = (bf16[528,512]{1,0:T(8,128)(2,1)S(1)}, bf16[528,512]{1,0:T(8,128)(2,1)S(1)}, u32[]{:S(2)}, u32[]{:S(2)}) collective-permute-start(bf16[528,512]{1,0:T(8,128)(2,1)S(1)} %get-tuple-element.59.refs_1_.rest_1_.refs_0_), channel_id=1, source_target_pairs={{1,2},{2,1},{5,6},{6,5},{9,10},{10,9},{13,14},{14,13},{17,18},{18,... | collective-permute-start | bytes 1622024 | tf_op jit(solution)/shard_map/ppermute | solution.py:27
  120.2 11.2 %collective-permute-start.34 = (bf16[512,512]{1,0:T(8,128)(2,1)S(1)}, bf16[512,512]{1,0:T(8,128)(2,1)S(1)}, u32[]{:S(2)}, u32[]{:S(2)}) collective-permute-start(bf16[512,512]{1,0:T(8,128)(2,1)S(1)} %shard_map.77.refs_0_.rest_0_), channel_id=1, source_target_pairs={{1,9},{2,10},{5,13},{6,14},{9,1},{10,2},{13,5},{14,6},{17,25},{18,... | collective-permute-start | bytes 1572872 | tf_op jit(solution)/shard_map/ppermute | solution.py:23
  120.9 11.3 %collective-permute-start.29 = (bf16[512,512]{1,0:T(8,128)(2,1)S(1)}, bf16[512,512]{1,0:T(8,128)(2,1)S(1)}, u32[]{:S(2)}, u32[]{:S(2)}) collective-permute-start(bf16[512,512]{1,0:T(8,128)(2,1)S(1)} %shard_map.77.refs_0_.rest_0_), channel_id=1, source_target_pairs={{1,2},{2,1},{5,6},{6,5},{9,10},{10,9},{13,14},{14,13},{17,18},{18,... | collective-permute-start | bytes 1572872 | tf_op jit(solution)/shard_map/ppermute | solution.py:27
  124.6 11.3 %collective-permute-start.33 = (bf16[512,512]{1,0:T(8,128)(2,1)S(1)}, bf16[512,512]{1,0:T(8,128)(2,1)S(1)}, u32[]{:S(2)}, u32[]{:S(2)}) collective-permute-start(bf16[512,512]{1,0:T(8,128)(2,1)S(1)} %shard_map.77.refs_0_.rest_0_), channel_id=1, source_target_pairs={{1,5},{2,6},{5,1},{6,2},{9,13},{10,14},{13,9},{14,10},{17,21},{18,... | collective-permute-start | bytes 1572872 | tf_op jit(solution)/shard_map/ppermute | solution.py:23
  132.7 77.0 %collective-permute-start.36 = (bf16[512,512]{1,0:T(8,128)(2,1)S(1)}, bf16[512,512]{1,0:T(8,128)(2,1)S(1)}, u32[]{:S(2)}, u32[]{:S(2)}) collective-permute-start(bf16[512,512]{1,0:T(8,128)(2,1)S(1)} %get-tuple-element.67), channel_id=1, source_target_pairs={{1,0},{2,3},{5,4},{6,7},{9,8},{10,11},{13,12},{14,15},{17,16},{18,... | collective-permute-start | bytes 1572872 | tf_op jit(solution)/shard_map/ppermute | solution.py:35
  137.9 72.7 %collective-permute-start.38 = (f32[1,512]{1,0:T(1,128)S(1)}, f32[1,512]{1,0:T(1,128)S(1)}, u32[]{:S(2)}, u32[]{:S(2)}) collective-permute-start(f32[1,512]{1,0:T(1,128)S(1)} %slice_add_fusion), channel_id=1, source_target_pairs={{1,0},{2,3},{5,4},{6,7},{9,8},{10,11},{13,12},{14,15},{17,16},{18,... | collective-permute-start | bytes 6152 | tf_op jit(solution)/shard_map/ppermute | solution.py:35
  (9 other events, 27.3 us)

commit v15 on v14

--- a/solution.py
+++ b/solution.py
@@ -324,8 +324,9 @@
 
     earlier_e, earlier_o = from_behind(whole_e, "loop", 1), from_behind(whole_o, "loop", 1)
     other = swap_middle(whole)
+    partial = panel(3, [(0, (whole, None, 0)), (1, (whole, None, size))])
+    earlier_e = after(earlier_e, partial)
     across_e, across_o = swap_rows(earlier_e, 2), swap_rows(earlier_o, 2)
-    partial = panel(3, [(0, (whole, None, 0)), (1, (whole, None, size))])
     views = tile_row(earlier_e, across_e, partial)
     moved = panel(3, [(2, (other, None, 0)), (3, (other, None, size))], partial)
     views_o = tile_row(earlier_o, across_o, moved)
@@ -336,7 +337,7 @@
     other_e, across_e = early(swap_middle(halved_e)), early(swap_rows(distant_e, 2))
     other_o, across_o = swap_middle(halved_o), swap_rows(distant_o, 2)
     partial = panel(4, [(0, (halved_o, None, 0)), (1, (halved_e, None, 0))])
-    views = tile_row(distant_e, across_e, partial)
+    views = tile_row(after(distant_e, partial), across_e, partial)
     partial = panel(4, [(3, (other_e, None, 0))], partial)
     base, applied = product(partial, [views], "open", size, vector)
     picked = pick_rows(pivots[4], 2, [view[0] for view in views])

time: 212 us -> 210 us (level)
    ppermute x2, waiting for transfers between devices: 19.5 us -> 16.5 us  [from_behind(): lax.ppermute(value, axis, [(i, (i + by) % devices) for i in range(devices)])]
  transfers between devices with their start and end apart: 39 -> 39, of which waited for: 6 -> 6; matrix products, arithmetic and copies ran while one was open for 0% -> 0% of each run, Pallas kernels for 23% -> 24%
where the time goes in v15:
time: 210 us; the launch traced here: 209 us
  waiting for transfers between devices  107 us (51%)
  Pallas kernels  50.8 us (24%)
  starting transfers between devices  44.7 us (21%)
  other arithmetic  2.56 us (1%)
  local copies, waits for them, and re-layouts  2.41 us (1%)
    ppermute x2, waiting for transfers between devices, outward(): return lax.ppermute(value, 'col', [(1, 0), (2, 3)])  71 us
    pallas_call x14, Pallas kernels, spread_columns(): pl.pallas_call(kernel, out_shape=jax.ShapeDtypeStruct((size, size * count...  33.2 us
    ppermute x3, waiting for transfers between devices, inward(): return lax.ppermute(value, 'col', [(0, 1), (3, 2)])  19 us
    ppermute x3, starting transfers between devices, inward(): return lax.ppermute(value, 'col', [(0, 1), (3, 2)])  17.3 us
    ppermute x24, starting transfers between devices, swap_rows(): return lax.ppermute(value, ('row', 'col'), pairs)  17.1 us
    ppermute x2, waiting for transfers between devices, from_behind(): lax.ppermute(value, axis, [(i, (i + by) % devices) for i in range(devices)])  16.5 us
    pallas_call x9, Pallas kernels, product(): pl.pallas_call(kernel, out_shape=tuple(outs), compiler_params=pltpu.Compi...  15.2 us
    ppermute x8, starting transfers between devices, swap_middle(): return lax.ppermute(value, 'col', [(1, 2), (2, 1)])  5.64 us
  transfers between devices with their start and end apart: 39, of which 6 were waited for; matrix products, arithmetic and copies ran while one was open for 0% of the time, Pallas kernels for 24%

profile of v15, /device:TPU:0, one launch (start us, length us, event | category | flops | bytes accessed | tf_op | source)
XLA Modules:
  0.0 208.6 jit_solution(2763473922596268538)
XLA Ops:
  2.8 1.3 slice_bitcast_fusion.1
  4.4 5.0 %collective-permute-start = (bf16[2,512,512]{2,1,0:T(8,128)(2,1)S(1)}, bf16[2,512,512]{2,1,0:T(8,128)(2,1)S(1)}, u32[]{:S(2)}, u32[]{:S(2)}) collective-permute-start(bf16[2,512,512]{2,1,0:T(8,128)(2,1)S(1)} %slice.29.refs_0_), channel_id=1, source_target_pairs={{0,1},{3,2},{4,5},{7,6},{8,9},{11,10},{12,13},{15,14},{16,17},{19,... | collective-permute-start | bytes 3145736 | tf_op jit(solution)/shard_map/ppermute | solution.py:31
  11.6 7.9 %collective-permute-start.6 = (bf16[528,512]{1,0:T(8,128)(2,1)S(1)}, bf16[528,512]{1,0:T(8,128)(2,1)S(1)}, u32[]{:S(2)}, u32[]{:S(2)}) collective-permute-start(bf16[528,512]{1,0:T(8,128)(2,1)S(1)} %get-tuple-element.48), channel_id=1, source_target_pairs={{0,1},{3,2},{4,5},{7,6},{8,9},{11,10},{12,13},{15,14},{16,17},{19,... | collective-permute-start | bytes 1622024 | tf_op jit(solution)/shard_map/ppermute | solution.py:31
  19.5 1.9 shard_map.61.refs_0_
  21.4 1.9 shard_map.59.refs_0_
  23.3 9.5 %collective-permute-done.refs_1_ = bf16[2,512,512]{2,1,0:T(8,128)(2,1)S(1)} collective-permute-done((bf16[2,512,512]{2,1,0:T(8,128)(2,1)S(1)}, bf16[2,512,512]{2,1,0:T(8,128)(2,1)S(1)}, u32[]{:S(2)}, u32[]{:S(2)}) %collective-permute-start) | collective-permute-done | bytes 1048608 | tf_op jit(solution)/shard_map/ppermute | solution.py:31
  32.9 4.4 %collective-permute-start.10 = (bf16[528,512]{1,0:T(8,128)(2,1)S(1)}, bf16[528,512]{1,0:T(8,128)(2,1)S(1)}, u32[]{:S(2)}, u32[]{:S(2)}) collective-permute-start(bf16[528,512]{1,0:T(8,128)(2,1)S(1)} %get-tuple-element.52), channel_id=1, source_target_pairs={{0,1},{3,2},{4,5},{7,6},{8,9},{11,10},{12,13},{15,14},{16,17},{19,... | collective-permute-start | bytes 1622024 | tf_op jit(solution)/shard_map/ppermute | solution.py:31
  38.1 3.0 %shard_map.63.refs_0_ = bf16[512,2048]{1,0:T(8,128)(2,1)S(1)} custom-call(s32[4,512]{1,0:T(4,128)S(1)} %get-tuple-element.44.q_ref, bf16[512,2048]{1,0:T(8,128)(2,1)S(1)} %shard_map.61.refs_0_, bf16[2,512,512]{2,1,0:T(8,128)(2,1)S(1)} %collective-permute-done.refs_1_, bf16[2,512,512]{2,1,0:T(8,128)(2,1)S(1)} %collective-permute-done.1.refs_2_), custom_call_target="tpu_custom_call" | custom-call | flops 2147483648 | bytes 2097152 | tf_op jit(solution)/shard_map/pallas_call | solution.py:83
  41.1 3.0 %shard_map.60.refs_0_ = bf16[512,2048]{1,0:T(8,128)(2,1)S(1)} custom-call(s32[4,512]{1,0:T(4,128)S(1)} %get-tuple-element.42.q_ref, bf16[512,2048]{1,0:T(8,128)(2,1)S(1)} %shard_map.59.refs_0_, bf16[2,512,512]{2,1,0:T(8,128)(2,1)S(1)} %collective-permute-done.refs_1_, bf16[2,512,512]{2,1,0:T(8,128)(2,1)S(1)} %collective-permute-done.1.refs_2_), custom_call_target="tpu_custom_call" | custom-call | flops 2147483648 | bytes 2097152 | tf_op jit(solution)/shard_map/pallas_call | solution.py:83
  45.9 9.0 %collective-permute-done.10.rest_1_ = bf16[528,512]{1,0:T(8,128)(2,1)S(1)} collective-permute-done((bf16[528,512]{1,0:T(8,128)(2,1)S(1)}, bf16[528,512]{1,0:T(8,128)(2,1)S(1)}, u32[]{:S(2)}, u32[]{:S(2)}) %collective-permute-start.10) | collective-permute-done | bytes 540704 | tf_op jit(solution)/shard_map/ppermute | solution.py:31
  57.0 1.9 shard_map.64.left_ref
  59.0 1.9 shard_map.62.left_ref
  61.6 3.4 %shard_map.65 = (bf16[528,1024]{1,0:T(8,128)(2,1)S(1)}, f32[16,512]{1,0:T(8,128)}) custom-call(bf16[512,2048]{1,0:T(8,128)(2,1)S(1)} %shard_map.64.left_ref, bf16[1,512]{1,0:T(2,128)(2,1)S(1)} %compare_convert_fusion.rest_0_, bf16[2,528,512]{2,1,0:T(8,128)(2,1)S(1)} %pad_maximum_fusion.rest_1_.rest_0_.rest_5_, ...), custom_call_target="tpu_custom_call" | custom-call | flops 2147483648 | bytes 6291456 | tf_op jit(solution)/shard_map/pallas_call | solution.py:145
  68.5 1.7 shard_map.67
  71.6 3.0 %shard_map.68.refs_0_ = bf16[512,2048]{1,0:T(8,128)(2,1)S(1)} custom-call(s32[4,512]{1,0:T(4,128)S(1)} %get-tuple-element.41.q_ref, bf16[512,512]{1,0:T(8,128)(2,1)S(1)} %shard_map.66.refs_0_, bf16[528,512]{1,0:T(8,128)(2,1)S(1)} %get-tuple-element.54.refs_1_), custom_call_target="tpu_custom_call" | custom-call | flops 2147483648 | bytes 2097152 | tf_op jit(solution)/shard_map/pallas_call | solution.py:83
  74.6 1.9 shard_map.69.refs_0_
  77.5 1.9 shard_map.70.left_ref
  79.4 1.7 shard_map.71
  81.2 1.5 collective-permute-start.20
  85.4 3.0 %shard_map.74.refs_0_ = bf16[512,2048]{1,0:T(8,128)(2,1)S(1)} custom-call(s32[4,512]{1,0:T(4,128)S(1)} %get-tuple-element.40.q_ref, bf16[512,1024]{1,0:T(8,128)(2,1)S(1)} %shard_map.73.refs_0_), custom_call_target="tpu_custom_call" | custom-call | flops 2147483648 | bytes 2097152 | tf_op jit(solution)/shard_map/pallas_call | solution.py:83
  88.4 8.0 %collective-permute-done.20.rest_1_ = bf16[528,512]{1,0:T(8,128)(2,1)S(1)} collective-permute-done((bf16[528,512]{1,0:T(8,128)(2,1)S(1)}, bf16[528,512]{1,0:T(8,128)(2,1)S(1)}, u32[]{:S(2)}, u32[]{:S(2)}) %collective-permute-start.20) | collective-permute-done | bytes 540704 | tf_op jit(solution)/shard_map/ppermute | solution.py:17
  97.1 8.5 %collective-permute-done.24.rest_0_ = bf16[512,512]{1,0:T(8,128)(2,1)S(1)} collective-permute-done((bf16[512,512]{1,0:T(8,128)(2,1)S(1)}, bf16[512,512]{1,0:T(8,128)(2,1)S(1)}, u32[]{:S(2)}, u32[]{:S(2)}) %collective-permute-start.24) | collective-permute-done | bytes 524320 | tf_op jit(solution)/shard_map/ppermute | solution.py:17
  108.4 3.0 %shard_map.75.left_ref = bf16[512,2048]{1,0:T(8,128)(2,1)S(1)} custom-call(s32[4,512]{1,0:T(4,128)S(1)} %get-tuple-element.40.q_ref, bf16[512,2048]{1,0:T(8,128)(2,1)S(1)} %shard_map.74.refs_0_, bf16[512,1024]{1,0:T(8,128)(2,1)S(1)} %collective-permute-done.19.refs_1_), custom_call_target="tpu_custom_call" | custom-call | flops 2147483648 | bytes 2097152 | tf_op jit(solution)/shard_map/pallas_call | solution.py:83
  112.1 1.7 shard_map.76
  118.6 3.0 %shard_map.78.refs_0_ = bf16[512,2048]{1,0:T(8,128)(2,1)S(1)} custom-call(s32[4,512]{1,0:T(4,128)S(1)} %get-tuple-element.39.q_ref, bf16[512,512]{1,0:T(8,128)(2,1)S(1)} %shard_map.77.refs_0_.rest_0_, bf16[528,512]{1,0:T(8,128)(2,1)S(1)} %get-tuple-element.66.refs_1_.rest_1_.refs_0_), custom_call_target="tpu_custom_call" | custom-call | flops 2147483648 | bytes 2097152 | tf_op jit(solution)/shard_map/pallas_call | solution.py:83
  123.1 1.9 shard_map.80.left_ref.refs_0_
  125.0 1.7 shard_map.83.picked_ref
  126.8 1.7 shard_map.82
  129.7 1.3 collective-permute-start.36
  131.0 1.9 shard_map.86.left_ref
  134.9 1.3 collective-permute-start.38
  136.2 71.0 %collective-permute-done.36 = bf16[512,512]{1,0:T(8,128)(2,1)S(1)} collective-permute-done((bf16[512,512]{1,0:T(8,128)(2,1)S(1)}, bf16[512,512]{1,0:T(8,128)(2,1)S(1)}, u32[]{:S(2)}, u32[]{:S(2)}) %collective-permute-start.36) | collective-permute-done | bytes 524320 | tf_op jit(solution)/shard_map/ppermute | solution.py:35
  (101 shorter events, 33.1 us)
Async XLA Ops:
  4.4 28.5 %collective-permute-start = (bf16[2,512,512]{2,1,0:T(8,128)(2,1)S(1)}, bf16[2,512,512]{2,1,0:T(8,128)(2,1)S(1)}, u32[]{:S(2)}, u32[]{:S(2)}) collective-permute-start(bf16[2,512,512]{2,1,0:T(8,128)(2,1)S(1)} %slice.29.refs_0_), channel_id=1, source_target_pairs={{0,1},{3,2},{4,5},{7,6},{8,9},{11,10},{12,13},{15,14},{16,17},{19,... | collective-permute-start | bytes 3145736 | tf_op jit(solution)/shard_map/ppermute | solution.py:31
  9.4 27.9 %collective-permute-start.1 = (bf16[2,512,512]{2,1,0:T(8,128)(2,1)S(1)}, bf16[2,512,512]{2,1,0:T(8,128)(2,1)S(1)}, u32[]{:S(2)}, u32[]{:S(2)}) collective-permute-start(bf16[2,512,512]{2,1,0:T(8,128)(2,1)S(1)} %slice.29.refs_0_), channel_id=1, source_target_pairs={{1,2},{2,1},{5,6},{6,5},{9,10},{10,9},{13,14},{14,13},{17,18},{18,... | collective-permute-start | bytes 3145736 | tf_op jit(solution)/shard_map/ppermute | solution.py:27
  10.1 35.0 %collective-permute-start.4 = (bf16[2,528,512]{2,1,0:T(8,128)(2,1)S(1)}, bf16[2,528,512]{2,1,0:T(8,128)(2,1)S(1)}, u32[]{:S(2)}, u32[]{:S(2)}) collective-permute-start(bf16[2,528,512]{2,1,0:T(8,128)(2,1)S(1)} %pad_maximum_fusion.rest_1_.rest_0_.rest_5_), channel_id=1, source_target_pairs={{1,9},{2,10},{5,13},{6,14},{9,1},{10,2},{13,5},{14,6},{17,25},{18,... | collective-permute-start | bytes 3244040 | tf_op jit(solution)/shard_map/ppermute | solution.py:23
  10.9 50.0 %collective-permute-start.3 = (bf16[2,528,512]{2,1,0:T(8,128)(2,1)S(1)}, bf16[2,528,512]{2,1,0:T(8,128)(2,1)S(1)}, u32[]{:S(2)}, u32[]{:S(2)}) collective-permute-start(bf16[2,528,512]{2,1,0:T(8,128)(2,1)S(1)} %pad_maximum_fusion.rest_1_.rest_0_.rest_5_), channel_id=1, source_target_pairs={{1,5},{2,6},{5,1},{6,2},{9,13},{10,14},{13,9},{14,10},{17,21},{18,... | collective-permute-start | bytes 3244040 | tf_op jit(solution)/shard_map/ppermute | solution.py:23
  11.6 32.9 %collective-permute-start.6 = (bf16[528,512]{1,0:T(8,128)(2,1)S(1)}, bf16[528,512]{1,0:T(8,128)(2,1)S(1)}, u32[]{:S(2)}, u32[]{:S(2)}) collective-permute-start(bf16[528,512]{1,0:T(8,128)(2,1)S(1)} %get-tuple-element.48), channel_id=1, source_target_pairs={{0,1},{3,2},{4,5},{7,6},{8,9},{11,10},{12,13},{15,14},{16,17},{19,... | collective-permute-start | bytes 1622024 | tf_op jit(solution)/shard_map/ppermute | solution.py:31
  32.9 22.0 %collective-permute-start.10 = (bf16[528,512]{1,0:T(8,128)(2,1)S(1)}, bf16[528,512]{1,0:T(8,128)(2,1)S(1)}, u32[]{:S(2)}, u32[]{:S(2)}) collective-permute-start(bf16[528,512]{1,0:T(8,128)(2,1)S(1)} %get-tuple-element.52), channel_id=1, source_target_pairs={{0,1},{3,2},{4,5},{7,6},{8,9},{11,10},{12,13},{15,14},{16,17},{19,... | collective-permute-start | bytes 1622024 | tf_op jit(solution)/shard_map/ppermute | solution.py:31
  37.3 19.0 %collective-permute-start.2 = (bf16[2,512,512]{2,1,0:T(8,128)(2,1)S(1)}, bf16[2,512,512]{2,1,0:T(8,128)(2,1)S(1)}, u32[]{:S(2)}, u32[]{:S(2)}) collective-permute-start(bf16[2,512,512]{2,1,0:T(8,128)(2,1)S(1)} %collective-permute-done.refs_1_), channel_id=1, source_target_pairs={{1,2},{2,1},{5,6},{6,5},{9,10},{10,9},{13,14},{14,13},{17,18},{18,... | collective-permute-start | bytes 3145736 | tf_op jit(solution)/shard_map/ppermute | solution.py:27
  44.5 11.1 %collective-permute-start.8 = (bf16[528,512]{1,0:T(8,128)(2,1)S(1)}, bf16[528,512]{1,0:T(8,128)(2,1)S(1)}, u32[]{:S(2)}, u32[]{:S(2)}) collective-permute-start(bf16[528,512]{1,0:T(8,128)(2,1)S(1)} %collective-permute-done.6.rest_5_), channel_id=1, source_target_pairs={{1,9},{2,10},{5,13},{6,14},{9,1},{10,2},{13,5},{14,6},{17,25},{18,... | collective-permute-start | bytes 1622024 | tf_op jit(solution)/shard_map/ppermute | solution.py:23
  45.2 16.4 %collective-permute-start.5 = (bf16[2,528,512]{2,1,0:T(8,128)(2,1)S(1)}, bf16[2,528,512]{2,1,0:T(8,128)(2,1)S(1)}, u32[]{:S(2)}, u32[]{:S(2)}) collective-permute-start(bf16[2,528,512]{2,1,0:T(8,128)(2,1)S(1)} %collective-permute-done.4.rest_3_.rest_2_.rest_7_), channel_id=1, source_target_pairs={{1,5},{2,6},{5,1},{6,2},{9,13},{10,14},{13,9},{14,10},{17,21},{18,... | collective-permute-start | bytes 3244040 | tf_op jit(solution)/shard_map/ppermute | solution.py:23
  54.9 6.7 %collective-permute-start.7 = (bf16[528,512]{1,0:T(8,128)(2,1)S(1)}, bf16[528,512]{1,0:T(8,128)(2,1)S(1)}, u32[]{:S(2)}, u32[]{:S(2)}) collective-permute-start(bf16[528,512]{1,0:T(8,128)(2,1)S(1)} %collective-permute-done.6.rest_5_), channel_id=1, source_target_pairs={{1,5},{2,6},{5,1},{6,2},{9,13},{10,14},{13,9},{14,10},{17,21},{18,... | collective-permute-start | bytes 1622024 | tf_op jit(solution)/shard_map/ppermute | solution.py:23
  55.6 6.0 %collective-permute-start.9 = (bf16[528,512]{1,0:T(8,128)(2,1)S(1)}, bf16[528,512]{1,0:T(8,128)(2,1)S(1)}, u32[]{:S(2)}, u32[]{:S(2)}) collective-permute-start(bf16[528,512]{1,0:T(8,128)(2,1)S(1)} %collective-permute-done.8.rest_7_), channel_id=1, source_target_pairs={{1,5},{2,6},{5,1},{6,2},{9,13},{10,14},{13,9},{14,10},{17,21},{18,... | collective-permute-start | bytes 1622024 | tf_op jit(solution)/shard_map/ppermute | solution.py:23
  56.3 10.0 %collective-permute-start.12 = (bf16[528,512]{1,0:T(8,128)(2,1)S(1)}, bf16[528,512]{1,0:T(8,128)(2,1)S(1)}, u32[]{:S(2)}, u32[]{:S(2)}) collective-permute-start(bf16[528,512]{1,0:T(8,128)(2,1)S(1)} %collective-permute-done.10.rest_1_), channel_id=1, source_target_pairs={{1,9},{2,10},{5,13},{6,14},{9,1},{10,2},{13,5},{14,6},{17,25},{18,... | collective-permute-start | bytes 1622024 | tf_op jit(solution)/shard_map/ppermute | solution.py:23
  60.9 7.6 %collective-permute-start.11 = (bf16[528,512]{1,0:T(8,128)(2,1)S(1)}, bf16[528,512]{1,0:T(8,128)(2,1)S(1)}, u32[]{:S(2)}, u32[]{:S(2)}) collective-permute-start(bf16[528,512]{1,0:T(8,128)(2,1)S(1)} %collective-permute-done.10.rest_1_), channel_id=1, source_target_pairs={{1,5},{2,6},{5,1},{6,2},{9,13},{10,14},{13,9},{14,10},{17,21},{18,... | collective-permute-start | bytes 1622024 | tf_op jit(solution)/shard_map/ppermute | solution.py:23
  67.0 9.6 %collective-permute-start.17 = (bf16[528,1024]{1,0:T(8,128)(2,1)S(1)}, bf16[528,1024]{1,0:T(8,128)(2,1)S(1)}, u32[]{:S(2)}, u32[]{:S(2)}) collective-permute-start(bf16[528,1024]{1,0:T(8,128)(2,1)S(1)} %get-tuple-element.50.rest_1_.rest_0_), channel_id=1, source_target_pairs={{1,9},{2,10},{5,13},{6,14},{9,1},{10,2},{13,5},{14,6},{17,25},{18,... | collective-permute-start | bytes 3244040 | tf_op jit(solution)/shard_map/ppermute | solution.py:23
  67.8 6.9 %collective-permute-start.14 = (bf16[512,512]{1,0:T(8,128)(2,1)S(1)}, bf16[512,512]{1,0:T(8,128)(2,1)S(1)}, u32[]{:S(2)}, u32[]{:S(2)}) collective-permute-start(bf16[512,512]{1,0:T(8,128)(2,1)S(1)} %shard_map.66.refs_0_), channel_id=1, source_target_pairs={{1,2},{2,1},{5,6},{6,5},{9,10},{10,9},{13,14},{14,13},{17,18},{18,... | collective-permute-start | bytes 1572872 | tf_op jit(solution)/shard_map/ppermute | solution.py:27
  70.2 6.4 %collective-permute-start.15 = (bf16[528,512]{1,0:T(8,128)(2,1)S(1)}, bf16[528,512]{1,0:T(8,128)(2,1)S(1)}, u32[]{:S(2)}, u32[]{:S(2)}) collective-permute-start(bf16[528,512]{1,0:T(8,128)(2,1)S(1)} %get-tuple-element.54.refs_1_), channel_id=1, source_target_pairs={{1,2},{2,1},{5,6},{6,5},{9,10},{10,9},{13,14},{14,13},{17,18},{18,... | collective-permute-start | bytes 1622024 | tf_op jit(solution)/shard_map/ppermute | solution.py:27
  70.9 8.5 %collective-permute-start.16 = (bf16[528,1024]{1,0:T(8,128)(2,1)S(1)}, bf16[528,1024]{1,0:T(8,128)(2,1)S(1)}, u32[]{:S(2)}, u32[]{:S(2)}) collective-permute-start(bf16[528,1024]{1,0:T(8,128)(2,1)S(1)} %get-tuple-element.50.rest_1_.rest_0_), channel_id=1, source_target_pairs={{1,5},{2,6},{5,1},{6,2},{9,13},{10,14},{13,9},{14,10},{17,21},{18,... | collective-permute-start | bytes 3244040 | tf_op jit(solution)/shard_map/ppermute | solution.py:23
  81.2 15.2 %collective-permute-start.20 = (bf16[528,512]{1,0:T(8,128)(2,1)S(1)}, bf16[528,512]{1,0:T(8,128)(2,1)S(1)}, u32[]{:S(2)}, u32[]{:S(2)}) collective-permute-start(bf16[528,512]{1,0:T(8,128)(2,1)S(1)} %get-tuple-element.57.right_ref), channel_id=1, source_target_pairs={{0,16},{16,0},{1,17},{17,1},{2,18},{18,2},{3,19},{19,3},{4,20},{20... | collective-permute-start | bytes 1622024 | tf_op jit(solution)/shard_map/ppermute | solution.py:17
  84.0 24.4 %collective-permute-start.19 = (bf16[512,1024]{1,0:T(8,128)(2,1)S(1)}, bf16[512,1024]{1,0:T(8,128)(2,1)S(1)}, u32[]{:S(2)}, u32[]{:S(2)}) collective-permute-start(bf16[512,1024]{1,0:T(8,128)(2,1)S(1)} %shard_map.73.refs_0_), channel_id=1, source_target_pairs={{1,2},{2,1},{5,6},{6,5},{9,10},{10,9},{13,14},{14,13},{17,18},{18,... | collective-permute-start | bytes 3145736 | tf_op jit(solution)/shard_map/ppermute | solution.py:27
  84.8 20.8 %collective-permute-start.24 = (bf16[512,512]{1,0:T(8,128)(2,1)S(1)}, bf16[512,512]{1,0:T(8,128)(2,1)S(1)}, u32[]{:S(2)}, u32[]{:S(2)}) collective-permute-start(bf16[512,512]{1,0:T(8,128)(2,1)S(1)} %shard_map.72.left_ref), channel_id=1, source_target_pairs={{0,16},{16,0},{1,17},{17,1},{2,18},{18,2},{3,19},{19,3},{4,20},{20... | collective-permute-start | bytes 1572872 | tf_op jit(solution)/shard_map/ppermute | solution.py:17
  96.4 10.6 %collective-permute-start.22 = (bf16[528,512]{1,0:T(8,128)(2,1)S(1)}, bf16[528,512]{1,0:T(8,128)(2,1)S(1)}, u32[]{:S(2)}, u32[]{:S(2)}) collective-permute-start(bf16[528,512]{1,0:T(8,128)(2,1)S(1)} %collective-permute-done.20.rest_1_), channel_id=1, source_target_pairs={{1,9},{2,10},{5,13},{6,14},{9,1},{10,2},{13,5},{14,6},{17,25},{18,... | collective-permute-start | bytes 1622024 | tf_op jit(solution)/shard_map/ppermute | solution.py:23
  105.6 5.8 %collective-permute-start.26 = (bf16[512,512]{1,0:T(8,128)(2,1)S(1)}, bf16[512,512]{1,0:T(8,128)(2,1)S(1)}, u32[]{:S(2)}, u32[]{:S(2)}) collective-permute-start(bf16[512,512]{1,0:T(8,128)(2,1)S(1)} %collective-permute-done.24.rest_0_), channel_id=1, source_target_pairs={{1,9},{2,10},{5,13},{6,14},{9,1},{10,2},{13,5},{14,6},{17,25},{18,... | collective-permute-start | bytes 1572872 | tf_op jit(solution)/shard_map/ppermute | solution.py:23
  106.3 5.9 %collective-permute-start.21 = (bf16[528,512]{1,0:T(8,128)(2,1)S(1)}, bf16[528,512]{1,0:T(8,128)(2,1)S(1)}, u32[]{:S(2)}, u32[]{:S(2)}) collective-permute-start(bf16[528,512]{1,0:T(8,128)(2,1)S(1)} %collective-permute-done.20.rest_1_), channel_id=1, source_target_pairs={{1,5},{2,6},{5,1},{6,2},{9,13},{10,14},{13,9},{14,10},{17,21},{18,... | collective-permute-start | bytes 1622024 | tf_op jit(solution)/shard_map/ppermute | solution.py:23
  107.0 5.1 %collective-permute-start.23 = (bf16[528,512]{1,0:T(8,128)(2,1)S(1)}, bf16[528,512]{1,0:T(8,128)(2,1)S(1)}, u32[]{:S(2)}, u32[]{:S(2)}) collective-permute-start(bf16[528,512]{1,0:T(8,128)(2,1)S(1)} %collective-permute-done.22.rest_3_), channel_id=1, source_target_pairs={{1,5},{2,6},{5,1},{6,2},{9,13},{10,14},{13,9},{14,10},{17,21},{18,... | collective-permute-start | bytes 1622024 | tf_op jit(solution)/shard_map/ppermute | solution.py:23
  107.7 7.6 %collective-permute-start.25 = (bf16[512,512]{1,0:T(8,128)(2,1)S(1)}, bf16[512,512]{1,0:T(8,128)(2,1)S(1)}, u32[]{:S(2)}, u32[]{:S(2)}) collective-permute-start(bf16[512,512]{1,0:T(8,128)(2,1)S(1)} %collective-permute-done.24.rest_0_), channel_id=1, source_target_pairs={{1,5},{2,6},{5,1},{6,2},{9,13},{10,14},{13,9},{14,10},{17,21},{18,... | collective-permute-start | bytes 1572872 | tf_op jit(solution)/shard_map/ppermute | solution.py:23
  113.8 7.8 %collective-permute-start.31 = (bf16[528,512]{1,0:T(8,128)(2,1)S(1)}, bf16[528,512]{1,0:T(8,128)(2,1)S(1)}, u32[]{:S(2)}, u32[]{:S(2)}) collective-permute-start(bf16[528,512]{1,0:T(8,128)(2,1)S(1)} %get-tuple-element.66.refs_1_.rest_1_.refs_0_), channel_id=1, source_target_pairs={{1,9},{2,10},{5,13},{6,14},{9,1},{10,2},{13,5},{14,6},{17,25},{18,... | collective-permute-start | bytes 1622024 | tf_op jit(solution)/shard_map/ppermute | solution.py:23
  114.6 7.8 %collective-permute-start.28 = (bf16[528,512]{1,0:T(8,128)(2,1)S(1)}, bf16[528,512]{1,0:T(8,128)(2,1)S(1)}, u32[]{:S(2)}, u32[]{:S(2)}) collective-permute-start(bf16[528,512]{1,0:T(8,128)(2,1)S(1)} %get-tuple-element.66.refs_1_.rest_1_.refs_0_), channel_id=1, source_target_pairs={{1,2},{2,1},{5,6},{6,5},{9,10},{10,9},{13,14},{14,13},{17,18},{18,... | collective-permute-start | bytes 1622024 | tf_op jit(solution)/shard_map/ppermute | solution.py:27
  116.5 11.9 %collective-permute-start.34 = (bf16[512,512]{1,0:T(8,128)(2,1)S(1)}, bf16[512,512]{1,0:T(8,128)(2,1)S(1)}, u32[]{:S(2)}, u32[]{:S(2)}) collective-permute-start(bf16[512,512]{1,0:T(8,128)(2,1)S(1)} %shard_map.77.refs_0_.rest_0_), channel_id=1, source_target_pairs={{1,9},{2,10},{5,13},{6,14},{9,1},{10,2},{13,5},{14,6},{17,25},{18,... | collective-permute-start | bytes 1572872 | tf_op jit(solution)/shard_map/ppermute | solution.py:23
  117.2 12.0 %collective-permute-start.29 = (bf16[512,512]{1,0:T(8,128)(2,1)S(1)}, bf16[512,512]{1,0:T(8,128)(2,1)S(1)}, u32[]{:S(2)}, u32[]{:S(2)}) collective-permute-start(bf16[512,512]{1,0:T(8,128)(2,1)S(1)} %shard_map.77.refs_0_.rest_0_), channel_id=1, source_target_pairs={{1,2},{2,1},{5,6},{6,5},{9,10},{10,9},{13,14},{14,13},{17,18},{18,... | collective-permute-start | bytes 1572872 | tf_op jit(solution)/shard_map/ppermute | solution.py:27
  117.9 15.0 %collective-permute-start.33 = (bf16[512,512]{1,0:T(8,128)(2,1)S(1)}, bf16[512,512]{1,0:T(8,128)(2,1)S(1)}, u32[]{:S(2)}, u32[]{:S(2)}) collective-permute-start(bf16[512,512]{1,0:T(8,128)(2,1)S(1)} %shard_map.77.refs_0_.rest_0_), channel_id=1, source_target_pairs={{1,5},{2,6},{5,1},{6,2},{9,13},{10,14},{13,9},{14,10},{17,21},{18,... | collective-permute-start | bytes 1572872 | tf_op jit(solution)/shard_map/ppermute | solution.py:23
  129.7 77.5 %collective-permute-start.36 = (bf16[512,512]{1,0:T(8,128)(2,1)S(1)}, bf16[512,512]{1,0:T(8,128)(2,1)S(1)}, u32[]{:S(2)}, u32[]{:S(2)}) collective-permute-start(bf16[512,512]{1,0:T(8,128)(2,1)S(1)} %get-tuple-element.71), channel_id=1, source_target_pairs={{1,0},{2,3},{5,4},{6,7},{9,8},{10,11},{13,12},{14,15},{17,16},{18,... | collective-permute-start | bytes 1572872 | tf_op jit(solution)/shard_map/ppermute | solution.py:35
  134.9 73.2 %collective-permute-start.38 = (f32[1,512]{1,0:T(1,128)S(1)}, f32[1,512]{1,0:T(1,128)S(1)}, u32[]{:S(2)}, u32[]{:S(2)}) collective-permute-start(f32[1,512]{1,0:T(1,128)S(1)} %slice_add_fusion), channel_id=1, source_target_pairs={{1,0},{2,3},{5,4},{6,7},{9,8},{10,11},{13,12},{14,15},{17,16},{18,... | collective-permute-start | bytes 6152 | tf_op jit(solution)/shard_map/ppermute | solution.py:35
  (9 other events, 24.8 us)

commit v16 on v15

--- a/solution.py
+++ b/solution.py
@@ -304,13 +304,13 @@
     def right_views(right, tie):
         parts = []
         for tile in right:
-            beside, across = swap_rows(tile, 1), swap_rows(tile, 2)
+            beside, across = swap_rows(tile, 1), early(swap_rows(tile, 2), 6)
             parts.append([tile, beside, across, swap_rows(after(across, *tie), 1)])
         if len(parts) == 1:
             return [[(tile, None, column) for tile in parts[0]] for column in (0, size)]
         return [plain(*part) for part in parts]
 
-    other_o, other_e = swap_middle(upper_o), swap_middle(upper_e)
+    other_o, other_e = early(swap_middle(upper_o), 4), swap_middle(upper_e)
     moved = panel(1, [(0, (upper_o, None, 0)), (1, (upper_e, None, 0))])
     moved = panel(1, [(2, (other_o, None, 0))], moved)
     views = right_views([lower], (moved, other_e))
@@ -334,7 +334,7 @@
     (halved_o,) = product(after(moved, halved_e), [views_o], "apart", size)
 
     distant_e, distant_o = from_behind(halved_e, "loop", 2), from_behind(halved_o, "loop", 2)
-    other_e, across_e = early(swap_middle(halved_e)), early(swap_rows(distant_e, 2))
+    other_e, across_e = early(swap_middle(halved_e)), swap_rows(distant_e, 2)
     other_o, across_o = swap_middle(halved_o), swap_rows(distant_o, 2)
     partial = panel(4, [(0, (halved_o, None, 0)), (1, (halved_e, None, 0))])
     views = tile_row(after(distant_e, partial), across_e, partial)

time: 210 us -> 206 us (0.981)
  waiting for transfers between devices: 107 us -> 102 us
    ppermute x2, waiting for transfers between devices: 71 us -> 66.7 us  [outward(): return lax.ppermute(value, 'col', [(1, 0), (2, 3)])]
where the time goes in v16:
time: 206 us; the launch traced here: 205 us
  waiting for transfers between devices  102 us (50%)
  Pallas kernels  50.8 us (25%)
  starting transfers between devices  44.7 us (22%)
  local copies, waits for them, and re-layouts  3.17 us (2%)
  other arithmetic  2.59 us (1%)
    ppermute x2, waiting for transfers between devices, outward(): return lax.ppermute(value, 'col', [(1, 0), (2, 3)])  66.7 us
    pallas_call x14, Pallas kernels, spread_columns(): pl.pallas_call(kernel, out_shape=jax.ShapeDtypeStruct((size, size * count...  33.2 us
    ppermute x3, waiting for transfers between devices, inward(): return lax.ppermute(value, 'col', [(0, 1), (3, 2)])  19 us
    ppermute x3, starting transfers between devices, inward(): return lax.ppermute(value, 'col', [(0, 1), (3, 2)])  17.3 us
    ppermute x24, starting transfers between devices, swap_rows(): return lax.ppermute(value, ('row', 'col'), pairs)  17.1 us
    ppermute x2, waiting for transfers between devices, from_behind(): lax.ppermute(value, axis, [(i, (i + by) % devices) for i in range(devices)])  16.5 us
    pallas_call x9, Pallas kernels, product(): pl.pallas_call(kernel, out_shape=tuple(outs), compiler_params=pltpu.Compi...  15.2 us
    ppermute x8, starting transfers between devices, swap_middle(): return lax.ppermute(value, 'col', [(1, 2), (2, 1)])  5.64 us
  transfers between devices with their start and end apart: 39, of which 6 were waited for; matrix products, arithmetic and copies ran while one was open for 0% of the time, Pallas kernels for 24%

profile of v16, /device:TPU:0, one launch (start us, length us, event | category | flops | bytes accessed | tf_op | source)
XLA Modules:
  0.0 205.1 jit_solution(8071274958182716935)
XLA Ops:
  2.7 1.4 slice_bitcast_fusion.1
  5.2 5.0 %collective-permute-start = (bf16[2,512,512]{2,1,0:T(8,128)(2,1)S(1)}, bf16[2,512,512]{2,1,0:T(8,128)(2,1)S(1)}, u32[]{:S(2)}, u32[]{:S(2)}) collective-permute-start(bf16[2,512,512]{2,1,0:T(8,128)(2,1)S(1)} %slice.29.refs_0_), channel_id=1, source_target_pairs={{0,1},{3,2},{4,5},{7,6},{8,9},{11,10},{12,13},{15,14},{16,17},{19,... | collective-permute-start | bytes 3145736 | tf_op jit(solution)/shard_map/ppermute | solution.py:31
  12.4 7.9 %collective-permute-start.6 = (bf16[528,512]{1,0:T(8,128)(2,1)S(1)}, bf16[528,512]{1,0:T(8,128)(2,1)S(1)}, u32[]{:S(2)}, u32[]{:S(2)}) collective-permute-start(bf16[528,512]{1,0:T(8,128)(2,1)S(1)} %get-tuple-element.48), channel_id=1, source_target_pairs={{0,1},{3,2},{4,5},{7,6},{8,9},{11,10},{12,13},{15,14},{16,17},{19,... | collective-permute-start | bytes 1622024 | tf_op jit(solution)/shard_map/ppermute | solution.py:31
  20.3 1.9 shard_map.61.refs_0_
  22.2 1.9 shard_map.59.refs_0_
  24.1 9.5 %collective-permute-done.refs_1_ = bf16[2,512,512]{2,1,0:T(8,128)(2,1)S(1)} collective-permute-done((bf16[2,512,512]{2,1,0:T(8,128)(2,1)S(1)}, bf16[2,512,512]{2,1,0:T(8,128)(2,1)S(1)}, u32[]{:S(2)}, u32[]{:S(2)}) %collective-permute-start) | collective-permute-done | bytes 1048608 | tf_op jit(solution)/shard_map/ppermute | solution.py:31
  33.7 4.4 %collective-permute-start.10 = (bf16[528,512]{1,0:T(8,128)(2,1)S(1)}, bf16[528,512]{1,0:T(8,128)(2,1)S(1)}, u32[]{:S(2)}, u32[]{:S(2)}) collective-permute-start(bf16[528,512]{1,0:T(8,128)(2,1)S(1)} %get-tuple-element.52), channel_id=1, source_target_pairs={{0,1},{3,2},{4,5},{7,6},{8,9},{11,10},{12,13},{15,14},{16,17},{19,... | collective-permute-start | bytes 1622024 | tf_op jit(solution)/shard_map/ppermute | solution.py:31
  38.8 3.0 %shard_map.63.refs_0_ = bf16[512,2048]{1,0:T(8,128)(2,1)S(1)} custom-call(s32[4,512]{1,0:T(4,128)S(1)} %get-tuple-element.44.q_ref, bf16[512,2048]{1,0:T(8,128)(2,1)S(1)} %shard_map.61.refs_0_, bf16[2,512,512]{2,1,0:T(8,128)(2,1)S(1)} %collective-permute-done.refs_1_, bf16[2,512,512]{2,1,0:T(8,128)(2,1)S(1)} %collective-permute-done.1.refs_2_), custom_call_target="tpu_custom_call" | custom-call | flops 2147483648 | bytes 2097152 | tf_op jit(solution)/shard_map/pallas_call | solution.py:83
  41.8 3.0 %shard_map.60.refs_0_ = bf16[512,2048]{1,0:T(8,128)(2,1)S(1)} custom-call(s32[4,512]{1,0:T(4,128)S(1)} %get-tuple-element.42.q_ref, bf16[512,2048]{1,0:T(8,128)(2,1)S(1)} %shard_map.59.refs_0_, bf16[2,512,512]{2,1,0:T(8,128)(2,1)S(1)} %collective-permute-done.refs_1_, bf16[2,512,512]{2,1,0:T(8,128)(2,1)S(1)} %collective-permute-done.1.refs_2_), custom_call_target="tpu_custom_call" | custom-call | flops 2147483648 | bytes 2097152 | tf_op jit(solution)/shard_map/pallas_call | solution.py:83
  46.7 9.0 %collective-permute-done.10.rest_1_ = bf16[528,512]{1,0:T(8,128)(2,1)S(1)} collective-permute-done((bf16[528,512]{1,0:T(8,128)(2,1)S(1)}, bf16[528,512]{1,0:T(8,128)(2,1)S(1)}, u32[]{:S(2)}, u32[]{:S(2)}) %collective-permute-start.10) | collective-permute-done | bytes 540704 | tf_op jit(solution)/shard_map/ppermute | solution.py:31
  57.8 1.9 shard_map.64.left_ref
  59.7 1.9 shard_map.62.left_ref
  61.7 3.4 %shard_map.65 = (bf16[528,1024]{1,0:T(8,128)(2,1)S(1)}, f32[16,512]{1,0:T(8,128)}) custom-call(bf16[512,2048]{1,0:T(8,128)(2,1)S(1)} %shard_map.64.left_ref, bf16[1,512]{1,0:T(2,128)(2,1)S(1)} %compare_convert_fusion.rest_0_, bf16[2,528,512]{2,1,0:T(8,128)(2,1)S(1)} %pad_maximum_fusion.rest_1_.rest_0_.rest_5_, ...), custom_call_target="tpu_custom_call" | custom-call | flops 2147483648 | bytes 6291456 | tf_op jit(solution)/shard_map/pallas_call | solution.py:145
  70.0 1.7 shard_map.67
  72.4 3.0 %shard_map.68.refs_0_ = bf16[512,2048]{1,0:T(8,128)(2,1)S(1)} custom-call(s32[4,512]{1,0:T(4,128)S(1)} %get-tuple-element.41.q_ref, bf16[512,512]{1,0:T(8,128)(2,1)S(1)} %shard_map.66.refs_0_, bf16[528,512]{1,0:T(8,128)(2,1)S(1)} %get-tuple-element.54.refs_1_), custom_call_target="tpu_custom_call" | custom-call | flops 2147483648 | bytes 2097152 | tf_op jit(solution)/shard_map/pallas_call | solution.py:83
  75.4 1.9 shard_map.70.refs_0_
  78.3 1.9 shard_map.71.left_ref
  80.2 1.7 shard_map.73
  82.0 1.5 collective-permute-start.20
  86.2 3.0 %shard_map.76.refs_0_ = bf16[512,2048]{1,0:T(8,128)(2,1)S(1)} custom-call(s32[4,512]{1,0:T(4,128)S(1)} %get-tuple-element.40.q_ref, bf16[512,1024]{1,0:T(8,128)(2,1)S(1)} %shard_map.75.refs_0_), custom_call_target="tpu_custom_call" | custom-call | flops 2147483648 | bytes 2097152 | tf_op jit(solution)/shard_map/pallas_call | solution.py:83
  89.2 8.0 %collective-permute-done.20.rest_1_ = bf16[528,512]{1,0:T(8,128)(2,1)S(1)} collective-permute-done((bf16[528,512]{1,0:T(8,128)(2,1)S(1)}, bf16[528,512]{1,0:T(8,128)(2,1)S(1)}, u32[]{:S(2)}, u32[]{:S(2)}) %collective-permute-start.20) | collective-permute-done | bytes 540704 | tf_op jit(solution)/shard_map/ppermute | solution.py:17
  97.9 8.5 %collective-permute-done.24.rest_0_ = bf16[512,512]{1,0:T(8,128)(2,1)S(1)} collective-permute-done((bf16[512,512]{1,0:T(8,128)(2,1)S(1)}, bf16[512,512]{1,0:T(8,128)(2,1)S(1)}, u32[]{:S(2)}, u32[]{:S(2)}) %collective-permute-start.24) | collective-permute-done | bytes 524320 | tf_op jit(solution)/shard_map/ppermute | solution.py:17
  109.2 3.0 %shard_map.77.left_ref = bf16[512,2048]{1,0:T(8,128)(2,1)S(1)} custom-call(s32[4,512]{1,0:T(4,128)S(1)} %get-tuple-element.40.q_ref, bf16[512,2048]{1,0:T(8,128)(2,1)S(1)} %shard_map.76.refs_0_, bf16[512,1024]{1,0:T(8,128)(2,1)S(1)} %collective-permute-done.19.refs_1_), custom_call_target="tpu_custom_call" | custom-call | flops 2147483648 | bytes 2097152 | tf_op jit(solution)/shard_map/pallas_call | solution.py:83
  112.9 1.7 shard_map.78
  119.4 3.0 %shard_map.80.refs_0_ = bf16[512,2048]{1,0:T(8,128)(2,1)S(1)} custom-call(s32[4,512]{1,0:T(4,128)S(1)} %get-tuple-element.39.q_ref, bf16[512,512]{1,0:T(8,128)(2,1)S(1)} %shard_map.79.refs_0_.rest_0_, bf16[528,512]{1,0:T(8,128)(2,1)S(1)} %get-tuple-element.66.refs_1_.rest_1_.refs_0_), custom_call_target="tpu_custom_call" | custom-call | flops 2147483648 | bytes 2097152 | tf_op jit(solution)/shard_map/pallas_call | solution.py:83
  123.9 1.9 shard_map.82.left_ref.refs_0_
  125.8 1.7 shard_map.84.picked_ref
  127.6 1.7 shard_map.83
  130.5 1.3 collective-permute-start.36
  131.8 1.9 shard_map.87.left_ref
  135.7 1.3 collective-permute-start.38
  137.0 66.7 %collective-permute-done.36 = bf16[512,512]{1,0:T(8,128)(2,1)S(1)} collective-permute-done((bf16[512,512]{1,0:T(8,128)(2,1)S(1)}, bf16[512,512]{1,0:T(8,128)(2,1)S(1)}, u32[]{:S(2)}, u32[]{:S(2)}) %collective-permute-start.36) | collective-permute-done | bytes 524320 | tf_op jit(solution)/shard_map/ppermute | solution.py:35
  (102 shorter events, 33.8 us)
Async XLA Ops:
  5.2 28.5 %collective-permute-start = (bf16[2,512,512]{2,1,0:T(8,128)(2,1)S(1)}, bf16[2,512,512]{2,1,0:T(8,128)(2,1)S(1)}, u32[]{:S(2)}, u32[]{:S(2)}) collective-permute-start(bf16[2,512,512]{2,1,0:T(8,128)(2,1)S(1)} %slice.29.refs_0_), channel_id=1, source_target_pairs={{0,1},{3,2},{4,5},{7,6},{8,9},{11,10},{12,13},{15,14},{16,17},{19,... | collective-permute-start | bytes 3145736 | tf_op jit(solution)/shard_map/ppermute | solution.py:31
  10.2 27.9 %collective-permute-start.1 = (bf16[2,512,512]{2,1,0:T(8,128)(2,1)S(1)}, bf16[2,512,512]{2,1,0:T(8,128)(2,1)S(1)}, u32[]{:S(2)}, u32[]{:S(2)}) collective-permute-start(bf16[2,512,512]{2,1,0:T(8,128)(2,1)S(1)} %slice.29.refs_0_), channel_id=1, source_target_pairs={{1,2},{2,1},{5,6},{6,5},{9,10},{10,9},{13,14},{14,13},{17,18},{18,... | collective-permute-start | bytes 3145736 | tf_op jit(solution)/shard_map/ppermute | solution.py:27
  10.9 35.0 %collective-permute-start.4 = (bf16[2,528,512]{2,1,0:T(8,128)(2,1)S(1)}, bf16[2,528,512]{2,1,0:T(8,128)(2,1)S(1)}, u32[]{:S(2)}, u32[]{:S(2)}) collective-permute-start(bf16[2,528,512]{2,1,0:T(8,128)(2,1)S(1)} %pad_maximum_fusion.rest_1_.rest_0_.rest_5_), channel_id=1, source_target_pairs={{1,9},{2,10},{5,13},{6,14},{9,1},{10,2},{13,5},{14,6},{17,25},{18,... | collective-permute-start | bytes 3244040 | tf_op jit(solution)/shard_map/ppermute | solution.py:23
  11.7 50.0 %collective-permute-start.3 = (bf16[2,528,512]{2,1,0:T(8,128)(2,1)S(1)}, bf16[2,528,512]{2,1,0:T(8,128)(2,1)S(1)}, u32[]{:S(2)}, u32[]{:S(2)}) collective-permute-start(bf16[2,528,512]{2,1,0:T(8,128)(2,1)S(1)} %pad_maximum_fusion.rest_1_.rest_0_.rest_5_), channel_id=1, source_target_pairs={{1,5},{2,6},{5,1},{6,2},{9,13},{10,14},{13,9},{14,10},{17,21},{18,... | collective-permute-start | bytes 3244040 | tf_op jit(solution)/shard_map/ppermute | solution.py:23
  12.4 32.9 %collective-permute-start.6 = (bf16[528,512]{1,0:T(8,128)(2,1)S(1)}, bf16[528,512]{1,0:T(8,128)(2,1)S(1)}, u32[]{:S(2)}, u32[]{:S(2)}) collective-permute-start(bf16[528,512]{1,0:T(8,128)(2,1)S(1)} %get-tuple-element.48), channel_id=1, source_target_pairs={{0,1},{3,2},{4,5},{7,6},{8,9},{11,10},{12,13},{15,14},{16,17},{19,... | collective-permute-start | bytes 1622024 | tf_op jit(solution)/shard_map/ppermute | solution.py:31
  33.7 22.0 %collective-permute-start.10 = (bf16[528,512]{1,0:T(8,128)(2,1)S(1)}, bf16[528,512]{1,0:T(8,128)(2,1)S(1)}, u32[]{:S(2)}, u32[]{:S(2)}) collective-permute-start(bf16[528,512]{1,0:T(8,128)(2,1)S(1)} %get-tuple-element.52), channel_id=1, source_target_pairs={{0,1},{3,2},{4,5},{7,6},{8,9},{11,10},{12,13},{15,14},{16,17},{19,... | collective-permute-start | bytes 1622024 | tf_op jit(solution)/shard_map/ppermute | solution.py:31
  38.1 19.0 %collective-permute-start.2 = (bf16[2,512,512]{2,1,0:T(8,128)(2,1)S(1)}, bf16[2,512,512]{2,1,0:T(8,128)(2,1)S(1)}, u32[]{:S(2)}, u32[]{:S(2)}) collective-permute-start(bf16[2,512,512]{2,1,0:T(8,128)(2,1)S(1)} %collective-permute-done.refs_1_), channel_id=1, source_target_pairs={{1,2},{2,1},{5,6},{6,5},{9,10},{10,9},{13,14},{14,13},{17,18},{18,... | collective-permute-start | bytes 3145736 | tf_op jit(solution)/shard_map/ppermute | solution.py:27
  45.2 11.1 %collective-permute-start.8 = (bf16[528,512]{1,0:T(8,128)(2,1)S(1)}, bf16[528,512]{1,0:T(8,128)(2,1)S(1)}, u32[]{:S(2)}, u32[]{:S(2)}) collective-permute-start(bf16[528,512]{1,0:T(8,128)(2,1)S(1)} %collective-permute-done.6.rest_5_), channel_id=1, source_target_pairs={{1,9},{2,10},{5,13},{6,14},{9,1},{10,2},{13,5},{14,6},{17,25},{18,... | collective-permute-start | bytes 1622024 | tf_op jit(solution)/shard_map/ppermute | solution.py:23
  46.0 15.7 %collective-permute-start.5 = (bf16[2,528,512]{2,1,0:T(8,128)(2,1)S(1)}, bf16[2,528,512]{2,1,0:T(8,128)(2,1)S(1)}, u32[]{:S(2)}, u32[]{:S(2)}) collective-permute-start(bf16[2,528,512]{2,1,0:T(8,128)(2,1)S(1)} %collective-permute-done.4.rest_3_.rest_2_.rest_7_), channel_id=1, source_target_pairs={{1,5},{2,6},{5,1},{6,2},{9,13},{10,14},{13,9},{14,10},{17,21},{18,... | collective-permute-start | bytes 3244040 | tf_op jit(solution)/shard_map/ppermute | solution.py:23
  55.7 6.0 %collective-permute-start.7 = (bf16[528,512]{1,0:T(8,128)(2,1)S(1)}, bf16[528,512]{1,0:T(8,128)(2,1)S(1)}, u32[]{:S(2)}, u32[]{:S(2)}) collective-permute-start(bf16[528,512]{1,0:T(8,128)(2,1)S(1)} %collective-permute-done.6.rest_5_), channel_id=1, source_target_pairs={{1,5},{2,6},{5,1},{6,2},{9,13},{10,14},{13,9},{14,10},{17,21},{18,... | collective-permute-start | bytes 1622024 | tf_op jit(solution)/shard_map/ppermute | solution.py:23
  56.4 5.3 %collective-permute-start.9 = (bf16[528,512]{1,0:T(8,128)(2,1)S(1)}, bf16[528,512]{1,0:T(8,128)(2,1)S(1)}, u32[]{:S(2)}, u32[]{:S(2)}) collective-permute-start(bf16[528,512]{1,0:T(8,128)(2,1)S(1)} %collective-permute-done.8.rest_7_), channel_id=1, source_target_pairs={{1,5},{2,6},{5,1},{6,2},{9,13},{10,14},{13,9},{14,10},{17,21},{18,... | collective-permute-start | bytes 1622024 | tf_op jit(solution)/shard_map/ppermute | solution.py:23
  57.1 11.4 %collective-permute-start.12 = (bf16[528,512]{1,0:T(8,128)(2,1)S(1)}, bf16[528,512]{1,0:T(8,128)(2,1)S(1)}, u32[]{:S(2)}, u32[]{:S(2)}) collective-permute-start(bf16[528,512]{1,0:T(8,128)(2,1)S(1)} %collective-permute-done.10.rest_1_), channel_id=1, source_target_pairs={{1,9},{2,10},{5,13},{6,14},{9,1},{10,2},{13,5},{14,6},{17,25},{18,... | collective-permute-start | bytes 1622024 | tf_op jit(solution)/shard_map/ppermute | solution.py:23
  67.1 10.3 %collective-permute-start.17 = (bf16[528,1024]{1,0:T(8,128)(2,1)S(1)}, bf16[528,1024]{1,0:T(8,128)(2,1)S(1)}, u32[]{:S(2)}, u32[]{:S(2)}) collective-permute-start(bf16[528,1024]{1,0:T(8,128)(2,1)S(1)} %get-tuple-element.50.rest_1_.rest_0_), channel_id=1, source_target_pairs={{1,9},{2,10},{5,13},{6,14},{9,1},{10,2},{13,5},{14,6},{17,25},{18,... | collective-permute-start | bytes 3244040 | tf_op jit(solution)/shard_map/ppermute | solution.py:23
  69.2 11.0 %collective-permute-start.16 = (bf16[528,1024]{1,0:T(8,128)(2,1)S(1)}, bf16[528,1024]{1,0:T(8,128)(2,1)S(1)}, u32[]{:S(2)}, u32[]{:S(2)}) collective-permute-start(bf16[528,1024]{1,0:T(8,128)(2,1)S(1)} %get-tuple-element.50.rest_1_.rest_0_), channel_id=1, source_target_pairs={{1,5},{2,6},{5,1},{6,2},{9,13},{10,14},{13,9},{14,10},{17,21},{18,... | collective-permute-start | bytes 3244040 | tf_op jit(solution)/shard_map/ppermute | solution.py:23
  71.7 5.7 %collective-permute-start.15 = (bf16[528,512]{1,0:T(8,128)(2,1)S(1)}, bf16[528,512]{1,0:T(8,128)(2,1)S(1)}, u32[]{:S(2)}, u32[]{:S(2)}) collective-permute-start(bf16[528,512]{1,0:T(8,128)(2,1)S(1)} %get-tuple-element.54.refs_1_), channel_id=1, source_target_pairs={{1,2},{2,1},{5,6},{6,5},{9,10},{10,9},{13,14},{14,13},{17,18},{18,... | collective-permute-start | bytes 1622024 | tf_op jit(solution)/shard_map/ppermute | solution.py:27
  82.0 15.2 %collective-permute-start.20 = (bf16[528,512]{1,0:T(8,128)(2,1)S(1)}, bf16[528,512]{1,0:T(8,128)(2,1)S(1)}, u32[]{:S(2)}, u32[]{:S(2)}) collective-permute-start(bf16[528,512]{1,0:T(8,128)(2,1)S(1)} %get-tuple-element.57.right_ref), channel_id=1, source_target_pairs={{0,16},{16,0},{1,17},{17,1},{2,18},{18,2},{3,19},{19,3},{4,20},{20... | collective-permute-start | bytes 1622024 | tf_op jit(solution)/shard_map/ppermute | solution.py:17
  84.8 24.4 %collective-permute-start.19 = (bf16[512,1024]{1,0:T(8,128)(2,1)S(1)}, bf16[512,1024]{1,0:T(8,128)(2,1)S(1)}, u32[]{:S(2)}, u32[]{:S(2)}) collective-permute-start(bf16[512,1024]{1,0:T(8,128)(2,1)S(1)} %shard_map.75.refs_0_), channel_id=1, source_target_pairs={{1,2},{2,1},{5,6},{6,5},{9,10},{10,9},{13,14},{14,13},{17,18},{18,... | collective-permute-start | bytes 3145736 | tf_op jit(solution)/shard_map/ppermute | solution.py:27
  85.6 20.8 %collective-permute-start.24 = (bf16[512,512]{1,0:T(8,128)(2,1)S(1)}, bf16[512,512]{1,0:T(8,128)(2,1)S(1)}, u32[]{:S(2)}, u32[]{:S(2)}) collective-permute-start(bf16[512,512]{1,0:T(8,128)(2,1)S(1)} %shard_map.74.left_ref), channel_id=1, source_target_pairs={{0,16},{16,0},{1,17},{17,1},{2,18},{18,2},{3,19},{19,3},{4,20},{20... | collective-permute-start | bytes 1572872 | tf_op jit(solution)/shard_map/ppermute | solution.py:17
  97.2 10.6 %collective-permute-start.22 = (bf16[528,512]{1,0:T(8,128)(2,1)S(1)}, bf16[528,512]{1,0:T(8,128)(2,1)S(1)}, u32[]{:S(2)}, u32[]{:S(2)}) collective-permute-start(bf16[528,512]{1,0:T(8,128)(2,1)S(1)} %collective-permute-done.20.rest_1_), channel_id=1, source_target_pairs={{1,9},{2,10},{5,13},{6,14},{9,1},{10,2},{13,5},{14,6},{17,25},{18,... | collective-permute-start | bytes 1622024 | tf_op jit(solution)/shard_map/ppermute | solution.py:23
  106.4 5.8 %collective-permute-start.26 = (bf16[512,512]{1,0:T(8,128)(2,1)S(1)}, bf16[512,512]{1,0:T(8,128)(2,1)S(1)}, u32[]{:S(2)}, u32[]{:S(2)}) collective-permute-start(bf16[512,512]{1,0:T(8,128)(2,1)S(1)} %collective-permute-done.24.rest_0_), channel_id=1, source_target_pairs={{1,9},{2,10},{5,13},{6,14},{9,1},{10,2},{13,5},{14,6},{17,25},{18,... | collective-permute-start | bytes 1572872 | tf_op jit(solution)/shard_map/ppermute | solution.py:23
  107.1 5.9 %collective-permute-start.21 = (bf16[528,512]{1,0:T(8,128)(2,1)S(1)}, bf16[528,512]{1,0:T(8,128)(2,1)S(1)}, u32[]{:S(2)}, u32[]{:S(2)}) collective-permute-start(bf16[528,512]{1,0:T(8,128)(2,1)S(1)} %collective-permute-done.20.rest_1_), channel_id=1, source_target_pairs={{1,5},{2,6},{5,1},{6,2},{9,13},{10,14},{13,9},{14,10},{17,21},{18,... | collective-permute-start | bytes 1622024 | tf_op jit(solution)/shard_map/ppermute | solution.py:23
  107.8 5.2 %collective-permute-start.23 = (bf16[528,512]{1,0:T(8,128)(2,1)S(1)}, bf16[528,512]{1,0:T(8,128)(2,1)S(1)}, u32[]{:S(2)}, u32[]{:S(2)}) collective-permute-start(bf16[528,512]{1,0:T(8,128)(2,1)S(1)} %collective-permute-done.22.rest_3_), channel_id=1, source_target_pairs={{1,5},{2,6},{5,1},{6,2},{9,13},{10,14},{13,9},{14,10},{17,21},{18,... | collective-permute-start | bytes 1622024 | tf_op jit(solution)/shard_map/ppermute | solution.py:23
  108.5 7.6 %collective-permute-start.25 = (bf16[512,512]{1,0:T(8,128)(2,1)S(1)}, bf16[512,512]{1,0:T(8,128)(2,1)S(1)}, u32[]{:S(2)}, u32[]{:S(2)}) collective-permute-start(bf16[512,512]{1,0:T(8,128)(2,1)S(1)} %collective-permute-done.24.rest_0_), channel_id=1, source_target_pairs={{1,5},{2,6},{5,1},{6,2},{9,13},{10,14},{13,9},{14,10},{17,21},{18,... | collective-permute-start | bytes 1572872 | tf_op jit(solution)/shard_map/ppermute | solution.py:23
  112.2 3.9 %collective-permute-start.27 = (bf16[512,512]{1,0:T(8,128)(2,1)S(1)}, bf16[512,512]{1,0:T(8,128)(2,1)S(1)}, u32[]{:S(2)}, u32[]{:S(2)}) collective-permute-start(bf16[512,512]{1,0:T(8,128)(2,1)S(1)} %collective-permute-done.26.rest_2_), channel_id=1, source_target_pairs={{1,5},{2,6},{5,1},{6,2},{9,13},{10,14},{13,9},{14,10},{17,21},{18,... | collective-permute-start | bytes 1572872 | tf_op jit(solution)/shard_map/ppermute | solution.py:23
  114.6 7.8 %collective-permute-start.31 = (bf16[528,512]{1,0:T(8,128)(2,1)S(1)}, bf16[528,512]{1,0:T(8,128)(2,1)S(1)}, u32[]{:S(2)}, u32[]{:S(2)}) collective-permute-start(bf16[528,512]{1,0:T(8,128)(2,1)S(1)} %get-tuple-element.66.refs_1_.rest_1_.refs_0_), channel_id=1, source_target_pairs={{1,9},{2,10},{5,13},{6,14},{9,1},{10,2},{13,5},{14,6},{17,25},{18,... | collective-permute-start | bytes 1622024 | tf_op jit(solution)/shard_map/ppermute | solution.py:23
  115.3 7.8 %collective-permute-start.28 = (bf16[528,512]{1,0:T(8,128)(2,1)S(1)}, bf16[528,512]{1,0:T(8,128)(2,1)S(1)}, u32[]{:S(2)}, u32[]{:S(2)}) collective-permute-start(bf16[528,512]{1,0:T(8,128)(2,1)S(1)} %get-tuple-element.66.refs_1_.rest_1_.refs_0_), channel_id=1, source_target_pairs={{1,2},{2,1},{5,6},{6,5},{9,10},{10,9},{13,14},{14,13},{17,18},{18,... | collective-permute-start | bytes 1622024 | tf_op jit(solution)/shard_map/ppermute | solution.py:27
  117.3 11.9 %collective-permute-start.34 = (bf16[512,512]{1,0:T(8,128)(2,1)S(1)}, bf16[512,512]{1,0:T(8,128)(2,1)S(1)}, u32[]{:S(2)}, u32[]{:S(2)}) collective-permute-start(bf16[512,512]{1,0:T(8,128)(2,1)S(1)} %shard_map.79.refs_0_.rest_0_), channel_id=1, source_target_pairs={{1,9},{2,10},{5,13},{6,14},{9,1},{10,2},{13,5},{14,6},{17,25},{18,... | collective-permute-start | bytes 1572872 | tf_op jit(solution)/shard_map/ppermute | solution.py:23
  118.0 12.0 %collective-permute-start.29 = (bf16[512,512]{1,0:T(8,128)(2,1)S(1)}, bf16[512,512]{1,0:T(8,128)(2,1)S(1)}, u32[]{:S(2)}, u32[]{:S(2)}) collective-permute-start(bf16[512,512]{1,0:T(8,128)(2,1)S(1)} %shard_map.79.refs_0_.rest_0_), channel_id=1, source_target_pairs={{1,2},{2,1},{5,6},{6,5},{9,10},{10,9},{13,14},{14,13},{17,18},{18,... | collective-permute-start | bytes 1572872 | tf_op jit(solution)/shard_map/ppermute | solution.py:27
  118.7 15.0 %collective-permute-start.33 = (bf16[512,512]{1,0:T(8,128)(2,1)S(1)}, bf16[512,512]{1,0:T(8,128)(2,1)S(1)}, u32[]{:S(2)}, u32[]{:S(2)}) collective-permute-start(bf16[512,512]{1,0:T(8,128)(2,1)S(1)} %shard_map.79.refs_0_.rest_0_), channel_id=1, source_target_pairs={{1,5},{2,6},{5,1},{6,2},{9,13},{10,14},{13,9},{14,10},{17,21},{18,... | collective-permute-start | bytes 1572872 | tf_op jit(solution)/shard_map/ppermute | solution.py:23
  129.2 4.5 %collective-permute-start.35 = (bf16[512,512]{1,0:T(8,128)(2,1)S(1)}, bf16[512,512]{1,0:T(8,128)(2,1)S(1)}, u32[]{:S(2)}, u32[]{:S(2)}) collective-permute-start(bf16[512,512]{1,0:T(8,128)(2,1)S(1)} %collective-permute-done.34.rest_2_), channel_id=1, source_target_pairs={{1,5},{2,6},{5,1},{6,2},{9,13},{10,14},{13,9},{14,10},{17,21},{18,... | collective-permute-start | bytes 1572872 | tf_op jit(solution)/shard_map/ppermute | solution.py:23
  130.5 73.2 %collective-permute-start.36 = (bf16[512,512]{1,0:T(8,128)(2,1)S(1)}, bf16[512,512]{1,0:T(8,128)(2,1)S(1)}, u32[]{:S(2)}, u32[]{:S(2)}) collective-permute-start(bf16[512,512]{1,0:T(8,128)(2,1)S(1)} %get-tuple-element.71), channel_id=1, source_target_pairs={{1,0},{2,3},{5,4},{6,7},{9,8},{10,11},{13,12},{14,15},{17,16},{18,... | collective-permute-start | bytes 1572872 | tf_op jit(solution)/shard_map/ppermute | solution.py:35
  135.7 68.9 %collective-permute-start.38 = (f32[1,512]{1,0:T(1,128)S(1)}, f32[1,512]{1,0:T(1,128)S(1)}, u32[]{:S(2)}, u32[]{:S(2)}) collective-permute-start(f32[1,512]{1,0:T(1,128)S(1)} %slice_add_fusion), channel_id=1, source_target_pairs={{1,0},{2,3},{5,4},{6,7},{9,8},{10,11},{13,12},{14,15},{17,16},{18,... | collective-permute-start | bytes 6152 | tf_op jit(solution)/shard_map/ppermute | solution.py:35
  (9 other events, 19.5 us)

commit v17 on v16

--- a/solution.py
+++ b/solution.py
@@ -310,10 +310,10 @@
             return [[(tile, None, column) for tile in parts[0]] for column in (0, size)]
         return [plain(*part) for part in parts]
 
-    other_o, other_e = early(swap_middle(upper_o), 4), swap_middle(upper_e)
+    other_o, other_e = early(swap_middle(upper_o), 4), early(swap_middle(upper_e), 10)
     moved = panel(1, [(0, (upper_o, None, 0)), (1, (upper_e, None, 0))])
     moved = panel(1, [(2, (other_o, None, 0))], moved)
-    views = right_views([lower], (moved, other_e))
+    views = right_views([lower], (moved,))
     moved = panel(1, [(3, (other_e, None, 0))], moved)
     whole_e, vector = product(moved, views[1:], "apart", size, vector)
     (whole_o,) = product(after(moved, whole_e), views[:1], "apart", size)

time: 206 us -> 204 us (level)
  no operation moved by 1% of the time
where the time goes in v17:
time: 204 us; the launch traced here: 203 us
  waiting for transfers between devices  100 us (49%)
  Pallas kernels  50.8 us (25%)
  starting transfers between devices  44.7 us (22%)
  local copies, waits for them, and re-layouts  3.17 us (2%)
  other arithmetic  2.59 us (1%)
    ppermute x2, waiting for transfers between devices, outward(): return lax.ppermute(value, 'col', [(1, 0), (2, 3)])  64.6 us
    pallas_call x14, Pallas kernels, spread_columns(): pl.pallas_call(kernel, out_shape=jax.ShapeDtypeStruct((size, size * count...  33.2 us
    ppermute x3, waiting for transfers between devices, inward(): return lax.ppermute(value, 'col', [(0, 1), (3, 2)])  19 us
    ppermute x3, starting transfers between devices, inward(): return lax.ppermute(value, 'col', [(0, 1), (3, 2)])  17.3 us
    ppermute x24, starting transfers between devices, swap_rows(): return lax.ppermute(value, ('row', 'col'), pairs)  17.1 us
    ppermute x2, waiting for transfers between devices, from_behind(): lax.ppermute(value, axis, [(i, (i + by) % devices) for i in range(devices)])  16.5 us
    pallas_call x9, Pallas kernels, product(): pl.pallas_call(kernel, out_shape=tuple(outs), compiler_params=pltpu.Compi...  15.2 us
    ppermute x8, starting transfers between devices, swap_middle(): return lax.ppermute(value, 'col', [(1, 2), (2, 1)])  5.64 us
  transfers between devices with their start and end apart: 39, of which 6 were waited for; matrix products, arithmetic and copies ran while one was open for 0% of the time, Pallas kernels for 24%

profile of v17, /device:TPU:0, one launch (start us, length us, event | category | flops | bytes accessed | tf_op | source)
XLA Modules:
  0.0 203.0 jit_solution(13375342441545869054)
XLA Ops:
  2.7 1.4 slice_bitcast_fusion.1
  5.2 5.0 %collective-permute-start = (bf16[2,512,512]{2,1,0:T(8,128)(2,1)S(1)}, bf16[2,512,512]{2,1,0:T(8,128)(2,1)S(1)}, u32[]{:S(2)}, u32[]{:S(2)}) collective-permute-start(bf16[2,512,512]{2,1,0:T(8,128)(2,1)S(1)} %slice.29.refs_0_), channel_id=1, source_target_pairs={{0,1},{3,2},{4,5},{7,6},{8,9},{11,10},{12,13},{15,14},{16,17},{19,... | collective-permute-start | bytes 3145736 | tf_op jit(solution)/shard_map/ppermute | solution.py:31
  12.4 7.9 %collective-permute-start.6 = (bf16[528,512]{1,0:T(8,128)(2,1)S(1)}, bf16[528,512]{1,0:T(8,128)(2,1)S(1)}, u32[]{:S(2)}, u32[]{:S(2)}) collective-permute-start(bf16[528,512]{1,0:T(8,128)(2,1)S(1)} %get-tuple-element.48), channel_id=1, source_target_pairs={{0,1},{3,2},{4,5},{7,6},{8,9},{11,10},{12,13},{15,14},{16,17},{19,... | collective-permute-start | bytes 1622024 | tf_op jit(solution)/shard_map/ppermute | solution.py:31
  20.3 1.9 shard_map.61.refs_0_
  22.2 1.9 shard_map.59.refs_0_
  24.1 9.5 %collective-permute-done.refs_1_ = bf16[2,512,512]{2,1,0:T(8,128)(2,1)S(1)} collective-permute-done((bf16[2,512,512]{2,1,0:T(8,128)(2,1)S(1)}, bf16[2,512,512]{2,1,0:T(8,128)(2,1)S(1)}, u32[]{:S(2)}, u32[]{:S(2)}) %collective-permute-start) | collective-permute-done | bytes 1048608 | tf_op jit(solution)/shard_map/ppermute | solution.py:31
  33.7 4.4 %collective-permute-start.10 = (bf16[528,512]{1,0:T(8,128)(2,1)S(1)}, bf16[528,512]{1,0:T(8,128)(2,1)S(1)}, u32[]{:S(2)}, u32[]{:S(2)}) collective-permute-start(bf16[528,512]{1,0:T(8,128)(2,1)S(1)} %get-tuple-element.52), channel_id=1, source_target_pairs={{0,1},{3,2},{4,5},{7,6},{8,9},{11,10},{12,13},{15,14},{16,17},{19,... | collective-permute-start | bytes 1622024 | tf_op jit(solution)/shard_map/ppermute | solution.py:31
  38.8 3.0 %shard_map.63.refs_0_ = bf16[512,2048]{1,0:T(8,128)(2,1)S(1)} custom-call(s32[4,512]{1,0:T(4,128)S(1)} %get-tuple-element.44.q_ref, bf16[512,2048]{1,0:T(8,128)(2,1)S(1)} %shard_map.61.refs_0_, bf16[2,512,512]{2,1,0:T(8,128)(2,1)S(1)} %collective-permute-done.refs_1_, bf16[2,512,512]{2,1,0:T(8,128)(2,1)S(1)} %collective-permute-done.1.refs_2_), custom_call_target="tpu_custom_call" | custom-call | flops 2147483648 | bytes 2097152 | tf_op jit(solution)/shard_map/pallas_call | solution.py:83
  41.8 3.0 %shard_map.60.refs_0_ = bf16[512,2048]{1,0:T(8,128)(2,1)S(1)} custom-call(s32[4,512]{1,0:T(4,128)S(1)} %get-tuple-element.42.q_ref, bf16[512,2048]{1,0:T(8,128)(2,1)S(1)} %shard_map.59.refs_0_, bf16[2,512,512]{2,1,0:T(8,128)(2,1)S(1)} %collective-permute-done.refs_1_, bf16[2,512,512]{2,1,0:T(8,128)(2,1)S(1)} %collective-permute-done.1.refs_2_), custom_call_target="tpu_custom_call" | custom-call | flops 2147483648 | bytes 2097152 | tf_op jit(solution)/shard_map/pallas_call | solution.py:83
  46.7 9.0 %collective-permute-done.10.rest_1_ = bf16[528,512]{1,0:T(8,128)(2,1)S(1)} collective-permute-done((bf16[528,512]{1,0:T(8,128)(2,1)S(1)}, bf16[528,512]{1,0:T(8,128)(2,1)S(1)}, u32[]{:S(2)}, u32[]{:S(2)}) %collective-permute-start.10) | collective-permute-done | bytes 540704 | tf_op jit(solution)/shard_map/ppermute | solution.py:31
  57.8 1.9 shard_map.64.left_ref
  59.7 1.9 shard_map.62.left_ref
  61.7 3.4 %shard_map.65 = (bf16[528,1024]{1,0:T(8,128)(2,1)S(1)}, f32[16,512]{1,0:T(8,128)}) custom-call(bf16[512,2048]{1,0:T(8,128)(2,1)S(1)} %shard_map.64.left_ref, bf16[1,512]{1,0:T(2,128)(2,1)S(1)} %compare_convert_fusion.rest_0_, bf16[2,528,512]{2,1,0:T(8,128)(2,1)S(1)} %pad_maximum_fusion.rest_1_.rest_0_.rest_5_, ...), custom_call_target="tpu_custom_call" | custom-call | flops 2147483648 | bytes 6291456 | tf_op jit(solution)/shard_map/pallas_call | solution.py:145
  70.0 1.7 shard_map.67
  72.4 3.0 %shard_map.68.refs_0_ = bf16[512,2048]{1,0:T(8,128)(2,1)S(1)} custom-call(s32[4,512]{1,0:T(4,128)S(1)} %get-tuple-element.41.q_ref, bf16[512,512]{1,0:T(8,128)(2,1)S(1)} %shard_map.66.refs_0_, bf16[528,512]{1,0:T(8,128)(2,1)S(1)} %get-tuple-element.54.refs_1_), custom_call_target="tpu_custom_call" | custom-call | flops 2147483648 | bytes 2097152 | tf_op jit(solution)/shard_map/pallas_call | solution.py:83
  75.4 1.9 shard_map.70.refs_0_
  78.3 1.9 shard_map.72.left_ref
  80.3 1.7 shard_map.74
  82.0 1.5 collective-permute-start.20
  86.2 3.0 %shard_map.77.refs_0_ = bf16[512,2048]{1,0:T(8,128)(2,1)S(1)} custom-call(s32[4,512]{1,0:T(4,128)S(1)} %get-tuple-element.40.q_ref, bf16[512,1024]{1,0:T(8,128)(2,1)S(1)} %shard_map.76.refs_0_), custom_call_target="tpu_custom_call" | custom-call | flops 2147483648 | bytes 2097152 | tf_op jit(solution)/shard_map/pallas_call | solution.py:83
  89.2 8.0 %collective-permute-done.20.rest_1_ = bf16[528,512]{1,0:T(8,128)(2,1)S(1)} collective-permute-done((bf16[528,512]{1,0:T(8,128)(2,1)S(1)}, bf16[528,512]{1,0:T(8,128)(2,1)S(1)}, u32[]{:S(2)}, u32[]{:S(2)}) %collective-permute-start.20) | collective-permute-done | bytes 540704 | tf_op jit(solution)/shard_map/ppermute | solution.py:17
  97.9 8.5 %collective-permute-done.24.rest_0_ = bf16[512,512]{1,0:T(8,128)(2,1)S(1)} collective-permute-done((bf16[512,512]{1,0:T(8,128)(2,1)S(1)}, bf16[512,512]{1,0:T(8,128)(2,1)S(1)}, u32[]{:S(2)}, u32[]{:S(2)}) %collective-permute-start.24) | collective-permute-done | bytes 524320 | tf_op jit(solution)/shard_map/ppermute | solution.py:17
  109.2 3.0 %shard_map.78.left_ref = bf16[512,2048]{1,0:T(8,128)(2,1)S(1)} custom-call(s32[4,512]{1,0:T(4,128)S(1)} %get-tuple-element.40.q_ref, bf16[512,2048]{1,0:T(8,128)(2,1)S(1)} %shard_map.77.refs_0_, bf16[512,1024]{1,0:T(8,128)(2,1)S(1)} %collective-permute-done.19.refs_1_), custom_call_target="tpu_custom_call" | custom-call | flops 2147483648 | bytes 2097152 | tf_op jit(solution)/shard_map/pallas_call | solution.py:83
  112.9 1.7 shard_map.79
  119.4 3.0 %shard_map.81.refs_0_ = bf16[512,2048]{1,0:T(8,128)(2,1)S(1)} custom-call(s32[4,512]{1,0:T(4,128)S(1)} %get-tuple-element.39.q_ref, bf16[512,512]{1,0:T(8,128)(2,1)S(1)} %shard_map.80.refs_0_.rest_0_, bf16[528,512]{1,0:T(8,128)(2,1)S(1)} %get-tuple-element.66.refs_1_.rest_1_.refs_0_), custom_call_target="tpu_custom_call" | custom-call | flops 2147483648 | bytes 2097152 | tf_op jit(solution)/shard_map/pallas_call | solution.py:83
  123.9 1.9 shard_map.83.left_ref.refs_0_
  125.8 1.7 shard_map.85.picked_ref
  127.6 1.7 shard_map.84
  130.5 1.3 collective-permute-start.36
  131.8 1.9 shard_map.88.left_ref
  135.7 1.3 collective-permute-start.38
  137.0 64.6 %collective-permute-done.36 = bf16[512,512]{1,0:T(8,128)(2,1)S(1)} collective-permute-done((bf16[512,512]{1,0:T(8,128)(2,1)S(1)}, bf16[512,512]{1,0:T(8,128)(2,1)S(1)}, u32[]{:S(2)}, u32[]{:S(2)}) %collective-permute-start.36) | collective-permute-done | bytes 524320 | tf_op jit(solution)/shard_map/ppermute | solution.py:35
  (103 shorter events, 33.8 us)
Async XLA Ops:
  5.2 28.5 %collective-permute-start = (bf16[2,512,512]{2,1,0:T(8,128)(2,1)S(1)}, bf16[2,512,512]{2,1,0:T(8,128)(2,1)S(1)}, u32[]{:S(2)}, u32[]{:S(2)}) collective-permute-start(bf16[2,512,512]{2,1,0:T(8,128)(2,1)S(1)} %slice.29.refs_0_), channel_id=1, source_target_pairs={{0,1},{3,2},{4,5},{7,6},{8,9},{11,10},{12,13},{15,14},{16,17},{19,... | collective-permute-start | bytes 3145736 | tf_op jit(solution)/shard_map/ppermute | solution.py:31
  10.2 27.9 %collective-permute-start.1 = (bf16[2,512,512]{2,1,0:T(8,128)(2,1)S(1)}, bf16[2,512,512]{2,1,0:T(8,128)(2,1)S(1)}, u32[]{:S(2)}, u32[]{:S(2)}) collective-permute-start(bf16[2,512,512]{2,1,0:T(8,128)(2,1)S(1)} %slice.29.refs_0_), channel_id=1, source_target_pairs={{1,2},{2,1},{5,6},{6,5},{9,10},{10,9},{13,14},{14,13},{17,18},{18,... | collective-permute-start | bytes 3145736 | tf_op jit(solution)/shard_map/ppermute | solution.py:27
  10.9 35.0 %collective-permute-start.4 = (bf16[2,528,512]{2,1,0:T(8,128)(2,1)S(1)}, bf16[2,528,512]{2,1,0:T(8,128)(2,1)S(1)}, u32[]{:S(2)}, u32[]{:S(2)}) collective-permute-start(bf16[2,528,512]{2,1,0:T(8,128)(2,1)S(1)} %pad_maximum_fusion.rest_1_.rest_0_.rest_5_), channel_id=1, source_target_pairs={{1,9},{2,10},{5,13},{6,14},{9,1},{10,2},{13,5},{14,6},{17,25},{18,... | collective-permute-start | bytes 3244040 | tf_op jit(solution)/shard_map/ppermute | solution.py:23
  11.7 50.0 %collective-permute-start.3 = (bf16[2,528,512]{2,1,0:T(8,128)(2,1)S(1)}, bf16[2,528,512]{2,1,0:T(8,128)(2,1)S(1)}, u32[]{:S(2)}, u32[]{:S(2)}) collective-permute-start(bf16[2,528,512]{2,1,0:T(8,128)(2,1)S(1)} %pad_maximum_fusion.rest_1_.rest_0_.rest_5_), channel_id=1, source_target_pairs={{1,5},{2,6},{5,1},{6,2},{9,13},{10,14},{13,9},{14,10},{17,21},{18,... | collective-permute-start | bytes 3244040 | tf_op jit(solution)/shard_map/ppermute | solution.py:23
  12.4 32.9 %collective-permute-start.6 = (bf16[528,512]{1,0:T(8,128)(2,1)S(1)}, bf16[528,512]{1,0:T(8,128)(2,1)S(1)}, u32[]{:S(2)}, u32[]{:S(2)}) collective-permute-start(bf16[528,512]{1,0:T(8,128)(2,1)S(1)} %get-tuple-element.48), channel_id=1, source_target_pairs={{0,1},{3,2},{4,5},{7,6},{8,9},{11,10},{12,13},{15,14},{16,17},{19,... | collective-permute-start | bytes 1622024 | tf_op jit(solution)/shard_map/ppermute | solution.py:31
  33.7 22.0 %collective-permute-start.10 = (bf16[528,512]{1,0:T(8,128)(2,1)S(1)}, bf16[528,512]{1,0:T(8,128)(2,1)S(1)}, u32[]{:S(2)}, u32[]{:S(2)}) collective-permute-start(bf16[528,512]{1,0:T(8,128)(2,1)S(1)} %get-tuple-element.52), channel_id=1, source_target_pairs={{0,1},{3,2},{4,5},{7,6},{8,9},{11,10},{12,13},{15,14},{16,17},{19,... | collective-permute-start | bytes 1622024 | tf_op jit(solution)/shard_map/ppermute | solution.py:31
  38.1 19.0 %collective-permute-start.2 = (bf16[2,512,512]{2,1,0:T(8,128)(2,1)S(1)}, bf16[2,512,512]{2,1,0:T(8,128)(2,1)S(1)}, u32[]{:S(2)}, u32[]{:S(2)}) collective-permute-start(bf16[2,512,512]{2,1,0:T(8,128)(2,1)S(1)} %collective-permute-done.refs_1_), channel_id=1, source_target_pairs={{1,2},{2,1},{5,6},{6,5},{9,10},{10,9},{13,14},{14,13},{17,18},{18,... | collective-permute-start | bytes 3145736 | tf_op jit(solution)/shard_map/ppermute | solution.py:27
  45.2 11.1 %collective-permute-start.8 = (bf16[528,512]{1,0:T(8,128)(2,1)S(1)}, bf16[528,512]{1,0:T(8,128)(2,1)S(1)}, u32[]{:S(2)}, u32[]{:S(2)}) collective-permute-start(bf16[528,512]{1,0:T(8,128)(2,1)S(1)} %collective-permute-done.6.rest_5_), channel_id=1, source_target_pairs={{1,9},{2,10},{5,13},{6,14},{9,1},{10,2},{13,5},{14,6},{17,25},{18,... | collective-permute-start | bytes 1622024 | tf_op jit(solution)/shard_map/ppermute | solution.py:23
  46.0 15.7 %collective-permute-start.5 = (bf16[2,528,512]{2,1,0:T(8,128)(2,1)S(1)}, bf16[2,528,512]{2,1,0:T(8,128)(2,1)S(1)}, u32[]{:S(2)}, u32[]{:S(2)}) collective-permute-start(bf16[2,528,512]{2,1,0:T(8,128)(2,1)S(1)} %collective-permute-done.4.rest_3_.rest_2_.rest_7_), channel_id=1, source_target_pairs={{1,5},{2,6},{5,1},{6,2},{9,13},{10,14},{13,9},{14,10},{17,21},{18,... | collective-permute-start | bytes 3244040 | tf_op jit(solution)/shard_map/ppermute | solution.py:23
  55.7 6.0 %collective-permute-start.7 = (bf16[528,512]{1,0:T(8,128)(2,1)S(1)}, bf16[528,512]{1,0:T(8,128)(2,1)S(1)}, u32[]{:S(2)}, u32[]{:S(2)}) collective-permute-start(bf16[528,512]{1,0:T(8,128)(2,1)S(1)} %collective-permute-done.6.rest_5_), channel_id=1, source_target_pairs={{1,5},{2,6},{5,1},{6,2},{9,13},{10,14},{13,9},{14,10},{17,21},{18,... | collective-permute-start | bytes 1622024 | tf_op jit(solution)/shard_map/ppermute | solution.py:23
  56.4 5.3 %collective-permute-start.9 = (bf16[528,512]{1,0:T(8,128)(2,1)S(1)}, bf16[528,512]{1,0:T(8,128)(2,1)S(1)}, u32[]{:S(2)}, u32[]{:S(2)}) collective-permute-start(bf16[528,512]{1,0:T(8,128)(2,1)S(1)} %collective-permute-done.8.rest_7_), channel_id=1, source_target_pairs={{1,5},{2,6},{5,1},{6,2},{9,13},{10,14},{13,9},{14,10},{17,21},{18,... | collective-permute-start | bytes 1622024 | tf_op jit(solution)/shard_map/ppermute | solution.py:23
  57.1 11.4 %collective-permute-start.12 = (bf16[528,512]{1,0:T(8,128)(2,1)S(1)}, bf16[528,512]{1,0:T(8,128)(2,1)S(1)}, u32[]{:S(2)}, u32[]{:S(2)}) collective-permute-start(bf16[528,512]{1,0:T(8,128)(2,1)S(1)} %collective-permute-done.10.rest_1_), channel_id=1, source_target_pairs={{1,9},{2,10},{5,13},{6,14},{9,1},{10,2},{13,5},{14,6},{17,25},{18,... | collective-permute-start | bytes 1622024 | tf_op jit(solution)/shard_map/ppermute | solution.py:23
  67.1 10.3 %collective-permute-start.17 = (bf16[528,1024]{1,0:T(8,128)(2,1)S(1)}, bf16[528,1024]{1,0:T(8,128)(2,1)S(1)}, u32[]{:S(2)}, u32[]{:S(2)}) collective-permute-start(bf16[528,1024]{1,0:T(8,128)(2,1)S(1)} %get-tuple-element.50.rest_1_.rest_0_), channel_id=1, source_target_pairs={{1,9},{2,10},{5,13},{6,14},{9,1},{10,2},{13,5},{14,6},{17,25},{18,... | collective-permute-start | bytes 3244040 | tf_op jit(solution)/shard_map/ppermute | solution.py:23
  69.2 11.0 %collective-permute-start.16 = (bf16[528,1024]{1,0:T(8,128)(2,1)S(1)}, bf16[528,1024]{1,0:T(8,128)(2,1)S(1)}, u32[]{:S(2)}, u32[]{:S(2)}) collective-permute-start(bf16[528,1024]{1,0:T(8,128)(2,1)S(1)} %get-tuple-element.50.rest_1_.rest_0_), channel_id=1, source_target_pairs={{1,5},{2,6},{5,1},{6,2},{9,13},{10,14},{13,9},{14,10},{17,21},{18,... | collective-permute-start | bytes 3244040 | tf_op jit(solution)/shard_map/ppermute | solution.py:23
  71.7 6.6 %collective-permute-start.15 = (bf16[528,512]{1,0:T(8,128)(2,1)S(1)}, bf16[528,512]{1,0:T(8,128)(2,1)S(1)}, u32[]{:S(2)}, u32[]{:S(2)}) collective-permute-start(bf16[528,512]{1,0:T(8,128)(2,1)S(1)} %get-tuple-element.54.refs_1_), channel_id=1, source_target_pairs={{1,2},{2,1},{5,6},{6,5},{9,10},{10,9},{13,14},{14,13},{17,18},{18,... | collective-permute-start | bytes 1622024 | tf_op jit(solution)/shard_map/ppermute | solution.py:27
  82.0 15.2 %collective-permute-start.20 = (bf16[528,512]{1,0:T(8,128)(2,1)S(1)}, bf16[528,512]{1,0:T(8,128)(2,1)S(1)}, u32[]{:S(2)}, u32[]{:S(2)}) collective-permute-start(bf16[528,512]{1,0:T(8,128)(2,1)S(1)} %get-tuple-element.57.right_ref), channel_id=1, source_target_pairs={{0,16},{16,0},{1,17},{17,1},{2,18},{18,2},{3,19},{19,3},{4,20},{20... | collective-permute-start | bytes 1622024 | tf_op jit(solution)/shard_map/ppermute | solution.py:17
  84.8 24.4 %collective-permute-start.19 = (bf16[512,1024]{1,0:T(8,128)(2,1)S(1)}, bf16[512,1024]{1,0:T(8,128)(2,1)S(1)}, u32[]{:S(2)}, u32[]{:S(2)}) collective-permute-start(bf16[512,1024]{1,0:T(8,128)(2,1)S(1)} %shard_map.76.refs_0_), channel_id=1, source_target_pairs={{1,2},{2,1},{5,6},{6,5},{9,10},{10,9},{13,14},{14,13},{17,18},{18,... | collective-permute-start | bytes 3145736 | tf_op jit(solution)/shard_map/ppermute | solution.py:27
  85.6 20.8 %collective-permute-start.24 = (bf16[512,512]{1,0:T(8,128)(2,1)S(1)}, bf16[512,512]{1,0:T(8,128)(2,1)S(1)}, u32[]{:S(2)}, u32[]{:S(2)}) collective-permute-start(bf16[512,512]{1,0:T(8,128)(2,1)S(1)} %shard_map.75.left_ref), channel_id=1, source_target_pairs={{0,16},{16,0},{1,17},{17,1},{2,18},{18,2},{3,19},{19,3},{4,20},{20... | collective-permute-start | bytes 1572872 | tf_op jit(solution)/shard_map/ppermute | solution.py:17
  97.2 10.6 %collective-permute-start.22 = (bf16[528,512]{1,0:T(8,128)(2,1)S(1)}, bf16[528,512]{1,0:T(8,128)(2,1)S(1)}, u32[]{:S(2)}, u32[]{:S(2)}) collective-permute-start(bf16[528,512]{1,0:T(8,128)(2,1)S(1)} %collective-permute-done.20.rest_1_), channel_id=1, source_target_pairs={{1,9},{2,10},{5,13},{6,14},{9,1},{10,2},{13,5},{14,6},{17,25},{18,... | collective-permute-start | bytes 1622024 | tf_op jit(solution)/shard_map/ppermute | solution.py:23
  106.4 5.8 %collective-permute-start.26 = (bf16[512,512]{1,0:T(8,128)(2,1)S(1)}, bf16[512,512]{1,0:T(8,128)(2,1)S(1)}, u32[]{:S(2)}, u32[]{:S(2)}) collective-permute-start(bf16[512,512]{1,0:T(8,128)(2,1)S(1)} %collective-permute-done.24.rest_0_), channel_id=1, source_target_pairs={{1,9},{2,10},{5,13},{6,14},{9,1},{10,2},{13,5},{14,6},{17,25},{18,... | collective-permute-start | bytes 1572872 | tf_op jit(solution)/shard_map/ppermute | solution.py:23
  107.1 5.8 %collective-permute-start.21 = (bf16[528,512]{1,0:T(8,128)(2,1)S(1)}, bf16[528,512]{1,0:T(8,128)(2,1)S(1)}, u32[]{:S(2)}, u32[]{:S(2)}) collective-permute-start(bf16[528,512]{1,0:T(8,128)(2,1)S(1)} %collective-permute-done.20.rest_1_), channel_id=1, source_target_pairs={{1,5},{2,6},{5,1},{6,2},{9,13},{10,14},{13,9},{14,10},{17,21},{18,... | collective-permute-start | bytes 1622024 | tf_op jit(solution)/shard_map/ppermute | solution.py:23
  107.8 5.1 %collective-permute-start.23 = (bf16[528,512]{1,0:T(8,128)(2,1)S(1)}, bf16[528,512]{1,0:T(8,128)(2,1)S(1)}, u32[]{:S(2)}, u32[]{:S(2)}) collective-permute-start(bf16[528,512]{1,0:T(8,128)(2,1)S(1)} %collective-permute-done.22.rest_3_), channel_id=1, source_target_pairs={{1,5},{2,6},{5,1},{6,2},{9,13},{10,14},{13,9},{14,10},{17,21},{18,... | collective-permute-start | bytes 1622024 | tf_op jit(solution)/shard_map/ppermute | solution.py:23
  108.5 7.6 %collective-permute-start.25 = (bf16[512,512]{1,0:T(8,128)(2,1)S(1)}, bf16[512,512]{1,0:T(8,128)(2,1)S(1)}, u32[]{:S(2)}, u32[]{:S(2)}) collective-permute-start(bf16[512,512]{1,0:T(8,128)(2,1)S(1)} %collective-permute-done.24.rest_0_), channel_id=1, source_target_pairs={{1,5},{2,6},{5,1},{6,2},{9,13},{10,14},{13,9},{14,10},{17,21},{18,... | collective-permute-start | bytes 1572872 | tf_op jit(solution)/shard_map/ppermute | solution.py:23
  112.2 3.9 %collective-permute-start.27 = (bf16[512,512]{1,0:T(8,128)(2,1)S(1)}, bf16[512,512]{1,0:T(8,128)(2,1)S(1)}, u32[]{:S(2)}, u32[]{:S(2)}) collective-permute-start(bf16[512,512]{1,0:T(8,128)(2,1)S(1)} %collective-permute-done.26.rest_2_), channel_id=1, source_target_pairs={{1,5},{2,6},{5,1},{6,2},{9,13},{10,14},{13,9},{14,10},{17,21},{18,... | collective-permute-start | bytes 1572872 | tf_op jit(solution)/shard_map/ppermute | solution.py:23
  114.6 7.8 %collective-permute-start.31 = (bf16[528,512]{1,0:T(8,128)(2,1)S(1)}, bf16[528,512]{1,0:T(8,128)(2,1)S(1)}, u32[]{:S(2)}, u32[]{:S(2)}) collective-permute-start(bf16[528,512]{1,0:T(8,128)(2,1)S(1)} %get-tuple-element.66.refs_1_.rest_1_.refs_0_), channel_id=1, source_target_pairs={{1,9},{2,10},{5,13},{6,14},{9,1},{10,2},{13,5},{14,6},{17,25},{18,... | collective-permute-start | bytes 1622024 | tf_op jit(solution)/shard_map/ppermute | solution.py:23
  115.4 7.8 %collective-permute-start.28 = (bf16[528,512]{1,0:T(8,128)(2,1)S(1)}, bf16[528,512]{1,0:T(8,128)(2,1)S(1)}, u32[]{:S(2)}, u32[]{:S(2)}) collective-permute-start(bf16[528,512]{1,0:T(8,128)(2,1)S(1)} %get-tuple-element.66.refs_1_.rest_1_.refs_0_), channel_id=1, source_target_pairs={{1,2},{2,1},{5,6},{6,5},{9,10},{10,9},{13,14},{14,13},{17,18},{18,... | collective-permute-start | bytes 1622024 | tf_op jit(solution)/shard_map/ppermute | solution.py:27
  117.3 11.9 %collective-permute-start.34 = (bf16[512,512]{1,0:T(8,128)(2,1)S(1)}, bf16[512,512]{1,0:T(8,128)(2,1)S(1)}, u32[]{:S(2)}, u32[]{:S(2)}) collective-permute-start(bf16[512,512]{1,0:T(8,128)(2,1)S(1)} %shard_map.80.refs_0_.rest_0_), channel_id=1, source_target_pairs={{1,9},{2,10},{5,13},{6,14},{9,1},{10,2},{13,5},{14,6},{17,25},{18,... | collective-permute-start | bytes 1572872 | tf_op jit(solution)/shard_map/ppermute | solution.py:23
  118.0 12.0 %collective-permute-start.29 = (bf16[512,512]{1,0:T(8,128)(2,1)S(1)}, bf16[512,512]{1,0:T(8,128)(2,1)S(1)}, u32[]{:S(2)}, u32[]{:S(2)}) collective-permute-start(bf16[512,512]{1,0:T(8,128)(2,1)S(1)} %shard_map.80.refs_0_.rest_0_), channel_id=1, source_target_pairs={{1,2},{2,1},{5,6},{6,5},{9,10},{10,9},{13,14},{14,13},{17,18},{18,... | collective-permute-start | bytes 1572872 | tf_op jit(solution)/shard_map/ppermute | solution.py:27
  118.7 15.0 %collective-permute-start.33 = (bf16[512,512]{1,0:T(8,128)(2,1)S(1)}, bf16[512,512]{1,0:T(8,128)(2,1)S(1)}, u32[]{:S(2)}, u32[]{:S(2)}) collective-permute-start(bf16[512,512]{1,0:T(8,128)(2,1)S(1)} %shard_map.80.refs_0_.rest_0_), channel_id=1, source_target_pairs={{1,5},{2,6},{5,1},{6,2},{9,13},{10,14},{13,9},{14,10},{17,21},{18,... | collective-permute-start | bytes 1572872 | tf_op jit(solution)/shard_map/ppermute | solution.py:23
  129.3 4.5 %collective-permute-start.35 = (bf16[512,512]{1,0:T(8,128)(2,1)S(1)}, bf16[512,512]{1,0:T(8,128)(2,1)S(1)}, u32[]{:S(2)}, u32[]{:S(2)}) collective-permute-start(bf16[512,512]{1,0:T(8,128)(2,1)S(1)} %collective-permute-done.34.rest_2_), channel_id=1, source_target_pairs={{1,5},{2,6},{5,1},{6,2},{9,13},{10,14},{13,9},{14,10},{17,21},{18,... | collective-permute-start | bytes 1572872 | tf_op jit(solution)/shard_map/ppermute | solution.py:23
  130.5 71.1 %collective-permute-start.36 = (bf16[512,512]{1,0:T(8,128)(2,1)S(1)}, bf16[512,512]{1,0:T(8,128)(2,1)S(1)}, u32[]{:S(2)}, u32[]{:S(2)}) collective-permute-start(bf16[512,512]{1,0:T(8,128)(2,1)S(1)} %get-tuple-element.71), channel_id=1, source_target_pairs={{1,0},{2,3},{5,4},{6,7},{9,8},{10,11},{13,12},{14,15},{17,16},{18,... | collective-permute-start | bytes 1572872 | tf_op jit(solution)/shard_map/ppermute | solution.py:35
  135.7 66.8 %collective-permute-start.38 = (f32[1,512]{1,0:T(1,128)S(1)}, f32[1,512]{1,0:T(1,128)S(1)}, u32[]{:S(2)}, u32[]{:S(2)}) collective-permute-start(f32[1,512]{1,0:T(1,128)S(1)} %slice_add_fusion), channel_id=1, source_target_pairs={{1,0},{2,3},{5,4},{6,7},{9,8},{10,11},{13,12},{14,15},{17,16},{18,... | collective-permute-start | bytes 6152 | tf_op jit(solution)/shard_map/ppermute | solution.py:35
  (9 other events, 19.5 us)

commit v18 on v17

--- a/solution.py
+++ b/solution.py
@@ -100,7 +100,7 @@
     extra = [] if added is None else [added]
     tall, wide = size + (EXTRA if extra else 0), size * len(halves)
     kind = jnp.float32 if form == "open" else jnp.bfloat16
-    shapes = {"joint": [(tall, wide)], "apart": [(tall, size)], "open": [(size, size)]}[form]
+    shapes = {"joint": [(tall, wide)], "apart": [(tall, size)], "open": [(size, size)], "twice": [(tall, size), (size, size)]}[form]
     outs = [jax.ShapeDtypeStruct(shape, kind) for shape in shapes]
     if extra:
         outs.append(jax.ShapeDtypeStruct((EXTRA, size), jnp.float32))
@@ -118,6 +118,8 @@
                 )
                 total = part if total is None else total + part
             results[0][0:size, i * size : (i + 1) * size] = total.astype(kind)
+            if form == "twice":
+                results[1][...] = total.astype(kind)
         if not extra:
             return
 
@@ -330,11 +332,11 @@
     views = tile_row(earlier_e, across_e, partial)
     moved = panel(3, [(2, (other, None, 0)), (3, (other, None, size))], partial)
     views_o = tile_row(earlier_o, across_o, moved)
-    halved_e, vector = product(moved, [views], "apart", size, vector)
+    halved_e, plain_e, vector = product(moved, [views], "twice", size, vector)
     (halved_o,) = product(after(moved, halved_e), [views_o], "apart", size)
 
     distant_e, distant_o = from_behind(halved_e, "loop", 2), from_behind(halved_o, "loop", 2)
-    other_e, across_e = early(swap_middle(halved_e)), swap_rows(distant_e, 2)
+    other_e, across_e = early(swap_middle(plain_e)), swap_rows(distant_e, 2)
     other_o, across_o = swap_middle(halved_o), swap_rows(distant_o, 2)
     partial = panel(4, [(0, (halved_o, None, 0)), (1, (halved_e, None, 0))])
     views = tile_row(after(distant_e, partial), across_e, partial)

time: 204 us -> 204 us (level)
  no operation moved by 1% of the time
where the time goes in v18:
time: 204 us; the launch traced here: 203 us
  waiting for transfers between devices  100 us (49%)
  Pallas kernels  50.8 us (25%)
  starting transfers between devices  44.7 us (22%)
  local copies, waits for them, and re-layouts  3.17 us (2%)
  other arithmetic  2.59 us (1%)
    ppermute x2, waiting for transfers between devices, outward(): return lax.ppermute(value, 'col', [(1, 0), (2, 3)])  64.6 us
    pallas_call x14, Pallas kernels, spread_columns(): pl.pallas_call(kernel, out_shape=jax.ShapeDtypeStruct((size, size * count...  33.2 us
    ppermute x3, waiting for transfers between devices, inward(): return lax.ppermute(value, 'col', [(0, 1), (3, 2)])  19 us
    ppermute x3, starting transfers between devices, inward(): return lax.ppermute(value, 'col', [(0, 1), (3, 2)])  17.3 us
    ppermute x24, starting transfers between devices, swap_rows(): return lax.ppermute(value, ('row', 'col'), pairs)  17.1 us
    ppermute x2, waiting for transfers between devices, from_behind(): lax.ppermute(value, axis, [(i, (i + by) % devices) for i in range(devices)])  16.5 us
    pallas_call x9, Pallas kernels, product(): pl.pallas_call(kernel, out_shape=tuple(outs), compiler_params=pltpu.Compi...  15.2 us
    ppermute x8, starting transfers between devices, swap_middle(): return lax.ppermute(value, 'col', [(1, 2), (2, 1)])  5.64 us
  transfers between devices with their start and end apart: 39, of which 6 were waited for; matrix products, arithmetic and copies ran while one was open for 0% of the time, Pallas kernels for 24%

profile of v18, /device:TPU:0, one launch (start us, length us, event | category | flops | bytes accessed | tf_op | source)
XLA Modules:
  0.0 203.0 jit_solution(18444909782307832015)
XLA Ops:
  2.7 1.4 slice_bitcast_fusion.1
  5.2 5.0 %collective-permute-start = (bf16[2,512,512]{2,1,0:T(8,128)(2,1)S(1)}, bf16[2,512,512]{2,1,0:T(8,128)(2,1)S(1)}, u32[]{:S(2)}, u32[]{:S(2)}) collective-permute-start(bf16[2,512,512]{2,1,0:T(8,128)(2,1)S(1)} %slice.29.refs_0_), channel_id=1, source_target_pairs={{0,1},{3,2},{4,5},{7,6},{8,9},{11,10},{12,13},{15,14},{16,17},{19,... | collective-permute-start | bytes 3145736 | tf_op jit(solution)/shard_map/ppermute | solution.py:31
  12.4 7.9 %collective-permute-start.6 = (bf16[528,512]{1,0:T(8,128)(2,1)S(1)}, bf16[528,512]{1,0:T(8,128)(2,1)S(1)}, u32[]{:S(2)}, u32[]{:S(2)}) collective-permute-start(bf16[528,512]{1,0:T(8,128)(2,1)S(1)} %get-tuple-element.49), channel_id=1, source_target_pairs={{0,1},{3,2},{4,5},{7,6},{8,9},{11,10},{12,13},{15,14},{16,17},{19,... | collective-permute-start | bytes 1622024 | tf_op jit(solution)/shard_map/ppermute | solution.py:31
  20.3 1.9 shard_map.61.refs_0_
  22.2 1.9 shard_map.59.refs_0_
  24.1 9.5 %collective-permute-done.refs_1_ = bf16[2,512,512]{2,1,0:T(8,128)(2,1)S(1)} collective-permute-done((bf16[2,512,512]{2,1,0:T(8,128)(2,1)S(1)}, bf16[2,512,512]{2,1,0:T(8,128)(2,1)S(1)}, u32[]{:S(2)}, u32[]{:S(2)}) %collective-permute-start) | collective-permute-done | bytes 1048608 | tf_op jit(solution)/shard_map/ppermute | solution.py:31
  33.7 4.4 %collective-permute-start.10 = (bf16[528,512]{1,0:T(8,128)(2,1)S(1)}, bf16[528,512]{1,0:T(8,128)(2,1)S(1)}, u32[]{:S(2)}, u32[]{:S(2)}) collective-permute-start(bf16[528,512]{1,0:T(8,128)(2,1)S(1)} %get-tuple-element.53), channel_id=1, source_target_pairs={{0,1},{3,2},{4,5},{7,6},{8,9},{11,10},{12,13},{15,14},{16,17},{19,... | collective-permute-start | bytes 1622024 | tf_op jit(solution)/shard_map/ppermute | solution.py:31
  38.8 3.0 %shard_map.63.refs_0_ = bf16[512,2048]{1,0:T(8,128)(2,1)S(1)} custom-call(s32[4,512]{1,0:T(4,128)S(1)} %get-tuple-element.45.q_ref, bf16[512,2048]{1,0:T(8,128)(2,1)S(1)} %shard_map.61.refs_0_, bf16[2,512,512]{2,1,0:T(8,128)(2,1)S(1)} %collective-permute-done.refs_1_, bf16[2,512,512]{2,1,0:T(8,128)(2,1)S(1)} %collective-permute-done.1.refs_2_), custom_call_target="tpu_custom_call" | custom-call | flops 2147483648 | bytes 2097152 | tf_op jit(solution)/shard_map/pallas_call | solution.py:83
  41.8 3.0 %shard_map.60.refs_0_ = bf16[512,2048]{1,0:T(8,128)(2,1)S(1)} custom-call(s32[4,512]{1,0:T(4,128)S(1)} %get-tuple-element.43.q_ref, bf16[512,2048]{1,0:T(8,128)(2,1)S(1)} %shard_map.59.refs_0_, bf16[2,512,512]{2,1,0:T(8,128)(2,1)S(1)} %collective-permute-done.refs_1_, bf16[2,512,512]{2,1,0:T(8,128)(2,1)S(1)} %collective-permute-done.1.refs_2_), custom_call_target="tpu_custom_call" | custom-call | flops 2147483648 | bytes 2097152 | tf_op jit(solution)/shard_map/pallas_call | solution.py:83
  46.7 9.0 %collective-permute-done.10.rest_1_ = bf16[528,512]{1,0:T(8,128)(2,1)S(1)} collective-permute-done((bf16[528,512]{1,0:T(8,128)(2,1)S(1)}, bf16[528,512]{1,0:T(8,128)(2,1)S(1)}, u32[]{:S(2)}, u32[]{:S(2)}) %collective-permute-start.10) | collective-permute-done | bytes 540704 | tf_op jit(solution)/shard_map/ppermute | solution.py:31
  57.8 1.9 shard_map.64.left_ref
  59.7 1.9 shard_map.62.left_ref
  61.7 3.4 %shard_map.65 = (bf16[528,1024]{1,0:T(8,128)(2,1)S(1)}, f32[16,512]{1,0:T(8,128)}) custom-call(bf16[512,2048]{1,0:T(8,128)(2,1)S(1)} %shard_map.64.left_ref, bf16[1,512]{1,0:T(2,128)(2,1)S(1)} %compare_convert_fusion.rest_0_, bf16[2,528,512]{2,1,0:T(8,128)(2,1)S(1)} %pad_maximum_fusion.rest_1_.rest_0_.rest_5_, ...), custom_call_target="tpu_custom_call" | custom-call | flops 2147483648 | bytes 6291456 | tf_op jit(solution)/shard_map/pallas_call | solution.py:147
  70.0 1.7 shard_map.67
  72.4 3.0 %shard_map.68.refs_0_ = bf16[512,2048]{1,0:T(8,128)(2,1)S(1)} custom-call(s32[4,512]{1,0:T(4,128)S(1)} %get-tuple-element.42.q_ref, bf16[512,512]{1,0:T(8,128)(2,1)S(1)} %shard_map.66.refs_0_, bf16[528,512]{1,0:T(8,128)(2,1)S(1)} %get-tuple-element.55.refs_1_), custom_call_target="tpu_custom_call" | custom-call | flops 2147483648 | bytes 2097152 | tf_op jit(solution)/shard_map/pallas_call | solution.py:83
  75.4 1.9 shard_map.70.refs_0_
  78.3 1.9 shard_map.72.left_ref
  80.3 1.7 shard_map.74
  82.0 1.5 collective-permute-start.20
  86.2 3.0 %shard_map.77.refs_0_ = bf16[512,2048]{1,0:T(8,128)(2,1)S(1)} custom-call(s32[4,512]{1,0:T(4,128)S(1)} %get-tuple-element.41.q_ref, bf16[512,1024]{1,0:T(8,128)(2,1)S(1)} %shard_map.76.refs_0_), custom_call_target="tpu_custom_call" | custom-call | flops 2147483648 | bytes 2097152 | tf_op jit(solution)/shard_map/pallas_call | solution.py:83
  89.2 8.0 %collective-permute-done.20.rest_1_ = bf16[528,512]{1,0:T(8,128)(2,1)S(1)} collective-permute-done((bf16[528,512]{1,0:T(8,128)(2,1)S(1)}, bf16[528,512]{1,0:T(8,128)(2,1)S(1)}, u32[]{:S(2)}, u32[]{:S(2)}) %collective-permute-start.20) | collective-permute-done | bytes 540704 | tf_op jit(solution)/shard_map/ppermute | solution.py:17
  97.9 8.5 %collective-permute-done.24.rest_0_ = bf16[512,512]{1,0:T(8,128)(2,1)S(1)} collective-permute-done((bf16[512,512]{1,0:T(8,128)(2,1)S(1)}, bf16[512,512]{1,0:T(8,128)(2,1)S(1)}, u32[]{:S(2)}, u32[]{:S(2)}) %collective-permute-start.24) | collective-permute-done | bytes 524320 | tf_op jit(solution)/shard_map/ppermute | solution.py:17
  109.2 3.0 %shard_map.78.left_ref = bf16[512,2048]{1,0:T(8,128)(2,1)S(1)} custom-call(s32[4,512]{1,0:T(4,128)S(1)} %get-tuple-element.41.q_ref, bf16[512,2048]{1,0:T(8,128)(2,1)S(1)} %shard_map.77.refs_0_, bf16[512,1024]{1,0:T(8,128)(2,1)S(1)} %collective-permute-done.19.refs_1_), custom_call_target="tpu_custom_call" | custom-call | flops 2147483648 | bytes 2097152 | tf_op jit(solution)/shard_map/pallas_call | solution.py:83
  112.9 1.7 shard_map.79
  119.4 3.0 %shard_map.81.refs_0_ = bf16[512,2048]{1,0:T(8,128)(2,1)S(1)} custom-call(s32[4,512]{1,0:T(4,128)S(1)} %get-tuple-element.40.q_ref, bf16[512,512]{1,0:T(8,128)(2,1)S(1)} %shard_map.80.refs_0_.rest_0_, bf16[528,512]{1,0:T(8,128)(2,1)S(1)} %get-tuple-element.68.refs_1_.rest_1_.refs_0_), custom_call_target="tpu_custom_call" | custom-call | flops 2147483648 | bytes 2097152 | tf_op jit(solution)/shard_map/pallas_call | solution.py:83
  123.9 1.9 shard_map.83.left_ref.refs_0_
  125.8 1.7 shard_map.85.picked_ref
  127.6 1.7 shard_map.84
  130.5 1.3 collective-permute-start.36
  131.8 1.9 shard_map.88.left_ref
  135.7 1.3 collective-permute-start.38
  137.0 64.6 %collective-permute-done.36 = bf16[512,512]{1,0:T(8,128)(2,1)S(1)} collective-permute-done((bf16[512,512]{1,0:T(8,128)(2,1)S(1)}, bf16[512,512]{1,0:T(8,128)(2,1)S(1)}, u32[]{:S(2)}, u32[]{:S(2)}) %collective-permute-start.36) | collective-permute-done | bytes 524320 | tf_op jit(solution)/shard_map/ppermute | solution.py:35
  (103 shorter events, 33.8 us)
Async XLA Ops:
  5.2 28.5 %collective-permute-start = (bf16[2,512,512]{2,1,0:T(8,128)(2,1)S(1)}, bf16[2,512,512]{2,1,0:T(8,128)(2,1)S(1)}, u32[]{:S(2)}, u32[]{:S(2)}) collective-permute-start(bf16[2,512,512]{2,1,0:T(8,128)(2,1)S(1)} %slice.29.refs_0_), channel_id=1, source_target_pairs={{0,1},{3,2},{4,5},{7,6},{8,9},{11,10},{12,13},{15,14},{16,17},{19,... | collective-permute-start | bytes 3145736 | tf_op jit(solution)/shard_map/ppermute | solution.py:31
  10.2 27.9 %collective-permute-start.1 = (bf16[2,512,512]{2,1,0:T(8,128)(2,1)S(1)}, bf16[2,512,512]{2,1,0:T(8,128)(2,1)S(1)}, u32[]{:S(2)}, u32[]{:S(2)}) collective-permute-start(bf16[2,512,512]{2,1,0:T(8,128)(2,1)S(1)} %slice.29.refs_0_), channel_id=1, source_target_pairs={{1,2},{2,1},{5,6},{6,5},{9,10},{10,9},{13,14},{14,13},{17,18},{18,... | collective-permute-start | bytes 3145736 | tf_op jit(solution)/shard_map/ppermute | solution.py:27
  10.9 35.0 %collective-permute-start.4 = (bf16[2,528,512]{2,1,0:T(8,128)(2,1)S(1)}, bf16[2,528,512]{2,1,0:T(8,128)(2,1)S(1)}, u32[]{:S(2)}, u32[]{:S(2)}) collective-permute-start(bf16[2,528,512]{2,1,0:T(8,128)(2,1)S(1)} %pad_maximum_fusion.rest_1_.rest_0_.rest_5_), channel_id=1, source_target_pairs={{1,9},{2,10},{5,13},{6,14},{9,1},{10,2},{13,5},{14,6},{17,25},{18,... | collective-permute-start | bytes 3244040 | tf_op jit(solution)/shard_map/ppermute | solution.py:23
  11.7 50.0 %collective-permute-start.3 = (bf16[2,528,512]{2,1,0:T(8,128)(2,1)S(1)}, bf16[2,528,512]{2,1,0:T(8,128)(2,1)S(1)}, u32[]{:S(2)}, u32[]{:S(2)}) collective-permute-start(bf16[2,528,512]{2,1,0:T(8,128)(2,1)S(1)} %pad_maximum_fusion.rest_1_.rest_0_.rest_5_), channel_id=1, source_target_pairs={{1,5},{2,6},{5,1},{6,2},{9,13},{10,14},{13,9},{14,10},{17,21},{18,... | collective-permute-start | bytes 3244040 | tf_op jit(solution)/shard_map/ppermute | solution.py:23
  12.4 32.9 %collective-permute-start.6 = (bf16[528,512]{1,0:T(8,128)(2,1)S(1)}, bf16[528,512]{1,0:T(8,128)(2,1)S(1)}, u32[]{:S(2)}, u32[]{:S(2)}) collective-permute-start(bf16[528,512]{1,0:T(8,128)(2,1)S(1)} %get-tuple-element.49), channel_id=1, source_target_pairs={{0,1},{3,2},{4,5},{7,6},{8,9},{11,10},{12,13},{15,14},{16,17},{19,... | collective-permute-start | bytes 1622024 | tf_op jit(solution)/shard_map/ppermute | solution.py:31
  33.7 22.0 %collective-permute-start.10 = (bf16[528,512]{1,0:T(8,128)(2,1)S(1)}, bf16[528,512]{1,0:T(8,128)(2,1)S(1)}, u32[]{:S(2)}, u32[]{:S(2)}) collective-permute-start(bf16[528,512]{1,0:T(8,128)(2,1)S(1)} %get-tuple-element.53), channel_id=1, source_target_pairs={{0,1},{3,2},{4,5},{7,6},{8,9},{11,10},{12,13},{15,14},{16,17},{19,... | collective-permute-start | bytes 1622024 | tf_op jit(solution)/shard_map/ppermute | solution.py:31
  38.1 19.0 %collective-permute-start.2 = (bf16[2,512,512]{2,1,0:T(8,128)(2,1)S(1)}, bf16[2,512,512]{2,1,0:T(8,128)(2,1)S(1)}, u32[]{:S(2)}, u32[]{:S(2)}) collective-permute-start(bf16[2,512,512]{2,1,0:T(8,128)(2,1)S(1)} %collective-permute-done.refs_1_), channel_id=1, source_target_pairs={{1,2},{2,1},{5,6},{6,5},{9,10},{10,9},{13,14},{14,13},{17,18},{18,... | collective-permute-start | bytes 3145736 | tf_op jit(solution)/shard_map/ppermute | solution.py:27
  45.2 11.1 %collective-permute-start.8 = (bf16[528,512]{1,0:T(8,128)(2,1)S(1)}, bf16[528,512]{1,0:T(8,128)(2,1)S(1)}, u32[]{:S(2)}, u32[]{:S(2)}) collective-permute-start(bf16[528,512]{1,0:T(8,128)(2,1)S(1)} %collective-permute-done.6.rest_5_), channel_id=1, source_target_pairs={{1,9},{2,10},{5,13},{6,14},{9,1},{10,2},{13,5},{14,6},{17,25},{18,... | collective-permute-start | bytes 1622024 | tf_op jit(solution)/shard_map/ppermute | solution.py:23
  46.0 15.7 %collective-permute-start.5 = (bf16[2,528,512]{2,1,0:T(8,128)(2,1)S(1)}, bf16[2,528,512]{2,1,0:T(8,128)(2,1)S(1)}, u32[]{:S(2)}, u32[]{:S(2)}) collective-permute-start(bf16[2,528,512]{2,1,0:T(8,128)(2,1)S(1)} %collective-permute-done.4.rest_3_.rest_2_.rest_7_), channel_id=1, source_target_pairs={{1,5},{2,6},{5,1},{6,2},{9,13},{10,14},{13,9},{14,10},{17,21},{18,... | collective-permute-start | bytes 3244040 | tf_op jit(solution)/shard_map/ppermute | solution.py:23
  55.7 6.0 %collective-permute-start.7 = (bf16[528,512]{1,0:T(8,128)(2,1)S(1)}, bf16[528,512]{1,0:T(8,128)(2,1)S(1)}, u32[]{:S(2)}, u32[]{:S(2)}) collective-permute-start(bf16[528,512]{1,0:T(8,128)(2,1)S(1)} %collective-permute-done.6.rest_5_), channel_id=1, source_target_pairs={{1,5},{2,6},{5,1},{6,2},{9,13},{10,14},{13,9},{14,10},{17,21},{18,... | collective-permute-start | bytes 1622024 | tf_op jit(solution)/shard_map/ppermute | solution.py:23
  56.4 5.3 %collective-permute-start.9 = (bf16[528,512]{1,0:T(8,128)(2,1)S(1)}, bf16[528,512]{1,0:T(8,128)(2,1)S(1)}, u32[]{:S(2)}, u32[]{:S(2)}) collective-permute-start(bf16[528,512]{1,0:T(8,128)(2,1)S(1)} %collective-permute-done.8.rest_7_), channel_id=1, source_target_pairs={{1,5},{2,6},{5,1},{6,2},{9,13},{10,14},{13,9},{14,10},{17,21},{18,... | collective-permute-start | bytes 1622024 | tf_op jit(solution)/shard_map/ppermute | solution.py:23
  57.1 11.4 %collective-permute-start.12 = (bf16[528,512]{1,0:T(8,128)(2,1)S(1)}, bf16[528,512]{1,0:T(8,128)(2,1)S(1)}, u32[]{:S(2)}, u32[]{:S(2)}) collective-permute-start(bf16[528,512]{1,0:T(8,128)(2,1)S(1)} %collective-permute-done.10.rest_1_), channel_id=1, source_target_pairs={{1,9},{2,10},{5,13},{6,14},{9,1},{10,2},{13,5},{14,6},{17,25},{18,... | collective-permute-start | bytes 1622024 | tf_op jit(solution)/shard_map/ppermute | solution.py:23
  67.1 10.3 %collective-permute-start.17 = (bf16[528,1024]{1,0:T(8,128)(2,1)S(1)}, bf16[528,1024]{1,0:T(8,128)(2,1)S(1)}, u32[]{:S(2)}, u32[]{:S(2)}) collective-permute-start(bf16[528,1024]{1,0:T(8,128)(2,1)S(1)} %get-tuple-element.51.rest_1_.rest_0_), channel_id=1, source_target_pairs={{1,9},{2,10},{5,13},{6,14},{9,1},{10,2},{13,5},{14,6},{17,25},{18,... | collective-permute-start | bytes 3244040 | tf_op jit(solution)/shard_map/ppermute | solution.py:23
  69.2 11.0 %collective-permute-start.16 = (bf16[528,1024]{1,0:T(8,128)(2,1)S(1)}, bf16[528,1024]{1,0:T(8,128)(2,1)S(1)}, u32[]{:S(2)}, u32[]{:S(2)}) collective-permute-start(bf16[528,1024]{1,0:T(8,128)(2,1)S(1)} %get-tuple-element.51.rest_1_.rest_0_), channel_id=1, source_target_pairs={{1,5},{2,6},{5,1},{6,2},{9,13},{10,14},{13,9},{14,10},{17,21},{18,... | collective-permute-start | bytes 3244040 | tf_op jit(solution)/shard_map/ppermute | solution.py:23
  71.7 6.6 %collective-permute-start.15 = (bf16[528,512]{1,0:T(8,128)(2,1)S(1)}, bf16[528,512]{1,0:T(8,128)(2,1)S(1)}, u32[]{:S(2)}, u32[]{:S(2)}) collective-permute-start(bf16[528,512]{1,0:T(8,128)(2,1)S(1)} %get-tuple-element.55.refs_1_), channel_id=1, source_target_pairs={{1,2},{2,1},{5,6},{6,5},{9,10},{10,9},{13,14},{14,13},{17,18},{18,... | collective-permute-start | bytes 1622024 | tf_op jit(solution)/shard_map/ppermute | solution.py:27
  82.0 15.2 %collective-permute-start.20 = (bf16[528,512]{1,0:T(8,128)(2,1)S(1)}, bf16[528,512]{1,0:T(8,128)(2,1)S(1)}, u32[]{:S(2)}, u32[]{:S(2)}) collective-permute-start(bf16[528,512]{1,0:T(8,128)(2,1)S(1)} %get-tuple-element.58.right_ref), channel_id=1, source_target_pairs={{0,16},{16,0},{1,17},{17,1},{2,18},{18,2},{3,19},{19,3},{4,20},{20... | collective-permute-start | bytes 1622024 | tf_op jit(solution)/shard_map/ppermute | solution.py:17
  84.8 24.4 %collective-permute-start.19 = (bf16[512,1024]{1,0:T(8,128)(2,1)S(1)}, bf16[512,1024]{1,0:T(8,128)(2,1)S(1)}, u32[]{:S(2)}, u32[]{:S(2)}) collective-permute-start(bf16[512,1024]{1,0:T(8,128)(2,1)S(1)} %shard_map.76.refs_0_), channel_id=1, source_target_pairs={{1,2},{2,1},{5,6},{6,5},{9,10},{10,9},{13,14},{14,13},{17,18},{18,... | collective-permute-start | bytes 3145736 | tf_op jit(solution)/shard_map/ppermute | solution.py:27
  85.6 20.8 %collective-permute-start.24 = (bf16[512,512]{1,0:T(8,128)(2,1)S(1)}, bf16[512,512]{1,0:T(8,128)(2,1)S(1)}, u32[]{:S(2)}, u32[]{:S(2)}) collective-permute-start(bf16[512,512]{1,0:T(8,128)(2,1)S(1)} %shard_map.75.left_ref), channel_id=1, source_target_pairs={{0,16},{16,0},{1,17},{17,1},{2,18},{18,2},{3,19},{19,3},{4,20},{20... | collective-permute-start | bytes 1572872 | tf_op jit(solution)/shard_map/ppermute | solution.py:17
  97.2 10.6 %collective-permute-start.22 = (bf16[528,512]{1,0:T(8,128)(2,1)S(1)}, bf16[528,512]{1,0:T(8,128)(2,1)S(1)}, u32[]{:S(2)}, u32[]{:S(2)}) collective-permute-start(bf16[528,512]{1,0:T(8,128)(2,1)S(1)} %collective-permute-done.20.rest_1_), channel_id=1, source_target_pairs={{1,9},{2,10},{5,13},{6,14},{9,1},{10,2},{13,5},{14,6},{17,25},{18,... | collective-permute-start | bytes 1622024 | tf_op jit(solution)/shard_map/ppermute | solution.py:23
  106.4 5.8 %collective-permute-start.26 = (bf16[512,512]{1,0:T(8,128)(2,1)S(1)}, bf16[512,512]{1,0:T(8,128)(2,1)S(1)}, u32[]{:S(2)}, u32[]{:S(2)}) collective-permute-start(bf16[512,512]{1,0:T(8,128)(2,1)S(1)} %collective-permute-done.24.rest_0_), channel_id=1, source_target_pairs={{1,9},{2,10},{5,13},{6,14},{9,1},{10,2},{13,5},{14,6},{17,25},{18,... | collective-permute-start | bytes 1572872 | tf_op jit(solution)/shard_map/ppermute | solution.py:23
  107.1 5.8 %collective-permute-start.21 = (bf16[528,512]{1,0:T(8,128)(2,1)S(1)}, bf16[528,512]{1,0:T(8,128)(2,1)S(1)}, u32[]{:S(2)}, u32[]{:S(2)}) collective-permute-start(bf16[528,512]{1,0:T(8,128)(2,1)S(1)} %collective-permute-done.20.rest_1_), channel_id=1, source_target_pairs={{1,5},{2,6},{5,1},{6,2},{9,13},{10,14},{13,9},{14,10},{17,21},{18,... | collective-permute-start | bytes 1622024 | tf_op jit(solution)/shard_map/ppermute | solution.py:23
  107.8 5.1 %collective-permute-start.23 = (bf16[528,512]{1,0:T(8,128)(2,1)S(1)}, bf16[528,512]{1,0:T(8,128)(2,1)S(1)}, u32[]{:S(2)}, u32[]{:S(2)}) collective-permute-start(bf16[528,512]{1,0:T(8,128)(2,1)S(1)} %collective-permute-done.22.rest_3_), channel_id=1, source_target_pairs={{1,5},{2,6},{5,1},{6,2},{9,13},{10,14},{13,9},{14,10},{17,21},{18,... | collective-permute-start | bytes 1622024 | tf_op jit(solution)/shard_map/ppermute | solution.py:23
  108.5 7.6 %collective-permute-start.25 = (bf16[512,512]{1,0:T(8,128)(2,1)S(1)}, bf16[512,512]{1,0:T(8,128)(2,1)S(1)}, u32[]{:S(2)}, u32[]{:S(2)}) collective-permute-start(bf16[512,512]{1,0:T(8,128)(2,1)S(1)} %collective-permute-done.24.rest_0_), channel_id=1, source_target_pairs={{1,5},{2,6},{5,1},{6,2},{9,13},{10,14},{13,9},{14,10},{17,21},{18,... | collective-permute-start | bytes 1572872 | tf_op jit(solution)/shard_map/ppermute | solution.py:23
  112.2 3.9 %collective-permute-start.27 = (bf16[512,512]{1,0:T(8,128)(2,1)S(1)}, bf16[512,512]{1,0:T(8,128)(2,1)S(1)}, u32[]{:S(2)}, u32[]{:S(2)}) collective-permute-start(bf16[512,512]{1,0:T(8,128)(2,1)S(1)} %collective-permute-done.26.rest_2_), channel_id=1, source_target_pairs={{1,5},{2,6},{5,1},{6,2},{9,13},{10,14},{13,9},{14,10},{17,21},{18,... | collective-permute-start | bytes 1572872 | tf_op jit(solution)/shard_map/ppermute | solution.py:23
  114.6 7.8 %collective-permute-start.31 = (bf16[528,512]{1,0:T(8,128)(2,1)S(1)}, bf16[528,512]{1,0:T(8,128)(2,1)S(1)}, u32[]{:S(2)}, u32[]{:S(2)}) collective-permute-start(bf16[528,512]{1,0:T(8,128)(2,1)S(1)} %get-tuple-element.68.refs_1_.rest_1_.refs_0_), channel_id=1, source_target_pairs={{1,9},{2,10},{5,13},{6,14},{9,1},{10,2},{13,5},{14,6},{17,25},{18,... | collective-permute-start | bytes 1622024 | tf_op jit(solution)/shard_map/ppermute | solution.py:23
  115.4 7.8 %collective-permute-start.28 = (bf16[512,512]{1,0:T(8,128)(2,1)S(1)}, bf16[512,512]{1,0:T(8,128)(2,1)S(1)}, u32[]{:S(2)}, u32[]{:S(2)}) collective-permute-start(bf16[512,512]{1,0:T(8,128)(2,1)S(1)} %get-tuple-element.66), channel_id=1, source_target_pairs={{1,2},{2,1},{5,6},{6,5},{9,10},{10,9},{13,14},{14,13},{17,18},{18,... | collective-permute-start | bytes 1572872 | tf_op jit(solution)/shard_map/ppermute | solution.py:27
  117.3 11.9 %collective-permute-start.34 = (bf16[512,512]{1,0:T(8,128)(2,1)S(1)}, bf16[512,512]{1,0:T(8,128)(2,1)S(1)}, u32[]{:S(2)}, u32[]{:S(2)}) collective-permute-start(bf16[512,512]{1,0:T(8,128)(2,1)S(1)} %shard_map.80.refs_0_.rest_0_), channel_id=1, source_target_pairs={{1,9},{2,10},{5,13},{6,14},{9,1},{10,2},{13,5},{14,6},{17,25},{18,... | collective-permute-start | bytes 1572872 | tf_op jit(solution)/shard_map/ppermute | solution.py:23
  118.0 12.0 %collective-permute-start.29 = (bf16[512,512]{1,0:T(8,128)(2,1)S(1)}, bf16[512,512]{1,0:T(8,128)(2,1)S(1)}, u32[]{:S(2)}, u32[]{:S(2)}) collective-permute-start(bf16[512,512]{1,0:T(8,128)(2,1)S(1)} %shard_map.80.refs_0_.rest_0_), channel_id=1, source_target_pairs={{1,2},{2,1},{5,6},{6,5},{9,10},{10,9},{13,14},{14,13},{17,18},{18,... | collective-permute-start | bytes 1572872 | tf_op jit(solution)/shard_map/ppermute | solution.py:27
  118.7 15.0 %collective-permute-start.33 = (bf16[512,512]{1,0:T(8,128)(2,1)S(1)}, bf16[512,512]{1,0:T(8,128)(2,1)S(1)}, u32[]{:S(2)}, u32[]{:S(2)}) collective-permute-start(bf16[512,512]{1,0:T(8,128)(2,1)S(1)} %shard_map.80.refs_0_.rest_0_), channel_id=1, source_target_pairs={{1,5},{2,6},{5,1},{6,2},{9,13},{10,14},{13,9},{14,10},{17,21},{18,... | collective-permute-start | bytes 1572872 | tf_op jit(solution)/shard_map/ppermute | solution.py:23
  129.3 4.5 %collective-permute-start.35 = (bf16[512,512]{1,0:T(8,128)(2,1)S(1)}, bf16[512,512]{1,0:T(8,128)(2,1)S(1)}, u32[]{:S(2)}, u32[]{:S(2)}) collective-permute-start(bf16[512,512]{1,0:T(8,128)(2,1)S(1)} %collective-permute-done.34.rest_2_), channel_id=1, source_target_pairs={{1,5},{2,6},{5,1},{6,2},{9,13},{10,14},{13,9},{14,10},{17,21},{18,... | collective-permute-start | bytes 1572872 | tf_op jit(solution)/shard_map/ppermute | solution.py:23
  130.5 71.1 %collective-permute-start.36 = (bf16[512,512]{1,0:T(8,128)(2,1)S(1)}, bf16[512,512]{1,0:T(8,128)(2,1)S(1)}, u32[]{:S(2)}, u32[]{:S(2)}) collective-permute-start(bf16[512,512]{1,0:T(8,128)(2,1)S(1)} %get-tuple-element.73), channel_id=1, source_target_pairs={{1,0},{2,3},{5,4},{6,7},{9,8},{10,11},{13,12},{14,15},{17,16},{18,... | collective-permute-start | bytes 1572872 | tf_op jit(solution)/shard_map/ppermute | solution.py:35
  135.7 66.8 %collective-permute-start.38 = (f32[1,512]{1,0:T(1,128)S(1)}, f32[1,512]{1,0:T(1,128)S(1)}, u32[]{:S(2)}, u32[]{:S(2)}) collective-permute-start(f32[1,512]{1,0:T(1,128)S(1)} %slice_add_fusion), channel_id=1, source_target_pairs={{1,0},{2,3},{5,4},{6,7},{9,8},{10,11},{13,12},{14,15},{17,16},{18,... | collective-permute-start | bytes 6152 | tf_op jit(solution)/shard_map/ppermute | solution.py:35
  (9 other events, 19.5 us)
